TPU v7x, 32 devices: a whole 2x2x4 slice. The times are simulated.
32 devices in a mesh: gx: 2 (over x), gy: 4 (over y, core), gz: 4 (over z).
Axes of the slice: x: 2, y: 2, z: 4, core: 2. Of those that a mesh axis runs over, the one named last changes fastest.
Arguments:
- field: bfloat16 [64, 32, 64, 256], P(None, 'gz', 'gy', 'gx'), may hold values from -8 to 8
- conv_first: bfloat16 [3, 3, 3, 64, 128], replicated, may hold values from -0.15625 to 0.15625
- norm_gain: float32 [128], replicated, may hold values from 0.5 to 1.5
- norm_shift: float32 [128], replicated, may hold values from -3 to 3
- conv_second: bfloat16 [3, 3, 3, 128, 128], replicated, may hold values from -0.109375 to 0.109375
Outputs:
- result: bfloat16 [128, 16, 32, 128], P(None, 'gz', 'gy', 'gx')
All inputs are finite; a program needn't handle non-finite values.
Results may differ from a plain program's by a relative error of at most 0.0017.
The roundings to bfloat16 on the way count: a program that leaves them out, or rounds other values in their place, can miss the bound.
Values may be sent and summed in bfloat16 or wider, within the bound.
No kernel may reach another device: no remote copies, remote signals or barrier semaphores. Data moves between devices by JAX's collectives and lax.ppermute only.
A program may use at most 128 MiB of HBM per device.

v0:
```python
import functools

import jax
import jax.numpy as jnp
from jax import lax
from jax.experimental import pallas as pl
from jax.experimental.pallas import tpu as pltpu
from jax.sharding import PartitionSpec as P

NEWTON = 5
EPSILON = 1e-05
LEAK = 0.2
F32, BF16 = jnp.float32, jnp.bfloat16
VMEM_LIMIT = 56 * 1024 * 1024


def dot(a, b, dims=((1,), (0,))):
    return lax.dot_general(a, b, (dims, ((), ())), preferred_element_type=F32)


def dot_full(a, b):
    return lax.dot_general(
        a, b, (((1,), (0,)), ((), ())), precision=lax.Precision.HIGHEST, preferred_element_type=F32
    )


def split(value):
    hi = value.astype(BF16)
    lo = (value - hi.astype(F32)).astype(BF16)
    return hi, lo


def iota(shape, dim):
    return lax.broadcasted_iota(jnp.int32, shape, dim)


def relayout_kernel(field_ref, cells_ref, yface_ref, xface_ref, rows_ref):
    cin, _, height, width = field_ref.shape
    half = width // 2
    rows_ref[...] = field_ref[:, 0].astype(F32).reshape(cin * height, width)
    out = iota((width, width), 0)
    source = jnp.where(out < half, 2 * out, 2 * (out - half) + 1)
    pick = (source == iota((width, width), 1)).astype(F32).astype(BF16)
    last = []
    for pair in range(height // 4):
        lines = [rows_ref[pl.ds(4 * pair + k, cin, stride=height), :] for k in range(4)]
        block = jnp.concatenate(lines, axis=0).astype(BF16)
        turned = dot(pick, block, ((1,), (1,)))
        for k in range(2):
            row = (2 * pair + k) * half
            lanes = slice(2 * cin * k, 2 * cin * (k + 1))
            even = turned[:half, lanes]
            odd = turned[half:, lanes]
            cells_ref[0, row : row + half, : 2 * cin] = even.astype(BF16)
            cells_ref[0, row : row + half, 2 * cin :] = odd.astype(BF16)
            last.append(odd[half - 1 :, :])
    yface_ref[0] = jnp.concatenate([even[:, cin:], odd[:, cin:]], axis=1).astype(BF16)
    xface_ref[0] = jnp.concatenate(last, axis=0).astype(BF16)


def relayout(field):
    cin, depth, height, width = field.shape
    half, rows = width // 2, height // 2 * (width // 2)
    return pl.pallas_call(
        relayout_kernel,
        grid=(depth,),
        in_specs=[pl.BlockSpec((cin, 1, height, width), lambda z: (0, z, 0, 0))],
        out_specs=[
            pl.BlockSpec((1, rows, 4 * cin), lambda z: (z, 0, 0)),
            pl.BlockSpec((1, half, 2 * cin), lambda z: (z, 0, 0)),
            pl.BlockSpec((1, height // 2, 2 * cin), lambda z: (z, 0, 0)),
        ],
        out_shape=[
            jax.ShapeDtypeStruct((depth, rows, 4 * cin), BF16),
            jax.ShapeDtypeStruct((depth, half, 2 * cin), BF16),
            jax.ShapeDtypeStruct((depth, height // 2, 2 * cin), BF16),
        ],
        scratch_shapes=[pltpu.VMEM((cin * height, width), F32)],
        compiler_params=pltpu.CompilerParams(vmem_limit_bytes=VMEM_LIMIT),
        name="relayout",
    )(field)


def features_kernel(
    cells_ref, zhalo_ref, yhalo_ref, xhalo_ref, w_ref, feat_ref, mom_ref, xface_ref, w4_ref, wy_ref, wx_ref, acc_ref
):
    depth = cells_ref.shape[0] // 2
    cin, cout = w_ref.shape[3:]
    rows = cells_ref.shape[1]
    half = yhalo_ref.shape[1]
    lines = rows // half
    w4_ref[...] = jnp.zeros(w4_ref.shape, BF16)
    wx_ref[...] = jnp.zeros(wx_ref.shape, BF16)
    wy_ref[...] = jnp.zeros(wy_ref.shape, BF16)
    for dz in range(3):
        for px in range(2):
            for py in range(2):
                k = (2 * px + py) * cin
                w4_ref[dz, k : k + cin, :cout] = w_ref[dz, 1 + py, 1 + px]
                if py == 1:
                    w4_ref[dz, k : k + cin, cout : 2 * cout] = w_ref[dz, 0, 1 + px]
                if px == 1:
                    w4_ref[dz, k : k + cin, 2 * cout : 3 * cout] = w_ref[dz, 1 + py, 0]
                if px == 1 and py == 1:
                    w4_ref[dz, k : k + cin, 3 * cout :] = w_ref[dz, 0, 0]
            k = (2 * dz + px) * cin
            wy_ref[k : k + cin, :cout] = w_ref[dz, 0, 1 + px]
        k = (2 * dz + 1) * cin
        wy_ref[k : k + cin, cout:] = w_ref[dz, 0, 0]
        k = 4 * dz * cin
        wx_ref[k : k + cin, :] = w_ref[dz, 1, 0]
        wx_ref[k + cin : k + 2 * cin, :] = w_ref[dz, 2, 0]
        wx_ref[k + 3 * cin : k + 4 * cin, :] = w_ref[dz, 0, 0]
    first = iota((half, cout), 0) == 0
    xh = xhalo_ref[...].astype(F32)
    total = jnp.zeros((1, cout), F32)
    for zo in range(depth):
        before = zhalo_ref[...] if zo == 0 else cells_ref[2 * zo - 1]
        acc_ref[...] = dot(
            jnp.concatenate([before, cells_ref[2 * zo], cells_ref[2 * zo + 1]], axis=1),
            w4_ref[...].reshape(3 * 4 * cin, 4 * cout),
        )
        ysum = dot(jnp.concatenate([yhalo_ref[2 * zo + dz] for dz in range(3)], axis=1), wy_ref[...])
        xparts = []
        for dz in range(3):
            xparts += [xh[2 * zo + dz, 1 : lines + 1], xh[2 * zo + dz, :lines]]
        xsum = dot(jnp.concatenate(xparts, axis=1).astype(BF16), wx_ref[...])
        for line in range(lines):
            here = pl.ds(line * half, half)
            straight = acc_ref[here, :cout]
            shifted = acc_ref[here, 2 * cout : 3 * cout]
            if line == 0:
                straight = straight + ysum[:, :cout]
                shifted = shifted + ysum[:, cout:]
            else:
                above = pl.ds((line - 1) * half, half)
                straight = straight + acc_ref[above, cout : 2 * cout]
                shifted = shifted + acc_ref[above, 3 * cout :]
            moved = jnp.where(first, xsum[line : line + 1], pltpu.roll(shifted, 1, 0))
            value = straight + moved
            feat_ref[zo, here, :] = value
            xface_ref[0, zo * lines + line : zo * lines + line + 1, :] = value[:1]
            xface_ref[1, zo * lines + line : zo * lines + line + 1, :] = value[half - 1 :]
            total = total + jnp.sum(value, axis=0, keepdims=True)
    count = depth * rows
    mean = total * (1.0 / count)
    gram = jnp.zeros((cout, 2 * cout), F32)
    for zo in range(depth):
        hi, lo = split(feat_ref[zo] - mean)
        gram = gram + dot(hi, jnp.concatenate([hi, lo], axis=1), ((0,), (0,)))
    cross = gram[:, cout:]
    gram = gram[:, :cout] + cross + cross.T
    eye = iota((cout, cout), 0) == iota((cout, cout), 1)
    column = jnp.sum(jnp.where(eye, jnp.broadcast_to(mean, (cout, cout)), 0.0), axis=1, keepdims=True)
    gram = gram + (column * mean) * float(count)
    left = iota((cout // 2, cout), 1) < cout // 2
    mom_ref[: cout // 2, :] = jnp.where(left, gram[: cout // 2], gram[cout // 2 :])
    mom_ref[cout // 2 :, :] = jnp.broadcast_to(total, (8, cout))


def features_of(cells, zhalo, yhalo, xhalo, weights):
    depth, rows, wide = cells.shape
    cin, cout = weights.shape[3:]
    half = yhalo.shape[1]
    vmem = pl.BlockSpec(memory_space=pltpu.VMEM)
    return pl.pallas_call(
        features_kernel,
        in_specs=[vmem] * 5,
        out_specs=[vmem] * 3,
        out_shape=[
            jax.ShapeDtypeStruct((depth // 2, rows, cout), F32),
            jax.ShapeDtypeStruct((cout // 2 + 8, cout), F32),
            jax.ShapeDtypeStruct((2, depth // 2 * rows // half, cout), F32),
        ],
        scratch_shapes=[
            pltpu.VMEM((3, wide, 4 * cout), BF16),
            pltpu.VMEM((6 * cin, 2 * cout), BF16),
            pltpu.VMEM((12 * cin, cout), BF16),
            pltpu.VMEM((rows, 4 * cout), F32),
        ],
        compiler_params=pltpu.CompilerParams(vmem_limit_bytes=VMEM_LIMIT),
        name="features",
    )(cells, zhalo, yhalo, xhalo, weights)


def block_kernel(
    total_cells,
    inside_ref, mom_ref, gain_ref, shift_ref, feat_ref, xb_ref, xa_ref, yb_ref, ya_ref, zb_ref, za_ref, w_ref,
    out_ref, pad_ref, wide_ref,
):
    depth, rows, cout = feat_ref.shape
    lines = xb_ref.shape[0] // depth
    half = rows // lines
    group = cout // 2
    square = (cout, cout)
    ri, ci = iota(square, 0), iota(square, 1)
    eye = ri == ci
    same = (ri < group) == (ci < group)
    moments = mom_ref[:group, :] * (1.0 / total_cells)
    average = mom_ref[group : group + 1, :] * (1.0 / total_cells)
    column = jnp.sum(jnp.where(eye, jnp.broadcast_to(average, square), 0.0), axis=1, keepdims=True)
    cov = jnp.concatenate([moments, moments], axis=0) - column * average
    cov = jnp.where(same, cov, 0.0) + jnp.where(eye, EPSILON, 0.0)
    diag = jnp.where(eye, cov, 0.0)
    trace0 = jnp.sum(jnp.sum(diag[:group], axis=1, keepdims=True), axis=0, keepdims=True)
    trace1 = jnp.sum(jnp.sum(diag[group:], axis=1, keepdims=True), axis=0, keepdims=True)
    trace = jnp.where(ri < group, trace0, trace1)
    scaled = cov / trace
    mat = jnp.where(eye, 1.5, 0.0) - 0.5 * scaled
    for _ in range(NEWTON - 1):
        mat = 1.5 * mat - 0.5 * dot_full(dot_full(mat, mat), dot_full(mat, scaled))
    gain = jnp.sum(jnp.where(eye, jnp.broadcast_to(gain_ref[...], square), 0.0), axis=1, keepdims=True)
    mat = mat / jnp.sqrt(trace) * gain
    hi, lo = split(mat)
    mixer = jnp.concatenate(
        [jnp.concatenate([hi, hi], axis=1), jnp.concatenate([lo, jnp.zeros_like(lo)], axis=1)], axis=0
    )
    shift = shift_ref[...]

    def whiten(value):
        hi, lo = split(value - average)
        both = dot(jnp.concatenate([hi, lo], axis=1), mixer, ((1,), (1,)))
        scaled = both[:, :cout] + both[:, cout:] + shift
        return jnp.where(scaled >= 0, scaled, LEAK * scaled)

    base = 8
    xb_in, xa_in, yb_in, ya_in, zb_in, za_in = (inside_ref[k] != 0 for k in range(6))

    def put(zp, yp, middle, ends, inside):
        left, right = ends
        pad_ref[zp, yp, base : base + half, :] = jnp.where(inside, middle, 0.0) if inside is not True else middle
        l_in = xb_in if inside is True else jnp.logical_and(xb_in, inside)
        r_in = xa_in if inside is True else jnp.logical_and(xa_in, inside)
        pad_ref[zp, yp, base - 1 : base, :] = jnp.where(l_in, left, 0.0)
        pad_ref[zp, yp, base + half : base + half + 1, :] = jnp.where(r_in, right, 0.0)

    xb, xa = whiten(xb_ref[...]), whiten(xa_ref[...])
    yb, ya = whiten(yb_ref[...]), whiten(ya_ref[...])
    for z in range(depth):
        plane = whiten(feat_ref[z])
        for y in range(lines):
            k = z * lines + y
            put(z + 1, y + 1, plane[y * half : (y + 1) * half], (xb[k : k + 1], xa[k : k + 1]), True)
        for yp, side, inside in ((0, yb, yb_in), (lines + 1, ya, ya_in)):
            k = depth * half + z
            put(z + 1, yp, side[z * half : (z + 1) * half], (side[k : k + 1], side[k + depth : k + depth + 1]), inside)
    for zp, ref, inside in ((0, zb_ref, zb_in), (depth + 1, za_ref, za_in)):
        plane = whiten(ref[...])
        ends = rows + 2 * half
        for y in range(lines):
            k = ends + y
            put(zp, y + 1, plane[y * half : (y + 1) * half], (plane[k : k + 1], plane[k + lines : k + lines + 1]), inside)
        for n, (yp, y_in) in enumerate(((0, yb_in), (lines + 1, ya_in))):
            k = ends + 2 * lines + 2 * n
            put(
                zp, yp, plane[rows + n * half : rows + (n + 1) * half], (plane[k : k + 1], plane[k + 1 : k + 2]),
                jnp.logical_and(inside, y_in),
            )
    for zp in range(depth + 2):
        for yp in range(lines + 2):
            for dx in range(3):
                wide_ref[zp, yp * half : (yp + 1) * half, dx * cout : (dx + 1) * cout] = pad_ref[
                    zp, yp, base - 1 + dx : base - 1 + dx + half, :
                ].astype(BF16)
    for z in range(depth):
        acc = jnp.zeros((rows, cout), F32)
        for dz in range(3):
            for dy in range(3):
                acc = acc + dot(wide_ref[z + dz, dy * half : dy * half + rows, :], w_ref[dz, dy])
        turned = jnp.stack([acc[y * half : (y + 1) * half].T for y in range(lines)], axis=0)
        out_ref[:, z] = jnp.swapaxes(turned, 0, 1).astype(BF16)


def block(total_cells, inside, moments, gain, shift, feats, xb, xa, yb, ya, zb, za, weights):
    depth, rows, cout = feats.shape
    lines = xb.shape[0] // depth
    half = rows // lines
    vmem = pl.BlockSpec(memory_space=pltpu.VMEM)
    return pl.pallas_call(
        functools.partial(block_kernel, total_cells),
        in_specs=[pl.BlockSpec(memory_space=pltpu.SMEM)] + [vmem] * 11,
        out_specs=vmem,
        out_shape=jax.ShapeDtypeStruct((cout, depth, lines, half), BF16),
        scratch_shapes=[
            pltpu.VMEM((depth + 2, lines + 2, half + 16, cout), F32),
            pltpu.VMEM((depth + 2, (lines + 2) * half, 3 * cout), BF16),
        ],
        compiler_params=pltpu.CompilerParams(vmem_limit_bytes=VMEM_LIMIT),
        name="block",
    )(inside, moments, gain, shift, feats, xb, xa, yb, ya, zb, za, weights)


def exchange(axis, moments, low, high):
    size = lax.axis_size(axis)
    if size == 1:
        return moments, jnp.zeros_like(low), jnp.zeros_like(high)
    if size & (size - 1):
        up = [(i, i + 1) for i in range(size - 1)]
        before = lax.ppermute(high, axis, up)
        after = lax.ppermute(low, axis, [(j, i) for i, j in up])
        return lax.psum(moments, axis), before, after
    even = lax.axis_index(axis) % 2 == 0
    count = moments.shape[0]
    swap = [(i, i ^ 1) for i in range(size)]
    got = lax.ppermute(jnp.concatenate([moments, jnp.where(even, high, low)], axis=0), axis, swap)
    moments, one = moments + got[:count], got[count:]
    if size == 2:
        return moments, one, one
    swap = [(i, (i + 1 if i % 2 else i - 1) % size) for i in range(size)]
    got = lax.ppermute(jnp.concatenate([moments, jnp.where(even, low, high)], axis=0), axis, swap)
    moments, two = moments + got[:count], got[count:]
    step = 4
    while step < size:
        moments = moments + lax.ppermute(moments, axis, [(i, (i + step) % size) for i in range(size)])
        step *= 2
    return moments, jnp.where(even, two, one), jnp.where(even, one, two)


def up_pairs(axis):
    return [(i, i + 1) for i in range(lax.axis_size(axis) - 1)]


def body(field, conv_first, norm_gain, norm_shift, conv_second):
    cin, depth_in, height_in, width_in = field.shape
    cout = conv_second.shape[-1]
    depth, lines, half = depth_in // 2, height_in // 2, width_in // 2
    cells, yface, xface = relayout(field)

    last = cells[-1]
    zhalo = lax.ppermute(last, "gz", up_pairs("gz"))
    yhalo = lax.ppermute(yface, "gy", up_pairs("gy"))
    nz = lax.axis_size("gz")
    diagonal = [(a * nz + b, (a + 1) * nz + b + 1) for a, _ in up_pairs("gy") for b, _ in up_pairs("gz")]
    yzhalo = lax.ppermute(yface[-1], ("gy", "gz"), diagonal)
    yhalo = jnp.concatenate([yzhalo[None], yhalo], axis=0)
    ztop = zhalo.reshape(lines, half, 4 * cin)[:, -1, 2 * cin :]
    xown = jnp.concatenate([ztop[None], xface], axis=0)
    ytop = yhalo[:, -1, cin:]
    ytop = jnp.concatenate([jnp.zeros_like(ytop), ytop], axis=1)
    xsend = jnp.concatenate([ytop[:, None], xown], axis=1)
    xsend = jnp.pad(xsend, ((0, 0), (0, (-xsend.shape[1]) % 16), (0, 0)))
    xhalo = lax.ppermute(xsend, "gx", up_pairs("gx"))

    feats, moments, faces = features_of(cells, zhalo, yhalo, xhalo, conv_first)
    rows = lines * half
    moments, xb, xa = exchange("gx", moments, faces[0], faces[1])
    xb3, xa3 = xb.reshape(depth, lines, cout), xa.reshape(depth, lines, cout)
    grid = feats.reshape(depth, lines, half, cout)

    def yside(y):
        return jnp.concatenate([grid[:, y].reshape(depth * half, cout), xb3[:, y], xa3[:, y]], axis=0)

    moments, yb, ya = exchange("gy", moments, yside(0), yside(lines - 1))

    def zside(z):
        k = depth * half + z
        own = [feats[z], yb[z * half : (z + 1) * half], ya[z * half : (z + 1) * half], xb3[z], xa3[z]]
        own += [yb[k : k + 1], yb[k + depth : k + depth + 1], ya[k : k + 1], ya[k + depth : k + depth + 1]]
        own += [jnp.zeros((4, cout), F32)]
        return jnp.concatenate(own, axis=0)

    moments, zb, za = exchange("gz", moments, zside(0), zside(depth - 1))
    inside = []
    for axis in ("gx", "gy", "gz"):
        place = lax.axis_index(axis)
        inside += [place > 0, place < lax.axis_size(axis) - 1]
    inside = jnp.stack(inside).astype(jnp.int32)
    total_cells = rows * depth * lax.axis_size("gx") * lax.axis_size("gy") * lax.axis_size("gz")
    return block(
        total_cells, inside, moments, norm_gain[None], norm_shift[None], feats, xb, xa, yb, ya, zb, za,
        conv_second.reshape(3, 3, 3 * cout, cout),
    )


def solution(mesh):
    in_specs = (P(None, "gz", "gy", "gx"), P(), P(), P(), P())
    out_specs = P(None, "gz", "gy", "gx")
    return jax.shard_map(body, mesh=mesh, in_specs=in_specs, out_specs=out_specs, check_vma=False)
```

profile of v0, /device:TPU:14, one launch (start us, length us, event | category | flops | bytes accessed | tf_op | source)
XLA Modules:
  0.0 92.8 jit_solution(6980965183286675372)
XLA Ops:
  0.0 6.9 %relayout.1 = (bf16[8,512,256]{2,1,0:T(8,128)(2,1)}, bf16[8,64,128]{2,1,0:T(8,128)(2,1)}, bf16[8,8,128]{2,1,0:T(8,128)(2,1)}) custom-call(bf16[64,8,16,128]{3,2,1,0:T(8,128)(2,1)} %field_ref.1), custom_call_target="tpu_custom_call" | custom-call | tf_op jit(solution)/shard_map/relayout/pallas_call | solution.py:64
  6.9 1.9 %collective-permute-start.2 = (bf16[8,64,128]{2,1,0:T(8,128)(2,1)}, bf16[8,64,128]{2,1,0:T(8,128)(2,1)S(1)}, u32[]{:S(2)}, u32[]{:S(2)}) collective-permute-start(bf16[8,64,128]{2,1,0:T(8,128)(2,1)} %get-tuple-element.12), channel_id=1, source_target_pairs={{0,4},{4,8},{8,12},{1,5},{5,9},{9,13},{2,6},{6,10},{10,14},{3,7},{... | collective-permute-start | bytes 393224 | tf_op jit(solution)/shard_map/ppermute | solution.py:331
  8.8 1.0 %slice_bitcast_fusion.2 = bf16[512,256]{1,0:T(8,128)(2,1)S(1)} fusion(bf16[8,512,256]{2,1,0:T(8,128)(2,1)} %get-tuple-element.11.cells_ref), kind=kLoop, calls=%fused_computation.6 | loop fusion | bytes 524288 | tf_op jit(solution)/shard_map/squeeze | solution.py:329
  9.8 3.5 %collective-permute-start = (bf16[512,256]{1,0:T(8,128)(2,1)S(1)}, bf16[512,256]{1,0:T(8,128)(2,1)S(1)}, u32[]{:S(2)}, u32[]{:S(2)}) collective-permute-start(bf16[512,256]{1,0:T(8,128)(2,1)S(1)} %slice_bitcast_fusion.2), channel_id=1, source_target_pairs={{0,1},{1,2},{2,3},{4,5},{5,6},{6,7},{8,9},{9,10},{10,11},{12,13},{... | collective-permute-start | bytes 786440 | tf_op jit(solution)/shard_map/ppermute | solution.py:330
  13.3 0.7 slice_bitcast_fusion.3
  14.0 2.0 %collective-permute-start.1 = (bf16[64,128]{1,0:T(8,128)(2,1)S(1)}, bf16[64,128]{1,0:T(8,128)(2,1)S(1)}, u32[]{:S(2)}, u32[]{:S(2)}) collective-permute-start(bf16[64,128]{1,0:T(8,128)(2,1)S(1)} %slice_bitcast_fusion.3), channel_id=1, source_target_pairs={{0,5},{1,6},{2,7},{4,9},{5,10},{6,11},{8,13},{9,14},{10,15},{16,21... | collective-permute-start | bytes 49160 | tf_op jit(solution)/shard_map/ppermute | solution.py:334
  16.1 4.9 %collective-permute-done.1 = bf16[64,128]{1,0:T(8,128)(2,1)S(1)} collective-permute-done((bf16[64,128]{1,0:T(8,128)(2,1)S(1)}, bf16[64,128]{1,0:T(8,128)(2,1)S(1)}, u32[]{:S(2)}, u32[]{:S(2)}) %collective-permute-start.1) | collective-permute-done | bytes 16416 | tf_op jit(solution)/shard_map/ppermute | solution.py:334
  21.0 0.0 collective-permute-done.2
  21.0 0.1 fusion.7
  21.1 0.1 pad_bitcast_fusion
  21.2 0.0 collective-permute-done.zhalo_ref
  21.2 0.0 copy-start.3
  21.2 0.8 fusion.5
  22.0 1.3 %collective-permute-start.3 = (bf16[9,16,128]{2,1,0:T(8,128)(2,1)S(1)}, bf16[9,16,128]{2,1,0:T(8,128)(2,1)S(1)}, u32[]{:S(2)}, u32[]{:S(2)}) collective-permute-start(bf16[9,16,128]{2,1,0:T(8,128)(2,1)S(1)} %fusion.5), channel_id=1, source_target_pairs={{0,16},{1,17},{2,18},{3,19},{4,20},{5,21},{6,22},{7,23},{8,24},{9,... | collective-permute-start | bytes 110600 | tf_op jit(solution)/shard_map/ppermute | solution.py:342
  23.3 0.7 pad_maximum_fusion.2.yhalo_ref
  24.0 3.9 %collective-permute-done.3.xhalo_ref = bf16[9,16,128]{2,1,0:T(8,128)(2,1)S(1)} collective-permute-done((bf16[9,16,128]{2,1,0:T(8,128)(2,1)S(1)}, bf16[9,16,128]{2,1,0:T(8,128)(2,1)S(1)}, u32[]{:S(2)}, u32[]{:S(2)}) %collective-permute-start.3) | collective-permute-done | bytes 36896 | tf_op jit(solution)/shard_map/ppermute | solution.py:342
  27.8 0.0 copy-done.3
  27.8 0.0 copy-start.4
  27.8 0.6 copy-done.4
  28.5 5.3 %features.1 = (f32[4,512,128]{2,1,0:T(8,128)}, f32[72,128]{1,0:T(8,128)}, f32[2,32,128]{2,1,0:T(8,128)}) custom-call(bf16[8,512,256]{2,1,0:T(8,128)(2,1)} %get-tuple-element.11.cells_ref, bf16[512,256]{1,0:T(8,128)(2,1)} %copy-done.3, bf16[9,64,128]{2,1,0:T(8,128)(2,1)} %pad_maximum_fusion.2.yhalo_ref, bf16[9,16,128]{2,1,0:T(8,128)(2,1)} %copy-done.4, ...), custom_call_target="tpu_custom_call" | custom-call | tf_op jit(solution)/shard_map/features/pallas_call | solution.py:166
  33.8 0.0 copy-start
  33.8 0.8 select_bitcast_fusion
  34.6 0.8 pad_maximum_fusion.7
  35.4 0.0 collective-permute-start.4
  35.4 1.0 %fusion.8 = (f32[4,1,64,128]{3,2,1,0:T(8,128)S(1)}, f32[4,1,64,128]{3,2,1,0:T(8,128)S(1)}) fusion(f32[4,8,64,128]{3,2,1,0:T(8,128)} %bitcast.44), kind=kLoop, calls=%fused_computation.39 | loop fusion | bytes 524288 | tf_op jit(solution)/shard_map/slice | solution.py:351
  36.4 3.1 %collective-permute-done.4 = f32[104,128]{1,0:T(8,128)S(1)} collective-permute-done((f32[104,128]{1,0:T(8,128)S(1)}, f32[104,128]{1,0:T(8,128)S(1)}, u32[]{:S(2)}, u32[]{:S(2)}) %collective-permute-start.4) | collective-permute-done | bytes 53280 | tf_op jit(solution)/shard_map/ppermute | solution.py:305
  39.5 0.6 fusion.13
  40.1 0.8 slice_add_fusion.4
  40.9 0.1 collective-permute-start.5
  41.0 0.0 copy-done
  41.1 1.3 %collective-permute-done.5 = f32[336,128]{1,0:T(8,128)S(1)} collective-permute-done((f32[336,128]{1,0:T(8,128)S(1)}, f32[336,128]{1,0:T(8,128)S(1)}, u32[]{:S(2)}, u32[]{:S(2)}) %collective-permute-start.5) | collective-permute-done | bytes 172064 | tf_op jit(solution)/shard_map/ppermute | solution.py:305
  42.4 0.1 collective-permute-start.6
  42.5 6.3 %collective-permute-done.6 = f32[336,128]{1,0:T(8,128)S(1)} collective-permute-done((f32[336,128]{1,0:T(8,128)S(1)}, f32[336,128]{1,0:T(8,128)S(1)}, u32[]{:S(2)}, u32[]{:S(2)}) %collective-permute-start.6) | collective-permute-done | bytes 172064 | tf_op jit(solution)/shard_map/ppermute | solution.py:310
  48.9 0.0 copy-start.1
  48.9 0.0 copy-start.2
  49.0 0.1 broadcast_select_fusion
  49.2 0.1 collective-permute-start.7
  49.2 10.8 %collective-permute-done.7 = f32[736,128]{1,0:T(8,128)S(1)} collective-permute-done((f32[736,128]{1,0:T(8,128)S(1)}, f32[736,128]{1,0:T(8,128)S(1)}, u32[]{:S(2)}, u32[]{:S(2)}) %collective-permute-start.7) | collective-permute-done | bytes 376864 | tf_op jit(solution)/shard_map/ppermute | solution.py:305
  60.1 0.0 copy-done.1
  60.1 0.0 copy-done.2
  60.1 1.6 %collective-permute-start.8 = (f32[736,128]{1,0:T(8,128)S(1)}, f32[736,128]{1,0:T(8,128)S(1)}, u32[]{:S(2)}, u32[]{:S(2)}) collective-permute-start(f32[736,128]{1,0:T(8,128)S(1)} %pad_maximum_fusion.1), channel_id=1, source_target_pairs={{0,3},{1,2},{2,1},{3,0},{4,7},{5,6},{6,5},{7,4},{8,11},{9,10},{10,... | collective-permute-start | bytes 1130504 | tf_op jit(solution)/shard_map/ppermute | solution.py:310
  61.7 0.1 stack.27
  61.8 0.5 convert_element_type.5.inside_ref
  62.4 15.8 %collective-permute-done.8 = f32[736,128]{1,0:T(8,128)S(1)} collective-permute-done((f32[736,128]{1,0:T(8,128)S(1)}, f32[736,128]{1,0:T(8,128)S(1)}, u32[]{:S(2)}, u32[]{:S(2)}) %collective-permute-start.8) | collective-permute-done | bytes 376864 | tf_op jit(solution)/shard_map/ppermute | solution.py:310
  78.2 0.9 slice_select_fusion
  79.1 0.6 slice_add_fusion.mom_ref
  79.8 10.0 %block.1 = bf16[128,4,8,64]{3,2,1,0:T(8,128)(2,1)} custom-call(s32[6]{0:T(128)} %convert_element_type.5.inside_ref, f32[72,128]{1,0:T(8,128)} %slice_add_fusion.mom_ref, f32[1,128]{1,0:T(1,128)} %bitcast.55, f32[1,128]{1,0:T(1,128)} %bitcast.56, f32[4,512,128]{2,1,0:T(8,128)} %get-tuple-element.16.feat_ref, f32[32,128]{1,0:T(8,128)} %get-tuple-element.41.xb_ref.xa_ref, ...), custom_call_target="tpu_custom_call" | custom-call | tf_op jit(solution)/shard_map/block/pallas_call | solution.py:279
  89.8 3.0 %copy.24 = bf16[128,4,8,64]{0,3,2,1:T(8,128)(2,1)} copy(bf16[128,4,8,64]{3,2,1,0:T(8,128)(2,1)} %block.1) | data formatting | bytes 1048576 | tf_op jit(solution)/shard_map/block/pallas_call | solution.py:279
  (21 shorter events, 0.3 us)
Async XLA Ops:
  6.9 14.1 %collective-permute-start.2 = (bf16[8,64,128]{2,1,0:T(8,128)(2,1)}, bf16[8,64,128]{2,1,0:T(8,128)(2,1)S(1)}, u32[]{:S(2)}, u32[]{:S(2)}) collective-permute-start(bf16[8,64,128]{2,1,0:T(8,128)(2,1)} %get-tuple-element.12), channel_id=1, source_target_pairs={{0,4},{4,8},{8,12},{1,5},{5,9},{9,13},{2,6},{6,10},{10,14},{3,7},{... | collective-permute-start | bytes 393224 | tf_op jit(solution)/shard_map/ppermute | solution.py:331
  9.8 11.4 %collective-permute-start = (bf16[512,256]{1,0:T(8,128)(2,1)S(1)}, bf16[512,256]{1,0:T(8,128)(2,1)S(1)}, u32[]{:S(2)}, u32[]{:S(2)}) collective-permute-start(bf16[512,256]{1,0:T(8,128)(2,1)S(1)} %slice_bitcast_fusion.2), channel_id=1, source_target_pairs={{0,1},{1,2},{2,3},{4,5},{5,6},{6,7},{8,9},{9,10},{10,11},{12,13},{... | collective-permute-start | bytes 786440 | tf_op jit(solution)/shard_map/ppermute | solution.py:330
  14.0 7.0 %collective-permute-start.1 = (bf16[64,128]{1,0:T(8,128)(2,1)S(1)}, bf16[64,128]{1,0:T(8,128)(2,1)S(1)}, u32[]{:S(2)}, u32[]{:S(2)}) collective-permute-start(bf16[64,128]{1,0:T(8,128)(2,1)S(1)} %slice_bitcast_fusion.3), channel_id=1, source_target_pairs={{0,5},{1,6},{2,7},{4,9},{5,10},{6,11},{8,13},{9,14},{10,15},{16,21... | collective-permute-start | bytes 49160 | tf_op jit(solution)/shard_map/ppermute | solution.py:334
  21.2 6.7 %copy-start.3 = (bf16[512,256]{1,0:T(8,128)(2,1)}, bf16[512,256]{1,0:T(8,128)(2,1)S(1)}, u32[]{:S(2)}) copy-start(bf16[512,256]{1,0:T(8,128)(2,1)S(1)} %collective-permute-done.zhalo_ref) | copy-start | bytes 786436
  22.0 5.9 %collective-permute-start.3 = (bf16[9,16,128]{2,1,0:T(8,128)(2,1)S(1)}, bf16[9,16,128]{2,1,0:T(8,128)(2,1)S(1)}, u32[]{:S(2)}, u32[]{:S(2)}) collective-permute-start(bf16[9,16,128]{2,1,0:T(8,128)(2,1)S(1)} %fusion.5), channel_id=1, source_target_pairs={{0,16},{1,17},{2,18},{3,19},{4,20},{5,21},{6,22},{7,23},{8,24},{9,... | collective-permute-start | bytes 110600 | tf_op jit(solution)/shard_map/ppermute | solution.py:342
  27.8 0.6 copy-start.4
  33.8 7.2 %copy-start = (f32[4,512,128]{2,1,0:T(8,128)S(1)}, f32[4,512,128]{2,1,0:T(8,128)}, u32[]{:S(2)}) copy-start(f32[4,512,128]{2,1,0:T(8,128)} %get-tuple-element.16.feat_ref) | copy-start | bytes 3145732
  35.4 4.1 %collective-permute-start.4 = (f32[104,128]{1,0:T(8,128)S(1)}, f32[104,128]{1,0:T(8,128)S(1)}, u32[]{:S(2)}, u32[]{:S(2)}) collective-permute-start(f32[104,128]{1,0:T(8,128)S(1)} %pad_maximum_fusion.7), channel_id=1, source_target_pairs={{0,16},{16,0},{1,17},{17,1},{2,18},{18,2},{3,19},{19,3},{4,20},{20... | collective-permute-start | bytes 159752 | tf_op jit(solution)/shard_map/ppermute | solution.py:305
  40.9 1.5 %collective-permute-start.5 = (f32[336,128]{1,0:T(8,128)S(1)}, f32[336,128]{1,0:T(8,128)S(1)}, u32[]{:S(2)}, u32[]{:S(2)}) collective-permute-start(f32[336,128]{1,0:T(8,128)S(1)} %pad_maximum_fusion.3), channel_id=1, source_target_pairs={{0,4},{4,0},{8,12},{12,8},{1,5},{5,1},{9,13},{13,9},{2,6},{6,2},{1... | collective-permute-start | bytes 516104 | tf_op jit(solution)/shard_map/ppermute | solution.py:305
  42.4 6.4 %collective-permute-start.6 = (f32[336,128]{1,0:T(8,128)S(1)}, f32[336,128]{1,0:T(8,128)S(1)}, u32[]{:S(2)}, u32[]{:S(2)}) collective-permute-start(f32[336,128]{1,0:T(8,128)S(1)} %pad_maximum_fusion.4), channel_id=1, source_target_pairs={{0,12},{4,8},{8,4},{12,0},{1,13},{5,9},{9,5},{13,1},{2,14},{6,10},... | collective-permute-start | bytes 516104 | tf_op jit(solution)/shard_map/ppermute | solution.py:310
  48.9 11.2 %copy-start.1 = (f32[264,128]{1,0:T(8,128)}, f32[264,128]{1,0:T(8,128)S(1)}, u32[]{:S(2)}) copy-start(f32[264,128]{1,0:T(8,128)S(1)} %get-tuple-element.25.ya_ref) | copy-start | bytes 405508
  48.9 11.2 %copy-start.2 = (f32[264,128]{1,0:T(8,128)}, f32[264,128]{1,0:T(8,128)S(1)}, u32[]{:S(2)}) copy-start(f32[264,128]{1,0:T(8,128)S(1)} %get-tuple-element.26.yb_ref) | copy-start | bytes 405508
  49.2 10.9 %collective-permute-start.7 = (f32[736,128]{1,0:T(8,128)S(1)}, f32[736,128]{1,0:T(8,128)S(1)}, u32[]{:S(2)}, u32[]{:S(2)}) collective-permute-start(f32[736,128]{1,0:T(8,128)S(1)} %pad_maximum_fusion), channel_id=1, source_target_pairs={{0,1},{1,0},{2,3},{3,2},{4,5},{5,4},{6,7},{7,6},{8,9},{9,8},{10,11... | collective-permute-start | bytes 1130504 | tf_op jit(solution)/shard_map/ppermute | solution.py:305
  60.1 18.1 %collective-permute-start.8 = (f32[736,128]{1,0:T(8,128)S(1)}, f32[736,128]{1,0:T(8,128)S(1)}, u32[]{:S(2)}, u32[]{:S(2)}) collective-permute-start(f32[736,128]{1,0:T(8,128)S(1)} %pad_maximum_fusion.1), channel_id=1, source_target_pairs={{0,3},{1,2},{2,1},{3,0},{4,7},{5,6},{6,5},{7,4},{8,11},{9,10},{10,... | collective-permute-start | bytes 1130504 | tf_op jit(solution)/shard_map/ppermute | solution.py:310
where the time goes:
time: 93.5 us; the launch traced here: 92.8 us
  waiting for transfers between devices  46.3 us (50%)
  Pallas kernels  22.2 us (24%)
  starting transfers between devices  10.5 us (11%)
  local copies, waits for them, and re-layouts  7.29 us (8%)
  other arithmetic  6.19 us (7%)
    ppermute x2, waiting for transfers between devices, exchange(): lax.ppermute(jnp.concatenate([moments, jnp.where(even, low, high)], axis=...  22.2 us
    ppermute x3, waiting for transfers between devices, exchange(): lax.ppermute(jnp.concatenate([moments, jnp.where(even, high, low)], axis=...  15.3 us
    pallas_call x1, Pallas kernels, block(): pl.pallas_call(functools.partial(block_kernel, total_cells), in_specs=[pl...  9.99 us
    pallas_call x1, Pallas kernels, relayout(): pl.pallas_call(relayout_kernel, grid=(depth,), in_specs=[pl.BlockSpec((ci...  6.91 us
    pallas_call x1, Pallas kernels, features_of(): pl.pallas_call(features_kernel, in_specs=[vmem] * 5, out_specs=[vmem] * 3...  5.3 us
    ppermute x1, waiting for transfers between devices, body(): yzhalo = lax.ppermute(yface[-1], ('gy', 'gz'), diagonal)  4.93 us
    ppermute x1, waiting for transfers between devices, body(): xhalo = lax.ppermute(xsend, 'gx', up_pairs('gx'))  3.89 us
    ppermute x1, starting transfers between devices, body(): zhalo = lax.ppermute(last, 'gz', up_pairs('gz'))  3.49 us
  transfers between devices with their start and end apart: 9, of which 7 were waited for; matrix products, arithmetic and copies ran while one was open for 5% of the time, Pallas kernels for 0%

commit v1 on v0

--- a/solution.py
+++ b/solution.py
@@ -11,7 +11,7 @@
 EPSILON = 1e-05
 LEAK = 0.2
 F32, BF16 = jnp.float32, jnp.bfloat16
-VMEM_LIMIT = 56 * 1024 * 1024
+MIB = 1024 * 1024
 
 
 def dot(a, b, dims=((1,), (0,))):
@@ -35,48 +35,50 @@
 
 
 def relayout_kernel(field_ref, cells_ref, yface_ref, xface_ref, rows_ref):
-    cin, _, height, width = field_ref.shape
+    cin, planes, height, width = field_ref.shape
     half = width // 2
-    rows_ref[...] = field_ref[:, 0].astype(F32).reshape(cin * height, width)
     out = iota((width, width), 0)
     source = jnp.where(out < half, 2 * out, 2 * (out - half) + 1)
     pick = (source == iota((width, width), 1)).astype(F32).astype(BF16)
-    last = []
-    for pair in range(height // 4):
-        lines = [rows_ref[pl.ds(4 * pair + k, cin, stride=height), :] for k in range(4)]
-        block = jnp.concatenate(lines, axis=0).astype(BF16)
-        turned = dot(pick, block, ((1,), (1,)))
-        for k in range(2):
-            row = (2 * pair + k) * half
-            lanes = slice(2 * cin * k, 2 * cin * (k + 1))
-            even = turned[:half, lanes]
-            odd = turned[half:, lanes]
-            cells_ref[0, row : row + half, : 2 * cin] = even.astype(BF16)
-            cells_ref[0, row : row + half, 2 * cin :] = odd.astype(BF16)
-            last.append(odd[half - 1 :, :])
-    yface_ref[0] = jnp.concatenate([even[:, cin:], odd[:, cin:]], axis=1).astype(BF16)
-    xface_ref[0] = jnp.concatenate(last, axis=0).astype(BF16)
+    for z in range(planes):
+        rows_ref[z] = field_ref[:, z].astype(F32).reshape(cin * height, width)
+        last = []
+        for pair in range(height // 4):
+            lines = [rows_ref[z, pl.ds(4 * pair + k, cin, stride=height), :] for k in range(4)]
+            block = jnp.concatenate(lines, axis=0).astype(BF16)
+            turned = dot(pick, block, ((1,), (1,)))
+            for k in range(2):
+                row = (2 * pair + k) * half
+                lanes = slice(2 * cin * k, 2 * cin * (k + 1))
+                even = turned[:half, lanes]
+                odd = turned[half:, lanes]
+                cells_ref[z, row : row + half, : 2 * cin] = even.astype(BF16)
+                cells_ref[z, row : row + half, 2 * cin :] = odd.astype(BF16)
+                last.append(odd[half - 1 :, :])
+        yface_ref[z] = jnp.concatenate([even[:, cin:], odd[:, cin:]], axis=1).astype(BF16)
+        xface_ref[z] = jnp.concatenate(last, axis=0).astype(BF16)
 
 
 def relayout(field):
     cin, depth, height, width = field.shape
     half, rows = width // 2, height // 2 * (width // 2)
+    step = 4 if depth % 4 == 0 else 1
     return pl.pallas_call(
         relayout_kernel,
-        grid=(depth,),
-        in_specs=[pl.BlockSpec((cin, 1, height, width), lambda z: (0, z, 0, 0))],
+        grid=(depth // step,),
+        in_specs=[pl.BlockSpec((cin, step, height, width), lambda z: (0, z, 0, 0))],
         out_specs=[
-            pl.BlockSpec((1, rows, 4 * cin), lambda z: (z, 0, 0)),
-            pl.BlockSpec((1, half, 2 * cin), lambda z: (z, 0, 0)),
-            pl.BlockSpec((1, height // 2, 2 * cin), lambda z: (z, 0, 0)),
+            pl.BlockSpec((step, rows, 4 * cin), lambda z: (z, 0, 0)),
+            pl.BlockSpec((step, half, 2 * cin), lambda z: (z, 0, 0)),
+            pl.BlockSpec((step, height // 2, 2 * cin), lambda z: (z, 0, 0)),
         ],
         out_shape=[
             jax.ShapeDtypeStruct((depth, rows, 4 * cin), BF16),
             jax.ShapeDtypeStruct((depth, half, 2 * cin), BF16),
             jax.ShapeDtypeStruct((depth, height // 2, 2 * cin), BF16),
         ],
-        scratch_shapes=[pltpu.VMEM((cin * height, width), F32)],
-        compiler_params=pltpu.CompilerParams(vmem_limit_bytes=VMEM_LIMIT),
+        scratch_shapes=[pltpu.VMEM((step, cin * height, width), F32)],
+        compiler_params=pltpu.CompilerParams(vmem_limit_bytes=16 * MIB),
         name="relayout",
     )(field)
 
@@ -178,19 +180,19 @@
             pltpu.VMEM((12 * cin, cout), BF16),
             pltpu.VMEM((rows, 4 * cout), F32),
         ],
-        compiler_params=pltpu.CompilerParams(vmem_limit_bytes=VMEM_LIMIT),
+        compiler_params=pltpu.CompilerParams(vmem_limit_bytes=20 * MIB),
         name="features",
     )(cells, zhalo, yhalo, xhalo, weights)
 
 
 def block_kernel(
     total_cells,
-    inside_ref, mom_ref, gain_ref, shift_ref, feat_ref, xb_ref, xa_ref, yb_ref, ya_ref, zb_ref, za_ref, w_ref,
+    place_ref, mom_ref, gain_ref, shift_ref, feat_ref, z1_ref, z2_ref, y1_ref, y2_ref, x1_ref, x2_ref, w_ref,
     out_ref, pad_ref, wide_ref,
 ):
     depth, rows, cout = feat_ref.shape
-    lines = xb_ref.shape[0] // depth
-    half = rows // lines
+    half = y1_ref.shape[0] // (depth + 2)
+    lines = rows // half
     group = cout // 2
     square = (cout, cout)
     ri, ci = iota(square, 0), iota(square, 1)
@@ -224,38 +226,34 @@
         return jnp.where(scaled >= 0, scaled, LEAK * scaled)
 
     base = 8
-    xb_in, xa_in, yb_in, ya_in, zb_in, za_in = (inside_ref[k] != 0 for k in range(6))
-
-    def put(zp, yp, middle, ends, inside):
-        left, right = ends
-        pad_ref[zp, yp, base : base + half, :] = jnp.where(inside, middle, 0.0) if inside is not True else middle
-        l_in = xb_in if inside is True else jnp.logical_and(xb_in, inside)
-        r_in = xa_in if inside is True else jnp.logical_and(xa_in, inside)
+    x_even, y_even, z_even, xb_in, xa_in, yb_in, ya_in, zb_in, za_in = (place_ref[k] != 0 for k in range(9))
+
+    def sides(even, one_ref, two_ref):
+        one, two = one_ref[...], two_ref[...]
+        return whiten(jnp.where(even, two, one)), whiten(jnp.where(even, one, two))
+
+    def put(zp, yp, middle, left, right, inside):
+        l_in, r_in = xb_in, xa_in
+        if inside is not None:
+            middle = jnp.where(inside, middle, 0.0)
+            l_in, r_in = jnp.logical_and(l_in, inside), jnp.logical_and(r_in, inside)
+        pad_ref[zp, yp, base : base + half, :] = middle
         pad_ref[zp, yp, base - 1 : base, :] = jnp.where(l_in, left, 0.0)
         pad_ref[zp, yp, base + half : base + half + 1, :] = jnp.where(r_in, right, 0.0)
 
-    xb, xa = whiten(xb_ref[...]), whiten(xa_ref[...])
-    yb, ya = whiten(yb_ref[...]), whiten(ya_ref[...])
-    for z in range(depth):
-        plane = whiten(feat_ref[z])
+    zsides = sides(z_even, z1_ref, z2_ref)
+    ysides = sides(y_even, y1_ref, y2_ref)
+    xsides = sides(x_even, x1_ref, x2_ref)
+    spots = [(z + 1, None) for z in range(depth)] + [(0, zb_in), (depth + 1, za_in)]
+    for n, (zp, z_in) in enumerate(spots):
+        plane = whiten(feat_ref[n]) if n < depth else zsides[n - depth]
         for y in range(lines):
-            k = z * lines + y
-            put(z + 1, y + 1, plane[y * half : (y + 1) * half], (xb[k : k + 1], xa[k : k + 1]), True)
-        for yp, side, inside in ((0, yb, yb_in), (lines + 1, ya, ya_in)):
-            k = depth * half + z
-            put(z + 1, yp, side[z * half : (z + 1) * half], (side[k : k + 1], side[k + depth : k + depth + 1]), inside)
-    for zp, ref, inside in ((0, zb_ref, zb_in), (depth + 1, za_ref, za_in)):
-        plane = whiten(ref[...])
-        ends = rows + 2 * half
-        for y in range(lines):
-            k = ends + y
-            put(zp, y + 1, plane[y * half : (y + 1) * half], (plane[k : k + 1], plane[k + lines : k + lines + 1]), inside)
-        for n, (yp, y_in) in enumerate(((0, yb_in), (lines + 1, ya_in))):
-            k = ends + 2 * lines + 2 * n
-            put(
-                zp, yp, plane[rows + n * half : rows + (n + 1) * half], (plane[k : k + 1], plane[k + 1 : k + 2]),
-                jnp.logical_and(inside, y_in),
-            )
+            k = n * lines + y
+            put(zp, y + 1, plane[y * half : (y + 1) * half], xsides[0][k : k + 1], xsides[1][k : k + 1], z_in)
+        for m, (yp, y_in) in enumerate(((0, yb_in), (lines + 1, ya_in))):
+            k = (depth + 2) * (lines + m) + n
+            inside = y_in if z_in is None else jnp.logical_and(z_in, y_in)
+            put(zp, yp, ysides[m][n * half : (n + 1) * half], xsides[0][k : k + 1], xsides[1][k : k + 1], inside)
     for zp in range(depth + 2):
         for yp in range(lines + 2):
             for dx in range(3):
@@ -267,53 +265,80 @@
         for dz in range(3):
             for dy in range(3):
                 acc = acc + dot(wide_ref[z + dz, dy * half : dy * half + rows, :], w_ref[dz, dy])
-        turned = jnp.stack([acc[y * half : (y + 1) * half].T for y in range(lines)], axis=0)
-        out_ref[:, z] = jnp.swapaxes(turned, 0, 1).astype(BF16)
-
-
-def block(total_cells, inside, moments, gain, shift, feats, xb, xa, yb, ya, zb, za, weights):
+        out_ref[z] = acc.astype(BF16)
+
+
+def block(total_cells, place, moments, gain, shift, feats, zs, ys, xs, weights):
     depth, rows, cout = feats.shape
-    lines = xb.shape[0] // depth
-    half = rows // lines
+    half = ys[0].shape[0] // (depth + 2)
+    lines = rows // half
     vmem = pl.BlockSpec(memory_space=pltpu.VMEM)
     return pl.pallas_call(
         functools.partial(block_kernel, total_cells),
         in_specs=[pl.BlockSpec(memory_space=pltpu.SMEM)] + [vmem] * 11,
         out_specs=vmem,
-        out_shape=jax.ShapeDtypeStruct((cout, depth, lines, half), BF16),
+        out_shape=jax.ShapeDtypeStruct((depth, rows, cout), BF16),
         scratch_shapes=[
             pltpu.VMEM((depth + 2, lines + 2, half + 16, cout), F32),
             pltpu.VMEM((depth + 2, (lines + 2) * half, 3 * cout), BF16),
         ],
-        compiler_params=pltpu.CompilerParams(vmem_limit_bytes=VMEM_LIMIT),
+        compiler_params=pltpu.CompilerParams(vmem_limit_bytes=24 * MIB),
         name="block",
-    )(inside, moments, gain, shift, feats, xb, xa, yb, ya, zb, za, weights)
-
-
-def exchange(axis, moments, low, high):
+    )(place, moments, gain, shift, feats, *zs, *ys, *xs, weights)
+
+
+def power_of_two(size):
+    return size & (size - 1) == 0
+
+
+def first_pairs(axis):
+    return [(i, i ^ 1) for i in range(lax.axis_size(axis))]
+
+
+def second_pairs(axis):
+    size = lax.axis_size(axis)
+    return [(i, (i + 1 if i % 2 else i - 1) % size) for i in range(size)]
+
+
+def is_even(axis):
+    size = lax.axis_size(axis)
+    return lax.axis_index(axis) % 2 == 0 if size > 1 and power_of_two(size) else jnp.bool_(True)
+
+
+def faces(axis, low, high):
     size = lax.axis_size(axis)
     if size == 1:
-        return moments, jnp.zeros_like(low), jnp.zeros_like(high)
-    if size & (size - 1):
-        up = [(i, i + 1) for i in range(size - 1)]
-        before = lax.ppermute(high, axis, up)
-        after = lax.ppermute(low, axis, [(j, i) for i, j in up])
-        return lax.psum(moments, axis), before, after
-    even = lax.axis_index(axis) % 2 == 0
-    count = moments.shape[0]
-    swap = [(i, i ^ 1) for i in range(size)]
-    got = lax.ppermute(jnp.concatenate([moments, jnp.where(even, high, low)], axis=0), axis, swap)
-    moments, one = moments + got[:count], got[count:]
+        return low, high
+    if not power_of_two(size):
+        up = up_pairs(axis)
+        return lax.ppermute(low, axis, [(j, i) for i, j in up]), lax.ppermute(high, axis, up)
+    even = is_even(axis)
+    one = lax.ppermute(jnp.where(even, high, low), axis, first_pairs(axis))
     if size == 2:
-        return moments, one, one
-    swap = [(i, (i + 1 if i % 2 else i - 1) % size) for i in range(size)]
-    got = lax.ppermute(jnp.concatenate([moments, jnp.where(even, low, high)], axis=0), axis, swap)
-    moments, two = moments + got[:count], got[count:]
+        return one, one
+    inner = [(i, j) for i, j in second_pairs(axis) if abs(i - j) == 1]
+    return one, lax.ppermute(jnp.where(even, low, high), axis, inner)
+
+
+def added(axis, value):
+    size = lax.axis_size(axis)
+    if size == 1:
+        return value
+    if not power_of_two(size):
+        return lax.psum(value, axis)
+    value = value + lax.ppermute(value, axis, first_pairs(axis))
+    if size > 2:
+        value = value + lax.ppermute(value, axis, second_pairs(axis))
     step = 4
     while step < size:
-        moments = moments + lax.ppermute(moments, axis, [(i, (i + step) % size) for i in range(size)])
+        value = value + lax.ppermute(value, axis, [(i, (i + step) % size) for i in range(size)])
         step *= 2
-    return moments, jnp.where(even, two, one), jnp.where(even, one, two)
+    return value
+
+
+def sided(even, pair):
+    one, two = pair
+    return jnp.where(even, two, one), jnp.where(even, one, two)
 
 
 def up_pairs(axis):
@@ -341,35 +366,44 @@
     xsend = jnp.pad(xsend, ((0, 0), (0, (-xsend.shape[1]) % 16), (0, 0)))
     xhalo = lax.ppermute(xsend, "gx", up_pairs("gx"))
 
-    feats, moments, faces = features_of(cells, zhalo, yhalo, xhalo, conv_first)
+    feats, moments, xfaces = features_of(cells, zhalo, yhalo, xhalo, conv_first)
     rows = lines * half
-    moments, xb, xa = exchange("gx", moments, faces[0], faces[1])
-    xb3, xa3 = xb.reshape(depth, lines, cout), xa.reshape(depth, lines, cout)
-    grid = feats.reshape(depth, lines, half, cout)
+    zs = faces("gz", feats[0], feats[-1])
+    moments = added("gz", moments)
+    zsides = sided(is_even("gz"), zs)
 
     def yside(y):
-        return jnp.concatenate([grid[:, y].reshape(depth * half, cout), xb3[:, y], xa3[:, y]], axis=0)
-
-    moments, yb, ya = exchange("gy", moments, yside(0), yside(lines - 1))
-
-    def zside(z):
-        k = depth * half + z
-        own = [feats[z], yb[z * half : (z + 1) * half], ya[z * half : (z + 1) * half], xb3[z], xa3[z]]
-        own += [yb[k : k + 1], yb[k + depth : k + depth + 1], ya[k : k + 1], ya[k + depth : k + depth + 1]]
-        own += [jnp.zeros((4, cout), F32)]
+        here = slice(y * half, (y + 1) * half)
+        return jnp.concatenate([feats[z, here] for z in range(depth)] + [side[here] for side in zsides], axis=0)
+
+    ys = faces("gy", yside(0), yside(lines - 1))
+    moments = added("gy", moments)
+    ysides = sided(is_even("gy"), ys)
+
+    def xside(n, x):
+        own = [xfaces[n]] + [side.reshape(-1, half, cout)[:, x] for side in zsides + ysides]
         return jnp.concatenate(own, axis=0)
 
-    moments, zb, za = exchange("gz", moments, zside(0), zside(depth - 1))
-    inside = []
+    low, high = xside(0, 0), xside(1, half - 1)
+    if lax.axis_size("gx") == 2:
+        count = moments.shape[0]
+        both = jnp.concatenate([moments, jnp.where(is_even("gx"), high, low)], axis=0)
+        both = lax.ppermute(both, "gx", first_pairs("gx"))
+        moments = moments + both[:count]
+        xs = (both[count:], both[count:])
+    else:
+        xs = faces("gx", low, high)
+        moments = added("gx", moments)
+    place = [is_even(axis) for axis in ("gx", "gy", "gz")]
     for axis in ("gx", "gy", "gz"):
-        place = lax.axis_index(axis)
-        inside += [place > 0, place < lax.axis_size(axis) - 1]
-    inside = jnp.stack(inside).astype(jnp.int32)
+        place += [lax.axis_index(axis) > 0, lax.axis_index(axis) < lax.axis_size(axis) - 1]
+    place = jnp.stack(place).astype(jnp.int32)
     total_cells = rows * depth * lax.axis_size("gx") * lax.axis_size("gy") * lax.axis_size("gz")
-    return block(
-        total_cells, inside, moments, norm_gain[None], norm_shift[None], feats, xb, xa, yb, ya, zb, za,
+    result = block(
+        total_cells, place, moments, norm_gain[None], norm_shift[None], feats, zs, ys, xs,
         conv_second.reshape(3, 3, 3 * cout, cout),
     )
+    return jnp.transpose(result.reshape(depth, lines, half, cout), (3, 0, 1, 2))
 
 
 def solution(mesh):

time: 93.5 us -> 68.5 us (0.73)
  the two profiles are of different devices: /device:TPU:14 before, /device:TPU:1 now
where the time goes in v1:
time: 68.5 us; the launch traced here: 68.2 us
  starting transfers between devices  27.8 us (41%)
  waiting for transfers between devices  23.4 us (34%)
  Pallas kernels  13.2 us (19%)
  local copies, waits for them, and re-layouts  3.14 us (5%)
    pallas_call x1, Pallas kernels, block(): pl.pallas_call(functools.partial(block_kernel, total_cells), in_specs=[pl...  8.03 us
    ppermute x2, waiting for transfers between devices, added(): value = value + lax.ppermute(value, axis, first_pairs(axis))  7.4 us
    ppermute x2, waiting for transfers between devices, added(): value = value + lax.ppermute(value, axis, second_pairs(axis))  6.4 us
    ppermute x1, starting transfers between devices, body(): yhalo = lax.ppermute(yface, 'gy', up_pairs('gy'))  4.54 us
    ppermute x2, waiting for transfers between devices, faces(): return (one, lax.ppermute(jnp.where(even, low, high), axis, inner))  4.42 us
    ppermute x2, starting transfers between devices, faces(): one = lax.ppermute(jnp.where(even, high, low), axis, first_pairs(axis))  4.08 us
    ppermute x1, starting transfers between devices, body(): zhalo = lax.ppermute(last, 'gz', up_pairs('gz'))  3.22 us
    ppermute x1, starting transfers between devices, body(): yzhalo = lax.ppermute(yface[-1], ('gy', 'gz'), diagonal)  3.2 us
  transfers between devices with their start and end apart: 13, of which 8 were waited for; matrix products, arithmetic and copies ran while one was open for 1% of the time, Pallas kernels for 0%

profile of v1, /device:TPU:1, one launch (start us, length us, event | category | flops | bytes accessed | tf_op | source)
XLA Modules:
  0.0 68.2 jit_solution(11482585158256023210)
XLA Ops:
  0.0 0.0 copy-start
  0.0 1.6 %copy-done = bf16[64,8,16,128]{3,2,1,0:T(8,128)(2,1)S(1)} copy-done((bf16[64,8,16,128]{3,2,1,0:T(8,128)(2,1)S(1)}, bf16[64,8,16,128]{3,2,1,0:T(8,128)(2,1)}, u32[]{:S(2)}) %copy-start) | copy-done | bytes 2097176
  1.6 2.3 %relayout.1 = (bf16[8,512,256]{2,1,0:T(8,128)(2,1)S(1)}, bf16[8,64,128]{2,1,0:T(8,128)(2,1)S(1)}, bf16[8,8,128]{2,1,0:T(8,128)(2,1)S(1)}) custom-call(bf16[64,8,16,128]{3,2,1,0:T(8,128)(2,1)S(1)} %copy-done), custom_call_target="tpu_custom_call" | custom-call | tf_op jit(solution)/shard_map/relayout/pallas_call | solution.py:66
  3.9 4.5 %collective-permute-start.2 = (bf16[8,64,128]{2,1,0:T(8,128)(2,1)S(1)}, bf16[8,64,128]{2,1,0:T(8,128)(2,1)S(1)}, u32[]{:S(2)}, u32[]{:S(2)}) collective-permute-start(bf16[8,64,128]{2,1,0:T(8,128)(2,1)S(1)} %get-tuple-element.12), channel_id=1, source_target_pairs={{0,4},{4,8},{8,12},{1,5},{5,9},{9,13},{2,6},{6,10},{10,14},{3,7},{... | collective-permute-start | bytes 393224 | tf_op jit(solution)/shard_map/ppermute | solution.py:356
  8.5 3.2 %collective-permute-start = (bf16[512,256]{1,0:T(8,128)(2,1)S(1)}, bf16[512,256]{1,0:T(8,128)(2,1)S(1)}, u32[]{:S(2)}, u32[]{:S(2)}) collective-permute-start(bf16[512,256]{1,0:T(8,128)(2,1)S(1)} %slice_bitcast_fusion), channel_id=1, source_target_pairs={{0,1},{1,2},{2,3},{4,5},{5,6},{6,7},{8,9},{9,10},{10,11},{12,13},{... | collective-permute-start | bytes 786440 | tf_op jit(solution)/shard_map/ppermute | solution.py:355
  11.7 3.2 %collective-permute-start.1 = (bf16[64,128]{1,0:T(8,128)(2,1)S(1)}, bf16[64,128]{1,0:T(8,128)(2,1)S(1)}, u32[]{:S(2)}, u32[]{:S(2)}) collective-permute-start(bf16[64,128]{1,0:T(8,128)(2,1)S(1)} %slice_bitcast_fusion.3), channel_id=1, source_target_pairs={{0,5},{1,6},{2,7},{4,9},{5,10},{6,11},{8,13},{9,14},{10,15},{16,21... | collective-permute-start | bytes 49160 | tf_op jit(solution)/shard_map/ppermute | solution.py:359
  14.9 2.4 %collective-permute-done.1 = bf16[64,128]{1,0:T(8,128)(2,1)S(1)} collective-permute-done((bf16[64,128]{1,0:T(8,128)(2,1)S(1)}, bf16[64,128]{1,0:T(8,128)(2,1)S(1)}, u32[]{:S(2)}, u32[]{:S(2)}) %collective-permute-start.1) | collective-permute-done | bytes 16416 | tf_op jit(solution)/shard_map/ppermute | solution.py:359
  17.3 0.0 collective-permute-done.2
  17.3 0.1 fusion.5
  17.4 0.1 pad_bitcast_fusion
  17.5 0.0 collective-permute-done.zhalo_ref
  17.5 3.1 %collective-permute-start.3 = (bf16[9,16,128]{2,1,0:T(8,128)(2,1)S(1)}, bf16[9,16,128]{2,1,0:T(8,128)(2,1)S(1)}, u32[]{:S(2)}, u32[]{:S(2)}) collective-permute-start(bf16[9,16,128]{2,1,0:T(8,128)(2,1)S(1)} %fusion.3), channel_id=1, source_target_pairs={{0,16},{1,17},{2,18},{3,19},{4,20},{5,21},{6,22},{7,23},{8,24},{9,... | collective-permute-start | bytes 110600 | tf_op jit(solution)/shard_map/ppermute | solution.py:367
  20.7 1.2 %collective-permute-done.3.xhalo_ref = bf16[9,16,128]{2,1,0:T(8,128)(2,1)S(1)} collective-permute-done((bf16[9,16,128]{2,1,0:T(8,128)(2,1)S(1)}, bf16[9,16,128]{2,1,0:T(8,128)(2,1)S(1)}, u32[]{:S(2)}, u32[]{:S(2)}) %collective-permute-start.3) | collective-permute-done | bytes 36896 | tf_op jit(solution)/shard_map/ppermute | solution.py:367
  21.9 0.0 copy-start.2
  21.9 1.0 %copy-done.2 = bf16[3,3,3,64,128]{4,3,2,1,0:T(8,128)(2,1)S(1)} copy-done((bf16[3,3,3,64,128]{4,3,2,1,0:T(8,128)(2,1)S(1)}, bf16[3,3,3,64,128]{4,3,2,1,0:T(8,128)(2,1)}, u32[]{:S(2)}) %copy-start.2) | copy-done | bytes 442392
  22.9 2.9 %features.1 = (f32[4,512,128]{2,1,0:T(8,128)S(1)}, f32[72,128]{1,0:T(8,128)S(1)}, f32[2,32,128]{2,1,0:T(8,128)S(1)}) custom-call(bf16[8,512,256]{2,1,0:T(8,128)(2,1)S(1)} %get-tuple-element.11.cells_ref, bf16[512,256]{1,0:T(8,128)(2,1)S(1)} %collective-permute-done.zhalo_ref, bf16[9,64,128]{2,1,0:T(8,128)(2,1)S(1)} %pad_maximum_fusion.yhalo_ref, ...), custom_call_target="tpu_custom_call" | custom-call | tf_op jit(solution)/shard_map/features/pallas_call | solution.py:168
  25.9 0.7 collective-permute-start.8
  26.5 4.0 %collective-permute-start.9 = (f32[512,128]{1,0:T(8,128)S(1)}, f32[512,128]{1,0:T(8,128)S(1)}, u32[]{:S(2)}, u32[]{:S(2)}) collective-permute-start(f32[512,128]{1,0:T(8,128)S(1)} %get-tuple-element.25), channel_id=1, source_target_pairs={{0,1},{1,0},{2,3},{3,2},{4,5},{5,4},{6,7},{7,6},{8,9},{9,8},{10,11... | collective-permute-start | bytes 786440 | tf_op jit(solution)/shard_map/ppermute | solution.py:316
  30.6 0.1 collective-permute-start.4
  30.6 6.5 %collective-permute-done.4 = f32[72,128]{1,0:T(8,128)S(1)} collective-permute-done((f32[72,128]{1,0:T(8,128)S(1)}, f32[72,128]{1,0:T(8,128)S(1)}, u32[]{:S(2)}, u32[]{:S(2)}) %collective-permute-start.4) | collective-permute-done | bytes 36896 | tf_op jit(solution)/shard_map/ppermute | solution.py:329
  37.2 1.1 %collective-permute-start.5 = (f32[72,128]{1,0:T(8,128)S(1)}, f32[72,128]{1,0:T(8,128)S(1)}, u32[]{:S(2)}, u32[]{:S(2)}) collective-permute-start(f32[72,128]{1,0:T(8,128)S(1)} %add.37), channel_id=1, source_target_pairs={{0,3},{1,2},{2,1},{3,0},{4,7},{5,6},{6,5},{7,4},{8,11},{9,10},{10,... | collective-permute-start | bytes 110600 | tf_op jit(solution)/shard_map/ppermute | solution.py:331
  38.3 0.0 copy-start.1
  38.3 0.0 copy-start.3
  38.3 0.0 copy-start.4
  38.3 3.5 %collective-permute-done.5 = f32[72,128]{1,0:T(8,128)S(1)} collective-permute-done((f32[72,128]{1,0:T(8,128)S(1)}, f32[72,128]{1,0:T(8,128)S(1)}, u32[]{:S(2)}, u32[]{:S(2)}) %collective-permute-start.5) | collective-permute-done | bytes 36896 | tf_op jit(solution)/shard_map/ppermute | solution.py:331
  41.8 2.6 %collective-permute-start.6 = (f32[72,128]{1,0:T(8,128)S(1)}, f32[72,128]{1,0:T(8,128)S(1)}, u32[]{:S(2)}, u32[]{:S(2)}) collective-permute-start(f32[72,128]{1,0:T(8,128)S(1)} %add.38), channel_id=1, source_target_pairs={{0,4},{4,0},{8,12},{12,8},{1,5},{5,1},{9,13},{13,9},{2,6},{6,2},{1... | collective-permute-start | bytes 110600 | tf_op jit(solution)/shard_map/ppermute | solution.py:329
  44.4 0.9 %collective-permute-done.6 = f32[72,128]{1,0:T(8,128)S(1)} collective-permute-done((f32[72,128]{1,0:T(8,128)S(1)}, f32[72,128]{1,0:T(8,128)S(1)}, u32[]{:S(2)}, u32[]{:S(2)}) %collective-permute-start.6) | collective-permute-done | bytes 36896 | tf_op jit(solution)/shard_map/ppermute | solution.py:329
  45.3 0.5 collective-permute-start.7
  45.8 2.9 %collective-permute-done.7 = f32[72,128]{1,0:T(8,128)S(1)} collective-permute-done((f32[72,128]{1,0:T(8,128)S(1)}, f32[72,128]{1,0:T(8,128)S(1)}, u32[]{:S(2)}, u32[]{:S(2)}) %collective-permute-start.7) | collective-permute-done | bytes 36896 | tf_op jit(solution)/shard_map/ppermute | solution.py:331
  48.7 0.0 collective-permute-done.8.z2_ref
  48.7 0.0 collective-permute-done.9.z1_ref
  48.8 2.5 %collective-permute-start.10 = (f32[384,128]{1,0:T(8,128)S(1)}, f32[384,128]{1,0:T(8,128)S(1)}, u32[]{:S(2)}, u32[]{:S(2)}) collective-permute-start(f32[384,128]{1,0:T(8,128)S(1)} %get-tuple-element.32), channel_id=1, source_target_pairs={{4,8},{8,4},{5,9},{9,5},{6,10},{10,6},{7,11},{11,7},{20,24},{24,20... | collective-permute-start | bytes 589832 | tf_op jit(solution)/shard_map/ppermute | solution.py:320
  51.3 0.1 collective-permute-start.11
  51.4 4.4 %collective-permute-done.10.y2_ref = f32[384,128]{1,0:T(8,128)S(1)} collective-permute-done((f32[384,128]{1,0:T(8,128)S(1)}, f32[384,128]{1,0:T(8,128)S(1)}, u32[]{:S(2)}, u32[]{:S(2)}) %collective-permute-start.10) | collective-permute-done | bytes 196640 | tf_op jit(solution)/shard_map/ppermute | solution.py:320
  55.8 0.0 collective-permute-done.11.y1_ref
  55.9 0.1 concatenate.34
  56.0 0.1 concatenate.33
  56.2 2.3 %collective-permute-start.12 = (f32[132,128]{1,0:T(8,128)S(1)}, f32[132,128]{1,0:T(8,128)S(1)}, u32[]{:S(2)}, u32[]{:S(2)}) collective-permute-start(f32[132,128]{1,0:T(8,128)S(1)} %pad_maximum_fusion.1), channel_id=1, source_target_pairs={{0,16},{16,0},{1,17},{17,1},{2,18},{18,2},{3,19},{19,3},{4,20},{20... | collective-permute-start | bytes 202760 | tf_op jit(solution)/shard_map/ppermute | solution.py:391
  58.4 0.1 stack.39
  58.5 1.6 %collective-permute-done.12 = f32[132,128]{1,0:T(8,128)S(1)} collective-permute-done((f32[132,128]{1,0:T(8,128)S(1)}, f32[132,128]{1,0:T(8,128)S(1)}, u32[]{:S(2)}, u32[]{:S(2)}) %collective-permute-start.12) | collective-permute-done | bytes 67616 | tf_op jit(solution)/shard_map/ppermute | solution.py:391
  60.1 0.0 copy-done.1
  60.1 0.0 copy-done.3
  60.2 0.0 copy-done.4
  60.2 8.0 %block.1 = bf16[4,512,128]{2,1,0:T(8,128)(2,1)} custom-call(s32[9]{0:T(128)S(1)} %convert_element_type.5.place_ref, f32[72,128]{1,0:T(8,128)S(1)} %slice_add_fusion.mom_ref, f32[1,128]{1,0:T(1,128)S(1)} %bitcast.79, f32[1,128]{1,0:T(1,128)S(1)} %bitcast.80, f32[4,512,128]{2,1,0:T(8,128)S(1)} %get-tuple-element.16.feat_ref, ...), custom_call_target="tpu_custom_call" | custom-call | tf_op jit(solution)/shard_map/block/pallas_call | solution.py:276
  (34 shorter events, 0.4 us)
Async XLA Ops:
  0.0 1.6 %copy-start = (bf16[64,8,16,128]{3,2,1,0:T(8,128)(2,1)S(1)}, bf16[64,8,16,128]{3,2,1,0:T(8,128)(2,1)}, u32[]{:S(2)}) copy-start(bf16[64,8,16,128]{3,2,1,0:T(8,128)(2,1)} %field_ref.1) | copy-start | bytes 6291460
  3.9 13.4 %collective-permute-start.2 = (bf16[8,64,128]{2,1,0:T(8,128)(2,1)S(1)}, bf16[8,64,128]{2,1,0:T(8,128)(2,1)S(1)}, u32[]{:S(2)}, u32[]{:S(2)}) collective-permute-start(bf16[8,64,128]{2,1,0:T(8,128)(2,1)S(1)} %get-tuple-element.12), channel_id=1, source_target_pairs={{0,4},{4,8},{8,12},{1,5},{5,9},{9,13},{2,6},{6,10},{10,14},{3,7},{... | collective-permute-start | bytes 393224 | tf_op jit(solution)/shard_map/ppermute | solution.py:356
  8.5 9.0 %collective-permute-start = (bf16[512,256]{1,0:T(8,128)(2,1)S(1)}, bf16[512,256]{1,0:T(8,128)(2,1)S(1)}, u32[]{:S(2)}, u32[]{:S(2)}) collective-permute-start(bf16[512,256]{1,0:T(8,128)(2,1)S(1)} %slice_bitcast_fusion), channel_id=1, source_target_pairs={{0,1},{1,2},{2,3},{4,5},{5,6},{6,7},{8,9},{9,10},{10,11},{12,13},{... | collective-permute-start | bytes 786440 | tf_op jit(solution)/shard_map/ppermute | solution.py:355
  11.7 5.6 %collective-permute-start.1 = (bf16[64,128]{1,0:T(8,128)(2,1)S(1)}, bf16[64,128]{1,0:T(8,128)(2,1)S(1)}, u32[]{:S(2)}, u32[]{:S(2)}) collective-permute-start(bf16[64,128]{1,0:T(8,128)(2,1)S(1)} %slice_bitcast_fusion.3), channel_id=1, source_target_pairs={{0,5},{1,6},{2,7},{4,9},{5,10},{6,11},{8,13},{9,14},{10,15},{16,21... | collective-permute-start | bytes 49160 | tf_op jit(solution)/shard_map/ppermute | solution.py:359
  17.5 4.4 %collective-permute-start.3 = (bf16[9,16,128]{2,1,0:T(8,128)(2,1)S(1)}, bf16[9,16,128]{2,1,0:T(8,128)(2,1)S(1)}, u32[]{:S(2)}, u32[]{:S(2)}) collective-permute-start(bf16[9,16,128]{2,1,0:T(8,128)(2,1)S(1)} %fusion.3), channel_id=1, source_target_pairs={{0,16},{1,17},{2,18},{3,19},{4,20},{5,21},{6,22},{7,23},{8,24},{9,... | collective-permute-start | bytes 110600 | tf_op jit(solution)/shard_map/ppermute | solution.py:367
  21.9 1.0 %copy-start.2 = (bf16[3,3,3,64,128]{4,3,2,1,0:T(8,128)(2,1)S(1)}, bf16[3,3,3,64,128]{4,3,2,1,0:T(8,128)(2,1)}, u32[]{:S(2)}) copy-start(bf16[3,3,3,64,128]{4,3,2,1,0:T(8,128)(2,1)} %w_ref.1) | copy-start | bytes 1327108
  25.9 22.8 %collective-permute-start.8 = (f32[512,128]{1,0:T(8,128)S(1)}, f32[512,128]{1,0:T(8,128)S(1)}, u32[]{:S(2)}, u32[]{:S(2)}) collective-permute-start(f32[512,128]{1,0:T(8,128)S(1)} %get-tuple-element.26), channel_id=1, source_target_pairs={{1,2},{2,1},{5,6},{6,5},{9,10},{10,9},{13,14},{14,13},{17,18},{18,... | collective-permute-start | bytes 786440 | tf_op jit(solution)/shard_map/ppermute | solution.py:320
  26.5 22.2 %collective-permute-start.9 = (f32[512,128]{1,0:T(8,128)S(1)}, f32[512,128]{1,0:T(8,128)S(1)}, u32[]{:S(2)}, u32[]{:S(2)}) collective-permute-start(f32[512,128]{1,0:T(8,128)S(1)} %get-tuple-element.25), channel_id=1, source_target_pairs={{0,1},{1,0},{2,3},{3,2},{4,5},{5,4},{6,7},{7,6},{8,9},{9,8},{10,11... | collective-permute-start | bytes 786440 | tf_op jit(solution)/shard_map/ppermute | solution.py:316
  30.6 6.6 %collective-permute-start.4 = (f32[72,128]{1,0:T(8,128)S(1)}, f32[72,128]{1,0:T(8,128)S(1)}, u32[]{:S(2)}, u32[]{:S(2)}) collective-permute-start(f32[72,128]{1,0:T(8,128)S(1)} %get-tuple-element.14), channel_id=1, source_target_pairs={{0,1},{1,0},{2,3},{3,2},{4,5},{5,4},{6,7},{7,6},{8,9},{9,8},{10,11... | collective-permute-start | bytes 110600 | tf_op jit(solution)/shard_map/ppermute | solution.py:329
  37.2 4.6 %collective-permute-start.5 = (f32[72,128]{1,0:T(8,128)S(1)}, f32[72,128]{1,0:T(8,128)S(1)}, u32[]{:S(2)}, u32[]{:S(2)}) collective-permute-start(f32[72,128]{1,0:T(8,128)S(1)} %add.37), channel_id=1, source_target_pairs={{0,3},{1,2},{2,1},{3,0},{4,7},{5,6},{6,5},{7,4},{8,11},{9,10},{10,... | collective-permute-start | bytes 110600 | tf_op jit(solution)/shard_map/ppermute | solution.py:331
  38.3 21.9 %copy-start.1 = (bf16[3,3,3,128,128]{4,3,2,1,0:T(8,128)(2,1)S(1)}, bf16[3,3,3,128,128]{4,3,2,1,0:T(8,128)(2,1)}, u32[]{:S(2)}) copy-start(bf16[3,3,3,128,128]{4,3,2,1,0:T(8,128)(2,1)} %param.9) | copy-start | bytes 2654212
  38.3 21.9 %copy-start.3 = (f32[128]{0:T(128)S(1)}, f32[128]{0:T(128)}, u32[]{:S(2)}) copy-start(f32[128]{0:T(128)} %param.7) | copy-start | bytes 1540
  38.3 21.9 %copy-start.4 = (f32[128]{0:T(128)S(1)}, f32[128]{0:T(128)}, u32[]{:S(2)}) copy-start(f32[128]{0:T(128)} %param.8) | copy-start | bytes 1540
  41.8 3.4 %collective-permute-start.6 = (f32[72,128]{1,0:T(8,128)S(1)}, f32[72,128]{1,0:T(8,128)S(1)}, u32[]{:S(2)}, u32[]{:S(2)}) collective-permute-start(f32[72,128]{1,0:T(8,128)S(1)} %add.38), channel_id=1, source_target_pairs={{0,4},{4,0},{8,12},{12,8},{1,5},{5,1},{9,13},{13,9},{2,6},{6,2},{1... | collective-permute-start | bytes 110600 | tf_op jit(solution)/shard_map/ppermute | solution.py:329
  45.3 3.4 %collective-permute-start.7 = (f32[72,128]{1,0:T(8,128)S(1)}, f32[72,128]{1,0:T(8,128)S(1)}, u32[]{:S(2)}, u32[]{:S(2)}) collective-permute-start(f32[72,128]{1,0:T(8,128)S(1)} %add.39), channel_id=1, source_target_pairs={{0,12},{4,8},{8,4},{12,0},{1,13},{5,9},{9,5},{13,1},{2,14},{6,10},... | collective-permute-start | bytes 110600 | tf_op jit(solution)/shard_map/ppermute | solution.py:331
  48.8 7.0 %collective-permute-start.10 = (f32[384,128]{1,0:T(8,128)S(1)}, f32[384,128]{1,0:T(8,128)S(1)}, u32[]{:S(2)}, u32[]{:S(2)}) collective-permute-start(f32[384,128]{1,0:T(8,128)S(1)} %get-tuple-element.32), channel_id=1, source_target_pairs={{4,8},{8,4},{5,9},{9,5},{6,10},{10,6},{7,11},{11,7},{20,24},{24,20... | collective-permute-start | bytes 589832 | tf_op jit(solution)/shard_map/ppermute | solution.py:320
  51.3 4.5 %collective-permute-start.11 = (f32[384,128]{1,0:T(8,128)S(1)}, f32[384,128]{1,0:T(8,128)S(1)}, u32[]{:S(2)}, u32[]{:S(2)}) collective-permute-start(f32[384,128]{1,0:T(8,128)S(1)} %get-tuple-element.31), channel_id=1, source_target_pairs={{0,4},{4,0},{8,12},{12,8},{1,5},{5,1},{9,13},{13,9},{2,6},{6,2},{1... | collective-permute-start | bytes 589832 | tf_op jit(solution)/shard_map/ppermute | solution.py:316
  56.2 4.0 %collective-permute-start.12 = (f32[132,128]{1,0:T(8,128)S(1)}, f32[132,128]{1,0:T(8,128)S(1)}, u32[]{:S(2)}, u32[]{:S(2)}) collective-permute-start(f32[132,128]{1,0:T(8,128)S(1)} %pad_maximum_fusion.1), channel_id=1, source_target_pairs={{0,16},{16,0},{1,17},{17,1},{2,18},{18,2},{3,19},{19,3},{4,20},{20... | collective-permute-start | bytes 202760 | tf_op jit(solution)/shard_map/ppermute | solution.py:391

commit v2 on v1

--- a/solution.py
+++ b/solution.py
@@ -84,13 +84,26 @@
 
 
 def features_kernel(
-    cells_ref, zhalo_ref, yhalo_ref, xhalo_ref, w_ref, feat_ref, mom_ref, xface_ref, w4_ref, wy_ref, wx_ref, acc_ref
+    place_ref, cells_ref, zhalo_ref, yhalo_ref, yzhalo_ref, xhalo_ref, xzhalo_ref, w_ref,
+    feat_ref, mom_ref, xface_ref, w4_ref, wy_ref, wx_ref, acc_ref,
 ):
     depth = cells_ref.shape[0] // 2
     cin, cout = w_ref.shape[3:]
     rows = cells_ref.shape[1]
-    half = yhalo_ref.shape[1]
-    lines = rows // half
+    lines = xhalo_ref.shape[0] // (2 * depth)
+    half = rows // lines
+    y_in, z_in = place_ref[5] != 0, place_ref[7] != 0
+    zhalo = jnp.where(z_in, zhalo_ref[...], jnp.zeros(zhalo_ref.shape, BF16))
+    yrest = yhalo_ref[2 * depth * half :, :].astype(F32)
+    yhalo = [yzhalo_ref[:half, :]] + [yhalo_ref[z * half : (z + 1) * half, :] for z in range(2 * depth)]
+    yhalo = [jnp.where(y_in, value, jnp.zeros_like(value)) for value in yhalo]
+    yhalo[0] = jnp.where(z_in, yhalo[0], jnp.zeros_like(yhalo[0]))
+    corner = jnp.where(jnp.logical_and(y_in, z_in), yzhalo_ref[half:, :].astype(F32)[:1], 0.0)
+    yrest = jnp.where(y_in, yrest, 0.0)
+    here = [jnp.where(z_in, xzhalo_ref[...].astype(F32)[:lines], 0.0)]
+    here += [xhalo_ref[...].astype(F32)[z * lines : (z + 1) * lines] for z in range(2 * depth)]
+    over = [corner] + [yrest[z : z + 1] for z in range(2 * depth)]
+    over = [jnp.concatenate([line, value[: lines - 1]], axis=0) for line, value in zip(over, here, strict=True)]
     w4_ref[...] = jnp.zeros(w4_ref.shape, BF16)
     wx_ref[...] = jnp.zeros(wx_ref.shape, BF16)
     wy_ref[...] = jnp.zeros(wy_ref.shape, BF16)
@@ -114,23 +127,22 @@
         wx_ref[k + cin : k + 2 * cin, :] = w_ref[dz, 2, 0]
         wx_ref[k + 3 * cin : k + 4 * cin, :] = w_ref[dz, 0, 0]
     first = iota((half, cout), 0) == 0
-    xh = xhalo_ref[...].astype(F32)
     total = jnp.zeros((1, cout), F32)
     for zo in range(depth):
-        before = zhalo_ref[...] if zo == 0 else cells_ref[2 * zo - 1]
+        before = zhalo if zo == 0 else cells_ref[2 * zo - 1]
         acc_ref[...] = dot(
             jnp.concatenate([before, cells_ref[2 * zo], cells_ref[2 * zo + 1]], axis=1),
             w4_ref[...].reshape(3 * 4 * cin, 4 * cout),
         )
-        ysum = dot(jnp.concatenate([yhalo_ref[2 * zo + dz] for dz in range(3)], axis=1), wy_ref[...])
+        ysum = dot(jnp.concatenate(yhalo[2 * zo : 2 * zo + 3], axis=1), wy_ref[...])
         xparts = []
         for dz in range(3):
-            xparts += [xh[2 * zo + dz, 1 : lines + 1], xh[2 * zo + dz, :lines]]
+            xparts += [here[2 * zo + dz], over[2 * zo + dz]]
         xsum = dot(jnp.concatenate(xparts, axis=1).astype(BF16), wx_ref[...])
         for line in range(lines):
-            here = pl.ds(line * half, half)
-            straight = acc_ref[here, :cout]
-            shifted = acc_ref[here, 2 * cout : 3 * cout]
+            span = pl.ds(line * half, half)
+            straight = acc_ref[span, :cout]
+            shifted = acc_ref[span, 2 * cout : 3 * cout]
             if line == 0:
                 straight = straight + ysum[:, :cout]
                 shifted = shifted + ysum[:, cout:]
@@ -140,7 +152,7 @@
                 shifted = shifted + acc_ref[above, 3 * cout :]
             moved = jnp.where(first, xsum[line : line + 1], pltpu.roll(shifted, 1, 0))
             value = straight + moved
-            feat_ref[zo, here, :] = value
+            feat_ref[zo, span, :] = value
             xface_ref[0, zo * lines + line : zo * lines + line + 1, :] = value[:1]
             xface_ref[1, zo * lines + line : zo * lines + line + 1, :] = value[half - 1 :]
             total = total + jnp.sum(value, axis=0, keepdims=True)
@@ -160,19 +172,19 @@
     mom_ref[cout // 2 :, :] = jnp.broadcast_to(total, (8, cout))
 
 
-def features_of(cells, zhalo, yhalo, xhalo, weights):
+def features_of(place, cells, zhalo, yhalo, yzhalo, xhalo, xzhalo, weights):
     depth, rows, wide = cells.shape
     cin, cout = weights.shape[3:]
-    half = yhalo.shape[1]
+    lines = xhalo.shape[0] // depth
     vmem = pl.BlockSpec(memory_space=pltpu.VMEM)
     return pl.pallas_call(
         features_kernel,
-        in_specs=[vmem] * 5,
+        in_specs=[pl.BlockSpec(memory_space=pltpu.SMEM)] + [vmem] * 7,
         out_specs=[vmem] * 3,
         out_shape=[
             jax.ShapeDtypeStruct((depth // 2, rows, cout), F32),
             jax.ShapeDtypeStruct((cout // 2 + 8, cout), F32),
-            jax.ShapeDtypeStruct((2, depth // 2 * rows // half, cout), F32),
+            jax.ShapeDtypeStruct((2, depth // 2 * lines, cout), F32),
         ],
         scratch_shapes=[
             pltpu.VMEM((3, wide, 4 * cout), BF16),
@@ -182,7 +194,7 @@
         ],
         compiler_params=pltpu.CompilerParams(vmem_limit_bytes=20 * MIB),
         name="features",
-    )(cells, zhalo, yhalo, xhalo, weights)
+    )(place, cells, zhalo, yhalo, yzhalo, xhalo, xzhalo, weights)
 
 
 def block_kernel(
@@ -320,13 +332,14 @@
     return one, lax.ppermute(jnp.where(even, low, high), axis, inner)
 
 
-def added(axis, value):
+def added(axis, value, first=True):
     size = lax.axis_size(axis)
     if size == 1:
         return value
     if not power_of_two(size):
         return lax.psum(value, axis)
-    value = value + lax.ppermute(value, axis, first_pairs(axis))
+    if first:
+        value = value + lax.ppermute(value, axis, first_pairs(axis))
     if size > 2:
         value = value + lax.ppermute(value, axis, second_pairs(axis))
     step = 4
@@ -336,6 +349,21 @@
     return value
 
 
+def added_with_faces(axis, value, low, high):
+    size = lax.axis_size(axis)
+    if size == 1 or not power_of_two(size):
+        return added(axis, value), faces(axis, low, high)
+    even, count = is_even(axis), value.shape[0]
+    both = jnp.concatenate([value, jnp.where(even, high, low)], axis=0)
+    both = lax.ppermute(both, axis, first_pairs(axis))
+    value, one = value + both[:count], both[count:]
+    if size == 2:
+        return value, (one, one)
+    inner = [(i, j) for i, j in second_pairs(axis) if abs(i - j) == 1]
+    two = lax.ppermute(jnp.where(even, low, high), axis, inner)
+    return added(axis, value, first=False), (one, two)
+
+
 def sided(even, pair):
     one, two = pair
     return jnp.where(even, two, one), jnp.where(even, one, two)
@@ -343,6 +371,17 @@
 
 def up_pairs(axis):
     return [(i, i + 1) for i in range(lax.axis_size(axis) - 1)]
+
+
+def ring(axis):
+    size = lax.axis_size(axis)
+    return [(i, (i + 1) % size) for i in range(size)]
+
+
+def stacked(parts):
+    count = sum(part.shape[0] for part in parts)
+    fill = jnp.zeros((-count % 16, parts[0].shape[1]), parts[0].dtype)
+    return jnp.concatenate(parts + [fill], axis=0)
 
 
 def body(field, conv_first, norm_gain, norm_shift, conv_second):
@@ -351,22 +390,21 @@
     depth, lines, half = depth_in // 2, height_in // 2, width_in // 2
     cells, yface, xface = relayout(field)
 
-    last = cells[-1]
-    zhalo = lax.ppermute(last, "gz", up_pairs("gz"))
-    yhalo = lax.ppermute(yface, "gy", up_pairs("gy"))
-    nz = lax.axis_size("gz")
-    diagonal = [(a * nz + b, (a + 1) * nz + b + 1) for a, _ in up_pairs("gy") for b, _ in up_pairs("gz")]
-    yzhalo = lax.ppermute(yface[-1], ("gy", "gz"), diagonal)
-    yhalo = jnp.concatenate([yzhalo[None], yhalo], axis=0)
-    ztop = zhalo.reshape(lines, half, 4 * cin)[:, -1, 2 * cin :]
-    xown = jnp.concatenate([ztop[None], xface], axis=0)
-    ytop = yhalo[:, -1, cin:]
-    ytop = jnp.concatenate([jnp.zeros_like(ytop), ytop], axis=1)
-    xsend = jnp.concatenate([ytop[:, None], xown], axis=1)
-    xsend = jnp.pad(xsend, ((0, 0), (0, (-xsend.shape[1]) % 16), (0, 0)))
-    xhalo = lax.ppermute(xsend, "gx", up_pairs("gx"))
-
-    feats, moments, xfaces = features_of(cells, zhalo, yhalo, xhalo, conv_first)
+    place = [is_even(axis) for axis in ("gx", "gy", "gz")]
+    for axis in ("gx", "gy", "gz"):
+        place += [lax.axis_index(axis) > 0, lax.axis_index(axis) < lax.axis_size(axis) - 1]
+    place = jnp.stack(place).astype(jnp.int32)
+    zhalo = lax.ppermute(cells[-1], "gz", ring("gz"))
+    xhalo = lax.ppermute(xface.reshape(depth_in * lines, 2 * cin), "gx", ring("gx"))
+    xhalo = jnp.where(lax.axis_index("gx") > 0, xhalo, jnp.zeros_like(xhalo))
+    rim = xhalo.reshape(depth_in, lines, 2 * cin)
+    yhalo = lax.ppermute(stacked([yface.reshape(depth_in * half, 2 * cin), rim[:, -1]]), "gy", ring("gy"))
+    ny, nz = lax.axis_size("gy"), lax.axis_size("gz")
+    diagonal = [(a * nz + b, (a + 1) % ny * nz + (b + 1) % nz) for a in range(ny) for b in range(nz)]
+    yzhalo = lax.ppermute(stacked([yface[-1], rim[-1, -1:]]), ("gy", "gz"), diagonal)
+    xzhalo = lax.ppermute(stacked([rim[-1]]), "gz", ring("gz"))
+
+    feats, moments, xfaces = features_of(place, cells, zhalo, yhalo, yzhalo, xhalo, xzhalo, conv_first)
     rows = lines * half
     zs = faces("gz", feats[0], feats[-1])
     moments = added("gz", moments)
@@ -376,8 +414,7 @@
         here = slice(y * half, (y + 1) * half)
         return jnp.concatenate([feats[z, here] for z in range(depth)] + [side[here] for side in zsides], axis=0)
 
-    ys = faces("gy", yside(0), yside(lines - 1))
-    moments = added("gy", moments)
+    moments, ys = added_with_faces("gy", moments, yside(0), yside(lines - 1))
     ysides = sided(is_even("gy"), ys)
 
     def xside(n, x):
@@ -385,19 +422,7 @@
         return jnp.concatenate(own, axis=0)
 
     low, high = xside(0, 0), xside(1, half - 1)
-    if lax.axis_size("gx") == 2:
-        count = moments.shape[0]
-        both = jnp.concatenate([moments, jnp.where(is_even("gx"), high, low)], axis=0)
-        both = lax.ppermute(both, "gx", first_pairs("gx"))
-        moments = moments + both[:count]
-        xs = (both[count:], both[count:])
-    else:
-        xs = faces("gx", low, high)
-        moments = added("gx", moments)
-    place = [is_even(axis) for axis in ("gx", "gy", "gz")]
-    for axis in ("gx", "gy", "gz"):
-        place += [lax.axis_index(axis) > 0, lax.axis_index(axis) < lax.axis_size(axis) - 1]
-    place = jnp.stack(place).astype(jnp.int32)
+    moments, xs = added_with_faces("gx", moments, low, high)
     total_cells = rows * depth * lax.axis_size("gx") * lax.axis_size("gy") * lax.axis_size("gz")
     result = block(
         total_cells, place, moments, norm_gain[None], norm_shift[None], feats, zs, ys, xs,

time: 68.5 us -> 54.8 us (0.80)
  the two profiles are of different devices: /device:TPU:1 before, /device:TPU:12 now
where the time goes in v2:
time: 54.8 us; the launch traced here: 54.5 us
  starting transfers between devices  17.2 us (31%)
  waiting for transfers between devices  16.9 us (31%)
  Pallas kernels  13.7 us (25%)
  local copies, waits for them, and re-layouts  5.88 us (11%)
    pallas_call x1, Pallas kernels, block(): pl.pallas_call(functools.partial(block_kernel, total_cells), in_specs=[pl...  8.03 us
    ppermute x2, waiting for transfers between devices, added(): value = value + lax.ppermute(value, axis, second_pairs(axis))  7.22 us
    unnamed x24, local copies, waits for them, and re-layouts  5.31 us
    ppermute x2, waiting for transfers between devices, added_with_faces(): both = lax.ppermute(both, axis, first_pairs(axis))  3.78 us
    ppermute x1, waiting for transfers between devices, added_with_faces(): two = lax.ppermute(jnp.where(even, low, high), axis, inner)  3.51 us
    pallas_call x1, Pallas kernels, features_of(): pl.pallas_call(features_kernel, in_specs=[pl.BlockSpec(memory_space=pltpu...  3.42 us
    ppermute x1, starting transfers between devices, faces(): return (one, lax.ppermute(jnp.where(even, low, high), axis, inner))  3.17 us
    ppermute x1, starting transfers between devices, added_with_faces(): two = lax.ppermute(jnp.where(even, low, high), axis, inner)  2.57 us
  transfers between devices with their start and end apart: 13, of which 6 were waited for; matrix products, arithmetic and copies ran while one was open for 2% of the time, Pallas kernels for 0%

profile of v2, /device:TPU:12, one launch (start us, length us, event | category | flops | bytes accessed | tf_op | source)
XLA Modules:
  0.0 54.5 jit_solution(2264845960241196932)
XLA Ops:
  0.0 1.6 %copy-done = bf16[64,8,16,128]{3,2,1,0:T(8,128)(2,1)S(1)} copy-done((bf16[64,8,16,128]{3,2,1,0:T(8,128)(2,1)S(1)}, bf16[64,8,16,128]{3,2,1,0:T(8,128)(2,1)}, u32[]{:S(2)}) %copy-start) | copy-done | bytes 2097176
  1.6 2.3 %relayout.1 = (bf16[8,512,256]{2,1,0:T(8,128)(2,1)S(1)}, bf16[8,64,128]{2,1,0:T(8,128)(2,1)S(1)}, bf16[8,8,128]{2,1,0:T(8,128)(2,1)S(1)}) custom-call(bf16[64,8,16,128]{3,2,1,0:T(8,128)(2,1)S(1)} %copy-done), custom_call_target="tpu_custom_call" | custom-call | tf_op jit(solution)/shard_map/relayout/pallas_call | solution.py:66
  3.9 1.6 %collective-permute-start.1 = (bf16[64,128]{1,0:T(8,128)(2,1)S(1)}, bf16[64,128]{1,0:T(8,128)(2,1)S(1)}, u32[]{:S(2)}, u32[]{:S(2)}) collective-permute-start(bf16[64,128]{1,0:T(8,128)(2,1)S(1)} %bitcast.80), channel_id=1, source_target_pairs={{0,16},{16,0},{1,17},{17,1},{2,18},{18,2},{3,19},{19,3},{4,20},{20... | collective-permute-start | bytes 49160 | tf_op jit(solution)/shard_map/ppermute | solution.py:398
  5.5 1.6 %collective-permute-start = (bf16[512,256]{1,0:T(8,128)(2,1)S(1)}, bf16[512,256]{1,0:T(8,128)(2,1)S(1)}, u32[]{:S(2)}, u32[]{:S(2)}) collective-permute-start(bf16[512,256]{1,0:T(8,128)(2,1)S(1)} %slice_bitcast_fusion), channel_id=1, source_target_pairs={{0,1},{1,2},{2,3},{3,0},{4,5},{5,6},{6,7},{7,4},{8,9},{9,10},{10,1... | collective-permute-start | bytes 786440 | tf_op jit(solution)/shard_map/ppermute | solution.py:397
  7.1 0.1 pad.7.clone
  7.2 0.1 pad.10.clone
  7.3 0.4 collective-permute-done.1
  7.7 0.1 maximum_maximum_fusion.1
  7.8 0.1 collective-permute-start.3
  7.9 0.1 maximum_maximum_fusion
  8.0 1.7 %collective-permute-start.2 = (bf16[528,128]{1,0:T(8,128)(2,1)S(1)}, bf16[528,128]{1,0:T(8,128)(2,1)S(1)}, u32[]{:S(2)}, u32[]{:S(2)}) collective-permute-start(bf16[528,128]{1,0:T(8,128)(2,1)S(1)} %maximum_maximum_fusion), channel_id=1, source_target_pairs={{0,4},{4,8},{8,12},{12,0},{1,5},{5,9},{9,13},{13,1},{2,6},{6,10},{... | collective-permute-start | bytes 405512 | tf_op jit(solution)/shard_map/ppermute | solution.py:401
  9.7 0.6 %copy-done.3 = bf16[64,128]{1,0:T(8,128)(2,1)} copy-done((bf16[64,128]{1,0:T(8,128)(2,1)}, bf16[64,128]{1,0:T(8,128)(2,1)S(1)}, u32[]{:S(2)}) %copy-start.3) | copy-done | bytes 16408
  10.3 1.6 %collective-permute-start.4 = (bf16[16,128]{1,0:T(8,128)(2,1)S(1)}, bf16[16,128]{1,0:T(8,128)(2,1)S(1)}, u32[]{:S(2)}, u32[]{:S(2)}) collective-permute-start(bf16[16,128]{1,0:T(8,128)(2,1)S(1)} %concatenate.29), channel_id=1, source_target_pairs={{0,1},{1,2},{2,3},{3,0},{4,5},{5,6},{6,7},{7,4},{8,9},{9,10},{10,1... | collective-permute-start | bytes 12296 | tf_op jit(solution)/shard_map/ppermute | solution.py:405
  11.9 0.1 stack.39
  12.0 1.9 %collective-permute-done.4.xzhalo_ref = bf16[16,128]{1,0:T(8,128)(2,1)S(1)} collective-permute-done((bf16[16,128]{1,0:T(8,128)(2,1)S(1)}, bf16[16,128]{1,0:T(8,128)(2,1)S(1)}, u32[]{:S(2)}, u32[]{:S(2)}) %collective-permute-start.4) | collective-permute-done | bytes 4128 | tf_op jit(solution)/shard_map/ppermute | solution.py:405
  13.9 0.0 collective-permute-done.3.yzhalo_ref
  13.9 0.6 %copy-done.5 = bf16[80,128]{1,0:T(8,128)(2,1)} copy-done((bf16[80,128]{1,0:T(8,128)(2,1)}, bf16[80,128]{1,0:T(8,128)(2,1)S(1)}, u32[]{:S(2)}) %copy-start.5) | copy-done | bytes 20504
  14.5 0.0 collective-permute-done.2.yhalo_ref
  14.5 0.0 collective-permute-done.zhalo_ref
  14.5 1.0 %copy-done.2 = bf16[3,3,3,64,128]{4,3,2,1,0:T(8,128)(2,1)S(1)} copy-done((bf16[3,3,3,64,128]{4,3,2,1,0:T(8,128)(2,1)S(1)}, bf16[3,3,3,64,128]{4,3,2,1,0:T(8,128)(2,1)}, u32[]{:S(2)}) %copy-start.2) | copy-done | bytes 442392
  15.5 0.7 %copy-done.4 = bf16[64,128]{1,0:T(8,128)(2,1)S(1)} copy-done((bf16[64,128]{1,0:T(8,128)(2,1)S(1)}, bf16[64,128]{1,0:T(8,128)(2,1)}, u32[]{:S(2)}) %copy-start.4) | copy-done | bytes 16408
  16.2 0.7 %copy-done.6 = bf16[80,128]{1,0:T(8,128)(2,1)S(1)} copy-done((bf16[80,128]{1,0:T(8,128)(2,1)S(1)}, bf16[80,128]{1,0:T(8,128)(2,1)}, u32[]{:S(2)}) %copy-start.6) | copy-done | bytes 20504
  17.0 3.4 %features.1 = (f32[4,512,128]{2,1,0:T(8,128)S(1)}, f32[72,128]{1,0:T(8,128)S(1)}, f32[2,32,128]{2,1,0:T(8,128)S(1)}) custom-call(s32[9]{0:T(128)S(1)} %convert_element_type.3.place_ref, bf16[8,512,256]{2,1,0:T(8,128)(2,1)S(1)} %get-tuple-element.11.cells_ref, bf16[512,256]{1,0:T(8,128)(2,1)S(1)} %collective-permute-done.zhalo_ref, ...), custom_call_target="tpu_custom_call" | custom-call | tf_op jit(solution)/shard_map/features/pallas_call | solution.py:180
  20.4 2.3 %collective-permute-start.5 = (f32[72,128]{1,0:T(8,128)S(1)}, f32[72,128]{1,0:T(8,128)S(1)}, u32[]{:S(2)}, u32[]{:S(2)}) collective-permute-start(f32[72,128]{1,0:T(8,128)S(1)} %get-tuple-element.14), channel_id=1, source_target_pairs={{0,1},{1,0},{2,3},{3,2},{4,5},{5,4},{6,7},{7,6},{8,9},{9,8},{10,11... | collective-permute-start | bytes 110600 | tf_op jit(solution)/shard_map/ppermute | solution.py:342
  22.8 0.1 collective-permute-start.8
  22.8 3.2 %collective-permute-start.7 = (f32[512,128]{1,0:T(8,128)S(1)}, f32[512,128]{1,0:T(8,128)S(1)}, u32[]{:S(2)}, u32[]{:S(2)}) collective-permute-start(f32[512,128]{1,0:T(8,128)S(1)} %get-tuple-element.26), channel_id=1, source_target_pairs={{1,2},{2,1},{5,6},{6,5},{9,10},{10,9},{13,14},{14,13},{17,18},{18,... | collective-permute-start | bytes 786440 | tf_op jit(solution)/shard_map/ppermute | solution.py:332
  26.1 0.0 collective-permute-done.5
  26.1 0.8 %collective-permute-start.6 = (f32[72,128]{1,0:T(8,128)S(1)}, f32[72,128]{1,0:T(8,128)S(1)}, u32[]{:S(2)}, u32[]{:S(2)}) collective-permute-start(f32[72,128]{1,0:T(8,128)S(1)} %add.35), channel_id=1, source_target_pairs={{0,3},{1,2},{2,1},{3,0},{4,7},{5,6},{6,5},{7,4},{8,11},{9,10},{10,... | collective-permute-start | bytes 110600 | tf_op jit(solution)/shard_map/ppermute | solution.py:344
  26.9 7.2 %collective-permute-done.6 = f32[72,128]{1,0:T(8,128)S(1)} collective-permute-done((f32[72,128]{1,0:T(8,128)S(1)}, f32[72,128]{1,0:T(8,128)S(1)}, u32[]{:S(2)}, u32[]{:S(2)}) %collective-permute-start.6) | collective-permute-done | bytes 36896 | tf_op jit(solution)/shard_map/ppermute | solution.py:344
  34.1 0.0 copy-start.7
  34.1 0.0 copy-start.8
  34.1 0.0 collective-permute-done.8.z1_ref
  34.1 0.0 collective-permute-done.7.z2_ref
  34.2 0.1 broadcast_select_fusion.4
  34.3 0.1 collective-permute-start.9
  34.4 2.6 %collective-permute-start.11 = (f32[384,128]{1,0:T(8,128)S(1)}, f32[384,128]{1,0:T(8,128)S(1)}, u32[]{:S(2)}, u32[]{:S(2)}) collective-permute-start(f32[384,128]{1,0:T(8,128)S(1)} %get-tuple-element.31), channel_id=1, source_target_pairs={{4,8},{8,4},{5,9},{9,5},{6,10},{10,6},{7,11},{11,7},{20,24},{24,20... | collective-permute-start | bytes 589832 | tf_op jit(solution)/shard_map/ppermute | solution.py:363
  37.0 0.0 collective-permute-done.9
  37.0 1.2 %collective-permute-start.10 = (f32[72,128]{1,0:T(8,128)S(1)}, f32[72,128]{1,0:T(8,128)S(1)}, u32[]{:S(2)}, u32[]{:S(2)}) collective-permute-start(f32[72,128]{1,0:T(8,128)S(1)} %slice_add_fusion.1), channel_id=1, source_target_pairs={{0,12},{4,8},{8,4},{12,0},{1,13},{5,9},{9,5},{13,1},{2,14},{6,10},... | collective-permute-start | bytes 110600 | tf_op jit(solution)/shard_map/ppermute | solution.py:344
  38.1 3.5 %collective-permute-done.11.y2_ref = f32[384,128]{1,0:T(8,128)S(1)} collective-permute-done((f32[384,128]{1,0:T(8,128)S(1)}, f32[384,128]{1,0:T(8,128)S(1)}, u32[]{:S(2)}, u32[]{:S(2)}) %collective-permute-start.11) | collective-permute-done | bytes 196640 | tf_op jit(solution)/shard_map/ppermute | solution.py:363
  41.7 0.1 concatenate.34
  41.8 0.1 concatenate.33
  42.0 0.1 collective-permute-done.10
  42.1 0.6 %collective-permute-start.12 = (f32[132,128]{1,0:T(8,128)S(1)}, f32[132,128]{1,0:T(8,128)S(1)}, u32[]{:S(2)}, u32[]{:S(2)}) collective-permute-start(f32[132,128]{1,0:T(8,128)S(1)} %pad_maximum_fusion.1), channel_id=1, source_target_pairs={{0,16},{16,0},{1,17},{17,1},{2,18},{18,2},{3,19},{19,3},{4,20},{20... | collective-permute-start | bytes 202760 | tf_op jit(solution)/shard_map/ppermute | solution.py:358
  42.7 3.8 %collective-permute-done.12 = f32[132,128]{1,0:T(8,128)S(1)} collective-permute-done((f32[132,128]{1,0:T(8,128)S(1)}, f32[132,128]{1,0:T(8,128)S(1)}, u32[]{:S(2)}, u32[]{:S(2)}) %collective-permute-start.12) | collective-permute-done | bytes 67616 | tf_op jit(solution)/shard_map/ppermute | solution.py:358
  46.4 0.0 copy-done.1
  46.5 0.0 copy-done.7
  46.5 0.0 copy-done.8
  46.5 8.0 %block.1 = bf16[4,512,128]{2,1,0:T(8,128)(2,1)} custom-call(s32[9]{0:T(128)S(1)} %convert_element_type.3.place_ref, f32[72,128]{1,0:T(8,128)S(1)} %slice_add_fusion.mom_ref, f32[1,128]{1,0:T(1,128)S(1)} %bitcast.78, f32[1,128]{1,0:T(1,128)S(1)} %bitcast.79, f32[4,512,128]{2,1,0:T(8,128)S(1)} %get-tuple-element.15.feat_ref, ...), custom_call_target="tpu_custom_call" | custom-call | tf_op jit(solution)/shard_map/block/pallas_call | solution.py:288
  (44 shorter events, 0.4 us)
Async XLA Ops:
  0.0 1.6 %copy-start = (bf16[64,8,16,128]{3,2,1,0:T(8,128)(2,1)S(1)}, bf16[64,8,16,128]{3,2,1,0:T(8,128)(2,1)}, u32[]{:S(2)}) copy-start(bf16[64,8,16,128]{3,2,1,0:T(8,128)(2,1)} %field_ref.1) | copy-start | bytes 6291460
  3.9 3.8 %collective-permute-start.1 = (bf16[64,128]{1,0:T(8,128)(2,1)S(1)}, bf16[64,128]{1,0:T(8,128)(2,1)S(1)}, u32[]{:S(2)}, u32[]{:S(2)}) collective-permute-start(bf16[64,128]{1,0:T(8,128)(2,1)S(1)} %bitcast.80), channel_id=1, source_target_pairs={{0,16},{16,0},{1,17},{17,1},{2,18},{18,2},{3,19},{19,3},{4,20},{20... | collective-permute-start | bytes 49160 | tf_op jit(solution)/shard_map/ppermute | solution.py:398
  5.5 9.0 %collective-permute-start = (bf16[512,256]{1,0:T(8,128)(2,1)S(1)}, bf16[512,256]{1,0:T(8,128)(2,1)S(1)}, u32[]{:S(2)}, u32[]{:S(2)}) collective-permute-start(bf16[512,256]{1,0:T(8,128)(2,1)S(1)} %slice_bitcast_fusion), channel_id=1, source_target_pairs={{0,1},{1,2},{2,3},{3,0},{4,5},{5,6},{6,7},{7,4},{8,9},{9,10},{10,1... | collective-permute-start | bytes 786440 | tf_op jit(solution)/shard_map/ppermute | solution.py:397
  7.8 6.1 %collective-permute-start.3 = (bf16[80,128]{1,0:T(8,128)(2,1)S(1)}, bf16[80,128]{1,0:T(8,128)(2,1)S(1)}, u32[]{:S(2)}, u32[]{:S(2)}) collective-permute-start(bf16[80,128]{1,0:T(8,128)(2,1)S(1)} %maximum_maximum_fusion.1), channel_id=1, source_target_pairs={{0,5},{1,6},{2,7},{3,4},{4,9},{5,10},{6,11},{7,8},{8,13},{9,14},{1... | collective-permute-start | bytes 61448 | tf_op jit(solution)/shard_map/ppermute | solution.py:404
  8.0 6.5 %collective-permute-start.2 = (bf16[528,128]{1,0:T(8,128)(2,1)S(1)}, bf16[528,128]{1,0:T(8,128)(2,1)S(1)}, u32[]{:S(2)}, u32[]{:S(2)}) collective-permute-start(bf16[528,128]{1,0:T(8,128)(2,1)S(1)} %maximum_maximum_fusion), channel_id=1, source_target_pairs={{0,4},{4,8},{8,12},{12,0},{1,5},{5,9},{9,13},{13,1},{2,6},{6,10},{... | collective-permute-start | bytes 405512 | tf_op jit(solution)/shard_map/ppermute | solution.py:401
  9.7 0.6 %copy-start.3 = (bf16[64,128]{1,0:T(8,128)(2,1)}, bf16[64,128]{1,0:T(8,128)(2,1)S(1)}, u32[]{:S(2)}) copy-start(bf16[64,128]{1,0:T(8,128)(2,1)S(1)} %broadcast_select_fusion.7.xhalo_ref) | copy-start | bytes 49156
  10.3 3.6 %collective-permute-start.4 = (bf16[16,128]{1,0:T(8,128)(2,1)S(1)}, bf16[16,128]{1,0:T(8,128)(2,1)S(1)}, u32[]{:S(2)}, u32[]{:S(2)}) collective-permute-start(bf16[16,128]{1,0:T(8,128)(2,1)S(1)} %concatenate.29), channel_id=1, source_target_pairs={{0,1},{1,2},{2,3},{3,0},{4,5},{5,6},{6,7},{7,4},{8,9},{9,10},{10,1... | collective-permute-start | bytes 12296 | tf_op jit(solution)/shard_map/ppermute | solution.py:405
  13.9 0.6 %copy-start.5 = (bf16[80,128]{1,0:T(8,128)(2,1)}, bf16[80,128]{1,0:T(8,128)(2,1)S(1)}, u32[]{:S(2)}) copy-start(bf16[80,128]{1,0:T(8,128)(2,1)S(1)} %collective-permute-done.3.yzhalo_ref) | copy-start | bytes 61444
  14.5 1.0 %copy-start.2 = (bf16[3,3,3,64,128]{4,3,2,1,0:T(8,128)(2,1)S(1)}, bf16[3,3,3,64,128]{4,3,2,1,0:T(8,128)(2,1)}, u32[]{:S(2)}) copy-start(bf16[3,3,3,64,128]{4,3,2,1,0:T(8,128)(2,1)} %w_ref.1) | copy-start | bytes 1327108
  15.5 0.7 %copy-start.4 = (bf16[64,128]{1,0:T(8,128)(2,1)S(1)}, bf16[64,128]{1,0:T(8,128)(2,1)}, u32[]{:S(2)}) copy-start(bf16[64,128]{1,0:T(8,128)(2,1)} %copy-done.3) | copy-start | bytes 49156
  16.2 0.7 %copy-start.6 = (bf16[80,128]{1,0:T(8,128)(2,1)S(1)}, bf16[80,128]{1,0:T(8,128)(2,1)}, u32[]{:S(2)}) copy-start(bf16[80,128]{1,0:T(8,128)(2,1)} %copy-done.5) | copy-start | bytes 61444
  20.4 5.6 %collective-permute-start.5 = (f32[72,128]{1,0:T(8,128)S(1)}, f32[72,128]{1,0:T(8,128)S(1)}, u32[]{:S(2)}, u32[]{:S(2)}) collective-permute-start(f32[72,128]{1,0:T(8,128)S(1)} %get-tuple-element.14), channel_id=1, source_target_pairs={{0,1},{1,0},{2,3},{3,2},{4,5},{5,4},{6,7},{7,6},{8,9},{9,8},{10,11... | collective-permute-start | bytes 110600 | tf_op jit(solution)/shard_map/ppermute | solution.py:342
  22.8 11.3 %collective-permute-start.8 = (f32[512,128]{1,0:T(8,128)S(1)}, f32[512,128]{1,0:T(8,128)S(1)}, u32[]{:S(2)}, u32[]{:S(2)}) collective-permute-start(f32[512,128]{1,0:T(8,128)S(1)} %get-tuple-element.25), channel_id=1, source_target_pairs={{0,1},{1,0},{2,3},{3,2},{4,5},{5,4},{6,7},{7,6},{8,9},{9,8},{10,11... | collective-permute-start | bytes 786440 | tf_op jit(solution)/shard_map/ppermute | solution.py:328
  22.8 11.3 %collective-permute-start.7 = (f32[512,128]{1,0:T(8,128)S(1)}, f32[512,128]{1,0:T(8,128)S(1)}, u32[]{:S(2)}, u32[]{:S(2)}) collective-permute-start(f32[512,128]{1,0:T(8,128)S(1)} %get-tuple-element.26), channel_id=1, source_target_pairs={{1,2},{2,1},{5,6},{6,5},{9,10},{10,9},{13,14},{14,13},{17,18},{18,... | collective-permute-start | bytes 786440 | tf_op jit(solution)/shard_map/ppermute | solution.py:332
  26.1 8.0 %collective-permute-start.6 = (f32[72,128]{1,0:T(8,128)S(1)}, f32[72,128]{1,0:T(8,128)S(1)}, u32[]{:S(2)}, u32[]{:S(2)}) collective-permute-start(f32[72,128]{1,0:T(8,128)S(1)} %add.35), channel_id=1, source_target_pairs={{0,3},{1,2},{2,1},{3,0},{4,7},{5,6},{6,5},{7,4},{8,11},{9,10},{10,... | collective-permute-start | bytes 110600 | tf_op jit(solution)/shard_map/ppermute | solution.py:344
  34.1 12.4 %copy-start.1 = (bf16[3,3,3,128,128]{4,3,2,1,0:T(8,128)(2,1)S(1)}, bf16[3,3,3,128,128]{4,3,2,1,0:T(8,128)(2,1)}, u32[]{:S(2)}) copy-start(bf16[3,3,3,128,128]{4,3,2,1,0:T(8,128)(2,1)} %param.9) | copy-start | bytes 2654212
  34.1 12.4 %copy-start.7 = (f32[128]{0:T(128)S(1)}, f32[128]{0:T(128)}, u32[]{:S(2)}) copy-start(f32[128]{0:T(128)} %param.7) | copy-start | bytes 1540
  34.1 12.4 %copy-start.8 = (f32[128]{0:T(128)S(1)}, f32[128]{0:T(128)}, u32[]{:S(2)}) copy-start(f32[128]{0:T(128)} %param.8) | copy-start | bytes 1540
  34.3 2.7 %collective-permute-start.9 = (f32[456,128]{1,0:T(8,128)S(1)}, f32[456,128]{1,0:T(8,128)S(1)}, u32[]{:S(2)}, u32[]{:S(2)}) collective-permute-start(f32[456,128]{1,0:T(8,128)S(1)} %pad_maximum_fusion), channel_id=1, source_target_pairs={{0,4},{4,0},{8,12},{12,8},{1,5},{5,1},{9,13},{13,9},{2,6},{6,2},{1... | collective-permute-start | bytes 700424 | tf_op jit(solution)/shard_map/ppermute | solution.py:358
  34.4 7.3 %collective-permute-start.11 = (f32[384,128]{1,0:T(8,128)S(1)}, f32[384,128]{1,0:T(8,128)S(1)}, u32[]{:S(2)}, u32[]{:S(2)}) collective-permute-start(f32[384,128]{1,0:T(8,128)S(1)} %get-tuple-element.31), channel_id=1, source_target_pairs={{4,8},{8,4},{5,9},{9,5},{6,10},{10,6},{7,11},{11,7},{20,24},{24,20... | collective-permute-start | bytes 589832 | tf_op jit(solution)/shard_map/ppermute | solution.py:363
  37.0 5.1 %collective-permute-start.10 = (f32[72,128]{1,0:T(8,128)S(1)}, f32[72,128]{1,0:T(8,128)S(1)}, u32[]{:S(2)}, u32[]{:S(2)}) collective-permute-start(f32[72,128]{1,0:T(8,128)S(1)} %slice_add_fusion.1), channel_id=1, source_target_pairs={{0,12},{4,8},{8,4},{12,0},{1,13},{5,9},{9,5},{13,1},{2,14},{6,10},... | collective-permute-start | bytes 110600 | tf_op jit(solution)/shard_map/ppermute | solution.py:344
  42.1 4.4 %collective-permute-start.12 = (f32[132,128]{1,0:T(8,128)S(1)}, f32[132,128]{1,0:T(8,128)S(1)}, u32[]{:S(2)}, u32[]{:S(2)}) collective-permute-start(f32[132,128]{1,0:T(8,128)S(1)} %pad_maximum_fusion.1), channel_id=1, source_target_pairs={{0,16},{16,0},{1,17},{17,1},{2,18},{18,2},{3,19},{19,3},{4,20},{20... | collective-permute-start | bytes 202760 | tf_op jit(solution)/shard_map/ppermute | solution.py:358

commit v3 on v2

--- a/solution.py
+++ b/solution.py
@@ -18,10 +18,20 @@
     return lax.dot_general(a, b, (dims, ((), ())), preferred_element_type=F32)
 
 
+def thirds(value):
+    one = value.astype(BF16)
+    rest = value - one.astype(F32)
+    two = rest.astype(BF16)
+    return one, two, (rest - two.astype(F32)).astype(BF16)
+
+
 def dot_full(a, b):
-    return lax.dot_general(
-        a, b, (((1,), (0,)), ((), ())), precision=lax.Precision.HIGHEST, preferred_element_type=F32
-    )
+    (a1, a2, a3), (b1, b2, b3) = a, b
+    pair = jnp.concatenate([b1, b2], axis=1)
+    main = dot(jnp.concatenate([a1, a2], axis=1), jnp.concatenate([pair, pair], axis=0))
+    rest = dot(jnp.concatenate([a3, a1], axis=1), jnp.concatenate([b1, b3], axis=0))
+    width = b1.shape[1]
+    return main[:, :width] + (main[:, width:] + rest)
 
 
 def split(value):
@@ -83,27 +93,28 @@
     )(field)
 
 
-def features_kernel(
-    place_ref, cells_ref, zhalo_ref, yhalo_ref, yzhalo_ref, xhalo_ref, xzhalo_ref, w_ref,
-    feat_ref, mom_ref, xface_ref, w4_ref, wy_ref, wx_ref, acc_ref,
+def moved_down(value):
+    return jnp.where(iota(value.shape, 0) == 0, 0.0, pltpu.roll(value, 1, 0))
+
+
+def line_sums(acc_ref, line, half, cout):
+    span = pl.ds(line * half, half)
+    straight = acc_ref[span, :cout]
+    shifted = acc_ref[span, 2 * cout : 3 * cout]
+    if line > 0:
+        above = pl.ds((line - 1) * half, half)
+        straight = straight + acc_ref[above, cout : 2 * cout]
+        shifted = shifted + acc_ref[above, 3 * cout :]
+    return straight + moved_down(shifted)
+
+
+def interior_kernel(
+    lines, cells_ref, w_ref, v_ref, part_ref, stat_ref, wz_ref, wy_ref, wx_ref, v3_ref, w4_ref, acc_ref
 ):
     depth = cells_ref.shape[0] // 2
     cin, cout = w_ref.shape[3:]
     rows = cells_ref.shape[1]
-    lines = xhalo_ref.shape[0] // (2 * depth)
     half = rows // lines
-    y_in, z_in = place_ref[5] != 0, place_ref[7] != 0
-    zhalo = jnp.where(z_in, zhalo_ref[...], jnp.zeros(zhalo_ref.shape, BF16))
-    yrest = yhalo_ref[2 * depth * half :, :].astype(F32)
-    yhalo = [yzhalo_ref[:half, :]] + [yhalo_ref[z * half : (z + 1) * half, :] for z in range(2 * depth)]
-    yhalo = [jnp.where(y_in, value, jnp.zeros_like(value)) for value in yhalo]
-    yhalo[0] = jnp.where(z_in, yhalo[0], jnp.zeros_like(yhalo[0]))
-    corner = jnp.where(jnp.logical_and(y_in, z_in), yzhalo_ref[half:, :].astype(F32)[:1], 0.0)
-    yrest = jnp.where(y_in, yrest, 0.0)
-    here = [jnp.where(z_in, xzhalo_ref[...].astype(F32)[:lines], 0.0)]
-    here += [xhalo_ref[...].astype(F32)[z * lines : (z + 1) * lines] for z in range(2 * depth)]
-    over = [corner] + [yrest[z : z + 1] for z in range(2 * depth)]
-    over = [jnp.concatenate([line, value[: lines - 1]], axis=0) for line, value in zip(over, here, strict=True)]
     w4_ref[...] = jnp.zeros(w4_ref.shape, BF16)
     wx_ref[...] = jnp.zeros(wx_ref.shape, BF16)
     wy_ref[...] = jnp.zeros(wy_ref.shape, BF16)
@@ -126,75 +137,152 @@
         wx_ref[k : k + cin, :] = w_ref[dz, 1, 0]
         wx_ref[k + cin : k + 2 * cin, :] = w_ref[dz, 2, 0]
         wx_ref[k + 3 * cin : k + 4 * cin, :] = w_ref[dz, 0, 0]
-    first = iota((half, cout), 0) == 0
+    wz_ref[...] = w4_ref[0]
+    for dz in range(3):
+        for dy in range(3):
+            v3_ref[dy * 3 * cout : (dy + 1) * 3 * cout, (2 - dz) * cout : (3 - dz) * cout] = v_ref[dz, dy]
+    for zo in range(depth):
+        first = 0 if zo else 1
+        planes = [cells_ref[2 * zo - 1 + dz] for dz in range(first, 3)]
+        acc_ref[...] = dot(
+            jnp.concatenate(planes, axis=1), w4_ref[first:].reshape((3 - first) * 4 * cin, 4 * cout)
+        )
+        for line in range(lines):
+            part_ref[zo, pl.ds(line * half, half), :] = line_sums(acc_ref, line, half, cout)
+    inner = (lines - 1) * half
+    inside = iota((inner, cout), 0) % half != 0
     total = jnp.zeros((1, cout), F32)
+    for zo in range(1, depth):
+        total = total + jnp.sum(part_ref[zo, half:, :], axis=0, keepdims=True)
+    offset = total * (1.0 / max(1, (depth - 1) * inner))
+    gram, sums = jnp.zeros((cout, 2 * cout), F32), jnp.zeros((1, cout), F32)
+    for zo in range(1, depth):
+        value = jnp.where(inside, part_ref[zo, half:, :] - offset, 0.0)
+        hi, lo = split(value)
+        gram = gram + dot(hi, jnp.concatenate([hi, lo], axis=1), ((0,), (0,)))
+        sums = sums + jnp.sum(value, axis=0, keepdims=True)
+    stat_ref[:cout, :] = gram[:, :cout]
+    stat_ref[cout : 2 * cout, :] = gram[:, cout:]
+    stat_ref[2 * cout : 2 * cout + 8, :] = jnp.broadcast_to(sums, (8, cout))
+    stat_ref[2 * cout + 8 :, :] = jnp.broadcast_to(offset, (8, cout))
+
+
+def interior(lines, cells, weights, second):
+    depth, rows, wide = cells.shape
+    cin, cout = weights.shape[3:]
+    vmem = pl.BlockSpec(memory_space=pltpu.VMEM)
+    flops = depth // 2 * rows * 3 * wide * 8 * cout
+    return pl.pallas_call(
+        functools.partial(interior_kernel, lines),
+        in_specs=[vmem] * 3,
+        out_specs=[vmem] * 6,
+        out_shape=[
+            jax.ShapeDtypeStruct((depth // 2, rows, cout), F32),
+            jax.ShapeDtypeStruct((2 * cout + 16, cout), F32),
+            jax.ShapeDtypeStruct((wide, 4 * cout), BF16),
+            jax.ShapeDtypeStruct((6 * cin, 2 * cout), BF16),
+            jax.ShapeDtypeStruct((12 * cin, cout), BF16),
+            jax.ShapeDtypeStruct((9 * cout, 3 * cout), BF16),
+        ],
+        scratch_shapes=[pltpu.VMEM((3, wide, 4 * cout), BF16), pltpu.VMEM((rows, 4 * cout), F32)],
+        compiler_params=pltpu.CompilerParams(vmem_limit_bytes=20 * MIB),
+        cost_estimate=pl.CostEstimate(flops=flops, bytes_accessed=6 * MIB, transcendentals=0),
+        name="interior",
+    )(cells, weights, second)
+
+
+def finish_kernel(
+    place_ref, part_ref, stat_ref, zhalo_ref, yhalo_ref, yzhalo_ref, xhalo_ref, xzhalo_ref, wz_ref, wy_ref, wx_ref,
+    feat_ref, mom_ref, xface_ref, acc_ref, rim_ref,
+):
+    depth, rows, cout = part_ref.shape
+    lines = xhalo_ref.shape[0] // (2 * depth)
+    half = rows // lines
+    y_in, z_in = place_ref[5] != 0, place_ref[7] != 0
+    zhalo = jnp.where(z_in, zhalo_ref[...], jnp.zeros(zhalo_ref.shape, BF16))
+    yrest = yhalo_ref[2 * depth * half :, :].astype(F32)
+    yhalo = [yzhalo_ref[:half, :]] + [yhalo_ref[z * half : (z + 1) * half, :] for z in range(2 * depth)]
+    yhalo = [jnp.where(y_in, value, jnp.zeros_like(value)) for value in yhalo]
+    yhalo[0] = jnp.where(z_in, yhalo[0], jnp.zeros_like(yhalo[0]))
+    corner = jnp.where(jnp.logical_and(y_in, z_in), yzhalo_ref[half:, :].astype(F32)[:1], 0.0)
+    yrest = jnp.where(y_in, yrest, 0.0)
+    here = [jnp.where(z_in, xzhalo_ref[...].astype(F32)[:lines], 0.0)]
+    here += [xhalo_ref[...].astype(F32)[z * lines : (z + 1) * lines] for z in range(2 * depth)]
+    over = [corner] + [yrest[z : z + 1] for z in range(2 * depth)]
+    over = [jnp.concatenate([line, value[: lines - 1]], axis=0) for line, value in zip(over, here, strict=True)]
+    xparts = []
     for zo in range(depth):
-        before = zhalo if zo == 0 else cells_ref[2 * zo - 1]
-        acc_ref[...] = dot(
-            jnp.concatenate([before, cells_ref[2 * zo], cells_ref[2 * zo + 1]], axis=1),
-            w4_ref[...].reshape(3 * 4 * cin, 4 * cout),
-        )
-        ysum = dot(jnp.concatenate(yhalo[2 * zo : 2 * zo + 3], axis=1), wy_ref[...])
-        xparts = []
-        for dz in range(3):
-            xparts += [here[2 * zo + dz], over[2 * zo + dz]]
-        xsum = dot(jnp.concatenate(xparts, axis=1).astype(BF16), wx_ref[...])
+        row = [part for dz in range(3) for part in (here[2 * zo + dz], over[2 * zo + dz])]
+        xparts.append(jnp.concatenate(row, axis=1))
+    xsum = dot(jnp.concatenate(xparts, axis=0).astype(BF16), wx_ref[...])
+    yparts = [jnp.concatenate(yhalo[2 * zo : 2 * zo + 3], axis=1) for zo in range(depth)]
+    ysum = dot(jnp.concatenate(yparts, axis=0), wy_ref[...])
+    acc_ref[...] = dot(zhalo, wz_ref[...])
+    offset = stat_ref[2 * cout + 8 : 2 * cout + 9, :]
+    rim_ref[...] = jnp.zeros(rim_ref.shape, F32)
+    first = iota((8, cout), 0) == 0
+    edges = rows + (depth - 1) * half
+    for zo in range(depth):
         for line in range(lines):
             span = pl.ds(line * half, half)
-            straight = acc_ref[span, :cout]
-            shifted = acc_ref[span, 2 * cout : 3 * cout]
-            if line == 0:
-                straight = straight + ysum[:, :cout]
-                shifted = shifted + ysum[:, cout:]
+            k = zo * lines + line
+            if zo == 0 or line == 0:
+                value = part_ref[zo, span, :]
+                if zo == 0:
+                    value = value + line_sums(acc_ref, line, half, cout)
+                if line == 0:
+                    more = ysum[zo * half : (zo + 1) * half]
+                    value = value + (more[:, :cout] + moved_down(more[:, cout:]))
+                value = value + jnp.where(iota((half, cout), 0) == 0, xsum[k : k + 1], 0.0)
+                feat_ref[zo, span, :] = value
+                spot = line * half if zo == 0 else rows + (zo - 1) * half
+                rim_ref[spot : spot + half, :] = value - offset
+                xface_ref[0, k : k + 1, :] = value[:1]
+                xface_ref[1, k : k + 1, :] = value[half - 1 :]
             else:
-                above = pl.ds((line - 1) * half, half)
-                straight = straight + acc_ref[above, cout : 2 * cout]
-                shifted = shifted + acc_ref[above, 3 * cout :]
-            moved = jnp.where(first, xsum[line : line + 1], pltpu.roll(shifted, 1, 0))
-            value = straight + moved
-            feat_ref[zo, span, :] = value
-            xface_ref[0, zo * lines + line : zo * lines + line + 1, :] = value[:1]
-            xface_ref[1, zo * lines + line : zo * lines + line + 1, :] = value[half - 1 :]
-            total = total + jnp.sum(value, axis=0, keepdims=True)
-    count = depth * rows
-    mean = total * (1.0 / count)
-    gram = jnp.zeros((cout, 2 * cout), F32)
-    for zo in range(depth):
-        hi, lo = split(feat_ref[zo] - mean)
-        gram = gram + dot(hi, jnp.concatenate([hi, lo], axis=1), ((0,), (0,)))
-    cross = gram[:, cout:]
-    gram = gram[:, :cout] + cross + cross.T
+                top = pl.ds(line * half, 8)
+                value = part_ref[zo, top, :] + jnp.where(first, xsum[k : k + 1], 0.0)
+                feat_ref[zo, top, :] = value
+                feat_ref[zo, pl.ds(line * half + 8, half - 8), :] = part_ref[zo, pl.ds(line * half + 8, half - 8), :]
+                spot = edges + (zo - 1) * (lines - 1) + line - 1
+                rim_ref[spot : spot + 1, :] = value[:1] - offset
+                xface_ref[0, k : k + 1, :] = value[:1]
+                xface_ref[1, k : k + 1, :] = part_ref[zo, pl.ds((line + 1) * half - 1, 1), :]
+    rim = rim_ref[...]
+    hi, lo = split(rim)
+    gram = dot(hi, jnp.concatenate([hi, lo], axis=1), ((0,), (0,)))
+    cross = gram[:, cout:] + stat_ref[cout : 2 * cout, :]
+    gram = gram[:, :cout] + stat_ref[:cout, :] + cross + cross.T
+    sums = jnp.sum(rim, axis=0, keepdims=True) + stat_ref[2 * cout : 2 * cout + 1, :]
+    total = sums + offset * float(depth * rows)
     eye = iota((cout, cout), 0) == iota((cout, cout), 1)
-    column = jnp.sum(jnp.where(eye, jnp.broadcast_to(mean, (cout, cout)), 0.0), axis=1, keepdims=True)
-    gram = gram + (column * mean) * float(count)
+    sums_column = jnp.sum(jnp.where(eye, sums, 0.0), axis=1, keepdims=True)
+    offset_column = jnp.sum(jnp.where(eye, offset, 0.0), axis=1, keepdims=True)
+    gram = gram + (sums_column * offset + offset_column * total)
     left = iota((cout // 2, cout), 1) < cout // 2
     mom_ref[: cout // 2, :] = jnp.where(left, gram[: cout // 2], gram[cout // 2 :])
     mom_ref[cout // 2 :, :] = jnp.broadcast_to(total, (8, cout))
 
 
-def features_of(place, cells, zhalo, yhalo, yzhalo, xhalo, xzhalo, weights):
-    depth, rows, wide = cells.shape
-    cin, cout = weights.shape[3:]
-    lines = xhalo.shape[0] // depth
+def finish(place, part, stats, zhalo, yhalo, yzhalo, xhalo, xzhalo, wz, wy, wx):
+    depth, rows, cout = part.shape
+    lines = xhalo.shape[0] // (2 * depth)
+    half = rows // lines
+    rim = rows + (depth - 1) * (half + lines - 1)
     vmem = pl.BlockSpec(memory_space=pltpu.VMEM)
     return pl.pallas_call(
-        features_kernel,
-        in_specs=[pl.BlockSpec(memory_space=pltpu.SMEM)] + [vmem] * 7,
+        finish_kernel,
+        in_specs=[pl.BlockSpec(memory_space=pltpu.SMEM)] + [vmem] * 10,
         out_specs=[vmem] * 3,
         out_shape=[
-            jax.ShapeDtypeStruct((depth // 2, rows, cout), F32),
+            jax.ShapeDtypeStruct((depth, rows, cout), F32),
             jax.ShapeDtypeStruct((cout // 2 + 8, cout), F32),
-            jax.ShapeDtypeStruct((2, depth // 2 * lines, cout), F32),
+            jax.ShapeDtypeStruct((2, depth * lines, cout), F32),
         ],
-        scratch_shapes=[
-            pltpu.VMEM((3, wide, 4 * cout), BF16),
-            pltpu.VMEM((6 * cin, 2 * cout), BF16),
-            pltpu.VMEM((12 * cin, cout), BF16),
-            pltpu.VMEM((rows, 4 * cout), F32),
-        ],
-        compiler_params=pltpu.CompilerParams(vmem_limit_bytes=20 * MIB),
-        name="features",
-    )(place, cells, zhalo, yhalo, yzhalo, xhalo, xzhalo, weights)
+        scratch_shapes=[pltpu.VMEM((rows, 4 * cout), F32), pltpu.VMEM((rim + (-rim) % 16, cout), F32)],
+        compiler_params=pltpu.CompilerParams(vmem_limit_bytes=16 * MIB),
+        name="finish",
+    )(place, part, stats, zhalo, yhalo, yzhalo, xhalo, xzhalo, wz, wy, wx)
 
 
 def block_kernel(
@@ -220,9 +308,11 @@
     trace1 = jnp.sum(jnp.sum(diag[group:], axis=1, keepdims=True), axis=0, keepdims=True)
     trace = jnp.where(ri < group, trace0, trace1)
     scaled = cov / trace
+    scaled_parts = thirds(scaled)
     mat = jnp.where(eye, 1.5, 0.0) - 0.5 * scaled
     for _ in range(NEWTON - 1):
-        mat = 1.5 * mat - 0.5 * dot_full(dot_full(mat, mat), dot_full(mat, scaled))
+        parts = thirds(mat)
+        mat = 1.5 * mat - 0.5 * dot_full(thirds(dot_full(parts, parts)), thirds(dot_full(parts, scaled_parts)))
     gain = jnp.sum(jnp.where(eye, jnp.broadcast_to(gain_ref[...], square), 0.0), axis=1, keepdims=True)
     mat = mat / jnp.sqrt(trace) * gain
     hi, lo = split(mat)
@@ -272,12 +362,17 @@
                 wide_ref[zp, yp * half : (yp + 1) * half, dx * cout : (dx + 1) * cout] = pad_ref[
                     zp, yp, base - 1 + dx : base - 1 + dx + half, :
                 ].astype(BF16)
-    for z in range(depth):
-        acc = jnp.zeros((rows, cout), F32)
-        for dz in range(3):
-            for dy in range(3):
-                acc = acc + dot(wide_ref[z + dz, dy * half : dy * half + rows, :], w_ref[dz, dy])
-        out_ref[z] = acc.astype(BF16)
+    sums = [None] * depth
+    for zp in range(depth + 2):
+        low, high = max(zp - 2, 0), min(zp, depth - 1)
+        lanes = slice((low - zp + 2) * cout, (high - zp + 3) * cout)
+        taken = [wide_ref[zp, dy * half : dy * half + rows, :] for dy in range(3)]
+        got = dot(jnp.concatenate(taken, axis=1), w_ref[:, lanes])
+        for n, z in enumerate(range(low, high + 1)):
+            piece = got[:, n * cout : (n + 1) * cout]
+            sums[z] = piece if sums[z] is None else sums[z] + piece
+        if zp >= 2:
+            out_ref[zp - 2] = sums[zp - 2].astype(BF16)
 
 
 def block(total_cells, place, moments, gain, shift, feats, zs, ys, xs, weights):
@@ -404,7 +499,8 @@
     yzhalo = lax.ppermute(stacked([yface[-1], rim[-1, -1:]]), ("gy", "gz"), diagonal)
     xzhalo = lax.ppermute(stacked([rim[-1]]), "gz", ring("gz"))
 
-    feats, moments, xfaces = features_of(place, cells, zhalo, yhalo, yzhalo, xhalo, xzhalo, conv_first)
+    part, stats, wz, wy, wx, second = interior(lines, cells, conv_first, conv_second.reshape(3, 3, 3 * cout, cout))
+    feats, moments, xfaces = finish(place, part, stats, zhalo, yhalo, yzhalo, xhalo, xzhalo, wz, wy, wx)
     rows = lines * half
     zs = faces("gz", feats[0], feats[-1])
     moments = added("gz", moments)
@@ -425,8 +521,7 @@
     moments, xs = added_with_faces("gx", moments, low, high)
     total_cells = rows * depth * lax.axis_size("gx") * lax.axis_size("gy") * lax.axis_size("gz")
     result = block(
-        total_cells, place, moments, norm_gain[None], norm_shift[None], feats, zs, ys, xs,
-        conv_second.reshape(3, 3, 3 * cout, cout),
+        total_cells, place, moments, norm_gain[None], norm_shift[None], feats, zs, ys, xs, second,
     )
     return jnp.transpose(result.reshape(depth, lines, half, cout), (3, 0, 1, 2))
 

time: 54.8 us -> 60.9 us (1.11)
  the two profiles are of different devices: /device:TPU:12 before, /device:TPU:1 now
where the time goes in v3:
time: 60.9 us; the launch traced here: 60.6 us
  starting transfers between devices  20.3 us (33%)
  local copies, waits for them, and re-layouts  13.2 us (22%)
  Pallas kernels  13 us (21%)
  waiting for transfers between devices  12.1 us (20%)
  other arithmetic  1.71 us (3%)
    unnamed x36, local copies, waits for them, and re-layouts  11.9 us
    pallas_call x1, Pallas kernels, block(): pl.pallas_call(functools.partial(block_kernel, total_cells), in_specs=[pl...  6.85 us
    ppermute x2, waiting for transfers between devices, added(): value = value + lax.ppermute(value, axis, second_pairs(axis))  5.1 us
    ppermute x2, starting transfers between devices, added(): value = value + lax.ppermute(value, axis, second_pairs(axis))  3.65 us
    ppermute x2, starting transfers between devices, added_with_faces(): both = lax.ppermute(both, axis, first_pairs(axis))  3.5 us
    ppermute x1, starting transfers between devices, body(): lax.ppermute(stacked([yface.reshape(depth_in * half, 2 * cin), rim[:, -1]...  3.23 us
    ppermute x1, waiting for transfers between devices, added_with_faces(): two = lax.ppermute(jnp.where(even, low, high), axis, inner)  3.22 us
    pallas_call x1, Pallas kernels, interior(): pl.pallas_call(functools.partial(interior_kernel, lines), in_specs=[vmem]...  2.45 us
  transfers between devices with their start and end apart: 13, of which 6 were waited for; matrix products, arithmetic and copies ran while one was open for 4% of the time, Pallas kernels for 4%

profile of v3, /device:TPU:1, one launch (start us, length us, event | category | flops | bytes accessed | tf_op | source)
XLA Modules:
  0.0 60.6 jit_solution(8016378289761155546)
XLA Ops:
  0.0 1.6 %copy-done = bf16[64,8,16,128]{3,2,1,0:T(8,128)(2,1)S(1)} copy-done((bf16[64,8,16,128]{3,2,1,0:T(8,128)(2,1)S(1)}, bf16[64,8,16,128]{3,2,1,0:T(8,128)(2,1)}, u32[]{:S(2)}) %copy-start) | copy-done | bytes 2097176
  1.6 2.3 %relayout.1 = (bf16[8,512,256]{2,1,0:T(8,128)(2,1)S(1)}, bf16[8,64,128]{2,1,0:T(8,128)(2,1)S(1)}, bf16[8,8,128]{2,1,0:T(8,128)(2,1)S(1)}) custom-call(bf16[64,8,16,128]{3,2,1,0:T(8,128)(2,1)S(1)} %copy-done), custom_call_target="tpu_custom_call" | custom-call | tf_op jit(solution)/shard_map/relayout/pallas_call | solution.py:76
  3.9 0.7 %slice_bitcast_fusion = bf16[512,256]{1,0:T(8,128)(2,1)} fusion(bf16[8,512,256]{2,1,0:T(8,128)(2,1)S(1)} %get-tuple-element.17.cells_ref), kind=kLoop, calls=%fused_computation.2 | loop fusion | bytes 524288 | tf_op jit(solution)/shard_map/squeeze | solution.py:492
  4.6 1.3 %copy-done.9 = bf16[8,512,256]{2,1,0:T(8,128)(2,1)} copy-done((bf16[8,512,256]{2,1,0:T(8,128)(2,1)}, bf16[8,512,256]{2,1,0:T(8,128)(2,1)S(1)}, u32[]{:S(2)}) %copy-start.9) | copy-done | bytes 2097176
  6.0 2.1 %collective-permute-start = (bf16[512,256]{1,0:T(8,128)(2,1)}, bf16[512,256]{1,0:T(8,128)(2,1)S(1)}, u32[]{:S(2)}, u32[]{:S(2)}) collective-permute-start(bf16[512,256]{1,0:T(8,128)(2,1)} %slice_bitcast_fusion), channel_id=1, source_target_pairs={{0,1},{1,2},{2,3},{3,0},{4,5},{5,6},{6,7},{7,4},{8,9},{9,10},{10,1... | collective-permute-start | bytes 786440 | tf_op jit(solution)/shard_map/ppermute | solution.py:492
  8.1 1.2 %collective-permute-start.1 = (bf16[64,128]{1,0:T(8,128)(2,1)S(1)}, bf16[64,128]{1,0:T(8,128)(2,1)S(1)}, u32[]{:S(2)}, u32[]{:S(2)}) collective-permute-start(bf16[64,128]{1,0:T(8,128)(2,1)S(1)} %bitcast.80), channel_id=1, source_target_pairs={{0,16},{16,0},{1,17},{17,1},{2,18},{18,2},{3,19},{19,3},{4,20},{20... | collective-permute-start | bytes 49160 | tf_op jit(solution)/shard_map/ppermute | solution.py:493
  9.3 0.1 pad.10.clone
  9.4 0.1 pad.7.clone
  9.5 1.2 %collective-permute-done.1 = bf16[64,128]{1,0:T(8,128)(2,1)S(1)} collective-permute-done((bf16[64,128]{1,0:T(8,128)(2,1)S(1)}, bf16[64,128]{1,0:T(8,128)(2,1)S(1)}, u32[]{:S(2)}, u32[]{:S(2)}) %collective-permute-start.1) | collective-permute-done | bytes 16416 | tf_op jit(solution)/shard_map/ppermute | solution.py:493
  10.7 0.8 %maximum_maximum_fusion = bf16[528,128]{1,0:T(8,128)(2,1)} fusion(bf16[8,128]{1,0:T(8,128)(2,1)S(1)} %bitcast.89, bf16[512,128]{1,0:T(8,128)(2,1)S(1)} %bitcast.76, bf16[528]{0:T(1024)(128)(2,1)S(1)} %pad.10.clone), kind=kLoop, calls=%fused_computation.4 | loop fusion | flops 405504 | bytes 269344 | tf_op jit(solution)/shard_map/concatenate | solution.py:479
  11.5 3.2 %collective-permute-start.2 = (bf16[528,128]{1,0:T(8,128)(2,1)}, bf16[528,128]{1,0:T(8,128)(2,1)S(1)}, u32[]{:S(2)}, u32[]{:S(2)}) collective-permute-start(bf16[528,128]{1,0:T(8,128)(2,1)} %maximum_maximum_fusion), channel_id=1, source_target_pairs={{0,4},{4,8},{8,12},{12,0},{1,5},{5,9},{9,13},{13,1},{2,6},{6,10},{... | collective-permute-start | bytes 405512 | tf_op jit(solution)/shard_map/ppermute | solution.py:496
  14.7 0.7 %maximum_maximum_fusion.1 = bf16[80,128]{1,0:T(8,128)(2,1)} fusion(bf16[1,128]{1,0:T(2,128)(2,1)S(1)} %slice_bitcast_fusion.4, bf16[64,128]{1,0:T(8,128)(2,1)S(1)} %slice_bitcast_fusion.3, bf16[80]{0:T(256)(128)(2,1)S(1)} %pad.7.clone), kind=kLoop, calls=%fused_computation.26 | loop fusion | flops 61440 | bytes 37280 | tf_op jit(solution)/shard_map/concatenate | solution.py:479
  15.4 1.0 %collective-permute-start.3 = (bf16[80,128]{1,0:T(8,128)(2,1)}, bf16[80,128]{1,0:T(8,128)(2,1)S(1)}, u32[]{:S(2)}, u32[]{:S(2)}) collective-permute-start(bf16[80,128]{1,0:T(8,128)(2,1)} %maximum_maximum_fusion.1), channel_id=1, source_target_pairs={{0,5},{1,6},{2,7},{3,4},{4,9},{5,10},{6,11},{7,8},{8,13},{9,14},{1... | collective-permute-start | bytes 61448 | tf_op jit(solution)/shard_map/ppermute | solution.py:499
  16.5 1.3 %collective-permute-start.4 = (bf16[16,128]{1,0:T(8,128)(2,1)S(1)}, bf16[16,128]{1,0:T(8,128)(2,1)S(1)}, u32[]{:S(2)}, u32[]{:S(2)}) collective-permute-start(bf16[16,128]{1,0:T(8,128)(2,1)S(1)} %concatenate.29), channel_id=1, source_target_pairs={{0,1},{1,2},{2,3},{3,0},{4,5},{5,6},{6,7},{7,4},{8,9},{9,10},{10,1... | collective-permute-start | bytes 12296 | tf_op jit(solution)/shard_map/ppermute | solution.py:500
  17.8 1.6 %copy-done.10 = bf16[8,512,256]{2,1,0:T(8,128)(2,1)S(1)} copy-done((bf16[8,512,256]{2,1,0:T(8,128)(2,1)S(1)}, bf16[8,512,256]{2,1,0:T(8,128)(2,1)}, u32[]{:S(2)}) %copy-start.10) | copy-done | bytes 2097176
  19.4 1.0 %copy-done.14 = bf16[3,3,3,64,128]{4,3,2,1,0:T(8,128)(2,1)S(1)} copy-done((bf16[3,3,3,64,128]{4,3,2,1,0:T(8,128)(2,1)S(1)}, bf16[3,3,3,64,128]{4,3,2,1,0:T(8,128)(2,1)}, u32[]{:S(2)}) %copy-start.14) | copy-done | bytes 442392
  20.4 2.5 %interior.1 = (f32[4,512,128]{2,1,0:T(8,128)S(1)}, f32[272,128]{1,0:T(8,128)S(1)}, bf16[256,512]{1,0:T(8,128)(2,1)S(1)}, bf16[384,256]{1,0:T(8,128)(2,1)S(1)}, b...) custom-call(bf16[8,512,256]{2,1,0:T(8,128)(2,1)S(1)} %copy-done.10, ...), custom_call_target="tpu_custom_call" | custom-call | flops 1610612736 | bytes 6291456 | tf_op jit(solution)/shard_map/interior/pallas_call | solution.py:175
  22.9 0.7 %copy-done.1 = bf16[384,256]{1,0:T(8,128)(2,1)} copy-done((bf16[384,256]{1,0:T(8,128)(2,1)}, bf16[384,256]{1,0:T(8,128)(2,1)S(1)}, u32[]{:S(2)}) %copy-start.1) | copy-done | bytes 196632
  23.6 0.7 %copy-done.3 = bf16[768,128]{1,0:T(8,128)(2,1)} copy-done((bf16[768,128]{1,0:T(8,128)(2,1)}, bf16[768,128]{1,0:T(8,128)(2,1)S(1)}, u32[]{:S(2)}) %copy-start.3) | copy-done | bytes 196632
  24.2 0.7 %copy-done.5 = f32[272,128]{1,0:T(8,128)} copy-done((f32[272,128]{1,0:T(8,128)}, f32[272,128]{1,0:T(8,128)S(1)}, u32[]{:S(2)}) %copy-start.5) | copy-done | bytes 139288
  24.9 0.1 stack.39
  25.0 0.0 collective-permute-done.4.xzhalo_ref
  25.0 0.0 collective-permute-done.3.yzhalo_ref
  25.0 0.7 %copy-done.7 = bf16[528,128]{1,0:T(8,128)(2,1)} copy-done((bf16[528,128]{1,0:T(8,128)(2,1)}, bf16[528,128]{1,0:T(8,128)(2,1)S(1)}, u32[]{:S(2)}) %copy-start.7) | copy-done | bytes 135192
  25.7 0.9 %copy-done.2 = bf16[384,256]{1,0:T(8,128)(2,1)S(1)} copy-done((bf16[384,256]{1,0:T(8,128)(2,1)S(1)}, bf16[384,256]{1,0:T(8,128)(2,1)}, u32[]{:S(2)}) %copy-start.2) | copy-done | bytes 196632
  26.6 0.9 %copy-done.4 = bf16[768,128]{1,0:T(8,128)(2,1)S(1)} copy-done((bf16[768,128]{1,0:T(8,128)(2,1)S(1)}, bf16[768,128]{1,0:T(8,128)(2,1)}, u32[]{:S(2)}) %copy-start.4) | copy-done | bytes 196632
  27.6 0.9 %copy-done.6 = f32[272,128]{1,0:T(8,128)S(1)} copy-done((f32[272,128]{1,0:T(8,128)S(1)}, f32[272,128]{1,0:T(8,128)}, u32[]{:S(2)}) %copy-start.6) | copy-done | bytes 139288
  28.5 0.9 %copy-done.8 = bf16[528,128]{1,0:T(8,128)(2,1)S(1)} copy-done((bf16[528,128]{1,0:T(8,128)(2,1)S(1)}, bf16[528,128]{1,0:T(8,128)(2,1)}, u32[]{:S(2)}) %copy-start.8) | copy-done | bytes 135192
  29.4 1.4 %finish.1 = (f32[4,512,128]{2,1,0:T(8,128)S(1)}, f32[72,128]{1,0:T(8,128)S(1)}, f32[2,32,128]{2,1,0:T(8,128)S(1)}) custom-call(s32[9]{0:T(128)S(1)} %convert_element_type.3.place_ref, f32[4,512,128]{2,1,0:T(8,128)S(1)} %get-tuple-element.18.part_ref, f32[272,128]{1,0:T(8,128)S(1)} %copy-done.6, bf16[512,256]{1,0:T(8,128)(2,1)S(1)} %collective-permute-done.zhalo_ref, ...), custom_call_target="tpu_custom_call" | custom-call | tf_op jit(solution)/shard_map/finish/pallas_call | solution.py:273
  30.8 0.4 collective-permute-start.5
  31.1 1.2 %collective-permute-start.8 = (f32[512,128]{1,0:T(8,128)S(1)}, f32[512,128]{1,0:T(8,128)S(1)}, u32[]{:S(2)}, u32[]{:S(2)}) collective-permute-start(f32[512,128]{1,0:T(8,128)S(1)} %get-tuple-element.37), channel_id=1, source_target_pairs={{0,1},{1,0},{2,3},{3,2},{4,5},{5,4},{6,7},{7,6},{8,9},{9,8},{10,11... | collective-permute-start | bytes 786440 | tf_op jit(solution)/shard_map/ppermute | solution.py:423
  32.3 0.7 %collective-permute-start.7 = (f32[512,128]{1,0:T(8,128)S(1)}, f32[512,128]{1,0:T(8,128)S(1)}, u32[]{:S(2)}, u32[]{:S(2)}) collective-permute-start(f32[512,128]{1,0:T(8,128)S(1)} %get-tuple-element.38), channel_id=1, source_target_pairs={{1,2},{2,1},{5,6},{6,5},{9,10},{10,9},{13,14},{14,13},{17,18},{18,... | collective-permute-start | bytes 786440 | tf_op jit(solution)/shard_map/ppermute | solution.py:427
  33.0 0.6 %collective-permute-done.5 = f32[72,128]{1,0:T(8,128)S(1)} collective-permute-done((f32[72,128]{1,0:T(8,128)S(1)}, f32[72,128]{1,0:T(8,128)S(1)}, u32[]{:S(2)}, u32[]{:S(2)}) %collective-permute-start.5) | collective-permute-done | bytes 36896 | tf_op jit(solution)/shard_map/ppermute | solution.py:437
  33.7 2.0 %collective-permute-start.6 = (f32[72,128]{1,0:T(8,128)S(1)}, f32[72,128]{1,0:T(8,128)S(1)}, u32[]{:S(2)}, u32[]{:S(2)}) collective-permute-start(f32[72,128]{1,0:T(8,128)S(1)} %add.35), channel_id=1, source_target_pairs={{0,3},{1,2},{2,1},{3,0},{4,7},{5,6},{6,5},{7,4},{8,11},{9,10},{10,... | collective-permute-start | bytes 110600 | tf_op jit(solution)/shard_map/ppermute | solution.py:439
  35.6 5.0 %collective-permute-done.6 = f32[72,128]{1,0:T(8,128)S(1)} collective-permute-done((f32[72,128]{1,0:T(8,128)S(1)}, f32[72,128]{1,0:T(8,128)S(1)}, u32[]{:S(2)}, u32[]{:S(2)}) %collective-permute-start.6) | collective-permute-done | bytes 36896 | tf_op jit(solution)/shard_map/ppermute | solution.py:439
  40.7 0.0 copy-start.12
  40.7 0.0 collective-permute-done.8.z1_ref
  40.7 0.0 collective-permute-done.7.z2_ref
  40.9 2.2 %collective-permute-start.9 = (f32[456,128]{1,0:T(8,128)S(1)}, f32[456,128]{1,0:T(8,128)S(1)}, u32[]{:S(2)}, u32[]{:S(2)}) collective-permute-start(f32[456,128]{1,0:T(8,128)S(1)} %pad_maximum_fusion), channel_id=1, source_target_pairs={{0,4},{4,0},{8,12},{12,8},{1,5},{5,1},{9,13},{13,9},{2,6},{6,2},{1... | collective-permute-start | bytes 700424 | tf_op jit(solution)/shard_map/ppermute | solution.py:453
  43.1 2.0 %collective-permute-start.11 = (f32[384,128]{1,0:T(8,128)S(1)}, f32[384,128]{1,0:T(8,128)S(1)}, u32[]{:S(2)}, u32[]{:S(2)}) collective-permute-start(f32[384,128]{1,0:T(8,128)S(1)} %get-tuple-element.43), channel_id=1, source_target_pairs={{4,8},{8,4},{5,9},{9,5},{6,10},{10,6},{7,11},{11,7},{20,24},{24,20... | collective-permute-start | bytes 589832 | tf_op jit(solution)/shard_map/ppermute | solution.py:458
  45.2 1.7 %collective-permute-start.10 = (f32[72,128]{1,0:T(8,128)S(1)}, f32[72,128]{1,0:T(8,128)S(1)}, u32[]{:S(2)}, u32[]{:S(2)}) collective-permute-start(f32[72,128]{1,0:T(8,128)S(1)} %slice_add_fusion.1), channel_id=1, source_target_pairs={{0,12},{4,8},{8,4},{12,0},{1,13},{5,9},{9,5},{13,1},{2,14},{6,10},... | collective-permute-start | bytes 110600 | tf_op jit(solution)/shard_map/ppermute | solution.py:439
  46.9 3.2 %collective-permute-done.11.y2_ref = f32[384,128]{1,0:T(8,128)S(1)} collective-permute-done((f32[384,128]{1,0:T(8,128)S(1)}, f32[384,128]{1,0:T(8,128)S(1)}, u32[]{:S(2)}, u32[]{:S(2)}) %collective-permute-start.11) | collective-permute-done | bytes 196640 | tf_op jit(solution)/shard_map/ppermute | solution.py:458
  50.2 0.1 concatenate.33
  50.3 0.1 concatenate.34
  50.4 0.1 collective-permute-done.10
  50.5 1.3 %collective-permute-start.12 = (f32[132,128]{1,0:T(8,128)S(1)}, f32[132,128]{1,0:T(8,128)S(1)}, u32[]{:S(2)}, u32[]{:S(2)}) collective-permute-start(f32[132,128]{1,0:T(8,128)S(1)} %pad_maximum_fusion.1), channel_id=1, source_target_pairs={{0,16},{16,0},{1,17},{17,1},{2,18},{18,2},{3,19},{19,3},{4,20},{20... | collective-permute-start | bytes 202760 | tf_op jit(solution)/shard_map/ppermute | solution.py:453
  51.8 2.0 %collective-permute-done.12 = f32[132,128]{1,0:T(8,128)S(1)} collective-permute-done((f32[132,128]{1,0:T(8,128)S(1)}, f32[132,128]{1,0:T(8,128)S(1)}, u32[]{:S(2)}, u32[]{:S(2)}) %collective-permute-start.12) | collective-permute-done | bytes 67616 | tf_op jit(solution)/shard_map/ppermute | solution.py:453
  53.7 6.9 %block.1 = bf16[4,512,128]{2,1,0:T(8,128)(2,1)} custom-call(s32[9]{0:T(128)S(1)} %convert_element_type.3.place_ref, f32[72,128]{1,0:T(8,128)S(1)} %slice_add_fusion.mom_ref, f32[1,128]{1,0:T(1,128)S(1)} %bitcast.77, f32[1,128]{1,0:T(1,128)S(1)} %bitcast.78, f32[4,512,128]{2,1,0:T(8,128)S(1)} %get-tuple-element.26.feat_ref, ...), custom_call_target="tpu_custom_call" | custom-call | tf_op jit(solution)/shard_map/block/pallas_call | solution.py:383
  (57 shorter events, 0.4 us)
Async XLA Ops:
  0.0 1.6 %copy-start = (bf16[64,8,16,128]{3,2,1,0:T(8,128)(2,1)S(1)}, bf16[64,8,16,128]{3,2,1,0:T(8,128)(2,1)}, u32[]{:S(2)}) copy-start(bf16[64,8,16,128]{3,2,1,0:T(8,128)(2,1)} %field_ref.1) | copy-start | bytes 6291460
  1.6 16.2 %copy-start.13 = (bf16[3,3,3,128,128]{4,3,2,1,0:T(8,128)(2,1)S(1)}, bf16[3,3,3,128,128]{4,3,2,1,0:T(8,128)(2,1)}, u32[]{:S(2)}) copy-start(bf16[3,3,3,128,128]{4,3,2,1,0:T(8,128)(2,1)} %param.9) | copy-start | bytes 2654212
  4.6 1.3 %copy-start.9 = (bf16[8,512,256]{2,1,0:T(8,128)(2,1)}, bf16[8,512,256]{2,1,0:T(8,128)(2,1)S(1)}, u32[]{:S(2)}) copy-start(bf16[8,512,256]{2,1,0:T(8,128)(2,1)S(1)} %get-tuple-element.17.cells_ref) | copy-start | bytes 6291460
  6.0 19.7 %collective-permute-start = (bf16[512,256]{1,0:T(8,128)(2,1)}, bf16[512,256]{1,0:T(8,128)(2,1)S(1)}, u32[]{:S(2)}, u32[]{:S(2)}) collective-permute-start(bf16[512,256]{1,0:T(8,128)(2,1)} %slice_bitcast_fusion), channel_id=1, source_target_pairs={{0,1},{1,2},{2,3},{3,0},{4,5},{5,6},{6,7},{7,4},{8,9},{9,10},{10,1... | collective-permute-start | bytes 786440 | tf_op jit(solution)/shard_map/ppermute | solution.py:492
  8.1 2.6 %collective-permute-start.1 = (bf16[64,128]{1,0:T(8,128)(2,1)S(1)}, bf16[64,128]{1,0:T(8,128)(2,1)S(1)}, u32[]{:S(2)}, u32[]{:S(2)}) collective-permute-start(bf16[64,128]{1,0:T(8,128)(2,1)S(1)} %bitcast.80), channel_id=1, source_target_pairs={{0,16},{16,0},{1,17},{17,1},{2,18},{18,2},{3,19},{19,3},{4,20},{20... | collective-permute-start | bytes 49160 | tf_op jit(solution)/shard_map/ppermute | solution.py:493
  11.5 13.5 %collective-permute-start.2 = (bf16[528,128]{1,0:T(8,128)(2,1)}, bf16[528,128]{1,0:T(8,128)(2,1)S(1)}, u32[]{:S(2)}, u32[]{:S(2)}) collective-permute-start(bf16[528,128]{1,0:T(8,128)(2,1)} %maximum_maximum_fusion), channel_id=1, source_target_pairs={{0,4},{4,8},{8,12},{12,0},{1,5},{5,9},{9,13},{13,1},{2,6},{6,10},{... | collective-permute-start | bytes 405512 | tf_op jit(solution)/shard_map/ppermute | solution.py:496
  15.4 9.6 %collective-permute-start.3 = (bf16[80,128]{1,0:T(8,128)(2,1)}, bf16[80,128]{1,0:T(8,128)(2,1)S(1)}, u32[]{:S(2)}, u32[]{:S(2)}) collective-permute-start(bf16[80,128]{1,0:T(8,128)(2,1)} %maximum_maximum_fusion.1), channel_id=1, source_target_pairs={{0,5},{1,6},{2,7},{3,4},{4,9},{5,10},{6,11},{7,8},{8,13},{9,14},{1... | collective-permute-start | bytes 61448 | tf_op jit(solution)/shard_map/ppermute | solution.py:499
  16.5 8.5 %collective-permute-start.4 = (bf16[16,128]{1,0:T(8,128)(2,1)S(1)}, bf16[16,128]{1,0:T(8,128)(2,1)S(1)}, u32[]{:S(2)}, u32[]{:S(2)}) collective-permute-start(bf16[16,128]{1,0:T(8,128)(2,1)S(1)} %concatenate.29), channel_id=1, source_target_pairs={{0,1},{1,2},{2,3},{3,0},{4,5},{5,6},{6,7},{7,4},{8,9},{9,10},{10,1... | collective-permute-start | bytes 12296 | tf_op jit(solution)/shard_map/ppermute | solution.py:500
  17.8 1.6 %copy-start.10 = (bf16[8,512,256]{2,1,0:T(8,128)(2,1)S(1)}, bf16[8,512,256]{2,1,0:T(8,128)(2,1)}, u32[]{:S(2)}) copy-start(bf16[8,512,256]{2,1,0:T(8,128)(2,1)} %copy-done.9) | copy-start | bytes 6291460
  19.4 1.0 %copy-start.14 = (bf16[3,3,3,64,128]{4,3,2,1,0:T(8,128)(2,1)S(1)}, bf16[3,3,3,64,128]{4,3,2,1,0:T(8,128)(2,1)}, u32[]{:S(2)}) copy-start(bf16[3,3,3,64,128]{4,3,2,1,0:T(8,128)(2,1)} %w_ref.1) | copy-start | bytes 1327108
  22.9 0.7 %copy-start.1 = (bf16[384,256]{1,0:T(8,128)(2,1)}, bf16[384,256]{1,0:T(8,128)(2,1)S(1)}, u32[]{:S(2)}) copy-start(bf16[384,256]{1,0:T(8,128)(2,1)S(1)} %get-tuple-element.23.wy_ref) | copy-start | bytes 589828
  23.6 0.7 %copy-start.3 = (bf16[768,128]{1,0:T(8,128)(2,1)}, bf16[768,128]{1,0:T(8,128)(2,1)S(1)}, u32[]{:S(2)}) copy-start(bf16[768,128]{1,0:T(8,128)(2,1)S(1)} %get-tuple-element.24.wx_ref) | copy-start | bytes 589828
  24.2 0.7 %copy-start.5 = (f32[272,128]{1,0:T(8,128)}, f32[272,128]{1,0:T(8,128)S(1)}, u32[]{:S(2)}) copy-start(f32[272,128]{1,0:T(8,128)S(1)} %get-tuple-element.19.stat_ref) | copy-start | bytes 417796
  25.0 0.7 %copy-start.7 = (bf16[528,128]{1,0:T(8,128)(2,1)}, bf16[528,128]{1,0:T(8,128)(2,1)S(1)}, u32[]{:S(2)}) copy-start(bf16[528,128]{1,0:T(8,128)(2,1)S(1)} %collective-permute-done.2.yhalo_ref) | copy-start | bytes 405508
  25.7 0.9 %copy-start.2 = (bf16[384,256]{1,0:T(8,128)(2,1)S(1)}, bf16[384,256]{1,0:T(8,128)(2,1)}, u32[]{:S(2)}) copy-start(bf16[384,256]{1,0:T(8,128)(2,1)} %copy-done.1) | copy-start | bytes 589828
  26.6 0.9 %copy-start.4 = (bf16[768,128]{1,0:T(8,128)(2,1)S(1)}, bf16[768,128]{1,0:T(8,128)(2,1)}, u32[]{:S(2)}) copy-start(bf16[768,128]{1,0:T(8,128)(2,1)} %copy-done.3) | copy-start | bytes 589828
  27.5 0.9 %copy-start.6 = (f32[272,128]{1,0:T(8,128)S(1)}, f32[272,128]{1,0:T(8,128)}, u32[]{:S(2)}) copy-start(f32[272,128]{1,0:T(8,128)} %copy-done.5) | copy-start | bytes 417796
  28.5 0.9 %copy-start.8 = (bf16[528,128]{1,0:T(8,128)(2,1)S(1)}, bf16[528,128]{1,0:T(8,128)(2,1)}, u32[]{:S(2)}) copy-start(bf16[528,128]{1,0:T(8,128)(2,1)} %copy-done.7) | copy-start | bytes 405508
  30.8 2.9 %collective-permute-start.5 = (f32[72,128]{1,0:T(8,128)S(1)}, f32[72,128]{1,0:T(8,128)S(1)}, u32[]{:S(2)}, u32[]{:S(2)}) collective-permute-start(f32[72,128]{1,0:T(8,128)S(1)} %get-tuple-element.25), channel_id=1, source_target_pairs={{0,1},{1,0},{2,3},{3,2},{4,5},{5,4},{6,7},{7,6},{8,9},{9,8},{10,11... | collective-permute-start | bytes 110600 | tf_op jit(solution)/shard_map/ppermute | solution.py:437
  31.1 9.5 %collective-permute-start.8 = (f32[512,128]{1,0:T(8,128)S(1)}, f32[512,128]{1,0:T(8,128)S(1)}, u32[]{:S(2)}, u32[]{:S(2)}) collective-permute-start(f32[512,128]{1,0:T(8,128)S(1)} %get-tuple-element.37), channel_id=1, source_target_pairs={{0,1},{1,0},{2,3},{3,2},{4,5},{5,4},{6,7},{7,6},{8,9},{9,8},{10,11... | collective-permute-start | bytes 786440 | tf_op jit(solution)/shard_map/ppermute | solution.py:423
  32.3 8.4 %collective-permute-start.7 = (f32[512,128]{1,0:T(8,128)S(1)}, f32[512,128]{1,0:T(8,128)S(1)}, u32[]{:S(2)}, u32[]{:S(2)}) collective-permute-start(f32[512,128]{1,0:T(8,128)S(1)} %get-tuple-element.38), channel_id=1, source_target_pairs={{1,2},{2,1},{5,6},{6,5},{9,10},{10,9},{13,14},{14,13},{17,18},{18,... | collective-permute-start | bytes 786440 | tf_op jit(solution)/shard_map/ppermute | solution.py:427
  33.7 7.0 %collective-permute-start.6 = (f32[72,128]{1,0:T(8,128)S(1)}, f32[72,128]{1,0:T(8,128)S(1)}, u32[]{:S(2)}, u32[]{:S(2)}) collective-permute-start(f32[72,128]{1,0:T(8,128)S(1)} %add.35), channel_id=1, source_target_pairs={{0,3},{1,2},{2,1},{3,0},{4,7},{5,6},{6,5},{7,4},{8,11},{9,10},{10,... | collective-permute-start | bytes 110600 | tf_op jit(solution)/shard_map/ppermute | solution.py:439
  40.7 13.1 %copy-start.11 = (f32[128]{0:T(128)S(1)}, f32[128]{0:T(128)}, u32[]{:S(2)}) copy-start(f32[128]{0:T(128)} %param.7) | copy-start | bytes 1540
  40.7 13.1 %copy-start.12 = (f32[128]{0:T(128)S(1)}, f32[128]{0:T(128)}, u32[]{:S(2)}) copy-start(f32[128]{0:T(128)} %param.8) | copy-start | bytes 1540
  40.9 4.3 %collective-permute-start.9 = (f32[456,128]{1,0:T(8,128)S(1)}, f32[456,128]{1,0:T(8,128)S(1)}, u32[]{:S(2)}, u32[]{:S(2)}) collective-permute-start(f32[456,128]{1,0:T(8,128)S(1)} %pad_maximum_fusion), channel_id=1, source_target_pairs={{0,4},{4,0},{8,12},{12,8},{1,5},{5,1},{9,13},{13,9},{2,6},{6,2},{1... | collective-permute-start | bytes 700424 | tf_op jit(solution)/shard_map/ppermute | solution.py:453
  43.1 7.0 %collective-permute-start.11 = (f32[384,128]{1,0:T(8,128)S(1)}, f32[384,128]{1,0:T(8,128)S(1)}, u32[]{:S(2)}, u32[]{:S(2)}) collective-permute-start(f32[384,128]{1,0:T(8,128)S(1)} %get-tuple-element.43), channel_id=1, source_target_pairs={{4,8},{8,4},{5,9},{9,5},{6,10},{10,6},{7,11},{11,7},{20,24},{24,20... | collective-permute-start | bytes 589832 | tf_op jit(solution)/shard_map/ppermute | solution.py:458
  45.2 5.3 %collective-permute-start.10 = (f32[72,128]{1,0:T(8,128)S(1)}, f32[72,128]{1,0:T(8,128)S(1)}, u32[]{:S(2)}, u32[]{:S(2)}) collective-permute-start(f32[72,128]{1,0:T(8,128)S(1)} %slice_add_fusion.1), channel_id=1, source_target_pairs={{0,12},{4,8},{8,4},{12,0},{1,13},{5,9},{9,5},{13,1},{2,14},{6,10},... | collective-permute-start | bytes 110600 | tf_op jit(solution)/shard_map/ppermute | solution.py:439
  50.5 3.2 %collective-permute-start.12 = (f32[132,128]{1,0:T(8,128)S(1)}, f32[132,128]{1,0:T(8,128)S(1)}, u32[]{:S(2)}, u32[]{:S(2)}) collective-permute-start(f32[132,128]{1,0:T(8,128)S(1)} %pad_maximum_fusion.1), channel_id=1, source_target_pairs={{0,16},{16,0},{1,17},{17,1},{2,18},{18,2},{3,19},{19,3},{4,20},{20... | collective-permute-start | bytes 202760 | tf_op jit(solution)/shard_map/ppermute | solution.py:453

commit v4 on v3

--- a/solution.py
+++ b/solution.py
@@ -12,6 +12,19 @@
 LEAK = 0.2
 F32, BF16 = jnp.float32, jnp.bfloat16
 MIB = 1024 * 1024
+
+
+def places():
+    even, inside = [], []
+    for axis in ("gx", "gy", "gz"):
+        size, place = lax.axis_size(axis), lax.axis_index(axis)
+        even.append(lax.rem(place, 2) == 0 if size > 1 and power_of_two(size) else place >= 0)
+        inside += [place > 0, place < size - 1]
+    return even + inside
+
+
+def in_vmem(*values):
+    return [pltpu.with_memory_space_constraint(value, pltpu.VMEM) for value in values]
 
 
 def dot(a, b, dims=((1,), (0,))):
@@ -44,7 +57,9 @@
     return lax.broadcasted_iota(jnp.int32, shape, dim)
 
 
-def relayout_kernel(field_ref, cells_ref, yface_ref, xface_ref, rows_ref):
+def relayout_kernel(field_ref, cells_ref, yface_ref, xface_ref, flag_ref, rows_ref):
+    for k, flag in enumerate(places()):
+        flag_ref[k : k + 1, :] = jnp.full((1, flag_ref.shape[1]), flag.astype(jnp.int32)).astype(F32)
     cin, planes, height, width = field_ref.shape
     half = width // 2
     out = iota((width, width), 0)
@@ -81,11 +96,13 @@
             pl.BlockSpec((step, rows, 4 * cin), lambda z: (z, 0, 0)),
             pl.BlockSpec((step, half, 2 * cin), lambda z: (z, 0, 0)),
             pl.BlockSpec((step, height // 2, 2 * cin), lambda z: (z, 0, 0)),
+            pl.BlockSpec((16, 2 * cin), lambda z: (0, 0)),
         ],
         out_shape=[
-            jax.ShapeDtypeStruct((depth, rows, 4 * cin), BF16),
-            jax.ShapeDtypeStruct((depth, half, 2 * cin), BF16),
-            jax.ShapeDtypeStruct((depth, height // 2, 2 * cin), BF16),
+            pltpu.VMEM((depth, rows, 4 * cin), BF16),
+            pltpu.VMEM((depth, half, 2 * cin), BF16),
+            pltpu.VMEM((depth, height // 2, 2 * cin), BF16),
+            pltpu.VMEM((16, 2 * cin), F32),
         ],
         scratch_shapes=[pltpu.VMEM((step, cin * height, width), F32)],
         compiler_params=pltpu.CompilerParams(vmem_limit_bytes=16 * MIB),
@@ -177,28 +194,28 @@
         in_specs=[vmem] * 3,
         out_specs=[vmem] * 6,
         out_shape=[
-            jax.ShapeDtypeStruct((depth // 2, rows, cout), F32),
-            jax.ShapeDtypeStruct((2 * cout + 16, cout), F32),
-            jax.ShapeDtypeStruct((wide, 4 * cout), BF16),
-            jax.ShapeDtypeStruct((6 * cin, 2 * cout), BF16),
-            jax.ShapeDtypeStruct((12 * cin, cout), BF16),
-            jax.ShapeDtypeStruct((9 * cout, 3 * cout), BF16),
+            pltpu.VMEM((depth // 2, rows, cout), F32),
+            pltpu.VMEM((2 * cout + 16, cout), F32),
+            pltpu.VMEM((wide, 4 * cout), BF16),
+            pltpu.VMEM((6 * cin, 2 * cout), BF16),
+            pltpu.VMEM((12 * cin, cout), BF16),
+            pltpu.VMEM((9 * cout, 3 * cout), BF16),
         ],
         scratch_shapes=[pltpu.VMEM((3, wide, 4 * cout), BF16), pltpu.VMEM((rows, 4 * cout), F32)],
         compiler_params=pltpu.CompilerParams(vmem_limit_bytes=20 * MIB),
         cost_estimate=pl.CostEstimate(flops=flops, bytes_accessed=6 * MIB, transcendentals=0),
         name="interior",
-    )(cells, weights, second)
+    )(*in_vmem(cells), weights, second)
 
 
 def finish_kernel(
-    place_ref, part_ref, stat_ref, zhalo_ref, yhalo_ref, yzhalo_ref, xhalo_ref, xzhalo_ref, wz_ref, wy_ref, wx_ref,
+    part_ref, stat_ref, zhalo_ref, yhalo_ref, yzhalo_ref, xhalo_ref, xzhalo_ref, wz_ref, wy_ref, wx_ref,
     feat_ref, mom_ref, xface_ref, acc_ref, rim_ref,
 ):
     depth, rows, cout = part_ref.shape
     lines = xhalo_ref.shape[0] // (2 * depth)
     half = rows // lines
-    y_in, z_in = place_ref[5] != 0, place_ref[7] != 0
+    _, _, _, _, _, y_in, _, z_in, _ = places()
     zhalo = jnp.where(z_in, zhalo_ref[...], jnp.zeros(zhalo_ref.shape, BF16))
     yrest = yhalo_ref[2 * depth * half :, :].astype(F32)
     yhalo = [yzhalo_ref[:half, :]] + [yhalo_ref[z * half : (z + 1) * half, :] for z in range(2 * depth)]
@@ -264,7 +281,7 @@
     mom_ref[cout // 2 :, :] = jnp.broadcast_to(total, (8, cout))
 
 
-def finish(place, part, stats, zhalo, yhalo, yzhalo, xhalo, xzhalo, wz, wy, wx):
+def finish(part, stats, zhalo, yhalo, yzhalo, xhalo, xzhalo, wz, wy, wx):
     depth, rows, cout = part.shape
     lines = xhalo.shape[0] // (2 * depth)
     half = rows // lines
@@ -272,22 +289,22 @@
     vmem = pl.BlockSpec(memory_space=pltpu.VMEM)
     return pl.pallas_call(
         finish_kernel,
-        in_specs=[pl.BlockSpec(memory_space=pltpu.SMEM)] + [vmem] * 10,
+        in_specs=[vmem] * 10,
         out_specs=[vmem] * 3,
         out_shape=[
-            jax.ShapeDtypeStruct((depth, rows, cout), F32),
-            jax.ShapeDtypeStruct((cout // 2 + 8, cout), F32),
-            jax.ShapeDtypeStruct((2, depth * lines, cout), F32),
+            pltpu.VMEM((depth, rows, cout), F32),
+            pltpu.VMEM((cout // 2 + 8, cout), F32),
+            pltpu.VMEM((2, depth * lines, cout), F32),
         ],
         scratch_shapes=[pltpu.VMEM((rows, 4 * cout), F32), pltpu.VMEM((rim + (-rim) % 16, cout), F32)],
         compiler_params=pltpu.CompilerParams(vmem_limit_bytes=16 * MIB),
         name="finish",
-    )(place, part, stats, zhalo, yhalo, yzhalo, xhalo, xzhalo, wz, wy, wx)
+    )(*in_vmem(part, stats, zhalo, yhalo, yzhalo, xhalo, xzhalo, wz, wy, wx))
 
 
 def block_kernel(
     total_cells,
-    place_ref, mom_ref, gain_ref, shift_ref, feat_ref, z1_ref, z2_ref, y1_ref, y2_ref, x1_ref, x2_ref, w_ref,
+    mom_ref, gain_ref, shift_ref, feat_ref, z1_ref, z2_ref, y1_ref, y2_ref, x1_ref, x2_ref, w_ref,
     out_ref, pad_ref, wide_ref,
 ):
     depth, rows, cout = feat_ref.shape
@@ -328,7 +345,7 @@
         return jnp.where(scaled >= 0, scaled, LEAK * scaled)
 
     base = 8
-    x_even, y_even, z_even, xb_in, xa_in, yb_in, ya_in, zb_in, za_in = (place_ref[k] != 0 for k in range(9))
+    x_even, y_even, z_even, xb_in, xa_in, yb_in, ya_in, zb_in, za_in = places()
 
     def sides(even, one_ref, two_ref):
         one, two = one_ref[...], two_ref[...]
@@ -375,14 +392,14 @@
             out_ref[zp - 2] = sums[zp - 2].astype(BF16)
 
 
-def block(total_cells, place, moments, gain, shift, feats, zs, ys, xs, weights):
+def block(total_cells, moments, gain, shift, feats, zs, ys, xs, weights):
     depth, rows, cout = feats.shape
     half = ys[0].shape[0] // (depth + 2)
     lines = rows // half
     vmem = pl.BlockSpec(memory_space=pltpu.VMEM)
     return pl.pallas_call(
         functools.partial(block_kernel, total_cells),
-        in_specs=[pl.BlockSpec(memory_space=pltpu.SMEM)] + [vmem] * 11,
+        in_specs=[vmem] * 11,
         out_specs=vmem,
         out_shape=jax.ShapeDtypeStruct((depth, rows, cout), BF16),
         scratch_shapes=[
@@ -391,7 +408,7 @@
         ],
         compiler_params=pltpu.CompilerParams(vmem_limit_bytes=24 * MIB),
         name="block",
-    )(place, moments, gain, shift, feats, *zs, *ys, *xs, weights)
+    )(moments, gain, shift, *in_vmem(feats, *zs, *ys, *xs, weights))
 
 
 def power_of_two(size):
@@ -407,19 +424,13 @@
     return [(i, (i + 1 if i % 2 else i - 1) % size) for i in range(size)]
 
 
-def is_even(axis):
-    size = lax.axis_size(axis)
-    return lax.axis_index(axis) % 2 == 0 if size > 1 and power_of_two(size) else jnp.bool_(True)
-
-
-def faces(axis, low, high):
+def faces(axis, even, low, high):
     size = lax.axis_size(axis)
     if size == 1:
         return low, high
     if not power_of_two(size):
         up = up_pairs(axis)
         return lax.ppermute(low, axis, [(j, i) for i, j in up]), lax.ppermute(high, axis, up)
-    even = is_even(axis)
     one = lax.ppermute(jnp.where(even, high, low), axis, first_pairs(axis))
     if size == 2:
         return one, one
@@ -444,11 +455,11 @@
     return value
 
 
-def added_with_faces(axis, value, low, high):
+def added_with_faces(axis, even, value, low, high):
     size = lax.axis_size(axis)
     if size == 1 or not power_of_two(size):
-        return added(axis, value), faces(axis, low, high)
-    even, count = is_even(axis), value.shape[0]
+        return added(axis, value), faces(axis, even, low, high)
+    count = value.shape[0]
     both = jnp.concatenate([value, jnp.where(even, high, low)], axis=0)
     both = lax.ppermute(both, axis, first_pairs(axis))
     value, one = value + both[:count], both[count:]
@@ -483,15 +494,11 @@
     cin, depth_in, height_in, width_in = field.shape
     cout = conv_second.shape[-1]
     depth, lines, half = depth_in // 2, height_in // 2, width_in // 2
-    cells, yface, xface = relayout(field)
-
-    place = [is_even(axis) for axis in ("gx", "gy", "gz")]
-    for axis in ("gx", "gy", "gz"):
-        place += [lax.axis_index(axis) > 0, lax.axis_index(axis) < lax.axis_size(axis) - 1]
-    place = jnp.stack(place).astype(jnp.int32)
+    cells, yface, xface, flags = relayout(field)
+    x_even, y_even, z_even, x_in = (flags[k : k + 1, :] > 0 for k in range(4))
     zhalo = lax.ppermute(cells[-1], "gz", ring("gz"))
     xhalo = lax.ppermute(xface.reshape(depth_in * lines, 2 * cin), "gx", ring("gx"))
-    xhalo = jnp.where(lax.axis_index("gx") > 0, xhalo, jnp.zeros_like(xhalo))
+    xhalo = jnp.where(x_in, xhalo, jnp.zeros_like(xhalo))
     rim = xhalo.reshape(depth_in, lines, 2 * cin)
     yhalo = lax.ppermute(stacked([yface.reshape(depth_in * half, 2 * cin), rim[:, -1]]), "gy", ring("gy"))
     ny, nz = lax.axis_size("gy"), lax.axis_size("gz")
@@ -500,28 +507,28 @@
     xzhalo = lax.ppermute(stacked([rim[-1]]), "gz", ring("gz"))
 
     part, stats, wz, wy, wx, second = interior(lines, cells, conv_first, conv_second.reshape(3, 3, 3 * cout, cout))
-    feats, moments, xfaces = finish(place, part, stats, zhalo, yhalo, yzhalo, xhalo, xzhalo, wz, wy, wx)
+    feats, moments, xfaces = finish(part, stats, zhalo, yhalo, yzhalo, xhalo, xzhalo, wz, wy, wx)
     rows = lines * half
-    zs = faces("gz", feats[0], feats[-1])
+    zs = faces("gz", z_even, feats[0], feats[-1])
     moments = added("gz", moments)
-    zsides = sided(is_even("gz"), zs)
+    zsides = sided(z_even, zs)
 
     def yside(y):
         here = slice(y * half, (y + 1) * half)
         return jnp.concatenate([feats[z, here] for z in range(depth)] + [side[here] for side in zsides], axis=0)
 
-    moments, ys = added_with_faces("gy", moments, yside(0), yside(lines - 1))
-    ysides = sided(is_even("gy"), ys)
+    moments, ys = added_with_faces("gy", y_even, moments, yside(0), yside(lines - 1))
+    ysides = sided(y_even, ys)
 
     def xside(n, x):
         own = [xfaces[n]] + [side.reshape(-1, half, cout)[:, x] for side in zsides + ysides]
         return jnp.concatenate(own, axis=0)
 
     low, high = xside(0, 0), xside(1, half - 1)
-    moments, xs = added_with_faces("gx", moments, low, high)
+    moments, xs = added_with_faces("gx", x_even, moments, low, high)
     total_cells = rows * depth * lax.axis_size("gx") * lax.axis_size("gy") * lax.axis_size("gz")
     result = block(
-        total_cells, place, moments, norm_gain[None], norm_shift[None], feats, zs, ys, xs, second,
+        total_cells, moments, norm_gain[None], norm_shift[None], feats, zs, ys, xs, second,
     )
     return jnp.transpose(result.reshape(depth, lines, half, cout), (3, 0, 1, 2))
 

time: 60.9 us -> 48 us (0.79)
  local copies, waits for them, and re-layouts: 13.2 us -> 2.11 us
  other arithmetic: 1.71 us -> 0.44 us
  Pallas kernels: 13 us -> 11.9 us
    unnamed x36 -> x16, local copies, waits for them, and re-layouts: 11.9 us -> 1.65 us
    concatenate x2, other arithmetic: 1.48 us -> 0.21 us  [stacked(): return jnp.concatenate(parts + [fill], axis=0)]
    pallas_call x2, Pallas kernels: 8.21 us -> 7.14 us  [the longest x1 6.31 us: block(): pl.pallas_call(functools.partial(block_kernel, total_cells), in_specs=[vm...]
    squeeze x1, local copies, waits for them, and re-layouts: 0.72 us -> 0.02 us  [body(): zhalo = lax.ppermute(cells[-1], 'gz', ring('gz'))]
  transfers between devices with their start and end apart: 13 -> 13, of which waited for: 6 -> 7; matrix products, arithmetic and copies ran while one was open for 4% -> 2% of each run, Pallas kernels for 4% -> 5%
where the time goes in v4:
time: 48 us; the launch traced here: 47.9 us
  starting transfers between devices  20.5 us (43%)
  waiting for transfers between devices  12.6 us (26%)
  Pallas kernels  11.9 us (25%)
  local copies, waits for them, and re-layouts  2.11 us (4%)
    pallas_call x1, Pallas kernels, block(): pl.pallas_call(functools.partial(block_kernel, total_cells), in_specs=[vm...  6.31 us
    ppermute x2, waiting for transfers between devices, added(): value = value + lax.ppermute(value, axis, second_pairs(axis))  5.21 us
    ppermute x2, starting transfers between devices, added_with_faces(): both = lax.ppermute(both, axis, first_pairs(axis))  3.97 us
    ppermute x1, starting transfers between devices, body(): lax.ppermute(stacked([yface.reshape(depth_in * half, 2 * cin), rim[:, -1]...  3.28 us
    ppermute x1, waiting for transfers between devices, added_with_faces(): two = lax.ppermute(jnp.where(even, low, high), axis, inner)  3.22 us
    ppermute x2, starting transfers between devices, added(): value = value + lax.ppermute(value, axis, second_pairs(axis))  3.19 us
    pallas_call x1, Pallas kernels, interior(): pl.pallas_call(functools.partial(interior_kernel, lines), in_specs=[vmem]...  2.46 us
    pallas_call x1, Pallas kernels, relayout(): pl.pallas_call(relayout_kernel, grid=(depth // step,), in_specs=[pl.Block...  2.32 us
  transfers between devices with their start and end apart: 13, of which 7 were waited for; matrix products, arithmetic and copies ran while one was open for 2% of the time, Pallas kernels for 5%

profile of v4, /device:TPU:1, one launch (start us, length us, event | category | flops | bytes accessed | tf_op | source)
XLA Modules:
  0.0 47.9 jit_solution(6831216814283226950)
XLA Ops:
  0.0 0.0 copy-start
  0.0 1.6 %copy-done = bf16[64,8,16,128]{3,2,1,0:T(8,128)(2,1)S(1)} copy-done((bf16[64,8,16,128]{3,2,1,0:T(8,128)(2,1)S(1)}, bf16[64,8,16,128]{3,2,1,0:T(8,128)(2,1)}, u32[]{:S(2)}) %copy-start) | copy-done | bytes 2097176
  1.6 0.0 copy-start.3
  1.6 0.0 copy-start.4
  1.6 2.3 %relayout.1 = (bf16[8,512,256]{2,1,0:T(8,128)(2,1)S(1)}, bf16[8,64,128]{2,1,0:T(8,128)(2,1)S(1)}, bf16[8,8,128]{2,1,0:T(8,128)(2,1)S(1)}, f32[16,128]{1,0:T(8,128)S(1)}) custom-call(bf16[64,8,16,128]{3,2,1,0:T(8,128)(2,1)S(1)} %copy-done), custom_call_target="tpu_custom_call" | custom-call | tf_op jit(solution)/shard_map/relayout/pallas_call | solution.py:91
  4.0 2.2 %collective-permute-start = (bf16[512,256]{1,0:T(8,128)(2,1)S(1)}, bf16[512,256]{1,0:T(8,128)(2,1)S(1)}, u32[]{:S(2)}, u32[]{:S(2)}) collective-permute-start(bf16[512,256]{1,0:T(8,128)(2,1)S(1)} %slice_bitcast_fusion), channel_id=1, source_target_pairs={{0,1},{1,2},{2,3},{3,0},{4,5},{5,6},{6,7},{7,4},{8,9},{9,10},{10,1... | collective-permute-start | bytes 786440 | tf_op jit(solution)/shard_map/ppermute | solution.py:499
  6.1 1.2 %collective-permute-start.1 = (bf16[64,128]{1,0:T(8,128)(2,1)S(1)}, bf16[64,128]{1,0:T(8,128)(2,1)S(1)}, u32[]{:S(2)}, u32[]{:S(2)}) collective-permute-start(bf16[64,128]{1,0:T(8,128)(2,1)S(1)} %bitcast.81), channel_id=1, source_target_pairs={{0,16},{16,0},{1,17},{17,1},{2,18},{18,2},{3,19},{19,3},{4,20},{20... | collective-permute-start | bytes 49160 | tf_op jit(solution)/shard_map/ppermute | solution.py:500
  7.4 0.1 pad.10.clone
  7.5 0.1 pad.7.clone
  7.5 1.2 %collective-permute-done.1 = bf16[64,128]{1,0:T(8,128)(2,1)S(1)} collective-permute-done((bf16[64,128]{1,0:T(8,128)(2,1)S(1)}, bf16[64,128]{1,0:T(8,128)(2,1)S(1)}, u32[]{:S(2)}, u32[]{:S(2)}) %collective-permute-start.1) | collective-permute-done | bytes 16416 | tf_op jit(solution)/shard_map/ppermute | solution.py:500
  8.8 0.1 maximum_maximum_fusion
  8.9 3.3 %collective-permute-start.2 = (bf16[528,128]{1,0:T(8,128)(2,1)S(1)}, bf16[528,128]{1,0:T(8,128)(2,1)S(1)}, u32[]{:S(2)}, u32[]{:S(2)}) collective-permute-start(bf16[528,128]{1,0:T(8,128)(2,1)S(1)} %maximum_maximum_fusion), channel_id=1, source_target_pairs={{0,4},{4,8},{8,12},{12,0},{1,5},{5,9},{9,13},{13,1},{2,6},{6,10},{... | collective-permute-start | bytes 405512 | tf_op jit(solution)/shard_map/ppermute | solution.py:503
  12.2 0.1 maximum_maximum_fusion.1
  12.3 1.1 %collective-permute-start.3 = (bf16[80,128]{1,0:T(8,128)(2,1)S(1)}, bf16[80,128]{1,0:T(8,128)(2,1)S(1)}, u32[]{:S(2)}, u32[]{:S(2)}) collective-permute-start(bf16[80,128]{1,0:T(8,128)(2,1)S(1)} %maximum_maximum_fusion.1), channel_id=1, source_target_pairs={{0,5},{1,6},{2,7},{3,4},{4,9},{5,10},{6,11},{7,8},{8,13},{9,14},{1... | collective-permute-start | bytes 61448 | tf_op jit(solution)/shard_map/ppermute | solution.py:506
  13.3 1.3 %collective-permute-start.4 = (bf16[16,128]{1,0:T(8,128)(2,1)S(1)}, bf16[16,128]{1,0:T(8,128)(2,1)S(1)}, u32[]{:S(2)}, u32[]{:S(2)}) collective-permute-start(bf16[16,128]{1,0:T(8,128)(2,1)S(1)} %concatenate.29), channel_id=1, source_target_pairs={{0,1},{1,2},{2,3},{3,0},{4,5},{5,6},{6,7},{7,4},{8,9},{9,10},{10,1... | collective-permute-start | bytes 12296 | tf_op jit(solution)/shard_map/ppermute | solution.py:507
  14.7 0.0 copy-done.3
  14.7 0.0 copy-done.4
  14.7 2.5 %interior.1 = (f32[4,512,128]{2,1,0:T(8,128)S(1)}, f32[272,128]{1,0:T(8,128)S(1)}, bf16[256,512]{1,0:T(8,128)(2,1)S(1)}, bf16[384,256]{1,0:T(8,128)(2,1)S(1)}, b...) custom-call(bf16[8,512,256]{2,1,0:T(8,128)(2,1)S(1)} %get-tuple-element.18.cells_ref, ...), custom_call_target="tpu_custom_call" | custom-call | flops 1610612736 | bytes 6291456 | tf_op jit(solution)/shard_map/interior/pallas_call | solution.py:192
  17.2 0.5 %collective-permute-done.4.xzhalo_ref = bf16[16,128]{1,0:T(8,128)(2,1)S(1)} collective-permute-done((bf16[16,128]{1,0:T(8,128)(2,1)S(1)}, bf16[16,128]{1,0:T(8,128)(2,1)S(1)}, u32[]{:S(2)}, u32[]{:S(2)}) %collective-permute-start.4) | collective-permute-done | bytes 4128 | tf_op jit(solution)/shard_map/ppermute | solution.py:507
  17.6 0.0 collective-permute-done.3.yzhalo_ref
  17.6 0.0 collective-permute-done.2.yhalo_ref
  17.6 0.0 collective-permute-done.zhalo_ref
  17.7 0.8 %finish.1 = (f32[4,512,128]{2,1,0:T(8,128)S(1)}, f32[72,128]{1,0:T(8,128)S(1)}, f32[2,32,128]{2,1,0:T(8,128)S(1)}) custom-call(f32[4,512,128]{2,1,0:T(8,128)S(1)} %get-tuple-element.19.part_ref, f32[272,128]{1,0:T(8,128)S(1)} %get-tuple-element.20.stat_ref, bf16[512,256]{1,0:T(8,128)(2,1)S(1)} %collective-permute-done.zhalo_ref, ...), custom_call_target="tpu_custom_call" | custom-call | tf_op jit(solution)/shard_map/finish/pallas_call | solution.py:290
  18.5 0.0 collective-permute-start.5
  18.6 1.5 %collective-permute-start.8 = (f32[512,128]{1,0:T(8,128)S(1)}, f32[512,128]{1,0:T(8,128)S(1)}, u32[]{:S(2)}, u32[]{:S(2)}) collective-permute-start(f32[512,128]{1,0:T(8,128)S(1)} %get-tuple-element.31), channel_id=1, source_target_pairs={{0,1},{1,0},{2,3},{3,2},{4,5},{5,4},{6,7},{7,6},{8,9},{9,8},{10,11... | collective-permute-start | bytes 786440 | tf_op jit(solution)/shard_map/ppermute | solution.py:434
  20.1 0.7 %collective-permute-start.7 = (f32[512,128]{1,0:T(8,128)S(1)}, f32[512,128]{1,0:T(8,128)S(1)}, u32[]{:S(2)}, u32[]{:S(2)}) collective-permute-start(f32[512,128]{1,0:T(8,128)S(1)} %get-tuple-element.32), channel_id=1, source_target_pairs={{1,2},{2,1},{5,6},{6,5},{9,10},{10,9},{13,14},{14,13},{17,18},{18,... | collective-permute-start | bytes 786440 | tf_op jit(solution)/shard_map/ppermute | solution.py:438
  20.8 0.5 %collective-permute-done.5 = f32[72,128]{1,0:T(8,128)S(1)} collective-permute-done((f32[72,128]{1,0:T(8,128)S(1)}, f32[72,128]{1,0:T(8,128)S(1)}, u32[]{:S(2)}, u32[]{:S(2)}) %collective-permute-start.5) | collective-permute-done | bytes 36896 | tf_op jit(solution)/shard_map/ppermute | solution.py:448
  21.3 1.5 %collective-permute-start.6 = (f32[72,128]{1,0:T(8,128)S(1)}, f32[72,128]{1,0:T(8,128)S(1)}, u32[]{:S(2)}, u32[]{:S(2)}) collective-permute-start(f32[72,128]{1,0:T(8,128)S(1)} %add.17), channel_id=1, source_target_pairs={{0,3},{1,2},{2,1},{3,0},{4,7},{5,6},{6,5},{7,4},{8,11},{9,10},{10,... | collective-permute-start | bytes 110600 | tf_op jit(solution)/shard_map/ppermute | solution.py:450
  22.8 5.1 %collective-permute-done.6 = f32[72,128]{1,0:T(8,128)S(1)} collective-permute-done((f32[72,128]{1,0:T(8,128)S(1)}, f32[72,128]{1,0:T(8,128)S(1)}, u32[]{:S(2)}, u32[]{:S(2)}) %collective-permute-start.6) | collective-permute-done | bytes 36896 | tf_op jit(solution)/shard_map/ppermute | solution.py:450
  28.0 0.0 copy-start.1
  28.0 0.0 copy-start.2
  28.0 0.0 collective-permute-done.8.z1_ref
  28.0 0.0 collective-permute-done.7.z2_ref
  28.2 2.7 %collective-permute-start.9 = (f32[456,128]{1,0:T(8,128)S(1)}, f32[456,128]{1,0:T(8,128)S(1)}, u32[]{:S(2)}, u32[]{:S(2)}) collective-permute-start(f32[456,128]{1,0:T(8,128)S(1)} %pad_maximum_fusion), channel_id=1, source_target_pairs={{0,4},{4,0},{8,12},{12,8},{1,5},{5,1},{9,13},{13,9},{2,6},{6,2},{1... | collective-permute-start | bytes 700424 | tf_op jit(solution)/shard_map/ppermute | solution.py:464
  30.9 2.0 %collective-permute-start.11 = (f32[384,128]{1,0:T(8,128)S(1)}, f32[384,128]{1,0:T(8,128)S(1)}, u32[]{:S(2)}, u32[]{:S(2)}) collective-permute-start(f32[384,128]{1,0:T(8,128)S(1)} %get-tuple-element.45), channel_id=1, source_target_pairs={{4,8},{8,4},{5,9},{9,5},{6,10},{10,6},{7,11},{11,7},{20,24},{24,20... | collective-permute-start | bytes 589832 | tf_op jit(solution)/shard_map/ppermute | solution.py:469
  32.9 0.0 collective-permute-done.9
  33.0 1.7 %collective-permute-start.10 = (f32[72,128]{1,0:T(8,128)S(1)}, f32[72,128]{1,0:T(8,128)S(1)}, u32[]{:S(2)}, u32[]{:S(2)}) collective-permute-start(f32[72,128]{1,0:T(8,128)S(1)} %slice_add_fusion.1), channel_id=1, source_target_pairs={{0,12},{4,8},{8,4},{12,0},{1,13},{5,9},{9,5},{13,1},{2,14},{6,10},... | collective-permute-start | bytes 110600 | tf_op jit(solution)/shard_map/ppermute | solution.py:450
  34.7 3.2 %collective-permute-done.11.y2_ref = f32[384,128]{1,0:T(8,128)S(1)} collective-permute-done((f32[384,128]{1,0:T(8,128)S(1)}, f32[384,128]{1,0:T(8,128)S(1)}, u32[]{:S(2)}, u32[]{:S(2)}) %collective-permute-start.11) | collective-permute-done | bytes 196640 | tf_op jit(solution)/shard_map/ppermute | solution.py:469
  38.0 0.1 concatenate.33
  38.1 0.1 concatenate.34
  38.2 0.1 collective-permute-done.10
  38.3 1.3 %collective-permute-start.12 = (f32[132,128]{1,0:T(8,128)S(1)}, f32[132,128]{1,0:T(8,128)S(1)}, u32[]{:S(2)}, u32[]{:S(2)}) collective-permute-start(f32[132,128]{1,0:T(8,128)S(1)} %pad_maximum_fusion.1), channel_id=1, source_target_pairs={{0,16},{16,0},{1,17},{17,1},{2,18},{18,2},{3,19},{19,3},{4,20},{20... | collective-permute-start | bytes 202760 | tf_op jit(solution)/shard_map/ppermute | solution.py:464
  39.6 2.0 %collective-permute-done.12 = f32[132,128]{1,0:T(8,128)S(1)} collective-permute-done((f32[132,128]{1,0:T(8,128)S(1)}, f32[132,128]{1,0:T(8,128)S(1)}, u32[]{:S(2)}, u32[]{:S(2)}) %collective-permute-start.12) | collective-permute-done | bytes 67616 | tf_op jit(solution)/shard_map/ppermute | solution.py:464
  41.5 0.0 copy-done.1
  41.5 0.0 copy-done.2
  41.5 6.3 %block.1 = bf16[4,512,128]{2,1,0:T(8,128)(2,1)} custom-call(f32[72,128]{1,0:T(8,128)S(1)} %slice_add_fusion.mom_ref, f32[1,128]{1,0:T(1,128)S(1)} %bitcast.78, f32[1,128]{1,0:T(1,128)S(1)} %bitcast.79, f32[4,512,128]{2,1,0:T(8,128)S(1)} %get-tuple-element.28.feat_ref, f32[512,128]{1,0:T(8,128)S(1)} %collective-permute-done.8.z1_ref, ...), custom_call_target="tpu_custom_call" | custom-call | tf_op jit(solution)/shard_map/block/pallas_call | solution.py:400
  (38 shorter events, 0.4 us)
Async XLA Ops:
  0.0 1.6 %copy-start = (bf16[64,8,16,128]{3,2,1,0:T(8,128)(2,1)S(1)}, bf16[64,8,16,128]{3,2,1,0:T(8,128)(2,1)}, u32[]{:S(2)}) copy-start(bf16[64,8,16,128]{3,2,1,0:T(8,128)(2,1)} %field_ref.1) | copy-start | bytes 6291460
  1.6 13.1 %copy-start.3 = (bf16[3,3,3,128,128]{4,3,2,1,0:T(8,128)(2,1)S(1)}, bf16[3,3,3,128,128]{4,3,2,1,0:T(8,128)(2,1)}, u32[]{:S(2)}) copy-start(bf16[3,3,3,128,128]{4,3,2,1,0:T(8,128)(2,1)} %param.9) | copy-start | bytes 2654212
  1.6 13.1 %copy-start.4 = (bf16[3,3,3,64,128]{4,3,2,1,0:T(8,128)(2,1)S(1)}, bf16[3,3,3,64,128]{4,3,2,1,0:T(8,128)(2,1)}, u32[]{:S(2)}) copy-start(bf16[3,3,3,64,128]{4,3,2,1,0:T(8,128)(2,1)} %w_ref.1) | copy-start | bytes 1327108
  4.0 13.7 %collective-permute-start = (bf16[512,256]{1,0:T(8,128)(2,1)S(1)}, bf16[512,256]{1,0:T(8,128)(2,1)S(1)}, u32[]{:S(2)}, u32[]{:S(2)}) collective-permute-start(bf16[512,256]{1,0:T(8,128)(2,1)S(1)} %slice_bitcast_fusion), channel_id=1, source_target_pairs={{0,1},{1,2},{2,3},{3,0},{4,5},{5,6},{6,7},{7,4},{8,9},{9,10},{10,1... | collective-permute-start | bytes 786440 | tf_op jit(solution)/shard_map/ppermute | solution.py:499
  6.1 2.6 %collective-permute-start.1 = (bf16[64,128]{1,0:T(8,128)(2,1)S(1)}, bf16[64,128]{1,0:T(8,128)(2,1)S(1)}, u32[]{:S(2)}, u32[]{:S(2)}) collective-permute-start(bf16[64,128]{1,0:T(8,128)(2,1)S(1)} %bitcast.81), channel_id=1, source_target_pairs={{0,16},{16,0},{1,17},{17,1},{2,18},{18,2},{3,19},{19,3},{4,20},{20... | collective-permute-start | bytes 49160 | tf_op jit(solution)/shard_map/ppermute | solution.py:500
  8.9 8.7 %collective-permute-start.2 = (bf16[528,128]{1,0:T(8,128)(2,1)S(1)}, bf16[528,128]{1,0:T(8,128)(2,1)S(1)}, u32[]{:S(2)}, u32[]{:S(2)}) collective-permute-start(bf16[528,128]{1,0:T(8,128)(2,1)S(1)} %maximum_maximum_fusion), channel_id=1, source_target_pairs={{0,4},{4,8},{8,12},{12,0},{1,5},{5,9},{9,13},{13,1},{2,6},{6,10},{... | collective-permute-start | bytes 405512 | tf_op jit(solution)/shard_map/ppermute | solution.py:503
  12.3 5.4 %collective-permute-start.3 = (bf16[80,128]{1,0:T(8,128)(2,1)S(1)}, bf16[80,128]{1,0:T(8,128)(2,1)S(1)}, u32[]{:S(2)}, u32[]{:S(2)}) collective-permute-start(bf16[80,128]{1,0:T(8,128)(2,1)S(1)} %maximum_maximum_fusion.1), channel_id=1, source_target_pairs={{0,5},{1,6},{2,7},{3,4},{4,9},{5,10},{6,11},{7,8},{8,13},{9,14},{1... | collective-permute-start | bytes 61448 | tf_op jit(solution)/shard_map/ppermute | solution.py:506
  13.3 4.3 %collective-permute-start.4 = (bf16[16,128]{1,0:T(8,128)(2,1)S(1)}, bf16[16,128]{1,0:T(8,128)(2,1)S(1)}, u32[]{:S(2)}, u32[]{:S(2)}) collective-permute-start(bf16[16,128]{1,0:T(8,128)(2,1)S(1)} %concatenate.29), channel_id=1, source_target_pairs={{0,1},{1,2},{2,3},{3,0},{4,5},{5,6},{6,7},{7,4},{8,9},{9,10},{10,1... | collective-permute-start | bytes 12296 | tf_op jit(solution)/shard_map/ppermute | solution.py:507
  18.5 2.9 %collective-permute-start.5 = (f32[72,128]{1,0:T(8,128)S(1)}, f32[72,128]{1,0:T(8,128)S(1)}, u32[]{:S(2)}, u32[]{:S(2)}) collective-permute-start(f32[72,128]{1,0:T(8,128)S(1)} %get-tuple-element.27), channel_id=1, source_target_pairs={{0,1},{1,0},{2,3},{3,2},{4,5},{5,4},{6,7},{7,6},{8,9},{9,8},{10,11... | collective-permute-start | bytes 110600 | tf_op jit(solution)/shard_map/ppermute | solution.py:448
  18.6 9.4 %collective-permute-start.8 = (f32[512,128]{1,0:T(8,128)S(1)}, f32[512,128]{1,0:T(8,128)S(1)}, u32[]{:S(2)}, u32[]{:S(2)}) collective-permute-start(f32[512,128]{1,0:T(8,128)S(1)} %get-tuple-element.31), channel_id=1, source_target_pairs={{0,1},{1,0},{2,3},{3,2},{4,5},{5,4},{6,7},{7,6},{8,9},{9,8},{10,11... | collective-permute-start | bytes 786440 | tf_op jit(solution)/shard_map/ppermute | solution.py:434
  20.1 7.9 %collective-permute-start.7 = (f32[512,128]{1,0:T(8,128)S(1)}, f32[512,128]{1,0:T(8,128)S(1)}, u32[]{:S(2)}, u32[]{:S(2)}) collective-permute-start(f32[512,128]{1,0:T(8,128)S(1)} %get-tuple-element.32), channel_id=1, source_target_pairs={{1,2},{2,1},{5,6},{6,5},{9,10},{10,9},{13,14},{14,13},{17,18},{18,... | collective-permute-start | bytes 786440 | tf_op jit(solution)/shard_map/ppermute | solution.py:438
  21.3 6.7 %collective-permute-start.6 = (f32[72,128]{1,0:T(8,128)S(1)}, f32[72,128]{1,0:T(8,128)S(1)}, u32[]{:S(2)}, u32[]{:S(2)}) collective-permute-start(f32[72,128]{1,0:T(8,128)S(1)} %add.17), channel_id=1, source_target_pairs={{0,3},{1,2},{2,1},{3,0},{4,7},{5,6},{6,5},{7,4},{8,11},{9,10},{10,... | collective-permute-start | bytes 110600 | tf_op jit(solution)/shard_map/ppermute | solution.py:450
  28.0 13.5 %copy-start.1 = (f32[128]{0:T(128)S(1)}, f32[128]{0:T(128)}, u32[]{:S(2)}) copy-start(f32[128]{0:T(128)} %param.7) | copy-start | bytes 1540
  28.0 13.5 %copy-start.2 = (f32[128]{0:T(128)S(1)}, f32[128]{0:T(128)}, u32[]{:S(2)}) copy-start(f32[128]{0:T(128)} %param.8) | copy-start | bytes 1540
  28.2 4.8 %collective-permute-start.9 = (f32[456,128]{1,0:T(8,128)S(1)}, f32[456,128]{1,0:T(8,128)S(1)}, u32[]{:S(2)}, u32[]{:S(2)}) collective-permute-start(f32[456,128]{1,0:T(8,128)S(1)} %pad_maximum_fusion), channel_id=1, source_target_pairs={{0,4},{4,0},{8,12},{12,8},{1,5},{5,1},{9,13},{13,9},{2,6},{6,2},{1... | collective-permute-start | bytes 700424 | tf_op jit(solution)/shard_map/ppermute | solution.py:464
  30.9 7.0 %collective-permute-start.11 = (f32[384,128]{1,0:T(8,128)S(1)}, f32[384,128]{1,0:T(8,128)S(1)}, u32[]{:S(2)}, u32[]{:S(2)}) collective-permute-start(f32[384,128]{1,0:T(8,128)S(1)} %get-tuple-element.45), channel_id=1, source_target_pairs={{4,8},{8,4},{5,9},{9,5},{6,10},{10,6},{7,11},{11,7},{20,24},{24,20... | collective-permute-start | bytes 589832 | tf_op jit(solution)/shard_map/ppermute | solution.py:469
  33.0 5.3 %collective-permute-start.10 = (f32[72,128]{1,0:T(8,128)S(1)}, f32[72,128]{1,0:T(8,128)S(1)}, u32[]{:S(2)}, u32[]{:S(2)}) collective-permute-start(f32[72,128]{1,0:T(8,128)S(1)} %slice_add_fusion.1), channel_id=1, source_target_pairs={{0,12},{4,8},{8,4},{12,0},{1,13},{5,9},{9,5},{13,1},{2,14},{6,10},... | collective-permute-start | bytes 110600 | tf_op jit(solution)/shard_map/ppermute | solution.py:450
  38.3 3.2 %collective-permute-start.12 = (f32[132,128]{1,0:T(8,128)S(1)}, f32[132,128]{1,0:T(8,128)S(1)}, u32[]{:S(2)}, u32[]{:S(2)}) collective-permute-start(f32[132,128]{1,0:T(8,128)S(1)} %pad_maximum_fusion.1), channel_id=1, source_target_pairs={{0,16},{16,0},{1,17},{17,1},{2,18},{18,2},{3,19},{19,3},{4,20},{20... | collective-permute-start | bytes 202760 | tf_op jit(solution)/shard_map/ppermute | solution.py:464

commit v5 on v4

--- a/solution.py
+++ b/solution.py
@@ -57,57 +57,86 @@
     return lax.broadcasted_iota(jnp.int32, shape, dim)
 
 
-def relayout_kernel(field_ref, cells_ref, yface_ref, xface_ref, flag_ref, rows_ref):
+def pick_matrix(width):
+    out, half = iota((width, width), 0), width // 2
+    source = jnp.where(out < half, 2 * out, 2 * (out - half) + 1)
+    return (source == iota((width, width), 1)).astype(F32).astype(BF16)
+
+
+def turn_plane(pick, plane, rows_ref, cells_ref):
+    cin, height, width = plane.shape
+    half, last = width // 2, []
+    rows_ref[...] = plane.astype(F32).reshape(cin * height, width)
+    for pair in range(height // 4):
+        lines = [rows_ref[pl.ds(4 * pair + k, cin, stride=height), :] for k in range(4)]
+        turned = dot(pick, jnp.concatenate(lines, axis=0).astype(BF16), ((1,), (1,)))
+        for k in range(2):
+            span = pl.ds((2 * pair + k) * half, half)
+            lanes = slice(2 * cin * k, 2 * cin * (k + 1))
+            cells_ref[span, : 2 * cin] = turned[:half, lanes].astype(BF16)
+            cells_ref[span, 2 * cin :] = turned[half:, lanes].astype(BF16)
+            last.append(turned[width - 1 :, lanes])
+    return jnp.concatenate(last, axis=0)
+
+
+def faces_kernel(field_ref, cells_ref, yface_ref, xface_ref, flag_ref, rows_ref, edge_ref):
+    cin, depth, height, width = field_ref.shape
+    half, part = width // 2, edge_ref.shape[1] // cin
     for k, flag in enumerate(places()):
         flag_ref[k : k + 1, :] = jnp.full((1, flag_ref.shape[1]), flag.astype(jnp.int32)).astype(F32)
-    cin, planes, height, width = field_ref.shape
-    half = width // 2
-    out = iota((width, width), 0)
-    source = jnp.where(out < half, 2 * out, 2 * (out - half) + 1)
-    pick = (source == iota((width, width), 1)).astype(F32).astype(BF16)
-    for z in range(planes):
-        rows_ref[z] = field_ref[:, z].astype(F32).reshape(cin * height, width)
-        last = []
-        for pair in range(height // 4):
-            lines = [rows_ref[z, pl.ds(4 * pair + k, cin, stride=height), :] for k in range(4)]
-            block = jnp.concatenate(lines, axis=0).astype(BF16)
-            turned = dot(pick, block, ((1,), (1,)))
-            for k in range(2):
-                row = (2 * pair + k) * half
-                lanes = slice(2 * cin * k, 2 * cin * (k + 1))
-                even = turned[:half, lanes]
-                odd = turned[half:, lanes]
-                cells_ref[z, row : row + half, : 2 * cin] = even.astype(BF16)
-                cells_ref[z, row : row + half, 2 * cin :] = odd.astype(BF16)
-                last.append(odd[half - 1 :, :])
-        yface_ref[z] = jnp.concatenate([even[:, cin:], odd[:, cin:]], axis=1).astype(BF16)
-        xface_ref[z] = jnp.concatenate(last, axis=0).astype(BF16)
+    pick = pick_matrix(width)
+    xface_ref[...] = turn_plane(pick, field_ref[:, depth - 1], rows_ref, cells_ref).astype(BF16)
+    for z in range(depth):
+        edge_ref[z] = field_ref[:, z].astype(F32)[:, height - part :].reshape(cin * part, width)
+    group = 4 if depth % 4 == 0 else 1
+    for first in range(0, depth, group):
+        lines = [edge_ref[first + k, pl.ds(part - 1, cin, stride=part), :] for k in range(group)]
+        turned = dot(pick, jnp.concatenate(lines, axis=0).astype(BF16), ((1,), (1,)))
+        for k in range(group):
+            line = turned[:, cin * k : cin * (k + 1)]
+            span = pl.ds((first + k) * half, half)
+            yface_ref[span, :] = jnp.concatenate([line[:half], line[half:]], axis=1).astype(BF16)
+
+
+def planes_kernel(field_ref, xlast_ref, cells_ref, xface_ref, rows_ref):
+    xface_ref[field_ref.shape[1] - 1] = xlast_ref[...]
+    pick = pick_matrix(field_ref.shape[3])
+    for z in range(field_ref.shape[1] - 1):
+        xface_ref[z] = turn_plane(pick, field_ref[:, z], rows_ref.at[z], cells_ref.at[z]).astype(BF16)
 
 
 def relayout(field):
     cin, depth, height, width = field.shape
-    half, rows = width // 2, height // 2 * (width // 2)
-    step = 4 if depth % 4 == 0 else 1
-    return pl.pallas_call(
-        relayout_kernel,
-        grid=(depth // step,),
-        in_specs=[pl.BlockSpec((cin, step, height, width), lambda z: (0, z, 0, 0))],
-        out_specs=[
-            pl.BlockSpec((step, rows, 4 * cin), lambda z: (z, 0, 0)),
-            pl.BlockSpec((step, half, 2 * cin), lambda z: (z, 0, 0)),
-            pl.BlockSpec((step, height // 2, 2 * cin), lambda z: (z, 0, 0)),
-            pl.BlockSpec((16, 2 * cin), lambda z: (0, 0)),
-        ],
+    half, lines = width // 2, height // 2
+    part = 8 if height % 8 == 0 else height
+    vmem = pl.BlockSpec(memory_space=pltpu.VMEM)
+    faces = pl.pallas_call(
+        faces_kernel,
+        in_specs=[vmem],
+        out_specs=[vmem] * 4,
         out_shape=[
-            pltpu.VMEM((depth, rows, 4 * cin), BF16),
-            pltpu.VMEM((depth, half, 2 * cin), BF16),
-            pltpu.VMEM((depth, height // 2, 2 * cin), BF16),
+            pltpu.VMEM((lines * half, 4 * cin), BF16),
+            pltpu.VMEM((depth * half, 2 * cin), BF16),
+            pltpu.VMEM((lines, 2 * cin), BF16),
             pltpu.VMEM((16, 2 * cin), F32),
         ],
-        scratch_shapes=[pltpu.VMEM((step, cin * height, width), F32)],
-        compiler_params=pltpu.CompilerParams(vmem_limit_bytes=16 * MIB),
-        name="relayout",
-    )(field)
+        scratch_shapes=[pltpu.VMEM((cin * height, width), F32), pltpu.VMEM((depth, cin * part, width), F32)],
+        compiler_params=pltpu.CompilerParams(vmem_limit_bytes=12 * MIB),
+        name="faces",
+    )(*in_vmem(field))
+    planes = pl.pallas_call(
+        planes_kernel,
+        in_specs=[vmem] * 2,
+        out_specs=[vmem] * 2,
+        out_shape=[
+            pltpu.VMEM((depth - 1, lines * half, 4 * cin), BF16),
+            pltpu.VMEM((depth, lines, 2 * cin), BF16),
+        ],
+        scratch_shapes=[pltpu.VMEM((depth - 1, cin * height, width), F32)],
+        compiler_params=pltpu.CompilerParams(vmem_limit_bytes=12 * MIB),
+        name="planes",
+    )(*in_vmem(field, faces[2]))
+    return faces, planes
 
 
 def moved_down(value):
@@ -126,9 +155,9 @@
 
 
 def interior_kernel(
-    lines, cells_ref, w_ref, v_ref, part_ref, stat_ref, wz_ref, wy_ref, wx_ref, v3_ref, w4_ref, acc_ref
+    lines, cells_ref, last_ref, w_ref, v_ref, part_ref, stat_ref, wz_ref, wy_ref, wx_ref, v3_ref, w4_ref, acc_ref
 ):
-    depth = cells_ref.shape[0] // 2
+    depth = (cells_ref.shape[0] + 1) // 2
     cin, cout = w_ref.shape[3:]
     rows = cells_ref.shape[1]
     half = rows // lines
@@ -160,7 +189,7 @@
             v3_ref[dy * 3 * cout : (dy + 1) * 3 * cout, (2 - dz) * cout : (3 - dz) * cout] = v_ref[dz, dy]
     for zo in range(depth):
         first = 0 if zo else 1
-        planes = [cells_ref[2 * zo - 1 + dz] for dz in range(first, 3)]
+        planes = [cells_ref[z] if z < 2 * depth - 1 else last_ref[...] for z in range(2 * zo - 1 + first, 2 * zo + 2)]
         acc_ref[...] = dot(
             jnp.concatenate(planes, axis=1), w4_ref[first:].reshape((3 - first) * 4 * cin, 4 * cout)
         )
@@ -184,14 +213,15 @@
     stat_ref[2 * cout + 8 :, :] = jnp.broadcast_to(offset, (8, cout))
 
 
-def interior(lines, cells, weights, second):
+def interior(lines, cells, last, weights, second):
     depth, rows, wide = cells.shape
+    depth += 1
     cin, cout = weights.shape[3:]
     vmem = pl.BlockSpec(memory_space=pltpu.VMEM)
     flops = depth // 2 * rows * 3 * wide * 8 * cout
     return pl.pallas_call(
         functools.partial(interior_kernel, lines),
-        in_specs=[vmem] * 3,
+        in_specs=[vmem] * 4,
         out_specs=[vmem] * 6,
         out_shape=[
             pltpu.VMEM((depth // 2, rows, cout), F32),
@@ -205,7 +235,7 @@
         compiler_params=pltpu.CompilerParams(vmem_limit_bytes=20 * MIB),
         cost_estimate=pl.CostEstimate(flops=flops, bytes_accessed=6 * MIB, transcendentals=0),
         name="interior",
-    )(*in_vmem(cells), weights, second)
+    )(*in_vmem(cells, last), weights, second)
 
 
 def finish_kernel(
@@ -213,19 +243,20 @@
     feat_ref, mom_ref, xface_ref, acc_ref, rim_ref,
 ):
     depth, rows, cout = part_ref.shape
-    lines = xhalo_ref.shape[0] // (2 * depth)
-    half = rows // lines
-    _, _, _, _, _, y_in, _, z_in, _ = places()
+    half = yzhalo_ref.shape[0]
+    lines = rows // half
+    _, _, _, x_in, _, y_in, _, z_in, _ = places()
     zhalo = jnp.where(z_in, zhalo_ref[...], jnp.zeros(zhalo_ref.shape, BF16))
-    yrest = yhalo_ref[2 * depth * half :, :].astype(F32)
-    yhalo = [yzhalo_ref[:half, :]] + [yhalo_ref[z * half : (z + 1) * half, :] for z in range(2 * depth)]
+    yhalo = [yzhalo_ref[...]] + [yhalo_ref[z * half : (z + 1) * half, :] for z in range(2 * depth)]
     yhalo = [jnp.where(y_in, value, jnp.zeros_like(value)) for value in yhalo]
     yhalo[0] = jnp.where(z_in, yhalo[0], jnp.zeros_like(yhalo[0]))
-    corner = jnp.where(jnp.logical_and(y_in, z_in), yzhalo_ref[half:, :].astype(F32)[:1], 0.0)
-    yrest = jnp.where(y_in, yrest, 0.0)
-    here = [jnp.where(z_in, xzhalo_ref[...].astype(F32)[:lines], 0.0)]
-    here += [xhalo_ref[...].astype(F32)[z * lines : (z + 1) * lines] for z in range(2 * depth)]
-    over = [corner] + [yrest[z : z + 1] for z in range(2 * depth)]
+    xhalo = jnp.where(x_in, xhalo_ref[...].astype(F32), 0.0)
+    here = [jnp.where(jnp.logical_and(x_in, z_in), xzhalo_ref[...].astype(F32)[:lines], 0.0)]
+    here += [xhalo[z * lines : (z + 1) * lines] for z in range(2 * depth)]
+    spot = 2 * depth * lines
+    over = [xhalo[spot + 2 * depth : spot + 2 * depth + 1]] + [xhalo[spot + z : spot + z + 1] for z in range(2 * depth)]
+    over = [jnp.where(y_in, value, 0.0) for value in over]
+    over[0] = jnp.where(z_in, over[0], 0.0)
     over = [jnp.concatenate([line, value[: lines - 1]], axis=0) for line, value in zip(over, here, strict=True)]
     xparts = []
     for zo in range(depth):
@@ -283,8 +314,8 @@
 
 def finish(part, stats, zhalo, yhalo, yzhalo, xhalo, xzhalo, wz, wy, wx):
     depth, rows, cout = part.shape
-    lines = xhalo.shape[0] // (2 * depth)
-    half = rows // lines
+    half = yzhalo.shape[0]
+    lines = rows // half
     rim = rows + (depth - 1) * (half + lines - 1)
     vmem = pl.BlockSpec(memory_space=pltpu.VMEM)
     return pl.pallas_call(
@@ -305,7 +336,7 @@
 def block_kernel(
     total_cells,
     mom_ref, gain_ref, shift_ref, feat_ref, z1_ref, z2_ref, y1_ref, y2_ref, x1_ref, x2_ref, w_ref,
-    out_ref, pad_ref, wide_ref,
+    out_ref, pad_ref, wide_ref, split_ref,
 ):
     depth, rows, cout = feat_ref.shape
     half = y1_ref.shape[0] // (depth + 2)
@@ -325,11 +356,38 @@
     trace1 = jnp.sum(jnp.sum(diag[group:], axis=1, keepdims=True), axis=0, keepdims=True)
     trace = jnp.where(ri < group, trace0, trace1)
     scaled = cov / trace
+    x_even, y_even, z_even, xb_in, xa_in, yb_in, ya_in, zb_in, za_in = places()
+    starts, jobs, spot = [], [], 0
+
+    def centre(read, start, count):
+        hi, lo = split(read() - average)
+        split_ref[start : start + count, :cout] = hi
+        split_ref[start : start + count, cout:] = lo
+
+    for n in range(depth):
+        starts.append((spot, rows))
+        jobs.append(functools.partial(centre, functools.partial(feat_ref.__getitem__, n), *starts[-1]))
+        spot += rows
+    for even, one_ref, two_ref in ((z_even, z1_ref, z2_ref), (y_even, y1_ref, y2_ref), (x_even, x1_ref, x2_ref)):
+        for before, after in ((two_ref, one_ref), (one_ref, two_ref)):
+            starts.append((spot, one_ref.shape[0]))
+            read = lambda even=even, a=before, b=after: jnp.where(even, a[...], b[...])
+            jobs.append(functools.partial(centre, read, *starts[-1]))
+            spot += one_ref.shape[0]
+
+    def some_jobs(count):
+        for _ in range(min(count, len(jobs))):
+            jobs.pop(0)()
+
     scaled_parts = thirds(scaled)
     mat = jnp.where(eye, 1.5, 0.0) - 0.5 * scaled
     for _ in range(NEWTON - 1):
         parts = thirds(mat)
-        mat = 1.5 * mat - 0.5 * dot_full(thirds(dot_full(parts, parts)), thirds(dot_full(parts, scaled_parts)))
+        twice, once = dot_full(parts, parts), dot_full(parts, scaled_parts)
+        some_jobs(1)
+        mat = 1.5 * mat - 0.5 * dot_full(thirds(twice), thirds(once))
+        some_jobs(2)
+    some_jobs(len(jobs))
     gain = jnp.sum(jnp.where(eye, jnp.broadcast_to(gain_ref[...], square), 0.0), axis=1, keepdims=True)
     mat = mat / jnp.sqrt(trace) * gain
     hi, lo = split(mat)
@@ -338,34 +396,28 @@
     )
     shift = shift_ref[...]
 
-    def whiten(value):
-        hi, lo = split(value - average)
-        both = dot(jnp.concatenate([hi, lo], axis=1), mixer, ((1,), (1,)))
+    def whitened(n):
+        start, count = starts[n]
+        both = dot(split_ref[start : start + count, :], mixer, ((1,), (1,)))
         scaled = both[:, :cout] + both[:, cout:] + shift
         return jnp.where(scaled >= 0, scaled, LEAK * scaled)
 
     base = 8
-    x_even, y_even, z_even, xb_in, xa_in, yb_in, ya_in, zb_in, za_in = places()
-
-    def sides(even, one_ref, two_ref):
-        one, two = one_ref[...], two_ref[...]
-        return whiten(jnp.where(even, two, one)), whiten(jnp.where(even, one, two))
-
     def put(zp, yp, middle, left, right, inside):
         l_in, r_in = xb_in, xa_in
         if inside is not None:
             middle = jnp.where(inside, middle, 0.0)
             l_in, r_in = jnp.logical_and(l_in, inside), jnp.logical_and(r_in, inside)
         pad_ref[zp, yp, base : base + half, :] = middle
+        wide_ref[zp, yp * half : (yp + 1) * half, cout : 2 * cout] = middle.astype(BF16)
         pad_ref[zp, yp, base - 1 : base, :] = jnp.where(l_in, left, 0.0)
         pad_ref[zp, yp, base + half : base + half + 1, :] = jnp.where(r_in, right, 0.0)
 
-    zsides = sides(z_even, z1_ref, z2_ref)
-    ysides = sides(y_even, y1_ref, y2_ref)
-    xsides = sides(x_even, x1_ref, x2_ref)
+    ysides = [whitened(depth + 2 + m) for m in range(2)]
+    xsides = [whitened(depth + 4 + m) for m in range(2)]
     spots = [(z + 1, None) for z in range(depth)] + [(0, zb_in), (depth + 1, za_in)]
     for n, (zp, z_in) in enumerate(spots):
-        plane = whiten(feat_ref[n]) if n < depth else zsides[n - depth]
+        plane = whitened(n)
         for y in range(lines):
             k = n * lines + y
             put(zp, y + 1, plane[y * half : (y + 1) * half], xsides[0][k : k + 1], xsides[1][k : k + 1], z_in)
@@ -375,7 +427,7 @@
             put(zp, yp, ysides[m][n * half : (n + 1) * half], xsides[0][k : k + 1], xsides[1][k : k + 1], inside)
     for zp in range(depth + 2):
         for yp in range(lines + 2):
-            for dx in range(3):
+            for dx in (0, 2):
                 wide_ref[zp, yp * half : (yp + 1) * half, dx * cout : (dx + 1) * cout] = pad_ref[
                     zp, yp, base - 1 + dx : base - 1 + dx + half, :
                 ].astype(BF16)
@@ -405,6 +457,7 @@
         scratch_shapes=[
             pltpu.VMEM((depth + 2, lines + 2, half + 16, cout), F32),
             pltpu.VMEM((depth + 2, (lines + 2) * half, 3 * cout), BF16),
+            pltpu.VMEM((depth * rows + 2 * sum(pair[0].shape[0] for pair in (zs, ys, xs)), 2 * cout), BF16),
         ],
         compiler_params=pltpu.CompilerParams(vmem_limit_bytes=24 * MIB),
         name="block",
@@ -422,6 +475,19 @@
 def second_pairs(axis):
     size = lax.axis_size(axis)
     return [(i, (i + 1 if i % 2 else i - 1) % size) for i in range(size)]
+
+
+def second_face(axis, value):
+    size = lax.axis_size(axis)
+    inner = [(i, j) for i, j in second_pairs(axis) if abs(i - j) == 1]
+    other = {"gz": "gy", "gy": "gx", "gx": "gy"}[axis]
+    count = lax.axis_size(other)
+    if count % 2:
+        return lax.ppermute(value, axis, inner)
+    place = (lambda k, i: i * count + k) if axis == "gx" else (lambda k, i: k * size + i)
+    pairs = [(place(k, i), place(k, j)) for k in range(count) for i, j in inner]
+    pairs += [(place(k, i), place(k ^ 1, i)) for k in range(count) for i in (0, size - 1)]
+    return lax.ppermute(value, (axis, other) if axis == "gx" else (other, axis), pairs)
 
 
 def faces(axis, even, low, high):
@@ -432,19 +498,14 @@
         up = up_pairs(axis)
         return lax.ppermute(low, axis, [(j, i) for i, j in up]), lax.ppermute(high, axis, up)
     one = lax.ppermute(jnp.where(even, high, low), axis, first_pairs(axis))
-    if size == 2:
-        return one, one
-    inner = [(i, j) for i, j in second_pairs(axis) if abs(i - j) == 1]
-    return one, lax.ppermute(jnp.where(even, low, high), axis, inner)
+    return one, one if size == 2 else second_face(axis, jnp.where(even, low, high))
 
 
 def added(axis, value, first=True):
     size = lax.axis_size(axis)
-    if size == 1:
-        return value
-    if not power_of_two(size):
+    if size > 1 and not power_of_two(size):
         return lax.psum(value, axis)
-    if first:
+    if first and size > 1:
         value = value + lax.ppermute(value, axis, first_pairs(axis))
     if size > 2:
         value = value + lax.ppermute(value, axis, second_pairs(axis))
@@ -465,8 +526,7 @@
     value, one = value + both[:count], both[count:]
     if size == 2:
         return value, (one, one)
-    inner = [(i, j) for i, j in second_pairs(axis) if abs(i - j) == 1]
-    two = lax.ppermute(jnp.where(even, low, high), axis, inner)
+    two = second_face(axis, jnp.where(even, low, high))
     return added(axis, value, first=False), (one, two)
 
 
@@ -484,29 +544,37 @@
     return [(i, (i + 1) % size) for i in range(size)]
 
 
+def diagonal(first, second):
+    n, m = lax.axis_size(first), lax.axis_size(second)
+    return [(a * m + b, (a + 1) % n * m + (b + 1) % m) for a in range(n) for b in range(m)]
+
+
 def stacked(parts):
     count = sum(part.shape[0] for part in parts)
-    fill = jnp.zeros((-count % 16, parts[0].shape[1]), parts[0].dtype)
-    return jnp.concatenate(parts + [fill], axis=0)
+    count += -count % 16
+    total, spot, zero = None, 0, jnp.zeros((), parts[0].dtype)
+    for part in parts:
+        wide = lax.pad(part, zero, ((spot, count - spot - part.shape[0], 0), (0, 0, 0)))
+        total = wide if total is None else total + wide
+        spot += part.shape[0]
+    return total
 
 
 def body(field, conv_first, norm_gain, norm_shift, conv_second):
     cin, depth_in, height_in, width_in = field.shape
     cout = conv_second.shape[-1]
     depth, lines, half = depth_in // 2, height_in // 2, width_in // 2
-    cells, yface, xface, flags = relayout(field)
-    x_even, y_even, z_even, x_in = (flags[k : k + 1, :] > 0 for k in range(4))
-    zhalo = lax.ppermute(cells[-1], "gz", ring("gz"))
-    xhalo = lax.ppermute(xface.reshape(depth_in * lines, 2 * cin), "gx", ring("gx"))
-    xhalo = jnp.where(x_in, xhalo, jnp.zeros_like(xhalo))
-    rim = xhalo.reshape(depth_in, lines, 2 * cin)
-    yhalo = lax.ppermute(stacked([yface.reshape(depth_in * half, 2 * cin), rim[:, -1]]), "gy", ring("gy"))
-    ny, nz = lax.axis_size("gy"), lax.axis_size("gz")
-    diagonal = [(a * nz + b, (a + 1) % ny * nz + (b + 1) % nz) for a in range(ny) for b in range(nz)]
-    yzhalo = lax.ppermute(stacked([yface[-1], rim[-1, -1:]]), ("gy", "gz"), diagonal)
-    xzhalo = lax.ppermute(stacked([rim[-1]]), "gz", ring("gz"))
-
-    part, stats, wz, wy, wx, second = interior(lines, cells, conv_first, conv_second.reshape(3, 3, 3 * cout, cout))
+    (last, yface, _, flags), (cells, xface) = relayout(field)
+    x_even, y_even, z_even = (flags[k : k + 1, :] > 0 for k in range(3))
+    yzhalo = lax.ppermute(yface[-half:], ("gy", "gz"), diagonal("gy", "gz"))
+    zhalo = lax.ppermute(last, "gz", ring("gz"))
+    yhalo = lax.ppermute(yface, "gy", ring("gy"))
+    xzhalo = lax.ppermute(stacked([xface[-1]]), ("gx", "gz"), diagonal("gx", "gz"))
+    xown = [xface.reshape(depth_in * lines, 2 * cin)]
+    xown += [yhalo.reshape(depth_in, half, 2 * cin)[:, -1], yzhalo[-1:]]
+    xhalo = lax.ppermute(stacked(xown), "gx", ring("gx"))
+
+    part, stats, wz, wy, wx, second = interior(lines, cells, last, conv_first, conv_second.reshape(3, 3, 3 * cout, cout))
     feats, moments, xfaces = finish(part, stats, zhalo, yhalo, yzhalo, xhalo, xzhalo, wz, wy, wx)
     rows = lines * half
     zs = faces("gz", z_even, feats[0], feats[-1])
@@ -522,7 +590,7 @@
 
     def xside(n, x):
         own = [xfaces[n]] + [side.reshape(-1, half, cout)[:, x] for side in zsides + ysides]
-        return jnp.concatenate(own, axis=0)
+        return stacked(own)
 
     low, high = xside(0, 0), xside(1, half - 1)
     moments, xs = added_with_faces("gx", x_even, moments, low, high)

time: 48 us -> 47 us (0.979)
  the two profiles are of different devices: /device:TPU:1 before, /device:TPU:0 now
where the time goes in v5:
time: 47 us; the launch traced here: 46.9 us
  starting transfers between devices  17.3 us (37%)
  waiting for transfers between devices  15 us (32%)
  Pallas kernels  12.3 us (26%)
  local copies, waits for them, and re-layouts  1.72 us (4%)
    pallas_call x1, Pallas kernels, block(): pl.pallas_call(functools.partial(block_kernel, total_cells), in_specs=[vm...  6.6 us
    ppermute x2, waiting for transfers between devices, added(): value = value + lax.ppermute(value, axis, second_pairs(axis))  4.52 us
    ppermute x2, waiting for transfers between devices, added_with_faces(): both = lax.ppermute(both, axis, first_pairs(axis))  4.02 us
    ppermute x1, starting transfers between devices, body(): zhalo = lax.ppermute(last, 'gz', ring('gz'))  3.08 us
    ppermute x2, starting transfers between devices, added(): value = value + lax.ppermute(value, axis, second_pairs(axis))  3.06 us
    ppermute x2, waiting for transfers between devices, second_face(): lax.ppermute(value, (axis, other) if axis == 'gx' else (other, axis), pairs)  2.87 us
    ppermute x1, starting transfers between devices, body(): yzhalo = lax.ppermute(yface[-half:], ('gy', 'gz'), diagonal('gy', 'gz'))  2.81 us
    ppermute x1, starting transfers between devices, body(): lax.ppermute(stacked([xface[-1]]), ('gx', 'gz'), diagonal('gx', 'gz'))  2.56 us
  transfers between devices with their start and end apart: 13, of which 6 were waited for; matrix products, arithmetic and copies ran while one was open for 1% of the time, Pallas kernels for 9%

profile of v5, /device:TPU:0, one launch (start us, length us, event | category | flops | bytes accessed | tf_op | source)
XLA Modules:
  0.0 46.9 jit_solution(11694598622720893042)
XLA Ops:
  0.0 0.0 copy-start
  0.0 1.6 %copy-done = bf16[64,8,16,128]{3,2,1,0:T(8,128)(2,1)S(1)} copy-done((bf16[64,8,16,128]{3,2,1,0:T(8,128)(2,1)S(1)}, bf16[64,8,16,128]{3,2,1,0:T(8,128)(2,1)}, u32[]{:S(2)}) %copy-start) | copy-done | bytes 2097176
  1.6 0.0 copy-start.3
  1.6 0.0 copy-start.4
  1.6 0.6 %faces.1 = (bf16[512,256]{1,0:T(8,128)(2,1)S(1)}, bf16[512,128]{1,0:T(8,128)(2,1)S(1)}, bf16[8,128]{1,0:T(8,128)(2,1)S(1)}, f32[16,128]{1,0:T(8,128)S(1)}) custom-call(bf16[64,8,16,128]{3,2,1,0:T(8,128)(2,1)S(1)} %copy-done), custom_call_target="tpu_custom_call" | custom-call | tf_op jit(solution)/shard_map/faces/pallas_call | solution.py:113
  2.2 3.1 %collective-permute-start = (bf16[512,256]{1,0:T(8,128)(2,1)S(1)}, bf16[512,256]{1,0:T(8,128)(2,1)S(1)}, u32[]{:S(2)}, u32[]{:S(2)}) collective-permute-start(bf16[512,256]{1,0:T(8,128)(2,1)S(1)} %get-tuple-element.22.last_ref), channel_id=1, source_target_pairs={{0,1},{1,2},{2,3},{3,0},{4,5},{5,6},{6,7},{7,4},{8,9},{9,10},{10,1... | collective-permute-start | bytes 786440 | tf_op jit(solution)/shard_map/ppermute | solution.py:570
  5.3 0.0 collective-permute-start.1
  5.3 2.8 %collective-permute-start.2 = (bf16[64,128]{1,0:T(8,128)(2,1)S(1)}, bf16[64,128]{1,0:T(8,128)(2,1)S(1)}, u32[]{:S(2)}, u32[]{:S(2)}) collective-permute-start(bf16[64,128]{1,0:T(8,128)(2,1)S(1)} %slice.105), channel_id=1, source_target_pairs={{0,5},{1,6},{2,7},{3,4},{4,9},{5,10},{6,11},{7,8},{8,13},{9,14},{1... | collective-permute-start | bytes 49160 | tf_op jit(solution)/shard_map/ppermute | solution.py:569
  8.1 1.8 %planes.1 = (bf16[7,512,256]{2,1,0:T(8,128)(2,1)S(1)}, bf16[8,8,128]{2,1,0:T(8,128)(2,1)S(1)}) custom-call(bf16[64,8,16,128]{3,2,1,0:T(8,128)(2,1)S(1)} %copy-done, bf16[8,128]{1,0:T(8,128)(2,1)S(1)} %get-tuple-element.20.xlast_ref), custom_call_target="tpu_custom_call" | custom-call | tf_op jit(solution)/shard_map/planes/pallas_call | solution.py:127
  9.9 2.6 %collective-permute-start.4 = (bf16[16,128]{1,0:T(8,128)(2,1)S(1)}, bf16[16,128]{1,0:T(8,128)(2,1)S(1)}, u32[]{:S(2)}, u32[]{:S(2)}) collective-permute-start(bf16[16,128]{1,0:T(8,128)(2,1)S(1)} %pad.45), channel_id=1, source_target_pairs={{0,17},{1,18},{2,19},{3,16},{16,1},{17,2},{18,3},{19,0},{4,21},{5,... | collective-permute-start | bytes 12296 | tf_op jit(solution)/shard_map/ppermute | solution.py:572
  12.5 1.4 %collective-permute-done.2.yzhalo_ref = bf16[64,128]{1,0:T(8,128)(2,1)S(1)} collective-permute-done((bf16[64,128]{1,0:T(8,128)(2,1)S(1)}, bf16[64,128]{1,0:T(8,128)(2,1)S(1)}, u32[]{:S(2)}, u32[]{:S(2)}) %collective-permute-start.2) | collective-permute-done | bytes 16416 | tf_op jit(solution)/shard_map/ppermute | solution.py:569
  13.9 0.0 collective-permute-done.1.yhalo_ref
  13.9 1.5 %collective-permute-start.3 = (bf16[80,128]{1,0:T(8,128)(2,1)S(1)}, bf16[80,128]{1,0:T(8,128)(2,1)S(1)}, u32[]{:S(2)}, u32[]{:S(2)}) collective-permute-start(bf16[80,128]{1,0:T(8,128)(2,1)S(1)} %pad_add_fusion), channel_id=1, source_target_pairs={{0,16},{16,0},{1,17},{17,1},{2,18},{18,2},{3,19},{19,3},{4,20},{20... | collective-permute-start | bytes 61448 | tf_op jit(solution)/shard_map/ppermute | solution.py:575
  15.5 0.0 copy-done.3
  15.5 0.0 copy-done.4
  15.5 2.4 %interior.1 = (f32[4,512,128]{2,1,0:T(8,128)S(1)}, f32[272,128]{1,0:T(8,128)S(1)}, bf16[256,512]{1,0:T(8,128)(2,1)S(1)}, bf16[384,256]{1,0:T(8,128)(2,1)S(1)}, b...) custom-call(bf16[7,512,256]{2,1,0:T(8,128)(2,1)S(1)} %get-tuple-element.21.cells_ref, ...), custom_call_target="tpu_custom_call" | custom-call | flops 1610612736 | bytes 6291456 | tf_op jit(solution)/shard_map/interior/pallas_call | solution.py:222
  17.9 0.0 collective-permute-done.4.xzhalo_ref
  18.0 0.0 collective-permute-done.3.xhalo_ref
  18.0 0.0 collective-permute-done.zhalo_ref
  18.0 0.8 %finish.1 = (f32[4,512,128]{2,1,0:T(8,128)S(1)}, f32[72,128]{1,0:T(8,128)S(1)}, f32[2,32,128]{2,1,0:T(8,128)S(1)}) custom-call(f32[4,512,128]{2,1,0:T(8,128)S(1)} %get-tuple-element.23.part_ref, f32[272,128]{1,0:T(8,128)S(1)} %get-tuple-element.24.stat_ref, bf16[512,256]{1,0:T(8,128)(2,1)S(1)} %collective-permute-done.zhalo_ref, ...), custom_call_target="tpu_custom_call" | custom-call | tf_op jit(solution)/shard_map/finish/pallas_call | solution.py:321
  18.8 0.0 collective-permute-start.5
  18.9 2.1 %collective-permute-start.8 = (f32[512,128]{1,0:T(8,128)S(1)}, f32[512,128]{1,0:T(8,128)S(1)}, u32[]{:S(2)}, u32[]{:S(2)}) collective-permute-start(f32[512,128]{1,0:T(8,128)S(1)} %get-tuple-element.35), channel_id=1, source_target_pairs={{0,1},{1,0},{2,3},{3,2},{4,5},{5,4},{6,7},{7,6},{8,9},{9,8},{10,11... | collective-permute-start | bytes 786440 | tf_op jit(solution)/shard_map/ppermute | solution.py:500
  21.0 0.0 collective-permute-start.7
  21.0 2.2 %collective-permute-done.5 = f32[72,128]{1,0:T(8,128)S(1)} collective-permute-done((f32[72,128]{1,0:T(8,128)S(1)}, f32[72,128]{1,0:T(8,128)S(1)}, u32[]{:S(2)}, u32[]{:S(2)}) %collective-permute-start.5) | collective-permute-done | bytes 36896 | tf_op jit(solution)/shard_map/ppermute | solution.py:509
  23.2 1.7 %collective-permute-start.6 = (f32[72,128]{1,0:T(8,128)S(1)}, f32[72,128]{1,0:T(8,128)S(1)}, u32[]{:S(2)}, u32[]{:S(2)}) collective-permute-start(f32[72,128]{1,0:T(8,128)S(1)} %add.75), channel_id=1, source_target_pairs={{0,3},{1,2},{2,1},{3,0},{4,7},{5,6},{6,5},{7,4},{8,11},{9,10},{10,... | collective-permute-start | bytes 110600 | tf_op jit(solution)/shard_map/ppermute | solution.py:511
  24.9 4.5 %collective-permute-done.6 = f32[72,128]{1,0:T(8,128)S(1)} collective-permute-done((f32[72,128]{1,0:T(8,128)S(1)}, f32[72,128]{1,0:T(8,128)S(1)}, u32[]{:S(2)}, u32[]{:S(2)}) %collective-permute-start.6) | collective-permute-done | bytes 36896 | tf_op jit(solution)/shard_map/ppermute | solution.py:511
  29.4 0.0 copy-start.1
  29.4 0.0 copy-start.2
  29.4 0.0 collective-permute-done.8.z1_ref
  29.4 0.0 collective-permute-done.7.z2_ref
  29.6 0.1 collective-permute-start.9
  29.7 1.0 %collective-permute-start.11 = (f32[384,128]{1,0:T(8,128)S(1)}, f32[384,128]{1,0:T(8,128)S(1)}, u32[]{:S(2)}, u32[]{:S(2)}) collective-permute-start(f32[384,128]{1,0:T(8,128)S(1)} %get-tuple-element.49), channel_id=1, source_target_pairs={{4,8},{8,4},{20,24},{24,20},{0,16},{12,28},{16,0},{28,12},{5,9},{9... | collective-permute-start | bytes 589832 | tf_op jit(solution)/shard_map/ppermute | solution.py:490
  30.7 0.4 collective-permute-done.9
  31.2 1.4 %collective-permute-start.10 = (f32[72,128]{1,0:T(8,128)S(1)}, f32[72,128]{1,0:T(8,128)S(1)}, u32[]{:S(2)}, u32[]{:S(2)}) collective-permute-start(f32[72,128]{1,0:T(8,128)S(1)} %slice_add_fusion.1), channel_id=1, source_target_pairs={{0,12},{4,8},{8,4},{12,0},{1,13},{5,9},{9,5},{13,1},{2,14},{6,10},... | collective-permute-start | bytes 110600 | tf_op jit(solution)/shard_map/ppermute | solution.py:511
  32.5 2.9 %collective-permute-done.11.y2_ref = f32[384,128]{1,0:T(8,128)S(1)} collective-permute-done((f32[384,128]{1,0:T(8,128)S(1)}, f32[384,128]{1,0:T(8,128)S(1)}, u32[]{:S(2)}, u32[]{:S(2)}) %collective-permute-start.11) | collective-permute-done | bytes 196640 | tf_op jit(solution)/shard_map/ppermute | solution.py:490
  35.4 0.1 broadcast_select_fusion.3
  35.6 0.0 collective-permute-done.10
  35.6 1.0 %collective-permute-start.12 = (f32[136,128]{1,0:T(8,128)S(1)}, f32[136,128]{1,0:T(8,128)S(1)}, u32[]{:S(2)}, u32[]{:S(2)}) collective-permute-start(f32[136,128]{1,0:T(8,128)S(1)} %pad_maximum_fusion.1), channel_id=1, source_target_pairs={{0,16},{16,0},{1,17},{17,1},{2,18},{18,2},{3,19},{19,3},{4,20},{20... | collective-permute-start | bytes 208904 | tf_op jit(solution)/shard_map/ppermute | solution.py:525
  36.6 3.6 %collective-permute-done.12 = f32[136,128]{1,0:T(8,128)S(1)} collective-permute-done((f32[136,128]{1,0:T(8,128)S(1)}, f32[136,128]{1,0:T(8,128)S(1)}, u32[]{:S(2)}, u32[]{:S(2)}) %collective-permute-start.12) | collective-permute-done | bytes 69664 | tf_op jit(solution)/shard_map/ppermute | solution.py:525
  40.2 0.0 copy-done.1
  40.2 0.0 copy-done.2
  40.3 6.6 %block.1 = bf16[4,512,128]{2,1,0:T(8,128)(2,1)} custom-call(f32[72,128]{1,0:T(8,128)S(1)} %slice_add_fusion.mom_ref, f32[1,128]{1,0:T(1,128)S(1)} %bitcast.71, f32[1,128]{1,0:T(1,128)S(1)} %bitcast.72, f32[4,512,128]{2,1,0:T(8,128)S(1)} %get-tuple-element.32.feat_ref, f32[512,128]{1,0:T(8,128)S(1)} %collective-permute-done.8.z1_ref, ...), custom_call_target="tpu_custom_call" | custom-call | tf_op jit(solution)/shard_map/block/pallas_call | solution.py:452
  (33 shorter events, 0.3 us)
Async XLA Ops:
  0.0 1.6 %copy-start = (bf16[64,8,16,128]{3,2,1,0:T(8,128)(2,1)S(1)}, bf16[64,8,16,128]{3,2,1,0:T(8,128)(2,1)}, u32[]{:S(2)}) copy-start(bf16[64,8,16,128]{3,2,1,0:T(8,128)(2,1)} %field_ref.3) | copy-start | bytes 6291460
  1.6 13.9 %copy-start.3 = (bf16[3,3,3,128,128]{4,3,2,1,0:T(8,128)(2,1)S(1)}, bf16[3,3,3,128,128]{4,3,2,1,0:T(8,128)(2,1)}, u32[]{:S(2)}) copy-start(bf16[3,3,3,128,128]{4,3,2,1,0:T(8,128)(2,1)} %param.9) | copy-start | bytes 2654212
  1.6 13.9 %copy-start.4 = (bf16[3,3,3,64,128]{4,3,2,1,0:T(8,128)(2,1)S(1)}, bf16[3,3,3,64,128]{4,3,2,1,0:T(8,128)(2,1)}, u32[]{:S(2)}) copy-start(bf16[3,3,3,64,128]{4,3,2,1,0:T(8,128)(2,1)} %w_ref.1) | copy-start | bytes 1327108
  2.2 15.7 %collective-permute-start = (bf16[512,256]{1,0:T(8,128)(2,1)S(1)}, bf16[512,256]{1,0:T(8,128)(2,1)S(1)}, u32[]{:S(2)}, u32[]{:S(2)}) collective-permute-start(bf16[512,256]{1,0:T(8,128)(2,1)S(1)} %get-tuple-element.22.last_ref), channel_id=1, source_target_pairs={{0,1},{1,2},{2,3},{3,0},{4,5},{5,6},{6,7},{7,4},{8,9},{9,10},{10,1... | collective-permute-start | bytes 786440 | tf_op jit(solution)/shard_map/ppermute | solution.py:570
  5.3 8.6 %collective-permute-start.1 = (bf16[512,128]{1,0:T(8,128)(2,1)S(1)}, bf16[512,128]{1,0:T(8,128)(2,1)S(1)}, u32[]{:S(2)}, u32[]{:S(2)}) collective-permute-start(bf16[512,128]{1,0:T(8,128)(2,1)S(1)} %get-tuple-element.25), channel_id=1, source_target_pairs={{0,4},{4,8},{8,12},{12,0},{1,5},{5,9},{9,13},{13,1},{2,6},{6,10},{... | collective-permute-start | bytes 393224 | tf_op jit(solution)/shard_map/ppermute | solution.py:571
  5.3 8.6 %collective-permute-start.2 = (bf16[64,128]{1,0:T(8,128)(2,1)S(1)}, bf16[64,128]{1,0:T(8,128)(2,1)S(1)}, u32[]{:S(2)}, u32[]{:S(2)}) collective-permute-start(bf16[64,128]{1,0:T(8,128)(2,1)S(1)} %slice.105), channel_id=1, source_target_pairs={{0,5},{1,6},{2,7},{3,4},{4,9},{5,10},{6,11},{7,8},{8,13},{9,14},{1... | collective-permute-start | bytes 49160 | tf_op jit(solution)/shard_map/ppermute | solution.py:569
  9.9 8.0 %collective-permute-start.4 = (bf16[16,128]{1,0:T(8,128)(2,1)S(1)}, bf16[16,128]{1,0:T(8,128)(2,1)S(1)}, u32[]{:S(2)}, u32[]{:S(2)}) collective-permute-start(bf16[16,128]{1,0:T(8,128)(2,1)S(1)} %pad.45), channel_id=1, source_target_pairs={{0,17},{1,18},{2,19},{3,16},{16,1},{17,2},{18,3},{19,0},{4,21},{5,... | collective-permute-start | bytes 12296 | tf_op jit(solution)/shard_map/ppermute | solution.py:572
  13.9 4.0 %collective-permute-start.3 = (bf16[80,128]{1,0:T(8,128)(2,1)S(1)}, bf16[80,128]{1,0:T(8,128)(2,1)S(1)}, u32[]{:S(2)}, u32[]{:S(2)}) collective-permute-start(bf16[80,128]{1,0:T(8,128)(2,1)S(1)} %pad_add_fusion), channel_id=1, source_target_pairs={{0,16},{16,0},{1,17},{17,1},{2,18},{18,2},{3,19},{19,3},{4,20},{20... | collective-permute-start | bytes 61448 | tf_op jit(solution)/shard_map/ppermute | solution.py:575
  18.8 4.4 %collective-permute-start.5 = (f32[72,128]{1,0:T(8,128)S(1)}, f32[72,128]{1,0:T(8,128)S(1)}, u32[]{:S(2)}, u32[]{:S(2)}) collective-permute-start(f32[72,128]{1,0:T(8,128)S(1)} %get-tuple-element.30), channel_id=1, source_target_pairs={{0,1},{1,0},{2,3},{3,2},{4,5},{5,4},{6,7},{7,6},{8,9},{9,8},{10,11... | collective-permute-start | bytes 110600 | tf_op jit(solution)/shard_map/ppermute | solution.py:509
  18.9 10.5 %collective-permute-start.8 = (f32[512,128]{1,0:T(8,128)S(1)}, f32[512,128]{1,0:T(8,128)S(1)}, u32[]{:S(2)}, u32[]{:S(2)}) collective-permute-start(f32[512,128]{1,0:T(8,128)S(1)} %get-tuple-element.35), channel_id=1, source_target_pairs={{0,1},{1,0},{2,3},{3,2},{4,5},{5,4},{6,7},{7,6},{8,9},{9,8},{10,11... | collective-permute-start | bytes 786440 | tf_op jit(solution)/shard_map/ppermute | solution.py:500
  21.0 8.5 %collective-permute-start.7 = (f32[512,128]{1,0:T(8,128)S(1)}, f32[512,128]{1,0:T(8,128)S(1)}, u32[]{:S(2)}, u32[]{:S(2)}) collective-permute-start(f32[512,128]{1,0:T(8,128)S(1)} %get-tuple-element.36), channel_id=1, source_target_pairs={{1,2},{2,1},{5,6},{6,5},{9,10},{10,9},{13,14},{14,13},{0,4},{3,7},... | collective-permute-start | bytes 786440 | tf_op jit(solution)/shard_map/ppermute | solution.py:490
  23.2 6.2 %collective-permute-start.6 = (f32[72,128]{1,0:T(8,128)S(1)}, f32[72,128]{1,0:T(8,128)S(1)}, u32[]{:S(2)}, u32[]{:S(2)}) collective-permute-start(f32[72,128]{1,0:T(8,128)S(1)} %add.75), channel_id=1, source_target_pairs={{0,3},{1,2},{2,1},{3,0},{4,7},{5,6},{6,5},{7,4},{8,11},{9,10},{10,... | collective-permute-start | bytes 110600 | tf_op jit(solution)/shard_map/ppermute | solution.py:511
  29.4 10.8 %copy-start.1 = (f32[128]{0:T(128)S(1)}, f32[128]{0:T(128)}, u32[]{:S(2)}) copy-start(f32[128]{0:T(128)} %param.7) | copy-start | bytes 1540
  29.4 10.8 %copy-start.2 = (f32[128]{0:T(128)S(1)}, f32[128]{0:T(128)}, u32[]{:S(2)}) copy-start(f32[128]{0:T(128)} %param.8) | copy-start | bytes 1540
  29.6 1.6 %collective-permute-start.9 = (f32[456,128]{1,0:T(8,128)S(1)}, f32[456,128]{1,0:T(8,128)S(1)}, u32[]{:S(2)}, u32[]{:S(2)}) collective-permute-start(f32[456,128]{1,0:T(8,128)S(1)} %pad_maximum_fusion), channel_id=1, source_target_pairs={{0,4},{4,0},{8,12},{12,8},{1,5},{5,1},{9,13},{13,9},{2,6},{6,2},{1... | collective-permute-start | bytes 700424 | tf_op jit(solution)/shard_map/ppermute | solution.py:525
  29.7 5.7 %collective-permute-start.11 = (f32[384,128]{1,0:T(8,128)S(1)}, f32[384,128]{1,0:T(8,128)S(1)}, u32[]{:S(2)}, u32[]{:S(2)}) collective-permute-start(f32[384,128]{1,0:T(8,128)S(1)} %get-tuple-element.49), channel_id=1, source_target_pairs={{4,8},{8,4},{20,24},{24,20},{0,16},{12,28},{16,0},{28,12},{5,9},{9... | collective-permute-start | bytes 589832 | tf_op jit(solution)/shard_map/ppermute | solution.py:490
  31.2 4.4 %collective-permute-start.10 = (f32[72,128]{1,0:T(8,128)S(1)}, f32[72,128]{1,0:T(8,128)S(1)}, u32[]{:S(2)}, u32[]{:S(2)}) collective-permute-start(f32[72,128]{1,0:T(8,128)S(1)} %slice_add_fusion.1), channel_id=1, source_target_pairs={{0,12},{4,8},{8,4},{12,0},{1,13},{5,9},{9,5},{13,1},{2,14},{6,10},... | collective-permute-start | bytes 110600 | tf_op jit(solution)/shard_map/ppermute | solution.py:511
  35.6 4.6 %collective-permute-start.12 = (f32[136,128]{1,0:T(8,128)S(1)}, f32[136,128]{1,0:T(8,128)S(1)}, u32[]{:S(2)}, u32[]{:S(2)}) collective-permute-start(f32[136,128]{1,0:T(8,128)S(1)} %pad_maximum_fusion.1), channel_id=1, source_target_pairs={{0,16},{16,0},{1,17},{17,1},{2,18},{18,2},{3,19},{19,3},{4,20},{20... | collective-permute-start | bytes 208904 | tf_op jit(solution)/shard_map/ppermute | solution.py:525

commit v6 on v5

--- a/solution.py
+++ b/solution.py
@@ -32,18 +32,30 @@
 
 
 def thirds(value):
-    one = value.astype(BF16)
-    rest = value - one.astype(F32)
-    two = rest.astype(BF16)
-    return one, two, (rest - two.astype(F32)).astype(BF16)
-
-
-def dot_full(a, b):
-    (a1, a2, a3), (b1, b2, b3) = a, b
-    pair = jnp.concatenate([b1, b2], axis=1)
-    main = dot(jnp.concatenate([a1, a2], axis=1), jnp.concatenate([pair, pair], axis=0))
-    rest = dot(jnp.concatenate([a3, a1], axis=1), jnp.concatenate([b1, b3], axis=0))
-    width = b1.shape[1]
+    one = value.astype(BF16).astype(F32)
+    rest = value - one
+    two = rest.astype(BF16).astype(F32)
+    return one, two, rest - two
+
+
+def as_left(parts):
+    one, two, three = (part.astype(BF16) for part in parts)
+    return jnp.concatenate([one, two], axis=1), jnp.concatenate([three, one], axis=1)
+
+
+def as_right(parts):
+    count, width = parts[0].shape
+    left = iota((count, width), 1) < width // 2
+    one, two, three = (
+        jnp.concatenate([jnp.where(left, part, 0.0), jnp.where(left, 0.0, part)], axis=0).astype(BF16) for part in parts
+    )
+    pair = jnp.concatenate([one, two], axis=1)
+    return jnp.concatenate([pair, pair], axis=0), jnp.concatenate([one, three], axis=0)
+
+
+def dot_blocks(a, b):
+    main, rest = dot(a[0], b[0]), dot(a[1], b[1])
+    width = rest.shape[1]
     return main[:, :width] + (main[:, width:] + rest)
 
 
@@ -336,25 +348,26 @@
 def block_kernel(
     total_cells,
     mom_ref, gain_ref, shift_ref, feat_ref, z1_ref, z2_ref, y1_ref, y2_ref, x1_ref, x2_ref, w_ref,
-    out_ref, pad_ref, wide_ref, split_ref,
+    out_ref, pad_ref, wide_ref, split_ref, done_ref, sem_ref,
 ):
     depth, rows, cout = feat_ref.shape
     half = y1_ref.shape[0] // (depth + 2)
     lines = rows // half
     group = cout // 2
-    square = (cout, cout)
-    ri, ci = iota(square, 0), iota(square, 1)
-    eye = ri == ci
-    same = (ri < group) == (ci < group)
+    side = (group, cout)
+    left = iota(side, 1) < group
+    eye = iota(side, 0) == iota(side, 1) % group
     moments = mom_ref[:group, :] * (1.0 / total_cells)
     average = mom_ref[group : group + 1, :] * (1.0 / total_cells)
-    column = jnp.sum(jnp.where(eye, jnp.broadcast_to(average, square), 0.0), axis=1, keepdims=True)
-    cov = jnp.concatenate([moments, moments], axis=0) - column * average
-    cov = jnp.where(same, cov, 0.0) + jnp.where(eye, EPSILON, 0.0)
-    diag = jnp.where(eye, cov, 0.0)
-    trace0 = jnp.sum(jnp.sum(diag[:group], axis=1, keepdims=True), axis=0, keepdims=True)
-    trace1 = jnp.sum(jnp.sum(diag[group:], axis=1, keepdims=True), axis=0, keepdims=True)
-    trace = jnp.where(ri < group, trace0, trace1)
+
+    def own(value, fill=0.0):
+        one = jnp.sum(jnp.where(left, value, fill), axis=1, keepdims=True)
+        two = jnp.sum(jnp.where(left, fill, value), axis=1, keepdims=True)
+        return jnp.where(left, one, two)
+
+    column = own(jnp.where(eye, average, 0.0))
+    cov = moments - column * average + jnp.where(eye, EPSILON, 0.0)
+    trace = jnp.sum(own(jnp.where(eye, cov, 0.0)), axis=0, keepdims=True)
     scaled = cov / trace
     x_even, y_even, z_even, xb_in, xa_in, yb_in, ya_in, zb_in, za_in = places()
     starts, jobs, spot = [], [], 0
@@ -379,17 +392,17 @@
         for _ in range(min(count, len(jobs))):
             jobs.pop(0)()
 
-    scaled_parts = thirds(scaled)
+    scaled_right = as_right(thirds(scaled))
     mat = jnp.where(eye, 1.5, 0.0) - 0.5 * scaled
     for _ in range(NEWTON - 1):
         parts = thirds(mat)
-        twice, once = dot_full(parts, parts), dot_full(parts, scaled_parts)
-        some_jobs(1)
-        mat = 1.5 * mat - 0.5 * dot_full(thirds(twice), thirds(once))
-        some_jobs(2)
+        taken = as_left(parts)
+        once = dot_blocks(taken, scaled_right)
+        twice = dot_blocks(taken, as_right(parts))
+        mat = 1.5 * mat - 0.5 * dot_blocks(as_left(thirds(twice)), as_right(thirds(once)))
     some_jobs(len(jobs))
-    gain = jnp.sum(jnp.where(eye, jnp.broadcast_to(gain_ref[...], square), 0.0), axis=1, keepdims=True)
-    mat = mat / jnp.sqrt(trace) * gain
+    mat = mat / jnp.sqrt(trace) * own(jnp.where(eye, gain_ref[...], 0.0))
+    mat = jnp.concatenate([jnp.where(left, mat, 0.0), jnp.where(left, 0.0, mat)], axis=0)
     hi, lo = split(mat)
     mixer = jnp.concatenate(
         [jnp.concatenate([hi, hi], axis=1), jnp.concatenate([lo, jnp.zeros_like(lo)], axis=1)], axis=0
@@ -431,7 +444,7 @@
                 wide_ref[zp, yp * half : (yp + 1) * half, dx * cout : (dx + 1) * cout] = pad_ref[
                     zp, yp, base - 1 + dx : base - 1 + dx + half, :
                 ].astype(BF16)
-    sums = [None] * depth
+    sums, copies = [None] * depth, []
     for zp in range(depth + 2):
         low, high = max(zp - 2, 0), min(zp, depth - 1)
         lanes = slice((low - zp + 2) * cout, (high - zp + 3) * cout)
@@ -441,7 +454,11 @@
             piece = got[:, n * cout : (n + 1) * cout]
             sums[z] = piece if sums[z] is None else sums[z] + piece
         if zp >= 2:
-            out_ref[zp - 2] = sums[zp - 2].astype(BF16)
+            done_ref[zp - 2] = sums[zp - 2].astype(BF16)
+            copies.append(pltpu.make_async_copy(done_ref.at[zp - 2], out_ref.at[zp - 2], sem_ref.at[zp - 2]))
+            copies[-1].start()
+    for copy in copies:
+        copy.wait()
 
 
 def block(total_cells, moments, gain, shift, feats, zs, ys, xs, weights):
@@ -452,12 +469,14 @@
     return pl.pallas_call(
         functools.partial(block_kernel, total_cells),
         in_specs=[vmem] * 11,
-        out_specs=vmem,
+        out_specs=pl.BlockSpec(memory_space=pl.ANY),
         out_shape=jax.ShapeDtypeStruct((depth, rows, cout), BF16),
         scratch_shapes=[
             pltpu.VMEM((depth + 2, lines + 2, half + 16, cout), F32),
             pltpu.VMEM((depth + 2, (lines + 2) * half, 3 * cout), BF16),
             pltpu.VMEM((depth * rows + 2 * sum(pair[0].shape[0] for pair in (zs, ys, xs)), 2 * cout), BF16),
+            pltpu.VMEM((depth, rows, cout), BF16),
+            pltpu.SemaphoreType.DMA((depth,)),
         ],
         compiler_params=pltpu.CompilerParams(vmem_limit_bytes=24 * MIB),
         name="block",

time: 47 us -> 46.6 us (level)
  no operation moved by 1% of the time
where the time goes in v6:
time: 46.6 us; the launch traced here: 46.5 us
  starting transfers between devices  17.3 us (37%)
  waiting for transfers between devices  15 us (32%)
  Pallas kernels  11.9 us (26%)
  local copies, waits for them, and re-layouts  1.72 us (4%)
    pallas_call x1, Pallas kernels, block(): pl.pallas_call(functools.partial(block_kernel, total_cells), in_specs=[vm...  6.25 us
    ppermute x2, waiting for transfers between devices, added(): value = value + lax.ppermute(value, axis, second_pairs(axis))  4.52 us
    ppermute x2, waiting for transfers between devices, added_with_faces(): both = lax.ppermute(both, axis, first_pairs(axis))  4.02 us
    ppermute x1, starting transfers between devices, body(): zhalo = lax.ppermute(last, 'gz', ring('gz'))  3.08 us
    ppermute x2, starting transfers between devices, added(): value = value + lax.ppermute(value, axis, second_pairs(axis))  3.06 us
    ppermute x2, waiting for transfers between devices, second_face(): lax.ppermute(value, (axis, other) if axis == 'gx' else (other, axis), pairs)  2.87 us
    ppermute x1, starting transfers between devices, body(): yzhalo = lax.ppermute(yface[-half:], ('gy', 'gz'), diagonal('gy', 'gz'))  2.81 us
    ppermute x1, starting transfers between devices, body(): lax.ppermute(stacked([xface[-1]]), ('gx', 'gz'), diagonal('gx', 'gz'))  2.56 us
  transfers between devices with their start and end apart: 13, of which 6 were waited for; matrix products, arithmetic and copies ran while one was open for 1% of the time, Pallas kernels for 9%

profile of v6, /device:TPU:0, one launch (start us, length us, event | category | flops | bytes accessed | tf_op | source)
XLA Modules:
  0.0 46.5 jit_solution(14952033856038441649)
XLA Ops:
  0.0 0.0 copy-start
  0.0 1.6 %copy-done = bf16[64,8,16,128]{3,2,1,0:T(8,128)(2,1)S(1)} copy-done((bf16[64,8,16,128]{3,2,1,0:T(8,128)(2,1)S(1)}, bf16[64,8,16,128]{3,2,1,0:T(8,128)(2,1)}, u32[]{:S(2)}) %copy-start) | copy-done | bytes 2097176
  1.6 0.0 copy-start.3
  1.6 0.0 copy-start.4
  1.6 0.6 %faces.1 = (bf16[512,256]{1,0:T(8,128)(2,1)S(1)}, bf16[512,128]{1,0:T(8,128)(2,1)S(1)}, bf16[8,128]{1,0:T(8,128)(2,1)S(1)}, f32[16,128]{1,0:T(8,128)S(1)}) custom-call(bf16[64,8,16,128]{3,2,1,0:T(8,128)(2,1)S(1)} %copy-done), custom_call_target="tpu_custom_call" | custom-call | tf_op jit(solution)/shard_map/faces/pallas_call | solution.py:125
  2.2 3.1 %collective-permute-start = (bf16[512,256]{1,0:T(8,128)(2,1)S(1)}, bf16[512,256]{1,0:T(8,128)(2,1)S(1)}, u32[]{:S(2)}, u32[]{:S(2)}) collective-permute-start(bf16[512,256]{1,0:T(8,128)(2,1)S(1)} %get-tuple-element.22.last_ref), channel_id=1, source_target_pairs={{0,1},{1,2},{2,3},{3,0},{4,5},{5,6},{6,7},{7,4},{8,9},{9,10},{10,1... | collective-permute-start | bytes 786440 | tf_op jit(solution)/shard_map/ppermute | solution.py:589
  5.3 0.0 collective-permute-start.1
  5.3 2.8 %collective-permute-start.2 = (bf16[64,128]{1,0:T(8,128)(2,1)S(1)}, bf16[64,128]{1,0:T(8,128)(2,1)S(1)}, u32[]{:S(2)}, u32[]{:S(2)}) collective-permute-start(bf16[64,128]{1,0:T(8,128)(2,1)S(1)} %slice.105), channel_id=1, source_target_pairs={{0,5},{1,6},{2,7},{3,4},{4,9},{5,10},{6,11},{7,8},{8,13},{9,14},{1... | collective-permute-start | bytes 49160 | tf_op jit(solution)/shard_map/ppermute | solution.py:588
  8.1 1.8 %planes.1 = (bf16[7,512,256]{2,1,0:T(8,128)(2,1)S(1)}, bf16[8,8,128]{2,1,0:T(8,128)(2,1)S(1)}) custom-call(bf16[64,8,16,128]{3,2,1,0:T(8,128)(2,1)S(1)} %copy-done, bf16[8,128]{1,0:T(8,128)(2,1)S(1)} %get-tuple-element.20.xlast_ref), custom_call_target="tpu_custom_call" | custom-call | tf_op jit(solution)/shard_map/planes/pallas_call | solution.py:139
  9.9 2.6 %collective-permute-start.4 = (bf16[16,128]{1,0:T(8,128)(2,1)S(1)}, bf16[16,128]{1,0:T(8,128)(2,1)S(1)}, u32[]{:S(2)}, u32[]{:S(2)}) collective-permute-start(bf16[16,128]{1,0:T(8,128)(2,1)S(1)} %pad.45), channel_id=1, source_target_pairs={{0,17},{1,18},{2,19},{3,16},{16,1},{17,2},{18,3},{19,0},{4,21},{5,... | collective-permute-start | bytes 12296 | tf_op jit(solution)/shard_map/ppermute | solution.py:591
  12.5 1.4 %collective-permute-done.2.yzhalo_ref = bf16[64,128]{1,0:T(8,128)(2,1)S(1)} collective-permute-done((bf16[64,128]{1,0:T(8,128)(2,1)S(1)}, bf16[64,128]{1,0:T(8,128)(2,1)S(1)}, u32[]{:S(2)}, u32[]{:S(2)}) %collective-permute-start.2) | collective-permute-done | bytes 16416 | tf_op jit(solution)/shard_map/ppermute | solution.py:588
  13.9 0.0 collective-permute-done.1.yhalo_ref
  13.9 1.5 %collective-permute-start.3 = (bf16[80,128]{1,0:T(8,128)(2,1)S(1)}, bf16[80,128]{1,0:T(8,128)(2,1)S(1)}, u32[]{:S(2)}, u32[]{:S(2)}) collective-permute-start(bf16[80,128]{1,0:T(8,128)(2,1)S(1)} %pad_add_fusion), channel_id=1, source_target_pairs={{0,16},{16,0},{1,17},{17,1},{2,18},{18,2},{3,19},{19,3},{4,20},{20... | collective-permute-start | bytes 61448 | tf_op jit(solution)/shard_map/ppermute | solution.py:594
  15.5 0.0 copy-done.3
  15.5 0.0 copy-done.4
  15.5 2.4 %interior.1 = (f32[4,512,128]{2,1,0:T(8,128)S(1)}, f32[272,128]{1,0:T(8,128)S(1)}, bf16[256,512]{1,0:T(8,128)(2,1)S(1)}, bf16[384,256]{1,0:T(8,128)(2,1)S(1)}, b...) custom-call(bf16[7,512,256]{2,1,0:T(8,128)(2,1)S(1)} %get-tuple-element.21.cells_ref, ...), custom_call_target="tpu_custom_call" | custom-call | flops 1610612736 | bytes 6291456 | tf_op jit(solution)/shard_map/interior/pallas_call | solution.py:234
  17.9 0.0 collective-permute-done.4.xzhalo_ref
  18.0 0.0 collective-permute-done.3.xhalo_ref
  18.0 0.0 collective-permute-done.zhalo_ref
  18.0 0.8 %finish.1 = (f32[4,512,128]{2,1,0:T(8,128)S(1)}, f32[72,128]{1,0:T(8,128)S(1)}, f32[2,32,128]{2,1,0:T(8,128)S(1)}) custom-call(f32[4,512,128]{2,1,0:T(8,128)S(1)} %get-tuple-element.23.part_ref, f32[272,128]{1,0:T(8,128)S(1)} %get-tuple-element.24.stat_ref, bf16[512,256]{1,0:T(8,128)(2,1)S(1)} %collective-permute-done.zhalo_ref, ...), custom_call_target="tpu_custom_call" | custom-call | tf_op jit(solution)/shard_map/finish/pallas_call | solution.py:333
  18.8 0.0 collective-permute-start.5
  18.9 2.1 %collective-permute-start.8 = (f32[512,128]{1,0:T(8,128)S(1)}, f32[512,128]{1,0:T(8,128)S(1)}, u32[]{:S(2)}, u32[]{:S(2)}) collective-permute-start(f32[512,128]{1,0:T(8,128)S(1)} %get-tuple-element.35), channel_id=1, source_target_pairs={{0,1},{1,0},{2,3},{3,2},{4,5},{5,4},{6,7},{7,6},{8,9},{9,8},{10,11... | collective-permute-start | bytes 786440 | tf_op jit(solution)/shard_map/ppermute | solution.py:519
  21.0 0.0 collective-permute-start.7
  21.0 2.2 %collective-permute-done.5 = f32[72,128]{1,0:T(8,128)S(1)} collective-permute-done((f32[72,128]{1,0:T(8,128)S(1)}, f32[72,128]{1,0:T(8,128)S(1)}, u32[]{:S(2)}, u32[]{:S(2)}) %collective-permute-start.5) | collective-permute-done | bytes 36896 | tf_op jit(solution)/shard_map/ppermute | solution.py:528
  23.2 1.7 %collective-permute-start.6 = (f32[72,128]{1,0:T(8,128)S(1)}, f32[72,128]{1,0:T(8,128)S(1)}, u32[]{:S(2)}, u32[]{:S(2)}) collective-permute-start(f32[72,128]{1,0:T(8,128)S(1)} %add.75), channel_id=1, source_target_pairs={{0,3},{1,2},{2,1},{3,0},{4,7},{5,6},{6,5},{7,4},{8,11},{9,10},{10,... | collective-permute-start | bytes 110600 | tf_op jit(solution)/shard_map/ppermute | solution.py:530
  24.9 4.5 %collective-permute-done.6 = f32[72,128]{1,0:T(8,128)S(1)} collective-permute-done((f32[72,128]{1,0:T(8,128)S(1)}, f32[72,128]{1,0:T(8,128)S(1)}, u32[]{:S(2)}, u32[]{:S(2)}) %collective-permute-start.6) | collective-permute-done | bytes 36896 | tf_op jit(solution)/shard_map/ppermute | solution.py:530
  29.4 0.0 copy-start.1
  29.4 0.0 copy-start.2
  29.4 0.0 collective-permute-done.8.z1_ref
  29.4 0.0 collective-permute-done.7.z2_ref
  29.6 0.1 collective-permute-start.9
  29.7 1.0 %collective-permute-start.11 = (f32[384,128]{1,0:T(8,128)S(1)}, f32[384,128]{1,0:T(8,128)S(1)}, u32[]{:S(2)}, u32[]{:S(2)}) collective-permute-start(f32[384,128]{1,0:T(8,128)S(1)} %get-tuple-element.49), channel_id=1, source_target_pairs={{4,8},{8,4},{20,24},{24,20},{0,16},{12,28},{16,0},{28,12},{5,9},{9... | collective-permute-start | bytes 589832 | tf_op jit(solution)/shard_map/ppermute | solution.py:509
  30.7 0.4 collective-permute-done.9
  31.2 1.4 %collective-permute-start.10 = (f32[72,128]{1,0:T(8,128)S(1)}, f32[72,128]{1,0:T(8,128)S(1)}, u32[]{:S(2)}, u32[]{:S(2)}) collective-permute-start(f32[72,128]{1,0:T(8,128)S(1)} %slice_add_fusion.1), channel_id=1, source_target_pairs={{0,12},{4,8},{8,4},{12,0},{1,13},{5,9},{9,5},{13,1},{2,14},{6,10},... | collective-permute-start | bytes 110600 | tf_op jit(solution)/shard_map/ppermute | solution.py:530
  32.5 2.9 %collective-permute-done.11.y2_ref = f32[384,128]{1,0:T(8,128)S(1)} collective-permute-done((f32[384,128]{1,0:T(8,128)S(1)}, f32[384,128]{1,0:T(8,128)S(1)}, u32[]{:S(2)}, u32[]{:S(2)}) %collective-permute-start.11) | collective-permute-done | bytes 196640 | tf_op jit(solution)/shard_map/ppermute | solution.py:509
  35.4 0.1 broadcast_select_fusion.3
  35.6 0.0 collective-permute-done.10
  35.6 1.0 %collective-permute-start.12 = (f32[136,128]{1,0:T(8,128)S(1)}, f32[136,128]{1,0:T(8,128)S(1)}, u32[]{:S(2)}, u32[]{:S(2)}) collective-permute-start(f32[136,128]{1,0:T(8,128)S(1)} %pad_maximum_fusion.1), channel_id=1, source_target_pairs={{0,16},{16,0},{1,17},{17,1},{2,18},{18,2},{3,19},{19,3},{4,20},{20... | collective-permute-start | bytes 208904 | tf_op jit(solution)/shard_map/ppermute | solution.py:544
  36.6 3.6 %collective-permute-done.12 = f32[136,128]{1,0:T(8,128)S(1)} collective-permute-done((f32[136,128]{1,0:T(8,128)S(1)}, f32[136,128]{1,0:T(8,128)S(1)}, u32[]{:S(2)}, u32[]{:S(2)}) %collective-permute-start.12) | collective-permute-done | bytes 69664 | tf_op jit(solution)/shard_map/ppermute | solution.py:544
  40.2 0.0 copy-done.1
  40.2 0.0 copy-done.2
  40.3 6.2 %block.1 = bf16[4,512,128]{2,1,0:T(8,128)(2,1)} custom-call(f32[72,128]{1,0:T(8,128)S(1)} %slice_add_fusion.mom_ref, f32[1,128]{1,0:T(1,128)S(1)} %bitcast.71, f32[1,128]{1,0:T(1,128)S(1)} %bitcast.72, f32[4,512,128]{2,1,0:T(8,128)S(1)} %get-tuple-element.32.feat_ref, f32[512,128]{1,0:T(8,128)S(1)} %collective-permute-done.8.z1_ref, ...), custom_call_target="tpu_custom_call" | custom-call | tf_op jit(solution)/shard_map/block/pallas_call | solution.py:469
  (33 shorter events, 0.3 us)
Async XLA Ops:
  0.0 1.6 %copy-start = (bf16[64,8,16,128]{3,2,1,0:T(8,128)(2,1)S(1)}, bf16[64,8,16,128]{3,2,1,0:T(8,128)(2,1)}, u32[]{:S(2)}) copy-start(bf16[64,8,16,128]{3,2,1,0:T(8,128)(2,1)} %field_ref.3) | copy-start | bytes 6291460
  1.6 13.9 %copy-start.3 = (bf16[3,3,3,128,128]{4,3,2,1,0:T(8,128)(2,1)S(1)}, bf16[3,3,3,128,128]{4,3,2,1,0:T(8,128)(2,1)}, u32[]{:S(2)}) copy-start(bf16[3,3,3,128,128]{4,3,2,1,0:T(8,128)(2,1)} %param.9) | copy-start | bytes 2654212
  1.6 13.9 %copy-start.4 = (bf16[3,3,3,64,128]{4,3,2,1,0:T(8,128)(2,1)S(1)}, bf16[3,3,3,64,128]{4,3,2,1,0:T(8,128)(2,1)}, u32[]{:S(2)}) copy-start(bf16[3,3,3,64,128]{4,3,2,1,0:T(8,128)(2,1)} %w_ref.1) | copy-start | bytes 1327108
  2.2 15.7 %collective-permute-start = (bf16[512,256]{1,0:T(8,128)(2,1)S(1)}, bf16[512,256]{1,0:T(8,128)(2,1)S(1)}, u32[]{:S(2)}, u32[]{:S(2)}) collective-permute-start(bf16[512,256]{1,0:T(8,128)(2,1)S(1)} %get-tuple-element.22.last_ref), channel_id=1, source_target_pairs={{0,1},{1,2},{2,3},{3,0},{4,5},{5,6},{6,7},{7,4},{8,9},{9,10},{10,1... | collective-permute-start | bytes 786440 | tf_op jit(solution)/shard_map/ppermute | solution.py:589
  5.3 8.6 %collective-permute-start.1 = (bf16[512,128]{1,0:T(8,128)(2,1)S(1)}, bf16[512,128]{1,0:T(8,128)(2,1)S(1)}, u32[]{:S(2)}, u32[]{:S(2)}) collective-permute-start(bf16[512,128]{1,0:T(8,128)(2,1)S(1)} %get-tuple-element.25), channel_id=1, source_target_pairs={{0,4},{4,8},{8,12},{12,0},{1,5},{5,9},{9,13},{13,1},{2,6},{6,10},{... | collective-permute-start | bytes 393224 | tf_op jit(solution)/shard_map/ppermute | solution.py:590
  5.3 8.6 %collective-permute-start.2 = (bf16[64,128]{1,0:T(8,128)(2,1)S(1)}, bf16[64,128]{1,0:T(8,128)(2,1)S(1)}, u32[]{:S(2)}, u32[]{:S(2)}) collective-permute-start(bf16[64,128]{1,0:T(8,128)(2,1)S(1)} %slice.105), channel_id=1, source_target_pairs={{0,5},{1,6},{2,7},{3,4},{4,9},{5,10},{6,11},{7,8},{8,13},{9,14},{1... | collective-permute-start | bytes 49160 | tf_op jit(solution)/shard_map/ppermute | solution.py:588
  9.9 8.0 %collective-permute-start.4 = (bf16[16,128]{1,0:T(8,128)(2,1)S(1)}, bf16[16,128]{1,0:T(8,128)(2,1)S(1)}, u32[]{:S(2)}, u32[]{:S(2)}) collective-permute-start(bf16[16,128]{1,0:T(8,128)(2,1)S(1)} %pad.45), channel_id=1, source_target_pairs={{0,17},{1,18},{2,19},{3,16},{16,1},{17,2},{18,3},{19,0},{4,21},{5,... | collective-permute-start | bytes 12296 | tf_op jit(solution)/shard_map/ppermute | solution.py:591
  13.9 4.0 %collective-permute-start.3 = (bf16[80,128]{1,0:T(8,128)(2,1)S(1)}, bf16[80,128]{1,0:T(8,128)(2,1)S(1)}, u32[]{:S(2)}, u32[]{:S(2)}) collective-permute-start(bf16[80,128]{1,0:T(8,128)(2,1)S(1)} %pad_add_fusion), channel_id=1, source_target_pairs={{0,16},{16,0},{1,17},{17,1},{2,18},{18,2},{3,19},{19,3},{4,20},{20... | collective-permute-start | bytes 61448 | tf_op jit(solution)/shard_map/ppermute | solution.py:594
  18.8 4.4 %collective-permute-start.5 = (f32[72,128]{1,0:T(8,128)S(1)}, f32[72,128]{1,0:T(8,128)S(1)}, u32[]{:S(2)}, u32[]{:S(2)}) collective-permute-start(f32[72,128]{1,0:T(8,128)S(1)} %get-tuple-element.30), channel_id=1, source_target_pairs={{0,1},{1,0},{2,3},{3,2},{4,5},{5,4},{6,7},{7,6},{8,9},{9,8},{10,11... | collective-permute-start | bytes 110600 | tf_op jit(solution)/shard_map/ppermute | solution.py:528
  18.9 10.5 %collective-permute-start.8 = (f32[512,128]{1,0:T(8,128)S(1)}, f32[512,128]{1,0:T(8,128)S(1)}, u32[]{:S(2)}, u32[]{:S(2)}) collective-permute-start(f32[512,128]{1,0:T(8,128)S(1)} %get-tuple-element.35), channel_id=1, source_target_pairs={{0,1},{1,0},{2,3},{3,2},{4,5},{5,4},{6,7},{7,6},{8,9},{9,8},{10,11... | collective-permute-start | bytes 786440 | tf_op jit(solution)/shard_map/ppermute | solution.py:519
  21.0 8.5 %collective-permute-start.7 = (f32[512,128]{1,0:T(8,128)S(1)}, f32[512,128]{1,0:T(8,128)S(1)}, u32[]{:S(2)}, u32[]{:S(2)}) collective-permute-start(f32[512,128]{1,0:T(8,128)S(1)} %get-tuple-element.36), channel_id=1, source_target_pairs={{1,2},{2,1},{5,6},{6,5},{9,10},{10,9},{13,14},{14,13},{0,4},{3,7},... | collective-permute-start | bytes 786440 | tf_op jit(solution)/shard_map/ppermute | solution.py:509
  23.2 6.2 %collective-permute-start.6 = (f32[72,128]{1,0:T(8,128)S(1)}, f32[72,128]{1,0:T(8,128)S(1)}, u32[]{:S(2)}, u32[]{:S(2)}) collective-permute-start(f32[72,128]{1,0:T(8,128)S(1)} %add.75), channel_id=1, source_target_pairs={{0,3},{1,2},{2,1},{3,0},{4,7},{5,6},{6,5},{7,4},{8,11},{9,10},{10,... | collective-permute-start | bytes 110600 | tf_op jit(solution)/shard_map/ppermute | solution.py:530
  29.4 10.8 %copy-start.1 = (f32[128]{0:T(128)S(1)}, f32[128]{0:T(128)}, u32[]{:S(2)}) copy-start(f32[128]{0:T(128)} %param.7) | copy-start | bytes 1540
  29.4 10.8 %copy-start.2 = (f32[128]{0:T(128)S(1)}, f32[128]{0:T(128)}, u32[]{:S(2)}) copy-start(f32[128]{0:T(128)} %param.8) | copy-start | bytes 1540
  29.6 1.6 %collective-permute-start.9 = (f32[456,128]{1,0:T(8,128)S(1)}, f32[456,128]{1,0:T(8,128)S(1)}, u32[]{:S(2)}, u32[]{:S(2)}) collective-permute-start(f32[456,128]{1,0:T(8,128)S(1)} %pad_maximum_fusion), channel_id=1, source_target_pairs={{0,4},{4,0},{8,12},{12,8},{1,5},{5,1},{9,13},{13,9},{2,6},{6,2},{1... | collective-permute-start | bytes 700424 | tf_op jit(solution)/shard_map/ppermute | solution.py:544
  29.7 5.7 %collective-permute-start.11 = (f32[384,128]{1,0:T(8,128)S(1)}, f32[384,128]{1,0:T(8,128)S(1)}, u32[]{:S(2)}, u32[]{:S(2)}) collective-permute-start(f32[384,128]{1,0:T(8,128)S(1)} %get-tuple-element.49), channel_id=1, source_target_pairs={{4,8},{8,4},{20,24},{24,20},{0,16},{12,28},{16,0},{28,12},{5,9},{9... | collective-permute-start | bytes 589832 | tf_op jit(solution)/shard_map/ppermute | solution.py:509
  31.2 4.4 %collective-permute-start.10 = (f32[72,128]{1,0:T(8,128)S(1)}, f32[72,128]{1,0:T(8,128)S(1)}, u32[]{:S(2)}, u32[]{:S(2)}) collective-permute-start(f32[72,128]{1,0:T(8,128)S(1)} %slice_add_fusion.1), channel_id=1, source_target_pairs={{0,12},{4,8},{8,4},{12,0},{1,13},{5,9},{9,5},{13,1},{2,14},{6,10},... | collective-permute-start | bytes 110600 | tf_op jit(solution)/shard_map/ppermute | solution.py:530
  35.6 4.6 %collective-permute-start.12 = (f32[136,128]{1,0:T(8,128)S(1)}, f32[136,128]{1,0:T(8,128)S(1)}, u32[]{:S(2)}, u32[]{:S(2)}) collective-permute-start(f32[136,128]{1,0:T(8,128)S(1)} %pad_maximum_fusion.1), channel_id=1, source_target_pairs={{0,16},{16,0},{1,17},{17,1},{2,18},{18,2},{3,19},{19,3},{4,20},{20... | collective-permute-start | bytes 208904 | tf_op jit(solution)/shard_map/ppermute | solution.py:544

commit v7 on v6

--- a/solution.py
+++ b/solution.py
@@ -319,9 +319,16 @@
     sums_column = jnp.sum(jnp.where(eye, sums, 0.0), axis=1, keepdims=True)
     offset_column = jnp.sum(jnp.where(eye, offset, 0.0), axis=1, keepdims=True)
     gram = gram + (sums_column * offset + offset_column * total)
-    left = iota((cout // 2, cout), 1) < cout // 2
-    mom_ref[: cout // 2, :] = jnp.where(left, gram[: cout // 2], gram[cout // 2 :])
-    mom_ref[cout // 2 :, :] = jnp.broadcast_to(total, (8, cout))
+    group = cout // 2
+    row, lane = iota((group, cout), 0), iota((group, cout), 1)
+    both = jnp.where(lane < group, gram[:group], gram[group:])
+    other = pltpu.roll(both, group, 1)
+    mixed = jnp.where(lane >= row, both, other)
+    beside = pltpu.roll(mixed, group, 1)
+    mom_ref[: group // 2, :] = jnp.where(lane[: group // 2] < group, mixed[: group // 2], beside[group // 2 :])
+    diag = jnp.sum(jnp.where(lane == row, other, 0.0), axis=0, keepdims=True)
+    place = iota((8, cout), 0)
+    mom_ref[group // 2 :, :] = jnp.where(place == 0, total, jnp.where(place == 1, diag, 0.0))
 
 
 def finish(part, stats, zhalo, yhalo, yzhalo, xhalo, xzhalo, wz, wy, wx):
@@ -336,7 +343,7 @@
         out_specs=[vmem] * 3,
         out_shape=[
             pltpu.VMEM((depth, rows, cout), F32),
-            pltpu.VMEM((cout // 2 + 8, cout), F32),
+            pltpu.VMEM((cout // 4 + 8, cout), F32),
             pltpu.VMEM((2, depth * lines, cout), F32),
         ],
         scratch_shapes=[pltpu.VMEM((rows, 4 * cout), F32), pltpu.VMEM((rim + (-rim) % 16, cout), F32)],
@@ -357,8 +364,13 @@
     side = (group, cout)
     left = iota(side, 1) < group
     eye = iota(side, 0) == iota(side, 1) % group
-    moments = mom_ref[:group, :] * (1.0 / total_cells)
-    average = mom_ref[group : group + 1, :] * (1.0 / total_cells)
+    row, lane = iota(side, 0), iota(side, 1)
+    mixed = mom_ref[: group // 2, :]
+    mixed = jnp.concatenate([mixed, pltpu.roll(mixed, group, 1)], axis=0)
+    turned = jnp.concatenate([jnp.where(left, mixed, 0.0), jnp.zeros(side, F32)], axis=0).T[:group]
+    two = jnp.where(lane < row, mixed, jnp.where(lane == row, mom_ref[group // 2 + 1 : group // 2 + 2, :], turned))
+    moments = jnp.where(left, jnp.where(lane >= row, mixed, turned), pltpu.roll(two, group, 1)) * (1.0 / total_cells)
+    average = mom_ref[group // 2 : group // 2 + 1, :] * (1.0 / total_cells)
 
     def own(value, fill=0.0):
         one = jnp.sum(jnp.where(left, value, fill), axis=1, keepdims=True)

time: 46.6 us -> 46 us (0.987)
  waiting for transfers between devices: 15 us -> 14.5 us
  transfers between devices with their start and end apart: 13 -> 13, of which waited for: 6 -> 6; matrix products, arithmetic and copies ran while one was open for 1% -> 0% of each run, Pallas kernels for 9% -> 9%
where the time goes in v7:
time: 46 us; the launch traced here: 45.8 us
  starting transfers between devices  16.9 us (37%)
  waiting for transfers between devices  14.5 us (32%)
  Pallas kernels  12.1 us (26%)
  local copies, waits for them, and re-layouts  1.72 us (4%)
    pallas_call x1, Pallas kernels, block(): pl.pallas_call(functools.partial(block_kernel, total_cells), in_specs=[vm...  6.37 us
    ppermute x2, waiting for transfers between devices, added(): value = value + lax.ppermute(value, axis, second_pairs(axis))  4.5 us
    ppermute x2, waiting for transfers between devices, added_with_faces(): both = lax.ppermute(both, axis, first_pairs(axis))  3.94 us
    ppermute x1, starting transfers between devices, body(): zhalo = lax.ppermute(last, 'gz', ring('gz'))  3.08 us
    ppermute x2, starting transfers between devices, added(): value = value + lax.ppermute(value, axis, second_pairs(axis))  3.04 us
    ppermute x2, waiting for transfers between devices, second_face(): lax.ppermute(value, (axis, other) if axis == 'gx' else (other, axis), pairs)  2.87 us
    ppermute x1, starting transfers between devices, body(): yzhalo = lax.ppermute(yface[-half:], ('gy', 'gz'), diagonal('gy', 'gz'))  2.81 us
    ppermute x1, starting transfers between devices, body(): lax.ppermute(stacked([xface[-1]]), ('gx', 'gz'), diagonal('gx', 'gz'))  2.56 us
  transfers between devices with their start and end apart: 13, of which 6 were waited for; matrix products, arithmetic and copies ran while one was open for 0% of the time, Pallas kernels for 9%

profile of v7, /device:TPU:0, one launch (start us, length us, event | category | flops | bytes accessed | tf_op | source)
XLA Modules:
  0.0 45.8 jit_solution(14970535102877473588)
XLA Ops:
  0.0 0.0 copy-start
  0.0 1.6 %copy-done = bf16[64,8,16,128]{3,2,1,0:T(8,128)(2,1)S(1)} copy-done((bf16[64,8,16,128]{3,2,1,0:T(8,128)(2,1)S(1)}, bf16[64,8,16,128]{3,2,1,0:T(8,128)(2,1)}, u32[]{:S(2)}) %copy-start) | copy-done | bytes 2097176
  1.6 0.0 copy-start.3
  1.6 0.0 copy-start.4
  1.6 0.6 %faces.1 = (bf16[512,256]{1,0:T(8,128)(2,1)S(1)}, bf16[512,128]{1,0:T(8,128)(2,1)S(1)}, bf16[8,128]{1,0:T(8,128)(2,1)S(1)}, f32[16,128]{1,0:T(8,128)S(1)}) custom-call(bf16[64,8,16,128]{3,2,1,0:T(8,128)(2,1)S(1)} %copy-done), custom_call_target="tpu_custom_call" | custom-call | tf_op jit(solution)/shard_map/faces/pallas_call | solution.py:125
  2.2 3.1 %collective-permute-start = (bf16[512,256]{1,0:T(8,128)(2,1)S(1)}, bf16[512,256]{1,0:T(8,128)(2,1)S(1)}, u32[]{:S(2)}, u32[]{:S(2)}) collective-permute-start(bf16[512,256]{1,0:T(8,128)(2,1)S(1)} %get-tuple-element.22.last_ref), channel_id=1, source_target_pairs={{0,1},{1,2},{2,3},{3,0},{4,5},{5,6},{6,7},{7,4},{8,9},{9,10},{10,1... | collective-permute-start | bytes 786440 | tf_op jit(solution)/shard_map/ppermute | solution.py:601
  5.3 0.0 collective-permute-start.1
  5.3 2.8 %collective-permute-start.2 = (bf16[64,128]{1,0:T(8,128)(2,1)S(1)}, bf16[64,128]{1,0:T(8,128)(2,1)S(1)}, u32[]{:S(2)}, u32[]{:S(2)}) collective-permute-start(bf16[64,128]{1,0:T(8,128)(2,1)S(1)} %slice.105), channel_id=1, source_target_pairs={{0,5},{1,6},{2,7},{3,4},{4,9},{5,10},{6,11},{7,8},{8,13},{9,14},{1... | collective-permute-start | bytes 49160 | tf_op jit(solution)/shard_map/ppermute | solution.py:600
  8.1 1.8 %planes.1 = (bf16[7,512,256]{2,1,0:T(8,128)(2,1)S(1)}, bf16[8,8,128]{2,1,0:T(8,128)(2,1)S(1)}) custom-call(bf16[64,8,16,128]{3,2,1,0:T(8,128)(2,1)S(1)} %copy-done, bf16[8,128]{1,0:T(8,128)(2,1)S(1)} %get-tuple-element.20.xlast_ref), custom_call_target="tpu_custom_call" | custom-call | tf_op jit(solution)/shard_map/planes/pallas_call | solution.py:139
  9.9 2.6 %collective-permute-start.4 = (bf16[16,128]{1,0:T(8,128)(2,1)S(1)}, bf16[16,128]{1,0:T(8,128)(2,1)S(1)}, u32[]{:S(2)}, u32[]{:S(2)}) collective-permute-start(bf16[16,128]{1,0:T(8,128)(2,1)S(1)} %pad.45), channel_id=1, source_target_pairs={{0,17},{1,18},{2,19},{3,16},{16,1},{17,2},{18,3},{19,0},{4,21},{5,... | collective-permute-start | bytes 12296 | tf_op jit(solution)/shard_map/ppermute | solution.py:603
  12.5 1.4 %collective-permute-done.2.yzhalo_ref = bf16[64,128]{1,0:T(8,128)(2,1)S(1)} collective-permute-done((bf16[64,128]{1,0:T(8,128)(2,1)S(1)}, bf16[64,128]{1,0:T(8,128)(2,1)S(1)}, u32[]{:S(2)}, u32[]{:S(2)}) %collective-permute-start.2) | collective-permute-done | bytes 16416 | tf_op jit(solution)/shard_map/ppermute | solution.py:600
  13.9 0.0 collective-permute-done.1.yhalo_ref
  13.9 1.5 %collective-permute-start.3 = (bf16[80,128]{1,0:T(8,128)(2,1)S(1)}, bf16[80,128]{1,0:T(8,128)(2,1)S(1)}, u32[]{:S(2)}, u32[]{:S(2)}) collective-permute-start(bf16[80,128]{1,0:T(8,128)(2,1)S(1)} %pad_add_fusion), channel_id=1, source_target_pairs={{0,16},{16,0},{1,17},{17,1},{2,18},{18,2},{3,19},{19,3},{4,20},{20... | collective-permute-start | bytes 61448 | tf_op jit(solution)/shard_map/ppermute | solution.py:606
  15.5 0.0 copy-done.3
  15.5 0.0 copy-done.4
  15.5 2.4 %interior.1 = (f32[4,512,128]{2,1,0:T(8,128)S(1)}, f32[272,128]{1,0:T(8,128)S(1)}, bf16[256,512]{1,0:T(8,128)(2,1)S(1)}, bf16[384,256]{1,0:T(8,128)(2,1)S(1)}, b...) custom-call(bf16[7,512,256]{2,1,0:T(8,128)(2,1)S(1)} %get-tuple-element.21.cells_ref, ...), custom_call_target="tpu_custom_call" | custom-call | flops 1610612736 | bytes 6291456 | tf_op jit(solution)/shard_map/interior/pallas_call | solution.py:234
  17.9 0.0 collective-permute-done.4.xzhalo_ref
  18.0 0.0 collective-permute-done.3.xhalo_ref
  18.0 0.0 collective-permute-done.zhalo_ref
  18.0 0.9 %finish.1 = (f32[4,512,128]{2,1,0:T(8,128)S(1)}, f32[40,128]{1,0:T(8,128)S(1)}, f32[2,32,128]{2,1,0:T(8,128)S(1)}) custom-call(f32[4,512,128]{2,1,0:T(8,128)S(1)} %get-tuple-element.23.part_ref, f32[272,128]{1,0:T(8,128)S(1)} %get-tuple-element.24.stat_ref, bf16[512,256]{1,0:T(8,128)(2,1)S(1)} %collective-permute-done.zhalo_ref, ...), custom_call_target="tpu_custom_call" | custom-call | tf_op jit(solution)/shard_map/finish/pallas_call | solution.py:340
  18.9 0.0 collective-permute-start.5
  19.0 2.1 %collective-permute-start.8 = (f32[512,128]{1,0:T(8,128)S(1)}, f32[512,128]{1,0:T(8,128)S(1)}, u32[]{:S(2)}, u32[]{:S(2)}) collective-permute-start(f32[512,128]{1,0:T(8,128)S(1)} %get-tuple-element.35), channel_id=1, source_target_pairs={{0,1},{1,0},{2,3},{3,2},{4,5},{5,4},{6,7},{7,6},{8,9},{9,8},{10,11... | collective-permute-start | bytes 786440 | tf_op jit(solution)/shard_map/ppermute | solution.py:531
  21.1 0.0 collective-permute-start.7
  21.1 1.8 %collective-permute-done.5 = f32[40,128]{1,0:T(8,128)S(1)} collective-permute-done((f32[40,128]{1,0:T(8,128)S(1)}, f32[40,128]{1,0:T(8,128)S(1)}, u32[]{:S(2)}, u32[]{:S(2)}) %collective-permute-start.5) | collective-permute-done | bytes 20512 | tf_op jit(solution)/shard_map/ppermute | solution.py:540
  22.9 1.6 %collective-permute-start.6 = (f32[40,128]{1,0:T(8,128)S(1)}, f32[40,128]{1,0:T(8,128)S(1)}, u32[]{:S(2)}, u32[]{:S(2)}) collective-permute-start(f32[40,128]{1,0:T(8,128)S(1)} %add.75), channel_id=1, source_target_pairs={{0,3},{1,2},{2,1},{3,0},{4,7},{5,6},{6,5},{7,4},{8,11},{9,10},{10,... | collective-permute-start | bytes 61448 | tf_op jit(solution)/shard_map/ppermute | solution.py:542
  24.6 0.0 copy-start.1
  24.6 0.0 copy-start.2
  24.6 4.5 %collective-permute-done.6 = f32[40,128]{1,0:T(8,128)S(1)} collective-permute-done((f32[40,128]{1,0:T(8,128)S(1)}, f32[40,128]{1,0:T(8,128)S(1)}, u32[]{:S(2)}, u32[]{:S(2)}) %collective-permute-start.6) | collective-permute-done | bytes 20512 | tf_op jit(solution)/shard_map/ppermute | solution.py:542
  29.1 0.0 collective-permute-done.8.z1_ref
  29.1 0.0 collective-permute-done.7.z2_ref
  29.2 0.1 collective-permute-start.9
  29.3 0.8 %collective-permute-start.11 = (f32[384,128]{1,0:T(8,128)S(1)}, f32[384,128]{1,0:T(8,128)S(1)}, u32[]{:S(2)}, u32[]{:S(2)}) collective-permute-start(f32[384,128]{1,0:T(8,128)S(1)} %get-tuple-element.49), channel_id=1, source_target_pairs={{4,8},{8,4},{20,24},{24,20},{0,16},{12,28},{16,0},{28,12},{5,9},{9... | collective-permute-start | bytes 589832 | tf_op jit(solution)/shard_map/ppermute | solution.py:521
  30.2 0.6 %collective-permute-done.9 = f32[424,128]{1,0:T(8,128)S(1)} collective-permute-done((f32[424,128]{1,0:T(8,128)S(1)}, f32[424,128]{1,0:T(8,128)S(1)}, u32[]{:S(2)}, u32[]{:S(2)}) %collective-permute-start.9) | collective-permute-done | bytes 217120 | tf_op jit(solution)/shard_map/ppermute | solution.py:556
  30.8 1.4 %collective-permute-start.10 = (f32[40,128]{1,0:T(8,128)S(1)}, f32[40,128]{1,0:T(8,128)S(1)}, u32[]{:S(2)}, u32[]{:S(2)}) collective-permute-start(f32[40,128]{1,0:T(8,128)S(1)} %slice_add_fusion.1), channel_id=1, source_target_pairs={{0,12},{4,8},{8,4},{12,0},{1,13},{5,9},{9,5},{13,1},{2,14},{6,10},... | collective-permute-start | bytes 61448 | tf_op jit(solution)/shard_map/ppermute | solution.py:542
  32.2 2.9 %collective-permute-done.11.y2_ref = f32[384,128]{1,0:T(8,128)S(1)} collective-permute-done((f32[384,128]{1,0:T(8,128)S(1)}, f32[384,128]{1,0:T(8,128)S(1)}, u32[]{:S(2)}, u32[]{:S(2)}) %collective-permute-start.11) | collective-permute-done | bytes 196640 | tf_op jit(solution)/shard_map/ppermute | solution.py:521
  35.2 0.0 collective-permute-done.10
  35.2 0.8 %collective-permute-start.12 = (f32[104,128]{1,0:T(8,128)S(1)}, f32[104,128]{1,0:T(8,128)S(1)}, u32[]{:S(2)}, u32[]{:S(2)}) collective-permute-start(f32[104,128]{1,0:T(8,128)S(1)} %pad_maximum_fusion.1), channel_id=1, source_target_pairs={{0,16},{16,0},{1,17},{17,1},{2,18},{18,2},{3,19},{19,3},{4,20},{20... | collective-permute-start | bytes 159752 | tf_op jit(solution)/shard_map/ppermute | solution.py:556
  36.1 3.3 %collective-permute-done.12 = f32[104,128]{1,0:T(8,128)S(1)} collective-permute-done((f32[104,128]{1,0:T(8,128)S(1)}, f32[104,128]{1,0:T(8,128)S(1)}, u32[]{:S(2)}, u32[]{:S(2)}) %collective-permute-start.12) | collective-permute-done | bytes 53280 | tf_op jit(solution)/shard_map/ppermute | solution.py:556
  39.4 0.0 copy-done.1
  39.4 0.0 copy-done.2
  39.5 6.4 %block.1 = bf16[4,512,128]{2,1,0:T(8,128)(2,1)} custom-call(f32[40,128]{1,0:T(8,128)S(1)} %slice_add_fusion.mom_ref, f32[1,128]{1,0:T(1,128)S(1)} %bitcast.71, f32[1,128]{1,0:T(1,128)S(1)} %bitcast.72, f32[4,512,128]{2,1,0:T(8,128)S(1)} %get-tuple-element.32.feat_ref, f32[512,128]{1,0:T(8,128)S(1)} %collective-permute-done.8.z1_ref, ...), custom_call_target="tpu_custom_call" | custom-call | tf_op jit(solution)/shard_map/block/pallas_call | solution.py:481
  (34 shorter events, 0.3 us)
Async XLA Ops:
  0.0 1.6 %copy-start = (bf16[64,8,16,128]{3,2,1,0:T(8,128)(2,1)S(1)}, bf16[64,8,16,128]{3,2,1,0:T(8,128)(2,1)}, u32[]{:S(2)}) copy-start(bf16[64,8,16,128]{3,2,1,0:T(8,128)(2,1)} %field_ref.3) | copy-start | bytes 6291460
  1.6 13.9 %copy-start.3 = (bf16[3,3,3,128,128]{4,3,2,1,0:T(8,128)(2,1)S(1)}, bf16[3,3,3,128,128]{4,3,2,1,0:T(8,128)(2,1)}, u32[]{:S(2)}) copy-start(bf16[3,3,3,128,128]{4,3,2,1,0:T(8,128)(2,1)} %param.9) | copy-start | bytes 2654212
  1.6 13.9 %copy-start.4 = (bf16[3,3,3,64,128]{4,3,2,1,0:T(8,128)(2,1)S(1)}, bf16[3,3,3,64,128]{4,3,2,1,0:T(8,128)(2,1)}, u32[]{:S(2)}) copy-start(bf16[3,3,3,64,128]{4,3,2,1,0:T(8,128)(2,1)} %w_ref.1) | copy-start | bytes 1327108
  2.2 15.7 %collective-permute-start = (bf16[512,256]{1,0:T(8,128)(2,1)S(1)}, bf16[512,256]{1,0:T(8,128)(2,1)S(1)}, u32[]{:S(2)}, u32[]{:S(2)}) collective-permute-start(bf16[512,256]{1,0:T(8,128)(2,1)S(1)} %get-tuple-element.22.last_ref), channel_id=1, source_target_pairs={{0,1},{1,2},{2,3},{3,0},{4,5},{5,6},{6,7},{7,4},{8,9},{9,10},{10,1... | collective-permute-start | bytes 786440 | tf_op jit(solution)/shard_map/ppermute | solution.py:601
  5.3 8.6 %collective-permute-start.1 = (bf16[512,128]{1,0:T(8,128)(2,1)S(1)}, bf16[512,128]{1,0:T(8,128)(2,1)S(1)}, u32[]{:S(2)}, u32[]{:S(2)}) collective-permute-start(bf16[512,128]{1,0:T(8,128)(2,1)S(1)} %get-tuple-element.25), channel_id=1, source_target_pairs={{0,4},{4,8},{8,12},{12,0},{1,5},{5,9},{9,13},{13,1},{2,6},{6,10},{... | collective-permute-start | bytes 393224 | tf_op jit(solution)/shard_map/ppermute | solution.py:602
  5.3 8.6 %collective-permute-start.2 = (bf16[64,128]{1,0:T(8,128)(2,1)S(1)}, bf16[64,128]{1,0:T(8,128)(2,1)S(1)}, u32[]{:S(2)}, u32[]{:S(2)}) collective-permute-start(bf16[64,128]{1,0:T(8,128)(2,1)S(1)} %slice.105), channel_id=1, source_target_pairs={{0,5},{1,6},{2,7},{3,4},{4,9},{5,10},{6,11},{7,8},{8,13},{9,14},{1... | collective-permute-start | bytes 49160 | tf_op jit(solution)/shard_map/ppermute | solution.py:600
  9.9 8.0 %collective-permute-start.4 = (bf16[16,128]{1,0:T(8,128)(2,1)S(1)}, bf16[16,128]{1,0:T(8,128)(2,1)S(1)}, u32[]{:S(2)}, u32[]{:S(2)}) collective-permute-start(bf16[16,128]{1,0:T(8,128)(2,1)S(1)} %pad.45), channel_id=1, source_target_pairs={{0,17},{1,18},{2,19},{3,16},{16,1},{17,2},{18,3},{19,0},{4,21},{5,... | collective-permute-start | bytes 12296 | tf_op jit(solution)/shard_map/ppermute | solution.py:603
  13.9 4.0 %collective-permute-start.3 = (bf16[80,128]{1,0:T(8,128)(2,1)S(1)}, bf16[80,128]{1,0:T(8,128)(2,1)S(1)}, u32[]{:S(2)}, u32[]{:S(2)}) collective-permute-start(bf16[80,128]{1,0:T(8,128)(2,1)S(1)} %pad_add_fusion), channel_id=1, source_target_pairs={{0,16},{16,0},{1,17},{17,1},{2,18},{18,2},{3,19},{19,3},{4,20},{20... | collective-permute-start | bytes 61448 | tf_op jit(solution)/shard_map/ppermute | solution.py:606
  18.9 4.0 %collective-permute-start.5 = (f32[40,128]{1,0:T(8,128)S(1)}, f32[40,128]{1,0:T(8,128)S(1)}, u32[]{:S(2)}, u32[]{:S(2)}) collective-permute-start(f32[40,128]{1,0:T(8,128)S(1)} %get-tuple-element.30), channel_id=1, source_target_pairs={{0,1},{1,0},{2,3},{3,2},{4,5},{5,4},{6,7},{7,6},{8,9},{9,8},{10,11... | collective-permute-start | bytes 61448 | tf_op jit(solution)/shard_map/ppermute | solution.py:540
  19.0 10.1 %collective-permute-start.8 = (f32[512,128]{1,0:T(8,128)S(1)}, f32[512,128]{1,0:T(8,128)S(1)}, u32[]{:S(2)}, u32[]{:S(2)}) collective-permute-start(f32[512,128]{1,0:T(8,128)S(1)} %get-tuple-element.35), channel_id=1, source_target_pairs={{0,1},{1,0},{2,3},{3,2},{4,5},{5,4},{6,7},{7,6},{8,9},{9,8},{10,11... | collective-permute-start | bytes 786440 | tf_op jit(solution)/shard_map/ppermute | solution.py:531
  21.1 8.0 %collective-permute-start.7 = (f32[512,128]{1,0:T(8,128)S(1)}, f32[512,128]{1,0:T(8,128)S(1)}, u32[]{:S(2)}, u32[]{:S(2)}) collective-permute-start(f32[512,128]{1,0:T(8,128)S(1)} %get-tuple-element.36), channel_id=1, source_target_pairs={{1,2},{2,1},{5,6},{6,5},{9,10},{10,9},{13,14},{14,13},{0,4},{3,7},... | collective-permute-start | bytes 786440 | tf_op jit(solution)/shard_map/ppermute | solution.py:521
  22.9 6.1 %collective-permute-start.6 = (f32[40,128]{1,0:T(8,128)S(1)}, f32[40,128]{1,0:T(8,128)S(1)}, u32[]{:S(2)}, u32[]{:S(2)}) collective-permute-start(f32[40,128]{1,0:T(8,128)S(1)} %add.75), channel_id=1, source_target_pairs={{0,3},{1,2},{2,1},{3,0},{4,7},{5,6},{6,5},{7,4},{8,11},{9,10},{10,... | collective-permute-start | bytes 61448 | tf_op jit(solution)/shard_map/ppermute | solution.py:542
  24.6 14.9 %copy-start.1 = (f32[128]{0:T(128)S(1)}, f32[128]{0:T(128)}, u32[]{:S(2)}) copy-start(f32[128]{0:T(128)} %param.7) | copy-start | bytes 1540
  24.6 14.9 %copy-start.2 = (f32[128]{0:T(128)S(1)}, f32[128]{0:T(128)}, u32[]{:S(2)}) copy-start(f32[128]{0:T(128)} %param.8) | copy-start | bytes 1540
  29.2 1.5 %collective-permute-start.9 = (f32[424,128]{1,0:T(8,128)S(1)}, f32[424,128]{1,0:T(8,128)S(1)}, u32[]{:S(2)}, u32[]{:S(2)}) collective-permute-start(f32[424,128]{1,0:T(8,128)S(1)} %pad_maximum_fusion), channel_id=1, source_target_pairs={{0,4},{4,0},{8,12},{12,8},{1,5},{5,1},{9,13},{13,9},{2,6},{6,2},{1... | collective-permute-start | bytes 651272 | tf_op jit(solution)/shard_map/ppermute | solution.py:556
  29.3 5.7 %collective-permute-start.11 = (f32[384,128]{1,0:T(8,128)S(1)}, f32[384,128]{1,0:T(8,128)S(1)}, u32[]{:S(2)}, u32[]{:S(2)}) collective-permute-start(f32[384,128]{1,0:T(8,128)S(1)} %get-tuple-element.49), channel_id=1, source_target_pairs={{4,8},{8,4},{20,24},{24,20},{0,16},{12,28},{16,0},{28,12},{5,9},{9... | collective-permute-start | bytes 589832 | tf_op jit(solution)/shard_map/ppermute | solution.py:521
  30.8 4.4 %collective-permute-start.10 = (f32[40,128]{1,0:T(8,128)S(1)}, f32[40,128]{1,0:T(8,128)S(1)}, u32[]{:S(2)}, u32[]{:S(2)}) collective-permute-start(f32[40,128]{1,0:T(8,128)S(1)} %slice_add_fusion.1), channel_id=1, source_target_pairs={{0,12},{4,8},{8,4},{12,0},{1,13},{5,9},{9,5},{13,1},{2,14},{6,10},... | collective-permute-start | bytes 61448 | tf_op jit(solution)/shard_map/ppermute | solution.py:542
  35.2 4.2 %collective-permute-start.12 = (f32[104,128]{1,0:T(8,128)S(1)}, f32[104,128]{1,0:T(8,128)S(1)}, u32[]{:S(2)}, u32[]{:S(2)}) collective-permute-start(f32[104,128]{1,0:T(8,128)S(1)} %pad_maximum_fusion.1), channel_id=1, source_target_pairs={{0,16},{16,0},{1,17},{17,1},{2,18},{18,2},{3,19},{19,3},{4,20},{20... | collective-permute-start | bytes 159752 | tf_op jit(solution)/shard_map/ppermute | solution.py:556

commit v8 on v7

--- a/solution.py
+++ b/solution.py
@@ -263,12 +263,11 @@
     yhalo = [jnp.where(y_in, value, jnp.zeros_like(value)) for value in yhalo]
     yhalo[0] = jnp.where(z_in, yhalo[0], jnp.zeros_like(yhalo[0]))
     xhalo = jnp.where(x_in, xhalo_ref[...].astype(F32), 0.0)
-    here = [jnp.where(jnp.logical_and(x_in, z_in), xzhalo_ref[...].astype(F32)[:lines], 0.0)]
-    here += [xhalo[z * lines : (z + 1) * lines] for z in range(2 * depth)]
+    xzhalo = jnp.where(jnp.logical_and(x_in, z_in), xzhalo_ref[...].astype(F32), 0.0)
+    here = [xzhalo[:lines]] + [xhalo[z * lines : (z + 1) * lines] for z in range(2 * depth)]
     spot = 2 * depth * lines
-    over = [xhalo[spot + 2 * depth : spot + 2 * depth + 1]] + [xhalo[spot + z : spot + z + 1] for z in range(2 * depth)]
+    over = [xzhalo[lines : lines + 1]] + [xhalo[spot + z : spot + z + 1] for z in range(2 * depth)]
     over = [jnp.where(y_in, value, 0.0) for value in over]
-    over[0] = jnp.where(z_in, over[0], 0.0)
     over = [jnp.concatenate([line, value[: lines - 1]], axis=0) for line, value in zip(over, here, strict=True)]
     xparts = []
     for zo in range(depth):
@@ -552,12 +551,25 @@
     if size == 1 or not power_of_two(size):
         return added(axis, value), faces(axis, even, low, high)
     count = value.shape[0]
+    two = second_face(axis, jnp.where(even, low, high)) if size > 2 else None
     both = jnp.concatenate([value, jnp.where(even, high, low)], axis=0)
     both = lax.ppermute(both, axis, first_pairs(axis))
     value, one = value + both[:count], both[count:]
     if size == 2:
         return value, (one, one)
-    two = second_face(axis, jnp.where(even, low, high))
+    value = added(axis, value, first=False)
+    value, two = lax.optimization_barrier((value, two))
+    return value, (one, two)
+
+
+def added_beside_faces(axis, even, value, low, high):
+    size = lax.axis_size(axis)
+    if size < 4 or not power_of_two(size):
+        return added(axis, value), faces(axis, even, low, high)
+    value = value + lax.ppermute(value, axis, first_pairs(axis))
+    one = lax.ppermute(jnp.where(even, high, low), axis, first_pairs(axis))
+    value, other = lax.optimization_barrier((value, jnp.where(even, low, high)))
+    two = second_face(axis, other)
     return added(axis, value, first=False), (one, two)
 
 
@@ -600,16 +612,14 @@
     yzhalo = lax.ppermute(yface[-half:], ("gy", "gz"), diagonal("gy", "gz"))
     zhalo = lax.ppermute(last, "gz", ring("gz"))
     yhalo = lax.ppermute(yface, "gy", ring("gy"))
-    xzhalo = lax.ppermute(stacked([xface[-1]]), ("gx", "gz"), diagonal("gx", "gz"))
-    xown = [xface.reshape(depth_in * lines, 2 * cin)]
-    xown += [yhalo.reshape(depth_in, half, 2 * cin)[:, -1], yzhalo[-1:]]
-    xhalo = lax.ppermute(stacked(xown), "gx", ring("gx"))
+    yrim = yhalo.reshape(depth_in, half, 2 * cin)[:, -1]
+    xhalo = lax.ppermute(stacked([xface.reshape(depth_in * lines, 2 * cin), yrim]), "gx", ring("gx"))
+    xzhalo = lax.ppermute(stacked([xface[-1], yrim[-1:]]), ("gx", "gz"), diagonal("gx", "gz"))
 
     part, stats, wz, wy, wx, second = interior(lines, cells, last, conv_first, conv_second.reshape(3, 3, 3 * cout, cout))
     feats, moments, xfaces = finish(part, stats, zhalo, yhalo, yzhalo, xhalo, xzhalo, wz, wy, wx)
     rows = lines * half
-    zs = faces("gz", z_even, feats[0], feats[-1])
-    moments = added("gz", moments)
+    moments, zs = added_beside_faces("gz", z_even, moments, feats[0], feats[-1])
     zsides = sided(z_even, zs)
 
     def yside(y):

time: 46 us -> 45.1 us (0.980)
  starting transfers between devices: 16.9 us -> 12.8 us
  waiting for transfers between devices: 14.5 us -> 17.9 us
    ppermute x2, waiting for transfers between devices: 4.5 us -> 8.35 us  [added(): value = value + lax.ppermute(value, axis, second_pairs(axis))]
    ppermute x2, starting transfers between devices: 3.04 us -> 0.7 us  [added(): value = value + lax.ppermute(value, axis, second_pairs(axis))]
    ppermute x4, waiting for transfers between devices: 1.84 us -> 4.02 us  [the longest x1 2.1 us: body(): lax.ppermute(stacked([xface[-1], yrim[-1:]]), ('gx', 'gz'), diagonal('gx'...]
    ppermute x2, waiting for transfers between devices: 2.87 us -> 0.88 us  [second_face(): lax.ppermute(value, (axis, other) if axis == 'gx' else (other, axis), pairs)]
    ppermute x1, waiting for transfers between devices: 1.4 us -> 0.19 us  [body(): yzhalo = lax.ppermute(yface[-half:], ('gy', 'gz'), diagonal('gy', 'gz'))]
    ppermute x4, starting transfers between devices: 6.2 us -> 5.21 us  [the longest x1 2.06 us: added_beside_faces(): one = lax.ppermute(jnp.where(even, high, low), axis, first_pairs(axis))]
    ppermute x2, waiting for transfers between devices: 3.94 us -> 4.44 us  [added_with_faces(): both = lax.ppermute(both, axis, first_pairs(axis))]
    ppermute x1, starting transfers between devices: 0.01 us -> 0.51 us  [body(): yhalo = lax.ppermute(yface, 'gy', ring('gy'))]
  transfers between devices with their start and end apart: 13 -> 13, of which waited for: 6 -> 8; matrix products, arithmetic and copies ran while one was open for 0% -> 0% of each run, Pallas kernels for 9% -> 9%
where the time goes in v8:
time: 45.1 us; the launch traced here: 45 us
  waiting for transfers between devices  17.9 us (40%)
  starting transfers between devices  12.8 us (28%)
  Pallas kernels  12.1 us (27%)
  local copies, waits for them, and re-layouts  1.72 us (4%)
    ppermute x2, waiting for transfers between devices, added(): value = value + lax.ppermute(value, axis, second_pairs(axis))  8.35 us
    pallas_call x1, Pallas kernels, block(): pl.pallas_call(functools.partial(block_kernel, total_cells), in_specs=[vm...  6.36 us
    ppermute x2, waiting for transfers between devices, added_with_faces(): both = lax.ppermute(both, axis, first_pairs(axis))  4.44 us
    ppermute x1, starting transfers between devices, body(): zhalo = lax.ppermute(last, 'gz', ring('gz'))  2.64 us
    ppermute x1, starting transfers between devices, body(): yzhalo = lax.ppermute(yface[-half:], ('gy', 'gz'), diagonal('gy', 'gz'))  2.47 us
    pallas_call x1, Pallas kernels, interior(): pl.pallas_call(functools.partial(interior_kernel, lines), in_specs=[vmem]...  2.45 us
    ppermute x1, waiting for transfers between devices, body(): lax.ppermute(stacked([xface[-1], yrim[-1:]]), ('gx', 'gz'), diagonal('gx'...  2.1 us
    ppermute x1, starting transfers between devices, added_beside_faces(): one = lax.ppermute(jnp.where(even, high, low), axis, first_pairs(axis))  2.06 us
  transfers between devices with their start and end apart: 13, of which 8 were waited for; matrix products, arithmetic and copies ran while one was open for 0% of the time, Pallas kernels for 9%

profile of v8, /device:TPU:0, one launch (start us, length us, event | category | flops | bytes accessed | tf_op | source)
XLA Modules:
  0.0 45.0 jit_solution(17299534790677159152)
XLA Ops:
  0.0 0.0 copy-start
  0.0 1.6 %copy-done = bf16[64,8,16,128]{3,2,1,0:T(8,128)(2,1)S(1)} copy-done((bf16[64,8,16,128]{3,2,1,0:T(8,128)(2,1)S(1)}, bf16[64,8,16,128]{3,2,1,0:T(8,128)(2,1)}, u32[]{:S(2)}) %copy-start) | copy-done | bytes 2097176
  1.6 0.0 copy-start.3
  1.6 0.0 copy-start.4
  1.6 0.6 %faces.1 = (bf16[512,256]{1,0:T(8,128)(2,1)S(1)}, bf16[512,128]{1,0:T(8,128)(2,1)S(1)}, bf16[8,128]{1,0:T(8,128)(2,1)S(1)}, f32[16,128]{1,0:T(8,128)S(1)}) custom-call(bf16[64,8,16,128]{3,2,1,0:T(8,128)(2,1)S(1)} %copy-done), custom_call_target="tpu_custom_call" | custom-call | tf_op jit(solution)/shard_map/faces/pallas_call | solution.py:125
  2.2 0.5 %collective-permute-start.1 = (bf16[512,128]{1,0:T(8,128)(2,1)S(1)}, bf16[512,128]{1,0:T(8,128)(2,1)S(1)}, u32[]{:S(2)}, u32[]{:S(2)}) collective-permute-start(bf16[512,128]{1,0:T(8,128)(2,1)S(1)} %get-tuple-element.29), channel_id=1, source_target_pairs={{0,4},{4,8},{8,12},{12,0},{1,5},{5,9},{9,13},{13,1},{2,6},{6,10},{... | collective-permute-start | bytes 393224 | tf_op jit(solution)/shard_map/ppermute | solution.py:614
  2.7 2.6 %collective-permute-start = (bf16[512,256]{1,0:T(8,128)(2,1)S(1)}, bf16[512,256]{1,0:T(8,128)(2,1)S(1)}, u32[]{:S(2)}, u32[]{:S(2)}) collective-permute-start(bf16[512,256]{1,0:T(8,128)(2,1)S(1)} %get-tuple-element.26.last_ref), channel_id=1, source_target_pairs={{0,1},{1,2},{2,3},{3,0},{4,5},{5,6},{6,7},{7,4},{8,9},{9,10},{10,1... | collective-permute-start | bytes 786440 | tf_op jit(solution)/shard_map/ppermute | solution.py:613
  5.4 2.5 %collective-permute-start.2 = (bf16[64,128]{1,0:T(8,128)(2,1)S(1)}, bf16[64,128]{1,0:T(8,128)(2,1)S(1)}, u32[]{:S(2)}, u32[]{:S(2)}) collective-permute-start(bf16[64,128]{1,0:T(8,128)(2,1)S(1)} %slice.109), channel_id=1, source_target_pairs={{0,5},{1,6},{2,7},{3,4},{4,9},{5,10},{6,11},{7,8},{8,13},{9,14},{1... | collective-permute-start | bytes 49160 | tf_op jit(solution)/shard_map/ppermute | solution.py:612
  7.9 1.8 %planes.1 = (bf16[7,512,256]{2,1,0:T(8,128)(2,1)S(1)}, bf16[8,8,128]{2,1,0:T(8,128)(2,1)S(1)}) custom-call(bf16[64,8,16,128]{3,2,1,0:T(8,128)(2,1)S(1)} %copy-done, bf16[8,128]{1,0:T(8,128)(2,1)S(1)} %get-tuple-element.24.xlast_ref), custom_call_target="tpu_custom_call" | custom-call | tf_op jit(solution)/shard_map/planes/pallas_call | solution.py:139
  9.6 0.0 collective-permute-done.1.yhalo_ref
  9.7 1.6 %collective-permute-start.3 = (bf16[80,128]{1,0:T(8,128)(2,1)S(1)}, bf16[80,128]{1,0:T(8,128)(2,1)S(1)}, u32[]{:S(2)}, u32[]{:S(2)}) collective-permute-start(bf16[80,128]{1,0:T(8,128)(2,1)S(1)} %pad_add_fusion), channel_id=1, source_target_pairs={{0,16},{16,0},{1,17},{17,1},{2,18},{18,2},{3,19},{19,3},{4,20},{20... | collective-permute-start | bytes 61448 | tf_op jit(solution)/shard_map/ppermute | solution.py:616
  11.3 1.5 %collective-permute-start.4 = (bf16[16,128]{1,0:T(8,128)(2,1)S(1)}, bf16[16,128]{1,0:T(8,128)(2,1)S(1)}, u32[]{:S(2)}, u32[]{:S(2)}) collective-permute-start(bf16[16,128]{1,0:T(8,128)(2,1)S(1)} %pad_add_fusion.1), channel_id=1, source_target_pairs={{0,17},{1,18},{2,19},{3,16},{16,1},{17,2},{18,3},{19,0},{4,21},{5,... | collective-permute-start | bytes 12296 | tf_op jit(solution)/shard_map/ppermute | solution.py:617
  12.8 0.0 copy-done.3
  12.8 0.0 copy-done.4
  12.8 2.4 %interior.1 = (f32[4,512,128]{2,1,0:T(8,128)S(1)}, f32[272,128]{1,0:T(8,128)S(1)}, bf16[256,512]{1,0:T(8,128)(2,1)S(1)}, bf16[384,256]{1,0:T(8,128)(2,1)S(1)}, b...) custom-call(bf16[7,512,256]{2,1,0:T(8,128)(2,1)S(1)} %get-tuple-element.25.cells_ref, ...), custom_call_target="tpu_custom_call" | custom-call | flops 1610612736 | bytes 6291456 | tf_op jit(solution)/shard_map/interior/pallas_call | solution.py:234
  15.3 0.2 collective-permute-done.2.yzhalo_ref
  15.5 2.1 %collective-permute-done.4.xzhalo_ref = bf16[16,128]{1,0:T(8,128)(2,1)S(1)} collective-permute-done((bf16[16,128]{1,0:T(8,128)(2,1)S(1)}, bf16[16,128]{1,0:T(8,128)(2,1)S(1)}, u32[]{:S(2)}, u32[]{:S(2)}) %collective-permute-start.4) | collective-permute-done | bytes 4128 | tf_op jit(solution)/shard_map/ppermute | solution.py:617
  17.6 0.0 collective-permute-done.3.xhalo_ref
  17.6 0.0 collective-permute-done.zhalo_ref
  17.6 0.9 %finish.1 = (f32[4,512,128]{2,1,0:T(8,128)S(1)}, f32[40,128]{1,0:T(8,128)S(1)}, f32[2,32,128]{2,1,0:T(8,128)S(1)}) custom-call(f32[4,512,128]{2,1,0:T(8,128)S(1)} %get-tuple-element.27.part_ref, f32[272,128]{1,0:T(8,128)S(1)} %get-tuple-element.28.stat_ref, bf16[512,256]{1,0:T(8,128)(2,1)S(1)} %collective-permute-done.zhalo_ref, ...), custom_call_target="tpu_custom_call" | custom-call | tf_op jit(solution)/shard_map/finish/pallas_call | solution.py:339
  18.5 0.0 collective-permute-start.5
  18.6 2.1 %collective-permute-start.8 = (f32[512,128]{1,0:T(8,128)S(1)}, f32[512,128]{1,0:T(8,128)S(1)}, u32[]{:S(2)}, u32[]{:S(2)}) collective-permute-start(f32[512,128]{1,0:T(8,128)S(1)} %get-tuple-element.43), channel_id=1, source_target_pairs={{0,1},{1,0},{2,3},{3,2},{4,5},{5,4},{6,7},{7,6},{8,9},{9,8},{10,11... | collective-permute-start | bytes 786440 | tf_op jit(solution)/shard_map/ppermute | solution.py:570
  20.7 1.9 %collective-permute-done.5 = f32[40,128]{1,0:T(8,128)S(1)} collective-permute-done((f32[40,128]{1,0:T(8,128)S(1)}, f32[40,128]{1,0:T(8,128)S(1)}, u32[]{:S(2)}, u32[]{:S(2)}) %collective-permute-start.5) | collective-permute-done | bytes 20512 | tf_op jit(solution)/shard_map/ppermute | solution.py:569
  22.6 0.0 collective-permute-start.7
  22.6 0.5 %collective-permute-start.6 = (f32[40,128]{1,0:T(8,128)S(1)}, f32[40,128]{1,0:T(8,128)S(1)}, u32[]{:S(2)}, u32[]{:S(2)}) collective-permute-start(f32[40,128]{1,0:T(8,128)S(1)} %add.75), channel_id=1, source_target_pairs={{0,3},{1,2},{2,1},{3,0},{4,7},{5,6},{6,5},{7,4},{8,11},{9,10},{10,... | collective-permute-start | bytes 61448 | tf_op jit(solution)/shard_map/ppermute | solution.py:541
  23.1 0.0 copy-start.1
  23.1 0.0 copy-start.2
  23.1 5.2 %collective-permute-done.6 = f32[40,128]{1,0:T(8,128)S(1)} collective-permute-done((f32[40,128]{1,0:T(8,128)S(1)}, f32[40,128]{1,0:T(8,128)S(1)}, u32[]{:S(2)}, u32[]{:S(2)}) %collective-permute-start.6) | collective-permute-done | bytes 20512 | tf_op jit(solution)/shard_map/ppermute | solution.py:541
  28.3 0.0 collective-permute-done.8.z1_ref
  28.3 0.0 collective-permute-done.7.z2_ref
  28.5 0.1 collective-permute-start.9
  28.5 0.6 %collective-permute-start.11 = (f32[384,128]{1,0:T(8,128)S(1)}, f32[384,128]{1,0:T(8,128)S(1)}, u32[]{:S(2)}, u32[]{:S(2)}) collective-permute-start(f32[384,128]{1,0:T(8,128)S(1)} %get-tuple-element.57), channel_id=1, source_target_pairs={{4,8},{8,4},{20,24},{24,20},{0,16},{12,28},{16,0},{28,12},{5,9},{9... | collective-permute-start | bytes 589832 | tf_op jit(solution)/shard_map/ppermute | solution.py:520
  29.1 0.8 %collective-permute-done.9 = f32[424,128]{1,0:T(8,128)S(1)} collective-permute-done((f32[424,128]{1,0:T(8,128)S(1)}, f32[424,128]{1,0:T(8,128)S(1)}, u32[]{:S(2)}, u32[]{:S(2)}) %collective-permute-start.9) | collective-permute-done | bytes 217120 | tf_op jit(solution)/shard_map/ppermute | solution.py:556
  30.0 0.2 collective-permute-start.10
  30.3 3.1 %collective-permute-done.10 = f32[40,128]{1,0:T(8,128)S(1)} collective-permute-done((f32[40,128]{1,0:T(8,128)S(1)}, f32[40,128]{1,0:T(8,128)S(1)}, u32[]{:S(2)}, u32[]{:S(2)}) %collective-permute-start.10) | collective-permute-done | bytes 20512 | tf_op jit(solution)/shard_map/ppermute | solution.py:541
  33.4 0.9 %collective-permute-done.11.y2_ref = f32[384,128]{1,0:T(8,128)S(1)} collective-permute-done((f32[384,128]{1,0:T(8,128)S(1)}, f32[384,128]{1,0:T(8,128)S(1)}, u32[]{:S(2)}, u32[]{:S(2)}) %collective-permute-start.11) | collective-permute-done | bytes 196640 | tf_op jit(solution)/shard_map/ppermute | solution.py:520
  34.4 0.6 %collective-permute-start.12 = (f32[104,128]{1,0:T(8,128)S(1)}, f32[104,128]{1,0:T(8,128)S(1)}, u32[]{:S(2)}, u32[]{:S(2)}) collective-permute-start(f32[104,128]{1,0:T(8,128)S(1)} %pad_maximum_fusion.1), channel_id=1, source_target_pairs={{0,16},{16,0},{1,17},{17,1},{2,18},{18,2},{3,19},{19,3},{4,20},{20... | collective-permute-start | bytes 159752 | tf_op jit(solution)/shard_map/ppermute | solution.py:556
  35.0 3.6 %collective-permute-done.12 = f32[104,128]{1,0:T(8,128)S(1)} collective-permute-done((f32[104,128]{1,0:T(8,128)S(1)}, f32[104,128]{1,0:T(8,128)S(1)}, u32[]{:S(2)}, u32[]{:S(2)}) %collective-permute-start.12) | collective-permute-done | bytes 53280 | tf_op jit(solution)/shard_map/ppermute | solution.py:556
  38.6 0.0 copy-done.1
  38.6 0.0 copy-done.2
  38.6 6.4 %block.1 = bf16[4,512,128]{2,1,0:T(8,128)(2,1)} custom-call(f32[40,128]{1,0:T(8,128)S(1)} %slice_add_fusion.mom_ref, f32[1,128]{1,0:T(1,128)S(1)} %bitcast.74, f32[1,128]{1,0:T(1,128)S(1)} %bitcast.75, f32[4,512,128]{2,1,0:T(8,128)S(1)} %get-tuple-element.36.feat_ref, f32[512,128]{1,0:T(8,128)S(1)} %collective-permute-done.8.z1_ref, ...), custom_call_target="tpu_custom_call" | custom-call | tf_op jit(solution)/shard_map/block/pallas_call | solution.py:480
  (34 shorter events, 0.3 us)
Async XLA Ops:
  0.0 1.6 %copy-start = (bf16[64,8,16,128]{3,2,1,0:T(8,128)(2,1)S(1)}, bf16[64,8,16,128]{3,2,1,0:T(8,128)(2,1)}, u32[]{:S(2)}) copy-start(bf16[64,8,16,128]{3,2,1,0:T(8,128)(2,1)} %field_ref.3) | copy-start | bytes 6291460
  1.6 11.2 %copy-start.3 = (bf16[3,3,3,128,128]{4,3,2,1,0:T(8,128)(2,1)S(1)}, bf16[3,3,3,128,128]{4,3,2,1,0:T(8,128)(2,1)}, u32[]{:S(2)}) copy-start(bf16[3,3,3,128,128]{4,3,2,1,0:T(8,128)(2,1)} %param.9) | copy-start | bytes 2654212
  1.6 11.2 %copy-start.4 = (bf16[3,3,3,64,128]{4,3,2,1,0:T(8,128)(2,1)S(1)}, bf16[3,3,3,64,128]{4,3,2,1,0:T(8,128)(2,1)}, u32[]{:S(2)}) copy-start(bf16[3,3,3,64,128]{4,3,2,1,0:T(8,128)(2,1)} %w_ref.1) | copy-start | bytes 1327108
  2.2 7.4 %collective-permute-start.1 = (bf16[512,128]{1,0:T(8,128)(2,1)S(1)}, bf16[512,128]{1,0:T(8,128)(2,1)S(1)}, u32[]{:S(2)}, u32[]{:S(2)}) collective-permute-start(bf16[512,128]{1,0:T(8,128)(2,1)S(1)} %get-tuple-element.29), channel_id=1, source_target_pairs={{0,4},{4,8},{8,12},{12,0},{1,5},{5,9},{9,13},{13,1},{2,6},{6,10},{... | collective-permute-start | bytes 393224 | tf_op jit(solution)/shard_map/ppermute | solution.py:614
  2.7 14.8 %collective-permute-start = (bf16[512,256]{1,0:T(8,128)(2,1)S(1)}, bf16[512,256]{1,0:T(8,128)(2,1)S(1)}, u32[]{:S(2)}, u32[]{:S(2)}) collective-permute-start(bf16[512,256]{1,0:T(8,128)(2,1)S(1)} %get-tuple-element.26.last_ref), channel_id=1, source_target_pairs={{0,1},{1,2},{2,3},{3,0},{4,5},{5,6},{6,7},{7,4},{8,9},{9,10},{10,1... | collective-permute-start | bytes 786440 | tf_op jit(solution)/shard_map/ppermute | solution.py:613
  5.4 10.1 %collective-permute-start.2 = (bf16[64,128]{1,0:T(8,128)(2,1)S(1)}, bf16[64,128]{1,0:T(8,128)(2,1)S(1)}, u32[]{:S(2)}, u32[]{:S(2)}) collective-permute-start(bf16[64,128]{1,0:T(8,128)(2,1)S(1)} %slice.109), channel_id=1, source_target_pairs={{0,5},{1,6},{2,7},{3,4},{4,9},{5,10},{6,11},{7,8},{8,13},{9,14},{1... | collective-permute-start | bytes 49160 | tf_op jit(solution)/shard_map/ppermute | solution.py:612
  9.7 7.9 %collective-permute-start.3 = (bf16[80,128]{1,0:T(8,128)(2,1)S(1)}, bf16[80,128]{1,0:T(8,128)(2,1)S(1)}, u32[]{:S(2)}, u32[]{:S(2)}) collective-permute-start(bf16[80,128]{1,0:T(8,128)(2,1)S(1)} %pad_add_fusion), channel_id=1, source_target_pairs={{0,16},{16,0},{1,17},{17,1},{2,18},{18,2},{3,19},{19,3},{4,20},{20... | collective-permute-start | bytes 61448 | tf_op jit(solution)/shard_map/ppermute | solution.py:616
  11.3 6.3 %collective-permute-start.4 = (bf16[16,128]{1,0:T(8,128)(2,1)S(1)}, bf16[16,128]{1,0:T(8,128)(2,1)S(1)}, u32[]{:S(2)}, u32[]{:S(2)}) collective-permute-start(bf16[16,128]{1,0:T(8,128)(2,1)S(1)} %pad_add_fusion.1), channel_id=1, source_target_pairs={{0,17},{1,18},{2,19},{3,16},{16,1},{17,2},{18,3},{19,0},{4,21},{5,... | collective-permute-start | bytes 12296 | tf_op jit(solution)/shard_map/ppermute | solution.py:617
  18.5 4.1 %collective-permute-start.5 = (f32[40,128]{1,0:T(8,128)S(1)}, f32[40,128]{1,0:T(8,128)S(1)}, u32[]{:S(2)}, u32[]{:S(2)}) collective-permute-start(f32[40,128]{1,0:T(8,128)S(1)} %get-tuple-element.34), channel_id=1, source_target_pairs={{0,1},{1,0},{2,3},{3,2},{4,5},{5,4},{6,7},{7,6},{8,9},{9,8},{10,11... | collective-permute-start | bytes 61448 | tf_op jit(solution)/shard_map/ppermute | solution.py:569
  18.6 9.7 %collective-permute-start.8 = (f32[512,128]{1,0:T(8,128)S(1)}, f32[512,128]{1,0:T(8,128)S(1)}, u32[]{:S(2)}, u32[]{:S(2)}) collective-permute-start(f32[512,128]{1,0:T(8,128)S(1)} %get-tuple-element.43), channel_id=1, source_target_pairs={{0,1},{1,0},{2,3},{3,2},{4,5},{5,4},{6,7},{7,6},{8,9},{9,8},{10,11... | collective-permute-start | bytes 786440 | tf_op jit(solution)/shard_map/ppermute | solution.py:570
  22.6 5.7 %collective-permute-start.7 = (f32[512,128]{1,0:T(8,128)S(1)}, f32[512,128]{1,0:T(8,128)S(1)}, u32[]{:S(2)}, u32[]{:S(2)}) collective-permute-start(f32[512,128]{1,0:T(8,128)S(1)} %get-tuple-element.38), channel_id=1, source_target_pairs={{1,2},{2,1},{5,6},{6,5},{9,10},{10,9},{13,14},{14,13},{0,4},{3,7},... | collective-permute-start | bytes 786440 | tf_op jit(solution)/shard_map/ppermute | solution.py:520
  22.6 5.7 %collective-permute-start.6 = (f32[40,128]{1,0:T(8,128)S(1)}, f32[40,128]{1,0:T(8,128)S(1)}, u32[]{:S(2)}, u32[]{:S(2)}) collective-permute-start(f32[40,128]{1,0:T(8,128)S(1)} %add.75), channel_id=1, source_target_pairs={{0,3},{1,2},{2,1},{3,0},{4,7},{5,6},{6,5},{7,4},{8,11},{9,10},{10,... | collective-permute-start | bytes 61448 | tf_op jit(solution)/shard_map/ppermute | solution.py:541
  23.1 15.5 %copy-start.1 = (f32[128]{0:T(128)S(1)}, f32[128]{0:T(128)}, u32[]{:S(2)}) copy-start(f32[128]{0:T(128)} %param.7) | copy-start | bytes 1540
  23.1 15.5 %copy-start.2 = (f32[128]{0:T(128)S(1)}, f32[128]{0:T(128)}, u32[]{:S(2)}) copy-start(f32[128]{0:T(128)} %param.8) | copy-start | bytes 1540
  28.5 1.5 %collective-permute-start.9 = (f32[424,128]{1,0:T(8,128)S(1)}, f32[424,128]{1,0:T(8,128)S(1)}, u32[]{:S(2)}, u32[]{:S(2)}) collective-permute-start(f32[424,128]{1,0:T(8,128)S(1)} %pad_maximum_fusion), channel_id=1, source_target_pairs={{0,4},{4,0},{8,12},{12,8},{1,5},{5,1},{9,13},{13,9},{2,6},{6,2},{1... | collective-permute-start | bytes 651272 | tf_op jit(solution)/shard_map/ppermute | solution.py:556
  28.5 5.7 %collective-permute-start.11 = (f32[384,128]{1,0:T(8,128)S(1)}, f32[384,128]{1,0:T(8,128)S(1)}, u32[]{:S(2)}, u32[]{:S(2)}) collective-permute-start(f32[384,128]{1,0:T(8,128)S(1)} %get-tuple-element.57), channel_id=1, source_target_pairs={{4,8},{8,4},{20,24},{24,20},{0,16},{12,28},{16,0},{28,12},{5,9},{9... | collective-permute-start | bytes 589832 | tf_op jit(solution)/shard_map/ppermute | solution.py:520
  30.0 3.4 %collective-permute-start.10 = (f32[40,128]{1,0:T(8,128)S(1)}, f32[40,128]{1,0:T(8,128)S(1)}, u32[]{:S(2)}, u32[]{:S(2)}) collective-permute-start(f32[40,128]{1,0:T(8,128)S(1)} %slice_add_fusion.1), channel_id=1, source_target_pairs={{0,12},{4,8},{8,4},{12,0},{1,13},{5,9},{9,5},{13,1},{2,14},{6,10},... | collective-permute-start | bytes 61448 | tf_op jit(solution)/shard_map/ppermute | solution.py:541
  34.4 4.2 %collective-permute-start.12 = (f32[104,128]{1,0:T(8,128)S(1)}, f32[104,128]{1,0:T(8,128)S(1)}, u32[]{:S(2)}, u32[]{:S(2)}) collective-permute-start(f32[104,128]{1,0:T(8,128)S(1)} %pad_maximum_fusion.1), channel_id=1, source_target_pairs={{0,16},{16,0},{1,17},{17,1},{2,18},{18,2},{3,19},{19,3},{4,20},{20... | collective-permute-start | bytes 159752 | tf_op jit(solution)/shard_map/ppermute | solution.py:556

commit v9 on v8

--- a/solution.py
+++ b/solution.py
@@ -566,11 +566,10 @@
     size = lax.axis_size(axis)
     if size < 4 or not power_of_two(size):
         return added(axis, value), faces(axis, even, low, high)
-    value = value + lax.ppermute(value, axis, first_pairs(axis))
     one = lax.ppermute(jnp.where(even, high, low), axis, first_pairs(axis))
-    value, other = lax.optimization_barrier((value, jnp.where(even, low, high)))
-    two = second_face(axis, other)
-    return added(axis, value, first=False), (one, two)
+    two = second_face(axis, jnp.where(even, low, high))
+    value, one, two = lax.optimization_barrier((added(axis, value), one, two))
+    return value, (one, two)
 
 
 def sided(even, pair):

time: 45.1 us -> 45 us (level)
  no operation moved by 1% of the time
where the time goes in v9:
time: 45 us; the launch traced here: 44.9 us
  waiting for transfers between devices  17.8 us (40%)
  starting transfers between devices  12.7 us (28%)
  Pallas kernels  12.1 us (27%)
  local copies, waits for them, and re-layouts  1.72 us (4%)
    ppermute x2, waiting for transfers between devices, added(): value = value + lax.ppermute(value, axis, second_pairs(axis))  8.32 us
    pallas_call x1, Pallas kernels, block(): pl.pallas_call(functools.partial(block_kernel, total_cells), in_specs=[vm...  6.36 us
    ppermute x2, waiting for transfers between devices, added_with_faces(): both = lax.ppermute(both, axis, first_pairs(axis))  4.44 us
    ppermute x1, starting transfers between devices, body(): zhalo = lax.ppermute(last, 'gz', ring('gz'))  2.64 us
    ppermute x1, starting transfers between devices, body(): yzhalo = lax.ppermute(yface[-half:], ('gy', 'gz'), diagonal('gy', 'gz'))  2.47 us
    pallas_call x1, Pallas kernels, interior(): pl.pallas_call(functools.partial(interior_kernel, lines), in_specs=[vmem]...  2.45 us
    ppermute x1, waiting for transfers between devices, body(): lax.ppermute(stacked([xface[-1], yrim[-1:]]), ('gx', 'gz'), diagonal('gx'...  2.1 us
    ppermute x1, starting transfers between devices, added_beside_faces(): one = lax.ppermute(jnp.where(even, high, low), axis, first_pairs(axis))  2.06 us
  transfers between devices with their start and end apart: 13, of which 8 were waited for; matrix products, arithmetic and copies ran while one was open for 0% of the time, Pallas kernels for 9%

profile of v9, /device:TPU:0, one launch (start us, length us, event | category | flops | bytes accessed | tf_op | source)
XLA Modules:
  0.0 44.9 jit_solution(16486148360061113960)
XLA Ops:
  0.0 0.0 copy-start
  0.0 1.6 %copy-done = bf16[64,8,16,128]{3,2,1,0:T(8,128)(2,1)S(1)} copy-done((bf16[64,8,16,128]{3,2,1,0:T(8,128)(2,1)S(1)}, bf16[64,8,16,128]{3,2,1,0:T(8,128)(2,1)}, u32[]{:S(2)}) %copy-start) | copy-done | bytes 2097176
  1.6 0.0 copy-start.3
  1.6 0.0 copy-start.4
  1.6 0.6 %faces.1 = (bf16[512,256]{1,0:T(8,128)(2,1)S(1)}, bf16[512,128]{1,0:T(8,128)(2,1)S(1)}, bf16[8,128]{1,0:T(8,128)(2,1)S(1)}, f32[16,128]{1,0:T(8,128)S(1)}) custom-call(bf16[64,8,16,128]{3,2,1,0:T(8,128)(2,1)S(1)} %copy-done), custom_call_target="tpu_custom_call" | custom-call | tf_op jit(solution)/shard_map/faces/pallas_call | solution.py:125
  2.2 0.5 %collective-permute-start.1 = (bf16[512,128]{1,0:T(8,128)(2,1)S(1)}, bf16[512,128]{1,0:T(8,128)(2,1)S(1)}, u32[]{:S(2)}, u32[]{:S(2)}) collective-permute-start(bf16[512,128]{1,0:T(8,128)(2,1)S(1)} %get-tuple-element.30), channel_id=1, source_target_pairs={{0,4},{4,8},{8,12},{12,0},{1,5},{5,9},{9,13},{13,1},{2,6},{6,10},{... | collective-permute-start | bytes 393224 | tf_op jit(solution)/shard_map/ppermute | solution.py:613
  2.7 2.6 %collective-permute-start = (bf16[512,256]{1,0:T(8,128)(2,1)S(1)}, bf16[512,256]{1,0:T(8,128)(2,1)S(1)}, u32[]{:S(2)}, u32[]{:S(2)}) collective-permute-start(bf16[512,256]{1,0:T(8,128)(2,1)S(1)} %get-tuple-element.27.last_ref), channel_id=1, source_target_pairs={{0,1},{1,2},{2,3},{3,0},{4,5},{5,6},{6,7},{7,4},{8,9},{9,10},{10,1... | collective-permute-start | bytes 786440 | tf_op jit(solution)/shard_map/ppermute | solution.py:612
  5.4 2.5 %collective-permute-start.2 = (bf16[64,128]{1,0:T(8,128)(2,1)S(1)}, bf16[64,128]{1,0:T(8,128)(2,1)S(1)}, u32[]{:S(2)}, u32[]{:S(2)}) collective-permute-start(bf16[64,128]{1,0:T(8,128)(2,1)S(1)} %slice.109), channel_id=1, source_target_pairs={{0,5},{1,6},{2,7},{3,4},{4,9},{5,10},{6,11},{7,8},{8,13},{9,14},{1... | collective-permute-start | bytes 49160 | tf_op jit(solution)/shard_map/ppermute | solution.py:611
  7.9 1.8 %planes.1 = (bf16[7,512,256]{2,1,0:T(8,128)(2,1)S(1)}, bf16[8,8,128]{2,1,0:T(8,128)(2,1)S(1)}) custom-call(bf16[64,8,16,128]{3,2,1,0:T(8,128)(2,1)S(1)} %copy-done, bf16[8,128]{1,0:T(8,128)(2,1)S(1)} %get-tuple-element.25.xlast_ref), custom_call_target="tpu_custom_call" | custom-call | tf_op jit(solution)/shard_map/planes/pallas_call | solution.py:139
  9.6 0.0 collective-permute-done.1.yhalo_ref
  9.7 1.6 %collective-permute-start.3 = (bf16[80,128]{1,0:T(8,128)(2,1)S(1)}, bf16[80,128]{1,0:T(8,128)(2,1)S(1)}, u32[]{:S(2)}, u32[]{:S(2)}) collective-permute-start(bf16[80,128]{1,0:T(8,128)(2,1)S(1)} %pad_add_fusion), channel_id=1, source_target_pairs={{0,16},{16,0},{1,17},{17,1},{2,18},{18,2},{3,19},{19,3},{4,20},{20... | collective-permute-start | bytes 61448 | tf_op jit(solution)/shard_map/ppermute | solution.py:615
  11.3 1.5 %collective-permute-start.4 = (bf16[16,128]{1,0:T(8,128)(2,1)S(1)}, bf16[16,128]{1,0:T(8,128)(2,1)S(1)}, u32[]{:S(2)}, u32[]{:S(2)}) collective-permute-start(bf16[16,128]{1,0:T(8,128)(2,1)S(1)} %pad_add_fusion.1), channel_id=1, source_target_pairs={{0,17},{1,18},{2,19},{3,16},{16,1},{17,2},{18,3},{19,0},{4,21},{5,... | collective-permute-start | bytes 12296 | tf_op jit(solution)/shard_map/ppermute | solution.py:616
  12.8 0.0 copy-done.3
  12.8 0.0 copy-done.4
  12.8 2.4 %interior.1 = (f32[4,512,128]{2,1,0:T(8,128)S(1)}, f32[272,128]{1,0:T(8,128)S(1)}, bf16[256,512]{1,0:T(8,128)(2,1)S(1)}, bf16[384,256]{1,0:T(8,128)(2,1)S(1)}, b...) custom-call(bf16[7,512,256]{2,1,0:T(8,128)(2,1)S(1)} %get-tuple-element.26.cells_ref, ...), custom_call_target="tpu_custom_call" | custom-call | flops 1610612736 | bytes 6291456 | tf_op jit(solution)/shard_map/interior/pallas_call | solution.py:234
  15.3 0.2 collective-permute-done.2.yzhalo_ref
  15.5 2.1 %collective-permute-done.4.xzhalo_ref = bf16[16,128]{1,0:T(8,128)(2,1)S(1)} collective-permute-done((bf16[16,128]{1,0:T(8,128)(2,1)S(1)}, bf16[16,128]{1,0:T(8,128)(2,1)S(1)}, u32[]{:S(2)}, u32[]{:S(2)}) %collective-permute-start.4) | collective-permute-done | bytes 4128 | tf_op jit(solution)/shard_map/ppermute | solution.py:616
  17.6 0.0 collective-permute-done.3.xhalo_ref
  17.6 0.0 collective-permute-done.zhalo_ref
  17.6 0.9 %finish.1 = (f32[4,512,128]{2,1,0:T(8,128)S(1)}, f32[40,128]{1,0:T(8,128)S(1)}, f32[2,32,128]{2,1,0:T(8,128)S(1)}) custom-call(f32[4,512,128]{2,1,0:T(8,128)S(1)} %get-tuple-element.28.part_ref, f32[272,128]{1,0:T(8,128)S(1)} %get-tuple-element.29.stat_ref, bf16[512,256]{1,0:T(8,128)(2,1)S(1)} %collective-permute-done.zhalo_ref, ...), custom_call_target="tpu_custom_call" | custom-call | tf_op jit(solution)/shard_map/finish/pallas_call | solution.py:339
  18.5 0.0 collective-permute-start.5
  18.6 2.1 %collective-permute-start.7 = (f32[512,128]{1,0:T(8,128)S(1)}, f32[512,128]{1,0:T(8,128)S(1)}, u32[]{:S(2)}, u32[]{:S(2)}) collective-permute-start(f32[512,128]{1,0:T(8,128)S(1)} %get-tuple-element.46), channel_id=1, source_target_pairs={{0,1},{1,0},{2,3},{3,2},{4,5},{5,4},{6,7},{7,6},{8,9},{9,8},{10,11... | collective-permute-start | bytes 786440 | tf_op jit(solution)/shard_map/ppermute | solution.py:569
  20.7 0.0 collective-permute-start.8
  20.7 1.9 %collective-permute-done.5 = f32[40,128]{1,0:T(8,128)S(1)} collective-permute-done((f32[40,128]{1,0:T(8,128)S(1)}, f32[40,128]{1,0:T(8,128)S(1)}, u32[]{:S(2)}, u32[]{:S(2)}) %collective-permute-start.5) | collective-permute-done | bytes 20512 | tf_op jit(solution)/shard_map/ppermute | solution.py:539
  22.6 0.4 collective-permute-start.6
  23.0 0.0 copy-start.1
  23.0 0.0 copy-start.2
  23.0 5.2 %collective-permute-done.6 = f32[40,128]{1,0:T(8,128)S(1)} collective-permute-done((f32[40,128]{1,0:T(8,128)S(1)}, f32[40,128]{1,0:T(8,128)S(1)}, u32[]{:S(2)}, u32[]{:S(2)}) %collective-permute-start.6) | collective-permute-done | bytes 20512 | tf_op jit(solution)/shard_map/ppermute | solution.py:541
  28.2 0.0 collective-permute-done.7.z1_ref
  28.2 0.0 collective-permute-done.8.z2_ref
  28.3 0.1 collective-permute-start.9
  28.4 0.6 %collective-permute-start.11 = (f32[384,128]{1,0:T(8,128)S(1)}, f32[384,128]{1,0:T(8,128)S(1)}, u32[]{:S(2)}, u32[]{:S(2)}) collective-permute-start(f32[384,128]{1,0:T(8,128)S(1)} %get-tuple-element.59), channel_id=1, source_target_pairs={{4,8},{8,4},{20,24},{24,20},{0,16},{12,28},{16,0},{28,12},{5,9},{9... | collective-permute-start | bytes 589832 | tf_op jit(solution)/shard_map/ppermute | solution.py:520
  29.0 0.8 %collective-permute-done.9 = f32[424,128]{1,0:T(8,128)S(1)} collective-permute-done((f32[424,128]{1,0:T(8,128)S(1)}, f32[424,128]{1,0:T(8,128)S(1)}, u32[]{:S(2)}, u32[]{:S(2)}) %collective-permute-start.9) | collective-permute-done | bytes 217120 | tf_op jit(solution)/shard_map/ppermute | solution.py:556
  29.9 0.2 collective-permute-start.10
  30.1 3.1 %collective-permute-done.10 = f32[40,128]{1,0:T(8,128)S(1)} collective-permute-done((f32[40,128]{1,0:T(8,128)S(1)}, f32[40,128]{1,0:T(8,128)S(1)}, u32[]{:S(2)}, u32[]{:S(2)}) %collective-permute-start.10) | collective-permute-done | bytes 20512 | tf_op jit(solution)/shard_map/ppermute | solution.py:541
  33.3 0.9 %collective-permute-done.11.y2_ref = f32[384,128]{1,0:T(8,128)S(1)} collective-permute-done((f32[384,128]{1,0:T(8,128)S(1)}, f32[384,128]{1,0:T(8,128)S(1)}, u32[]{:S(2)}, u32[]{:S(2)}) %collective-permute-start.11) | collective-permute-done | bytes 196640 | tf_op jit(solution)/shard_map/ppermute | solution.py:520
  34.3 0.6 %collective-permute-start.12 = (f32[104,128]{1,0:T(8,128)S(1)}, f32[104,128]{1,0:T(8,128)S(1)}, u32[]{:S(2)}, u32[]{:S(2)}) collective-permute-start(f32[104,128]{1,0:T(8,128)S(1)} %pad_maximum_fusion.1), channel_id=1, source_target_pairs={{0,16},{16,0},{1,17},{17,1},{2,18},{18,2},{3,19},{19,3},{4,20},{20... | collective-permute-start | bytes 159752 | tf_op jit(solution)/shard_map/ppermute | solution.py:556
  34.9 3.6 %collective-permute-done.12 = f32[104,128]{1,0:T(8,128)S(1)} collective-permute-done((f32[104,128]{1,0:T(8,128)S(1)}, f32[104,128]{1,0:T(8,128)S(1)}, u32[]{:S(2)}, u32[]{:S(2)}) %collective-permute-start.12) | collective-permute-done | bytes 53280 | tf_op jit(solution)/shard_map/ppermute | solution.py:556
  38.5 0.0 copy-done.1
  38.5 0.0 copy-done.2
  38.5 6.4 %block.1 = bf16[4,512,128]{2,1,0:T(8,128)(2,1)} custom-call(f32[40,128]{1,0:T(8,128)S(1)} %slice_add_fusion.mom_ref, f32[1,128]{1,0:T(1,128)S(1)} %bitcast.74, f32[1,128]{1,0:T(1,128)S(1)} %bitcast.75, f32[4,512,128]{2,1,0:T(8,128)S(1)} %get-tuple-element.37.feat_ref, f32[512,128]{1,0:T(8,128)S(1)} %collective-permute-done.7.z1_ref, ...), custom_call_target="tpu_custom_call" | custom-call | tf_op jit(solution)/shard_map/block/pallas_call | solution.py:480
  (34 shorter events, 0.3 us)
Async XLA Ops:
  0.0 1.6 %copy-start = (bf16[64,8,16,128]{3,2,1,0:T(8,128)(2,1)S(1)}, bf16[64,8,16,128]{3,2,1,0:T(8,128)(2,1)}, u32[]{:S(2)}) copy-start(bf16[64,8,16,128]{3,2,1,0:T(8,128)(2,1)} %field_ref.3) | copy-start | bytes 6291460
  1.6 11.2 %copy-start.3 = (bf16[3,3,3,128,128]{4,3,2,1,0:T(8,128)(2,1)S(1)}, bf16[3,3,3,128,128]{4,3,2,1,0:T(8,128)(2,1)}, u32[]{:S(2)}) copy-start(bf16[3,3,3,128,128]{4,3,2,1,0:T(8,128)(2,1)} %param.9) | copy-start | bytes 2654212
  1.6 11.2 %copy-start.4 = (bf16[3,3,3,64,128]{4,3,2,1,0:T(8,128)(2,1)S(1)}, bf16[3,3,3,64,128]{4,3,2,1,0:T(8,128)(2,1)}, u32[]{:S(2)}) copy-start(bf16[3,3,3,64,128]{4,3,2,1,0:T(8,128)(2,1)} %w_ref.1) | copy-start | bytes 1327108
  2.2 7.4 %collective-permute-start.1 = (bf16[512,128]{1,0:T(8,128)(2,1)S(1)}, bf16[512,128]{1,0:T(8,128)(2,1)S(1)}, u32[]{:S(2)}, u32[]{:S(2)}) collective-permute-start(bf16[512,128]{1,0:T(8,128)(2,1)S(1)} %get-tuple-element.30), channel_id=1, source_target_pairs={{0,4},{4,8},{8,12},{12,0},{1,5},{5,9},{9,13},{13,1},{2,6},{6,10},{... | collective-permute-start | bytes 393224 | tf_op jit(solution)/shard_map/ppermute | solution.py:613
  2.7 14.8 %collective-permute-start = (bf16[512,256]{1,0:T(8,128)(2,1)S(1)}, bf16[512,256]{1,0:T(8,128)(2,1)S(1)}, u32[]{:S(2)}, u32[]{:S(2)}) collective-permute-start(bf16[512,256]{1,0:T(8,128)(2,1)S(1)} %get-tuple-element.27.last_ref), channel_id=1, source_target_pairs={{0,1},{1,2},{2,3},{3,0},{4,5},{5,6},{6,7},{7,4},{8,9},{9,10},{10,1... | collective-permute-start | bytes 786440 | tf_op jit(solution)/shard_map/ppermute | solution.py:612
  5.4 10.1 %collective-permute-start.2 = (bf16[64,128]{1,0:T(8,128)(2,1)S(1)}, bf16[64,128]{1,0:T(8,128)(2,1)S(1)}, u32[]{:S(2)}, u32[]{:S(2)}) collective-permute-start(bf16[64,128]{1,0:T(8,128)(2,1)S(1)} %slice.109), channel_id=1, source_target_pairs={{0,5},{1,6},{2,7},{3,4},{4,9},{5,10},{6,11},{7,8},{8,13},{9,14},{1... | collective-permute-start | bytes 49160 | tf_op jit(solution)/shard_map/ppermute | solution.py:611
  9.7 7.9 %collective-permute-start.3 = (bf16[80,128]{1,0:T(8,128)(2,1)S(1)}, bf16[80,128]{1,0:T(8,128)(2,1)S(1)}, u32[]{:S(2)}, u32[]{:S(2)}) collective-permute-start(bf16[80,128]{1,0:T(8,128)(2,1)S(1)} %pad_add_fusion), channel_id=1, source_target_pairs={{0,16},{16,0},{1,17},{17,1},{2,18},{18,2},{3,19},{19,3},{4,20},{20... | collective-permute-start | bytes 61448 | tf_op jit(solution)/shard_map/ppermute | solution.py:615
  11.3 6.3 %collective-permute-start.4 = (bf16[16,128]{1,0:T(8,128)(2,1)S(1)}, bf16[16,128]{1,0:T(8,128)(2,1)S(1)}, u32[]{:S(2)}, u32[]{:S(2)}) collective-permute-start(bf16[16,128]{1,0:T(8,128)(2,1)S(1)} %pad_add_fusion.1), channel_id=1, source_target_pairs={{0,17},{1,18},{2,19},{3,16},{16,1},{17,2},{18,3},{19,0},{4,21},{5,... | collective-permute-start | bytes 12296 | tf_op jit(solution)/shard_map/ppermute | solution.py:616
  18.5 4.1 %collective-permute-start.5 = (f32[40,128]{1,0:T(8,128)S(1)}, f32[40,128]{1,0:T(8,128)S(1)}, u32[]{:S(2)}, u32[]{:S(2)}) collective-permute-start(f32[40,128]{1,0:T(8,128)S(1)} %get-tuple-element.35), channel_id=1, source_target_pairs={{0,1},{1,0},{2,3},{3,2},{4,5},{5,4},{6,7},{7,6},{8,9},{9,8},{10,11... | collective-permute-start | bytes 61448 | tf_op jit(solution)/shard_map/ppermute | solution.py:539
  18.6 9.6 %collective-permute-start.7 = (f32[512,128]{1,0:T(8,128)S(1)}, f32[512,128]{1,0:T(8,128)S(1)}, u32[]{:S(2)}, u32[]{:S(2)}) collective-permute-start(f32[512,128]{1,0:T(8,128)S(1)} %get-tuple-element.46), channel_id=1, source_target_pairs={{0,1},{1,0},{2,3},{3,2},{4,5},{5,4},{6,7},{7,6},{8,9},{9,8},{10,11... | collective-permute-start | bytes 786440 | tf_op jit(solution)/shard_map/ppermute | solution.py:569
  20.7 7.5 %collective-permute-start.8 = (f32[512,128]{1,0:T(8,128)S(1)}, f32[512,128]{1,0:T(8,128)S(1)}, u32[]{:S(2)}, u32[]{:S(2)}) collective-permute-start(f32[512,128]{1,0:T(8,128)S(1)} %get-tuple-element.45), channel_id=1, source_target_pairs={{1,2},{2,1},{5,6},{6,5},{9,10},{10,9},{13,14},{14,13},{0,4},{3,7},... | collective-permute-start | bytes 786440 | tf_op jit(solution)/shard_map/ppermute | solution.py:520
  22.6 5.6 %collective-permute-start.6 = (f32[40,128]{1,0:T(8,128)S(1)}, f32[40,128]{1,0:T(8,128)S(1)}, u32[]{:S(2)}, u32[]{:S(2)}) collective-permute-start(f32[40,128]{1,0:T(8,128)S(1)} %add.75), channel_id=1, source_target_pairs={{0,3},{1,2},{2,1},{3,0},{4,7},{5,6},{6,5},{7,4},{8,11},{9,10},{10,... | collective-permute-start | bytes 61448 | tf_op jit(solution)/shard_map/ppermute | solution.py:541
  23.0 15.5 %copy-start.1 = (f32[128]{0:T(128)S(1)}, f32[128]{0:T(128)}, u32[]{:S(2)}) copy-start(f32[128]{0:T(128)} %param.7) | copy-start | bytes 1540
  23.0 15.5 %copy-start.2 = (f32[128]{0:T(128)S(1)}, f32[128]{0:T(128)}, u32[]{:S(2)}) copy-start(f32[128]{0:T(128)} %param.8) | copy-start | bytes 1540
  28.3 1.5 %collective-permute-start.9 = (f32[424,128]{1,0:T(8,128)S(1)}, f32[424,128]{1,0:T(8,128)S(1)}, u32[]{:S(2)}, u32[]{:S(2)}) collective-permute-start(f32[424,128]{1,0:T(8,128)S(1)} %pad_maximum_fusion), channel_id=1, source_target_pairs={{0,4},{4,0},{8,12},{12,8},{1,5},{5,1},{9,13},{13,9},{2,6},{6,2},{1... | collective-permute-start | bytes 651272 | tf_op jit(solution)/shard_map/ppermute | solution.py:556
  28.4 5.7 %collective-permute-start.11 = (f32[384,128]{1,0:T(8,128)S(1)}, f32[384,128]{1,0:T(8,128)S(1)}, u32[]{:S(2)}, u32[]{:S(2)}) collective-permute-start(f32[384,128]{1,0:T(8,128)S(1)} %get-tuple-element.59), channel_id=1, source_target_pairs={{4,8},{8,4},{20,24},{24,20},{0,16},{12,28},{16,0},{28,12},{5,9},{9... | collective-permute-start | bytes 589832 | tf_op jit(solution)/shard_map/ppermute | solution.py:520
  29.9 3.4 %collective-permute-start.10 = (f32[40,128]{1,0:T(8,128)S(1)}, f32[40,128]{1,0:T(8,128)S(1)}, u32[]{:S(2)}, u32[]{:S(2)}) collective-permute-start(f32[40,128]{1,0:T(8,128)S(1)} %slice_add_fusion.1), channel_id=1, source_target_pairs={{0,12},{4,8},{8,4},{12,0},{1,13},{5,9},{9,5},{13,1},{2,14},{6,10},... | collective-permute-start | bytes 61448 | tf_op jit(solution)/shard_map/ppermute | solution.py:541
  34.3 4.2 %collective-permute-start.12 = (f32[104,128]{1,0:T(8,128)S(1)}, f32[104,128]{1,0:T(8,128)S(1)}, u32[]{:S(2)}, u32[]{:S(2)}) collective-permute-start(f32[104,128]{1,0:T(8,128)S(1)} %pad_maximum_fusion.1), channel_id=1, source_target_pairs={{0,16},{16,0},{1,17},{17,1},{2,18},{18,2},{3,19},{19,3},{4,20},{20... | collective-permute-start | bytes 159752 | tf_op jit(solution)/shard_map/ppermute | solution.py:556

commit v10 on v9

--- a/solution.py
+++ b/solution.py
@@ -415,15 +415,13 @@
     mat = mat / jnp.sqrt(trace) * own(jnp.where(eye, gain_ref[...], 0.0))
     mat = jnp.concatenate([jnp.where(left, mat, 0.0), jnp.where(left, 0.0, mat)], axis=0)
     hi, lo = split(mat)
-    mixer = jnp.concatenate(
-        [jnp.concatenate([hi, hi], axis=1), jnp.concatenate([lo, jnp.zeros_like(lo)], axis=1)], axis=0
-    )
+    mixer = jnp.concatenate([hi, hi, lo], axis=1)
     shift = shift_ref[...]
 
     def whitened(n):
         start, count = starts[n]
-        both = dot(split_ref[start : start + count, :], mixer, ((1,), (1,)))
-        scaled = both[:, :cout] + both[:, cout:] + shift
+        parts = split_ref[start : start + count, :]
+        scaled = dot(jnp.concatenate([parts, parts[:, :cout]], axis=1), mixer, ((1,), (1,))) + shift
         return jnp.where(scaled >= 0, scaled, LEAK * scaled)
 
     base = 8

time: 45 us -> 45.1 us (level)
  no operation moved by 1% of the time
where the time goes in v10:
time: 45.1 us; the launch traced here: 44.9 us
  waiting for transfers between devices  17.8 us (39%)
  starting transfers between devices  12.7 us (28%)
  Pallas kernels  12.2 us (27%)
  local copies, waits for them, and re-layouts  1.72 us (4%)
    ppermute x2, waiting for transfers between devices, added(): value = value + lax.ppermute(value, axis, second_pairs(axis))  8.32 us
    pallas_call x1, Pallas kernels, block(): pl.pallas_call(functools.partial(block_kernel, total_cells), in_specs=[vm...  6.39 us
    ppermute x2, waiting for transfers between devices, added_with_faces(): both = lax.ppermute(both, axis, first_pairs(axis))  4.44 us
    ppermute x1, starting transfers between devices, body(): zhalo = lax.ppermute(last, 'gz', ring('gz'))  2.64 us
    ppermute x1, starting transfers between devices, body(): yzhalo = lax.ppermute(yface[-half:], ('gy', 'gz'), diagonal('gy', 'gz'))  2.47 us
    pallas_call x1, Pallas kernels, interior(): pl.pallas_call(functools.partial(interior_kernel, lines), in_specs=[vmem]...  2.45 us
    ppermute x1, waiting for transfers between devices, body(): lax.ppermute(stacked([xface[-1], yrim[-1:]]), ('gx', 'gz'), diagonal('gx'...  2.1 us
    ppermute x1, starting transfers between devices, added_beside_faces(): one = lax.ppermute(jnp.where(even, high, low), axis, first_pairs(axis))  2.06 us
  transfers between devices with their start and end apart: 13, of which 8 were waited for; matrix products, arithmetic and copies ran while one was open for 0% of the time, Pallas kernels for 9%

profile of v10, /device:TPU:0, one launch (start us, length us, event | category | flops | bytes accessed | tf_op | source)
XLA Modules:
  0.0 44.9 jit_solution(1017228839284778278)
XLA Ops:
  0.0 0.0 copy-start
  0.0 1.6 %copy-done = bf16[64,8,16,128]{3,2,1,0:T(8,128)(2,1)S(1)} copy-done((bf16[64,8,16,128]{3,2,1,0:T(8,128)(2,1)S(1)}, bf16[64,8,16,128]{3,2,1,0:T(8,128)(2,1)}, u32[]{:S(2)}) %copy-start) | copy-done | bytes 2097176
  1.6 0.0 copy-start.3
  1.6 0.0 copy-start.4
  1.6 0.6 %faces.1 = (bf16[512,256]{1,0:T(8,128)(2,1)S(1)}, bf16[512,128]{1,0:T(8,128)(2,1)S(1)}, bf16[8,128]{1,0:T(8,128)(2,1)S(1)}, f32[16,128]{1,0:T(8,128)S(1)}) custom-call(bf16[64,8,16,128]{3,2,1,0:T(8,128)(2,1)S(1)} %copy-done), custom_call_target="tpu_custom_call" | custom-call | tf_op jit(solution)/shard_map/faces/pallas_call | solution.py:125
  2.2 0.5 %collective-permute-start.1 = (bf16[512,128]{1,0:T(8,128)(2,1)S(1)}, bf16[512,128]{1,0:T(8,128)(2,1)S(1)}, u32[]{:S(2)}, u32[]{:S(2)}) collective-permute-start(bf16[512,128]{1,0:T(8,128)(2,1)S(1)} %get-tuple-element.30), channel_id=1, source_target_pairs={{0,4},{4,8},{8,12},{12,0},{1,5},{5,9},{9,13},{13,1},{2,6},{6,10},{... | collective-permute-start | bytes 393224 | tf_op jit(solution)/shard_map/ppermute | solution.py:611
  2.7 2.6 %collective-permute-start = (bf16[512,256]{1,0:T(8,128)(2,1)S(1)}, bf16[512,256]{1,0:T(8,128)(2,1)S(1)}, u32[]{:S(2)}, u32[]{:S(2)}) collective-permute-start(bf16[512,256]{1,0:T(8,128)(2,1)S(1)} %get-tuple-element.27.last_ref), channel_id=1, source_target_pairs={{0,1},{1,2},{2,3},{3,0},{4,5},{5,6},{6,7},{7,4},{8,9},{9,10},{10,1... | collective-permute-start | bytes 786440 | tf_op jit(solution)/shard_map/ppermute | solution.py:610
  5.4 2.5 %collective-permute-start.2 = (bf16[64,128]{1,0:T(8,128)(2,1)S(1)}, bf16[64,128]{1,0:T(8,128)(2,1)S(1)}, u32[]{:S(2)}, u32[]{:S(2)}) collective-permute-start(bf16[64,128]{1,0:T(8,128)(2,1)S(1)} %slice.109), channel_id=1, source_target_pairs={{0,5},{1,6},{2,7},{3,4},{4,9},{5,10},{6,11},{7,8},{8,13},{9,14},{1... | collective-permute-start | bytes 49160 | tf_op jit(solution)/shard_map/ppermute | solution.py:609
  7.9 1.8 %planes.1 = (bf16[7,512,256]{2,1,0:T(8,128)(2,1)S(1)}, bf16[8,8,128]{2,1,0:T(8,128)(2,1)S(1)}) custom-call(bf16[64,8,16,128]{3,2,1,0:T(8,128)(2,1)S(1)} %copy-done, bf16[8,128]{1,0:T(8,128)(2,1)S(1)} %get-tuple-element.25.xlast_ref), custom_call_target="tpu_custom_call" | custom-call | tf_op jit(solution)/shard_map/planes/pallas_call | solution.py:139
  9.6 0.0 collective-permute-done.1.yhalo_ref
  9.7 1.6 %collective-permute-start.3 = (bf16[80,128]{1,0:T(8,128)(2,1)S(1)}, bf16[80,128]{1,0:T(8,128)(2,1)S(1)}, u32[]{:S(2)}, u32[]{:S(2)}) collective-permute-start(bf16[80,128]{1,0:T(8,128)(2,1)S(1)} %pad_add_fusion), channel_id=1, source_target_pairs={{0,16},{16,0},{1,17},{17,1},{2,18},{18,2},{3,19},{19,3},{4,20},{20... | collective-permute-start | bytes 61448 | tf_op jit(solution)/shard_map/ppermute | solution.py:613
  11.3 1.5 %collective-permute-start.4 = (bf16[16,128]{1,0:T(8,128)(2,1)S(1)}, bf16[16,128]{1,0:T(8,128)(2,1)S(1)}, u32[]{:S(2)}, u32[]{:S(2)}) collective-permute-start(bf16[16,128]{1,0:T(8,128)(2,1)S(1)} %pad_add_fusion.1), channel_id=1, source_target_pairs={{0,17},{1,18},{2,19},{3,16},{16,1},{17,2},{18,3},{19,0},{4,21},{5,... | collective-permute-start | bytes 12296 | tf_op jit(solution)/shard_map/ppermute | solution.py:614
  12.8 0.0 copy-done.3
  12.8 0.0 copy-done.4
  12.8 2.4 %interior.1 = (f32[4,512,128]{2,1,0:T(8,128)S(1)}, f32[272,128]{1,0:T(8,128)S(1)}, bf16[256,512]{1,0:T(8,128)(2,1)S(1)}, bf16[384,256]{1,0:T(8,128)(2,1)S(1)}, b...) custom-call(bf16[7,512,256]{2,1,0:T(8,128)(2,1)S(1)} %get-tuple-element.26.cells_ref, ...), custom_call_target="tpu_custom_call" | custom-call | flops 1610612736 | bytes 6291456 | tf_op jit(solution)/shard_map/interior/pallas_call | solution.py:234
  15.3 0.2 collective-permute-done.2.yzhalo_ref
  15.5 2.1 %collective-permute-done.4.xzhalo_ref = bf16[16,128]{1,0:T(8,128)(2,1)S(1)} collective-permute-done((bf16[16,128]{1,0:T(8,128)(2,1)S(1)}, bf16[16,128]{1,0:T(8,128)(2,1)S(1)}, u32[]{:S(2)}, u32[]{:S(2)}) %collective-permute-start.4) | collective-permute-done | bytes 4128 | tf_op jit(solution)/shard_map/ppermute | solution.py:614
  17.6 0.0 collective-permute-done.3.xhalo_ref
  17.6 0.0 collective-permute-done.zhalo_ref
  17.6 0.9 %finish.1 = (f32[4,512,128]{2,1,0:T(8,128)S(1)}, f32[40,128]{1,0:T(8,128)S(1)}, f32[2,32,128]{2,1,0:T(8,128)S(1)}) custom-call(f32[4,512,128]{2,1,0:T(8,128)S(1)} %get-tuple-element.28.part_ref, f32[272,128]{1,0:T(8,128)S(1)} %get-tuple-element.29.stat_ref, bf16[512,256]{1,0:T(8,128)(2,1)S(1)} %collective-permute-done.zhalo_ref, ...), custom_call_target="tpu_custom_call" | custom-call | tf_op jit(solution)/shard_map/finish/pallas_call | solution.py:339
  18.5 0.0 collective-permute-start.5
  18.6 2.1 %collective-permute-start.7 = (f32[512,128]{1,0:T(8,128)S(1)}, f32[512,128]{1,0:T(8,128)S(1)}, u32[]{:S(2)}, u32[]{:S(2)}) collective-permute-start(f32[512,128]{1,0:T(8,128)S(1)} %get-tuple-element.46), channel_id=1, source_target_pairs={{0,1},{1,0},{2,3},{3,2},{4,5},{5,4},{6,7},{7,6},{8,9},{9,8},{10,11... | collective-permute-start | bytes 786440 | tf_op jit(solution)/shard_map/ppermute | solution.py:567
  20.7 0.0 collective-permute-start.8
  20.7 1.9 %collective-permute-done.5 = f32[40,128]{1,0:T(8,128)S(1)} collective-permute-done((f32[40,128]{1,0:T(8,128)S(1)}, f32[40,128]{1,0:T(8,128)S(1)}, u32[]{:S(2)}, u32[]{:S(2)}) %collective-permute-start.5) | collective-permute-done | bytes 20512 | tf_op jit(solution)/shard_map/ppermute | solution.py:537
  22.6 0.4 collective-permute-start.6
  23.0 0.0 copy-start.1
  23.0 0.0 copy-start.2
  23.0 5.2 %collective-permute-done.6 = f32[40,128]{1,0:T(8,128)S(1)} collective-permute-done((f32[40,128]{1,0:T(8,128)S(1)}, f32[40,128]{1,0:T(8,128)S(1)}, u32[]{:S(2)}, u32[]{:S(2)}) %collective-permute-start.6) | collective-permute-done | bytes 20512 | tf_op jit(solution)/shard_map/ppermute | solution.py:539
  28.2 0.0 collective-permute-done.7.z1_ref
  28.2 0.0 collective-permute-done.8.z2_ref
  28.3 0.1 collective-permute-start.9
  28.4 0.6 %collective-permute-start.11 = (f32[384,128]{1,0:T(8,128)S(1)}, f32[384,128]{1,0:T(8,128)S(1)}, u32[]{:S(2)}, u32[]{:S(2)}) collective-permute-start(f32[384,128]{1,0:T(8,128)S(1)} %get-tuple-element.59), channel_id=1, source_target_pairs={{4,8},{8,4},{20,24},{24,20},{0,16},{12,28},{16,0},{28,12},{5,9},{9... | collective-permute-start | bytes 589832 | tf_op jit(solution)/shard_map/ppermute | solution.py:518
  29.0 0.8 %collective-permute-done.9 = f32[424,128]{1,0:T(8,128)S(1)} collective-permute-done((f32[424,128]{1,0:T(8,128)S(1)}, f32[424,128]{1,0:T(8,128)S(1)}, u32[]{:S(2)}, u32[]{:S(2)}) %collective-permute-start.9) | collective-permute-done | bytes 217120 | tf_op jit(solution)/shard_map/ppermute | solution.py:554
  29.9 0.2 collective-permute-start.10
  30.1 3.1 %collective-permute-done.10 = f32[40,128]{1,0:T(8,128)S(1)} collective-permute-done((f32[40,128]{1,0:T(8,128)S(1)}, f32[40,128]{1,0:T(8,128)S(1)}, u32[]{:S(2)}, u32[]{:S(2)}) %collective-permute-start.10) | collective-permute-done | bytes 20512 | tf_op jit(solution)/shard_map/ppermute | solution.py:539
  33.3 0.9 %collective-permute-done.11.y2_ref = f32[384,128]{1,0:T(8,128)S(1)} collective-permute-done((f32[384,128]{1,0:T(8,128)S(1)}, f32[384,128]{1,0:T(8,128)S(1)}, u32[]{:S(2)}, u32[]{:S(2)}) %collective-permute-start.11) | collective-permute-done | bytes 196640 | tf_op jit(solution)/shard_map/ppermute | solution.py:518
  34.3 0.6 %collective-permute-start.12 = (f32[104,128]{1,0:T(8,128)S(1)}, f32[104,128]{1,0:T(8,128)S(1)}, u32[]{:S(2)}, u32[]{:S(2)}) collective-permute-start(f32[104,128]{1,0:T(8,128)S(1)} %pad_maximum_fusion.1), channel_id=1, source_target_pairs={{0,16},{16,0},{1,17},{17,1},{2,18},{18,2},{3,19},{19,3},{4,20},{20... | collective-permute-start | bytes 159752 | tf_op jit(solution)/shard_map/ppermute | solution.py:554
  34.9 3.6 %collective-permute-done.12 = f32[104,128]{1,0:T(8,128)S(1)} collective-permute-done((f32[104,128]{1,0:T(8,128)S(1)}, f32[104,128]{1,0:T(8,128)S(1)}, u32[]{:S(2)}, u32[]{:S(2)}) %collective-permute-start.12) | collective-permute-done | bytes 53280 | tf_op jit(solution)/shard_map/ppermute | solution.py:554
  38.5 0.0 copy-done.1
  38.5 0.0 copy-done.2
  38.5 6.4 %block.1 = bf16[4,512,128]{2,1,0:T(8,128)(2,1)} custom-call(f32[40,128]{1,0:T(8,128)S(1)} %slice_add_fusion.mom_ref, f32[1,128]{1,0:T(1,128)S(1)} %bitcast.74, f32[1,128]{1,0:T(1,128)S(1)} %bitcast.75, f32[4,512,128]{2,1,0:T(8,128)S(1)} %get-tuple-element.37.feat_ref, f32[512,128]{1,0:T(8,128)S(1)} %collective-permute-done.7.z1_ref, ...), custom_call_target="tpu_custom_call" | custom-call | tf_op jit(solution)/shard_map/block/pallas_call | solution.py:478
  (34 shorter events, 0.3 us)
Async XLA Ops:
  0.0 1.6 %copy-start = (bf16[64,8,16,128]{3,2,1,0:T(8,128)(2,1)S(1)}, bf16[64,8,16,128]{3,2,1,0:T(8,128)(2,1)}, u32[]{:S(2)}) copy-start(bf16[64,8,16,128]{3,2,1,0:T(8,128)(2,1)} %field_ref.3) | copy-start | bytes 6291460
  1.6 11.2 %copy-start.3 = (bf16[3,3,3,128,128]{4,3,2,1,0:T(8,128)(2,1)S(1)}, bf16[3,3,3,128,128]{4,3,2,1,0:T(8,128)(2,1)}, u32[]{:S(2)}) copy-start(bf16[3,3,3,128,128]{4,3,2,1,0:T(8,128)(2,1)} %param.9) | copy-start | bytes 2654212
  1.6 11.2 %copy-start.4 = (bf16[3,3,3,64,128]{4,3,2,1,0:T(8,128)(2,1)S(1)}, bf16[3,3,3,64,128]{4,3,2,1,0:T(8,128)(2,1)}, u32[]{:S(2)}) copy-start(bf16[3,3,3,64,128]{4,3,2,1,0:T(8,128)(2,1)} %w_ref.1) | copy-start | bytes 1327108
  2.2 7.4 %collective-permute-start.1 = (bf16[512,128]{1,0:T(8,128)(2,1)S(1)}, bf16[512,128]{1,0:T(8,128)(2,1)S(1)}, u32[]{:S(2)}, u32[]{:S(2)}) collective-permute-start(bf16[512,128]{1,0:T(8,128)(2,1)S(1)} %get-tuple-element.30), channel_id=1, source_target_pairs={{0,4},{4,8},{8,12},{12,0},{1,5},{5,9},{9,13},{13,1},{2,6},{6,10},{... | collective-permute-start | bytes 393224 | tf_op jit(solution)/shard_map/ppermute | solution.py:611
  2.7 14.8 %collective-permute-start = (bf16[512,256]{1,0:T(8,128)(2,1)S(1)}, bf16[512,256]{1,0:T(8,128)(2,1)S(1)}, u32[]{:S(2)}, u32[]{:S(2)}) collective-permute-start(bf16[512,256]{1,0:T(8,128)(2,1)S(1)} %get-tuple-element.27.last_ref), channel_id=1, source_target_pairs={{0,1},{1,2},{2,3},{3,0},{4,5},{5,6},{6,7},{7,4},{8,9},{9,10},{10,1... | collective-permute-start | bytes 786440 | tf_op jit(solution)/shard_map/ppermute | solution.py:610
  5.4 10.1 %collective-permute-start.2 = (bf16[64,128]{1,0:T(8,128)(2,1)S(1)}, bf16[64,128]{1,0:T(8,128)(2,1)S(1)}, u32[]{:S(2)}, u32[]{:S(2)}) collective-permute-start(bf16[64,128]{1,0:T(8,128)(2,1)S(1)} %slice.109), channel_id=1, source_target_pairs={{0,5},{1,6},{2,7},{3,4},{4,9},{5,10},{6,11},{7,8},{8,13},{9,14},{1... | collective-permute-start | bytes 49160 | tf_op jit(solution)/shard_map/ppermute | solution.py:609
  9.7 7.9 %collective-permute-start.3 = (bf16[80,128]{1,0:T(8,128)(2,1)S(1)}, bf16[80,128]{1,0:T(8,128)(2,1)S(1)}, u32[]{:S(2)}, u32[]{:S(2)}) collective-permute-start(bf16[80,128]{1,0:T(8,128)(2,1)S(1)} %pad_add_fusion), channel_id=1, source_target_pairs={{0,16},{16,0},{1,17},{17,1},{2,18},{18,2},{3,19},{19,3},{4,20},{20... | collective-permute-start | bytes 61448 | tf_op jit(solution)/shard_map/ppermute | solution.py:613
  11.3 6.3 %collective-permute-start.4 = (bf16[16,128]{1,0:T(8,128)(2,1)S(1)}, bf16[16,128]{1,0:T(8,128)(2,1)S(1)}, u32[]{:S(2)}, u32[]{:S(2)}) collective-permute-start(bf16[16,128]{1,0:T(8,128)(2,1)S(1)} %pad_add_fusion.1), channel_id=1, source_target_pairs={{0,17},{1,18},{2,19},{3,16},{16,1},{17,2},{18,3},{19,0},{4,21},{5,... | collective-permute-start | bytes 12296 | tf_op jit(solution)/shard_map/ppermute | solution.py:614
  18.5 4.1 %collective-permute-start.5 = (f32[40,128]{1,0:T(8,128)S(1)}, f32[40,128]{1,0:T(8,128)S(1)}, u32[]{:S(2)}, u32[]{:S(2)}) collective-permute-start(f32[40,128]{1,0:T(8,128)S(1)} %get-tuple-element.35), channel_id=1, source_target_pairs={{0,1},{1,0},{2,3},{3,2},{4,5},{5,4},{6,7},{7,6},{8,9},{9,8},{10,11... | collective-permute-start | bytes 61448 | tf_op jit(solution)/shard_map/ppermute | solution.py:537
  18.6 9.6 %collective-permute-start.7 = (f32[512,128]{1,0:T(8,128)S(1)}, f32[512,128]{1,0:T(8,128)S(1)}, u32[]{:S(2)}, u32[]{:S(2)}) collective-permute-start(f32[512,128]{1,0:T(8,128)S(1)} %get-tuple-element.46), channel_id=1, source_target_pairs={{0,1},{1,0},{2,3},{3,2},{4,5},{5,4},{6,7},{7,6},{8,9},{9,8},{10,11... | collective-permute-start | bytes 786440 | tf_op jit(solution)/shard_map/ppermute | solution.py:567
  20.7 7.5 %collective-permute-start.8 = (f32[512,128]{1,0:T(8,128)S(1)}, f32[512,128]{1,0:T(8,128)S(1)}, u32[]{:S(2)}, u32[]{:S(2)}) collective-permute-start(f32[512,128]{1,0:T(8,128)S(1)} %get-tuple-element.45), channel_id=1, source_target_pairs={{1,2},{2,1},{5,6},{6,5},{9,10},{10,9},{13,14},{14,13},{0,4},{3,7},... | collective-permute-start | bytes 786440 | tf_op jit(solution)/shard_map/ppermute | solution.py:518
  22.6 5.6 %collective-permute-start.6 = (f32[40,128]{1,0:T(8,128)S(1)}, f32[40,128]{1,0:T(8,128)S(1)}, u32[]{:S(2)}, u32[]{:S(2)}) collective-permute-start(f32[40,128]{1,0:T(8,128)S(1)} %add.75), channel_id=1, source_target_pairs={{0,3},{1,2},{2,1},{3,0},{4,7},{5,6},{6,5},{7,4},{8,11},{9,10},{10,... | collective-permute-start | bytes 61448 | tf_op jit(solution)/shard_map/ppermute | solution.py:539
  23.0 15.5 %copy-start.1 = (f32[128]{0:T(128)S(1)}, f32[128]{0:T(128)}, u32[]{:S(2)}) copy-start(f32[128]{0:T(128)} %param.7) | copy-start | bytes 1540
  23.0 15.5 %copy-start.2 = (f32[128]{0:T(128)S(1)}, f32[128]{0:T(128)}, u32[]{:S(2)}) copy-start(f32[128]{0:T(128)} %param.8) | copy-start | bytes 1540
  28.3 1.5 %collective-permute-start.9 = (f32[424,128]{1,0:T(8,128)S(1)}, f32[424,128]{1,0:T(8,128)S(1)}, u32[]{:S(2)}, u32[]{:S(2)}) collective-permute-start(f32[424,128]{1,0:T(8,128)S(1)} %pad_maximum_fusion), channel_id=1, source_target_pairs={{0,4},{4,0},{8,12},{12,8},{1,5},{5,1},{9,13},{13,9},{2,6},{6,2},{1... | collective-permute-start | bytes 651272 | tf_op jit(solution)/shard_map/ppermute | solution.py:554
  28.4 5.7 %collective-permute-start.11 = (f32[384,128]{1,0:T(8,128)S(1)}, f32[384,128]{1,0:T(8,128)S(1)}, u32[]{:S(2)}, u32[]{:S(2)}) collective-permute-start(f32[384,128]{1,0:T(8,128)S(1)} %get-tuple-element.59), channel_id=1, source_target_pairs={{4,8},{8,4},{20,24},{24,20},{0,16},{12,28},{16,0},{28,12},{5,9},{9... | collective-permute-start | bytes 589832 | tf_op jit(solution)/shard_map/ppermute | solution.py:518
  29.9 3.4 %collective-permute-start.10 = (f32[40,128]{1,0:T(8,128)S(1)}, f32[40,128]{1,0:T(8,128)S(1)}, u32[]{:S(2)}, u32[]{:S(2)}) collective-permute-start(f32[40,128]{1,0:T(8,128)S(1)} %slice_add_fusion.1), channel_id=1, source_target_pairs={{0,12},{4,8},{8,4},{12,0},{1,13},{5,9},{9,5},{13,1},{2,14},{6,10},... | collective-permute-start | bytes 61448 | tf_op jit(solution)/shard_map/ppermute | solution.py:539
  34.3 4.2 %collective-permute-start.12 = (f32[104,128]{1,0:T(8,128)S(1)}, f32[104,128]{1,0:T(8,128)S(1)}, u32[]{:S(2)}, u32[]{:S(2)}) collective-permute-start(f32[104,128]{1,0:T(8,128)S(1)} %pad_maximum_fusion.1), channel_id=1, source_target_pairs={{0,16},{16,0},{1,17},{17,1},{2,18},{18,2},{3,19},{19,3},{4,20},{20... | collective-permute-start | bytes 159752 | tf_op jit(solution)/shard_map/ppermute | solution.py:554
